TPU v7x, 32 devices: a whole 2x2x4 slice. The times are simulated.
32 devices in a mesh: strips: 2 (over y), spax: 16 (over z, x, core).
Axes of the slice: x: 2, y: 2, z: 4, core: 2. Of those that a mesh axis runs over, the one named last changes fastest.
Arguments:
- cube: float32 [4096, 3584], P('strips', 'spax'), parts along dimension 0, may hold values from -6 to 6
- templates: float32 [256, 3584], replicated, may hold values from -0.5 to 6.5
- bin_id: int32 [4096], P('strips'), parts along dimension 0, may hold values from 0 to 511, never falling along the last dimension, each value on 1 to 16 neighbouring positions
- owner_bins: int32 [1024], P('strips'), parts along dimension 0, may hold values from 0 to 511, each once
- line_start: int32 [8, 4096], P(None, 'strips'), parts along dimension 1, may hold values from 0 to 3536
- line_width: int32 [8, 4096], P(None, 'strips'), parts along dimension 1, may hold values from 9 to 48
Outputs:
- weights: float32 [1024, 256], P(('strips', 'spax')), parts along dimension 0
- moments: float32 [24, 4096], P(None, ('strips', 'spax')), parts along dimension 1
There are 2 independent parts, one for each index of `strips`. A program takes and returns all parts, laid end to end along the dimension named above; an argument that names none is the same for every part. Nothing has to cross between parts.
All inputs are finite; a program needn't handle non-finite values.
Results may differ from a plain program's by a relative error of at most 0.0003.
Values sent between devices are 32-bit elements; how exact they have to be, the bound alone decides.
No kernel may reach another device: no remote copies, remote signals or barrier semaphores. Data moves between devices by JAX's collectives and lax.ppermute only.
A program may use at most 128 MiB of HBM per device.

v0:
```python
import jax
import jax.numpy as jnp
from jax import lax
from jax.sharding import PartitionSpec as P


def line_moments(residual, wave_index, starts, widths):
    zeroth = []
    first = []
    second = []
    for line in range(starts.shape[0]):
        begin = starts[line][:, None]
        span = widths[line][:, None]
        inside = (wave_index[None, :] >= begin) & (wave_index[None, :] < begin + span)
        masked = jnp.where(inside, residual, jnp.zeros_like(residual))
        velocity = (2.0 * (wave_index[None, :] - begin).astype(jnp.float32) + 1.0) / span.astype(
            jnp.float32
        ) - 1.0
        weighted = masked * velocity
        zeroth.append(jnp.sum(masked, axis=1))
        first.append(jnp.sum(weighted, axis=1))
        second.append(jnp.sum(weighted * velocity, axis=1))
    return jnp.stack(zeroth + first + second, axis=0)


def shards(cube, templates, bin_id, owner_bins, line_start, line_width):
    devices = lax.axis_size("spax")
    device = lax.axis_index("spax")
    spaxels = cube.shape[0]
    slice_width = cube.shape[1]
    total_bins = owner_bins.shape[0]
    full_width = templates.shape[1]
    gram = jnp.dot(templates, templates.T, precision=lax.Precision.HIGHEST) / full_width
    factor = jnp.linalg.cholesky(gram)
    slot_of_bin = (
        jnp.zeros((total_bins,), jnp.int32)
        .at[owner_bins]
        .set(jnp.arange(total_bins, dtype=jnp.int32))
    )
    owned_spaxels = spaxels // devices
    own_widths = lax.dynamic_slice_in_dim(line_width, device * owned_spaxels, owned_spaxels, 1)
    divisor = jnp.concatenate([own_widths, own_widths, own_widths], axis=0).astype(jnp.float32)
    counts = jax.ops.segment_sum(
        jnp.ones((spaxels,), jnp.float32), bin_id, total_bins, indices_are_sorted=True
    )
    bin_sums = jax.ops.segment_sum(cube, bin_id, total_bins, indices_are_sorted=True)
    slot_means = jnp.take(bin_sums / counts[:, None], owner_bins, axis=0)
    my_templates = lax.dynamic_slice_in_dim(templates, device * slice_width, slice_width, 1)
    projections = lax.psum_scatter(
        jnp.dot(slot_means, my_templates.T, precision=lax.Precision.HIGHEST) / full_width,
        "spax",
        scatter_dimension=0,
        tiled=True,
    )
    weights = jax.scipy.linalg.cho_solve((factor, True), projections.T).T
    slot_continua = jnp.dot(
        lax.all_gather(weights, "spax", axis=0, tiled=True),
        my_templates,
        precision=lax.Precision.HIGHEST,
    )
    residual = cube - jnp.take(slot_continua, jnp.take(slot_of_bin, bin_id), axis=0)
    wave_index = device * slice_width + jnp.arange(slice_width, dtype=jnp.int32)
    partial_sums = line_moments(residual, wave_index, line_start, line_width)
    moment_total = lax.psum_scatter(partial_sums, "spax", scatter_dimension=1, tiled=True)
    return (weights, moment_total / divisor)


def solution(mesh):
    placed = (
        P("strips", "spax"),
        P(),
        P("strips"),
        P("strips"),
        P(None, "strips"),
        P(None, "strips"),
    )
    return jax.shard_map(
        shards,
        mesh=mesh,
        in_specs=placed,
        out_specs=(P(("strips", "spax"), None), P(None, ("strips", "spax"))),
        check_vma=False,
    )
```

profile of v0, /device:TPU:0, one launch (start us, length us, event | category | flops | bytes accessed | tf_op | source)
XLA Modules:
  0.0 238.8 jit_solution(4439000289109813261)
XLA Ops:
  8.6 1.9 copy.15
  10.5 12.5 %scatter_custom_fusion = f32[512,224]{1,0:T(8,128)S(1)} fusion(s32[2048]{0:T(1024)S(1)} %copy-done.3, f32[2048,224]{1,0:T(8,128)S(1)} %copy.15, f32[]{:T(128)} %constant.150.clone.1), kind=kCustom, calls=%fused_computation.60 | custom fusion | flops 458752 | bytes 458756 | tf_op jit(solution)/shard_map/scatter-add | solution.py:46
  23.0 14.7 %scatter_custom_fusion.1 = f32[512]{0:T(512)S(1)} fusion(s32[2048]{0:T(1024)S(1)} %copy-done.3, f32[2048]{0:T(1024)S(1)} %broadcast.192, f32[]{:T(128)} %constant.150.clone.1), kind=kCustom, calls=%fused_computation.98 | custom fusion | flops 2048 | bytes 2052 | tf_op jit(solution)/shard_map/scatter-add | solution.py:43
  37.8 1.6 gather_fusion
  39.4 2.5 %convolution_multiply_fusion = f32[512,256]{1,0:T(8,128)} fusion(f32[512,224]{1,0:T(8,128)S(1)} %gather_fusion, pred[512]{0:T(512)(128)(4,1)S(1)} %compare_and_fusion.1, f32[256,3584]{1,0:T(8,128)} %param.7, s32[]{:T(128)S(6)} %select_n.75), kind=kOutput, calls=%fused_computation.41 | convolution fusion | flops 352567296 | bytes 1245700 | tf_op jit(solution)/shard_map/dot_general | solution.py:50
  42.1 6.3 %convolution_multiply_fusion.1 = f32[256,256]{0,1:T(8,128)S(1)} fusion(f32[256,3584]{1,0:T(8,128)} %param.7), kind=kOutput, calls=%fused_computation.42 | convolution fusion | flops 2818637824 | bytes 3932160 | tf_op jit(solution)/shard_map/dot_general | solution.py:33
  48.6 11.7 %cholesky.50 = f32[128,128]{1,0:T(8,128)S(1)} custom-call(f32[128,128]{1,0:T(8,128)S(1)} %cholesky.118), custom_call_target="Cholesky" | custom-call | tf_op jit(solution)/shard_map/jit(cholesky)/cholesky | solution.py:34
  60.4 9.8 %custom-call.18 = f32[1,128,128]{1,2,0:T(8,128)S(1)} custom-call(f32[1,128,128]{2,1,0:T(8,128)S(1)} %get-tuple-element.82), custom_call_target="InvertDiagBlocksLowerTriangular" | custom-call | tf_op jit(solution)/shard_map/jit(cholesky)/cholesky | solution.py:34
  70.7 11.9 %cholesky.105 = f32[128,128]{1,0:T(8,128)S(1)} custom-call(f32[128,128]{1,0:T(8,128)S(1)} %convolution_subtract_fusion), custom_call_target="Cholesky" | custom-call | tf_op jit(solution)/shard_map/jit(cholesky)/cholesky | solution.py:34
  84.6 3.8 %while.1 = (s32[]{:T(128)}, f32[256,256]{1,0:T(8,128)S(1)}, s32[2,2]{1,0:T(2,128)S(1)}, f32[2,128,128]{2,1,0:T(8,128)S(1)}, s32[]{:T(128)}) while((s32[]{:T(128)}, f32[256,256]{1,0:T(8,128)S(1)}, s32[2,2]{1,0:T(2,128)S(1)}, f32[2,128,128]{2,1,0:T(8,128)S(1)}, s32[]{:T(128)}) %tuple.76), condition=%wide.while_cond, body=%wide.while_body.sunk | while | flops 2 | bytes 131181 | solution.py:55
  85.2 1.3 bitcast_dynamic-update-slice_fusion.2
  87.2 1.3 bitcast_dynamic-update-slice_fusion.2
  88.5 19.7 %custom-call.19 = f32[2,128,128]{1,2,0:T(8,128)S(1)} custom-call(f32[2,128,128]{2,1,0:T(8,128)S(1)} %get-tuple-element.9), custom_call_target="InvertDiagBlocksLowerTriangular" | custom-call | tf_op jit(solution)/shard_map/jit(_cho_solve)/triangular_solve | solution.py:55
  108.2 2.4 %scatter_custom_fusion.2 = s32[512]{0:T(512)S(1)} fusion(s32[512]{0:T(512)S(1)} %compare_select_fusion.2, s32[512]{0:T(512)S(1)} %iota.64, s32[]{:T(128)} %constant.154.clone.1), kind=kCustom, calls=%fused_computation.100 | custom fusion | bytes 2052 | tf_op jit(solution)/shard_map/scatter | solution.py:38
  110.9 13.2 %gather_fusion.1 = s32[2048]{0:T(1024)S(1)} fusion(s32[512]{0:T(512)S(1)} %scatter_custom_fusion.2, s32[2048]{0:T(1024)S(1)} %fusion.28), kind=kCustom, calls=%fused_computation.1 | custom fusion | bytes 24576 | tf_op jit(solution)/shard_map/jit(_take)/gather | solution.py:61
  125.1 0.9 convolution_subtract_fusion.2
  127.0 24.6 %all_gather.3 = f32[512,256]{1,0:T(8,128)S(1)} all-gather(f32[32,256]{1,0:T(8,128)S(1)} %maximum_bitcast_fusion), channel_id=1, replica_groups=mesh['strips'=2,'spax'=16] {'spax'}, dimensions={0}, use_global_device_ids=true | all-gather | bytes 557056 | tf_op jit(solution)/shard_map/all_gather | solution.py:57
  151.6 1.7 fusion.14
  153.3 6.6 %gather_fusion.2 = f32[2048,224]{1,0:T(8,128)S(1)} fusion(f32[512,224]{1,0:T(8,128)S(1)} %fusion.14, s32[2048]{0:T(1024)S(1)} %broadcast_clamp_fusion), kind=kCustom, calls=%fused_computation.2 | custom fusion | bytes 3678208 | tf_op jit(solution)/shard_map/jit(_take)/gather | solution.py:61
  160.0 11.2 %multiply_reduce_fusion = (f32[2048]{0:T(1024)S(1)}, f32[2048]{0:T(1024)S(1)}, f32[2048]{0:T(1024)S(1)}, f32[2048]{0:T(1024)S(1)}, f32[2048]{0:T(1024)S(1)}, /*i...) fusion(f32[2048]{0:T(1024)S(1)} %convert_element_type.106, ...), kind=kLoop, calls=%fused_computation.8 | loop fusion | flops 35293184 | bytes 5753728 | tf_op jit(solution)/shard_map/reduce_sum | solution.py:22
  171.2 6.2 %multiply_reduce_fusion.5 = (f32[2048]{0:T(1024)S(1)}, f32[2048]{0:T(1024)S(1)}, f32[2048]{0:T(1024)S(1)}, f32[2048]{0:T(1024)S(1)}, f32[2048]{0:T(1024)S(1)}, /...) fusion(f32[2048,224]{1,0:T(8,128)S(1)} %get-tuple-element.60, ...), kind=kLoop, calls=%fused_computation.13 | loop fusion | flops 20625408 | bytes 1983360 | tf_op jit(solution)/shard_map/reduce_sum | solution.py:22
  177.4 2.1 stack.99
  179.6 51.0 %reduce-scatter.5.cloned.1.call-done = f32[24,128]{1,0:T(8,128)} async-done(((f32[24,2048]{1,0:T(8,128)}), f32[24,128]{1,0:T(8,128)}) %reduce-scatter.5.cloned.1.call-update) | async-done | bytes 12304 | tf_op jit(solution)/shard_map/reduce_scatter | solution.py:64
  230.6 1.3 fusion.27
  (67 shorter events, 6.5 us)
Async XLA Ops:
  7.2 3.3 %copy-start.3 = (s32[2048]{0:T(1024)S(1)}, s32[2048]{0:T(1024)}, u32[]{:S(2)}) copy-start(s32[2048]{0:T(1024)} %param.8) | copy-start | bytes 24580
  7.2 117.0 %reduce-scatter.3.cloned.1.call-start = ((), (), s32[]{:S(2)}) async-start(), calls=%async_computation.2 | async-start | bytes 557056 | tf_op jit(solution)/shard_map/reduce_scatter | solution.py:49
  10.5 27.2 %copy-start = (f32[2048,224]{1,0:T(8,128)}, f32[2048,224]{1,0:T(8,128)S(1)}, u32[]{:S(2)}) copy-start(f32[2048,224]{1,0:T(8,128)S(1)} %copy.15) | copy-start | bytes 5505028
  41.9 188.7 %reduce-scatter.5.cloned.1.call-start = ((), (), s32[]{:S(2)}) async-start(), calls=%async_computation.3 | async-start | bytes 208896 | tf_op jit(solution)/shard_map/reduce_scatter | solution.py:64
  48.4 62.2 %copy-start.4 = (s32[8,2048]{1,0:T(8,128)S(1)}, s32[8,2048]{1,0:T(8,128)}, u32[]{:S(2)}) copy-start(s32[8,2048]{1,0:T(8,128)} %param.10) | copy-start | bytes 196612
  48.4 62.2 %copy-start.2 = (s32[8,2048]{1,0:T(8,128)S(1)}, s32[8,2048]{1,0:T(8,128)}, u32[]{:S(2)}) copy-start(s32[8,2048]{1,0:T(8,128)} %param.11) | copy-start | bytes 196612
  127.0 32.9 %copy-start.1 = (f32[32,256]{1,0:T(8,128)}, f32[32,256]{1,0:T(8,128)S(1)}, u32[]{:S(2)}) copy-start(f32[32,256]{1,0:T(8,128)S(1)} %maximum_bitcast_fusion) | copy-start | bytes 98308
Sparse Core Ops, SparseCore 0:
  42.0 59.0 reduce-scatter.2
  179.7 50.8 reduce-scatter.4
where the time goes:
time: 239 us
  other arithmetic  101 us (42%)
  waiting for transfers between devices  51.1 us (21%)
  local copies, waits for them, and re-layouts  32 us (13%)
  blocking collectives  24.6 us (10%)
  between operations  15.8 us (7%)
  matrix products  13.6 us (6%)
    reduce_scatter x1, waiting for transfers between devices, shards(): lax.psum_scatter(partial_sums, 'spax', scatter_dimension=1, tiled=True)  51 us
    another operation x6, other arithmetic, shards(): factor = jnp.linalg.cholesky(gram)  34.1 us
    all_gather x1, blocking collectives, shards(): lax.all_gather(weights, 'spax', axis=0, tiled=True)  24.6 us
    another operation x3, other arithmetic, shards(): weights = jax.scipy.linalg.cho_solve((factor, True), projections.T).T  19.7 us
    reduce_sum x2, other arithmetic, line_moments(): second.append(jnp.sum(weighted * velocity, axis=1))  17.4 us
    scatter-add x1, other arithmetic, shards(): jax.ops.segment_sum(jnp.ones((spaxels,), jnp.float32), bin_id, total_bins...  14.7 us
    gather x1, local copies, waits for them, and re-layouts, shards(): jnp.take(slot_of_bin, bin_id)  13.2 us
    scatter-add x1, other arithmetic, shards(): jax.ops.segment_sum(cube, bin_id, total_bins, indices_are_sorted=True)  12.5 us
  transfers between devices with their start and end apart: 2, of which 1 were waited for; matrix products, arithmetic and copies ran while one was open for 34% of the time, Pallas kernels for 0%

commit v1 on v0

v1 whole, which is shorter than its diff:
```python
import functools

import jax
import jax.numpy as jnp
from jax import lax
from jax.experimental import pallas as pl
from jax.experimental.pallas import tpu as pltpu
from jax.sharding import PartitionSpec as P

HIGHEST = lax.Precision.HIGHEST
F32 = jnp.float32
BF16 = jnp.bfloat16
LANES = 128
SUB = 8
VMEM_LIMIT = 48 * 1024 * 1024

NT = (((1,), (1,)), ((), ()))
NN = (((1,), (0,)), ((), ()))


def split3(x):
    hi = x.astype(BF16)
    rest = x - hi.astype(F32)
    mid = rest.astype(BF16)
    low = (rest - mid.astype(F32)).astype(BF16)
    return hi, mid, low


def dot(a, b, dims):
    return lax.dot_general(a, b, dims, preferred_element_type=F32)


def dot_f32(a, b, dims):
    return lax.dot_general(a, b, dims, precision=HIGHEST, preferred_element_type=F32)


def project_kernel(device_ref, bins_ref, owner_ref, cube_ref, templates_ref, out_ref, *, chunk):
    width, spaxels = cube_ref.shape
    slots = owner_ref.shape[0]
    full_width = templates_ref.shape[1]
    owner = owner_ref[...]
    sums = jnp.zeros((slots, width), F32)
    counts = jnp.zeros((slots, LANES), F32)
    for at in range(0, spaxels, chunk):
        here = owner == bins_ref[:, at : at + chunk]
        ones = jnp.where(here, 1.0, 0.0)
        for lane in range(0, chunk, LANES):
            counts = counts + ones[:, lane : lane + LANES]
        member = ones.astype(BF16)
        for part in split3(cube_ref[:, at : at + chunk]):
            sums = sums + dot(member, part, NT)
    means = sums / jnp.sum(counts, axis=1, keepdims=True)
    first = device_ref[0] * width
    window = min(full_width, -(-(width + LANES - 1) // LANES) * LANES)
    base = jnp.minimum(first // LANES * LANES, full_width - window)
    held = templates_ref[:, pl.ds(pl.multiple_of(base, LANES), window)]
    mine = pltpu.roll(held, window - (first - base), 1)[:, :width]
    out_ref[...] = dot_f32(means, mine, NT) * (1.0 / full_width)


def project(device, bins, owner, cube, templates):
    width, spaxels = cube.shape
    slots = owner.shape[0]
    block = min(slots, 512)
    whole = lambda i: (0, 0)
    return pl.pallas_call(
        functools.partial(project_kernel, chunk=min(spaxels, 512)),
        grid=(slots // block,),
        in_specs=[
            pl.BlockSpec(memory_space=pltpu.SMEM),
            pl.BlockSpec((1, spaxels), whole),
            pl.BlockSpec((block, 1), lambda i: (i, 0)),
            pl.BlockSpec((width, spaxels), whole),
            pl.BlockSpec(templates.shape, whole),
        ],
        out_specs=pl.BlockSpec((block, templates.shape[0]), lambda i: (i, 0)),
        out_shape=jax.ShapeDtypeStruct((slots, templates.shape[0]), F32),
        compiler_params=pltpu.CompilerParams(vmem_limit_bytes=VMEM_LIMIT),
        name="project",
    )(device, bins, owner, cube, templates)


def invert_tile(tile):
    size = tile.shape[0]
    count = size // SUB
    lanes = lax.broadcasted_iota(jnp.int32, (SUB, size), 1)
    rows_at = lax.broadcasted_iota(jnp.int32, (SUB, size), 0)
    rows = [tile[i * SUB : (i + 1) * SUB, :] for i in range(count)]
    for k in range(count):
        block = rows[k]
        first = k * SUB
        a = {}
        for i in range(SUB):
            for j in range(i, SUB):
                a[i, j] = jnp.broadcast_to(block[i : i + 1, first + j : first + j + 1], (SUB, size))

        def at(i, j):
            return a[(i, j) if i <= j else (j, i)]

        for p in range(SUB):
            inverse = 1.0 / a[p, p]
            others = [i for i in range(SUB) if i != p]
            scaled = {i: at(i, p) * inverse for i in others}
            old = {i: at(i, p) for i in others}
            for i in others:
                for j in others:
                    if i <= j:
                        a[i, j] = a[i, j] - scaled[i] * old[j]
            for i in others:
                a[(i, p) if i <= p else (p, i)] = scaled[i]
            a[p, p] = -inverse
        columns = []
        for j in range(SUB):
            column = at(0, j)
            for i in range(1, SUB):
                column = jnp.where(rows_at == i, at(i, j), column)
            columns.append(column)
        swept = jnp.zeros((SUB, size), F32)
        for j in range(SUB):
            swept = swept - columns[j] * jnp.broadcast_to(block[j : j + 1, :], (SUB, size))
        for j in range(SUB):
            swept = jnp.where(lanes == first + j, columns[j], swept)
        inside = (lanes >= first) & (lanes < first + SUB)
        for i in range(count):
            if i == k:
                continue
            new = jnp.where(inside, 0.0, rows[i])
            for j in range(SUB):
                spread = jnp.broadcast_to(rows[i][:, first + j : first + j + 1], (SUB, size))
                new = new - spread * jnp.broadcast_to(swept[j : j + 1, :], (SUB, size))
            rows[i] = new
        rows[k] = swept
    return -jnp.concatenate(rows, axis=0)


def gram_kernel(templates_ref, gram_ref, first_ref, *, chunk):
    count, full_width = templates_ref.shape
    even = jnp.zeros((count, count), F32)
    mixed = jnp.zeros((count, count), F32)
    for at in range(0, full_width, chunk):
        hi, mid, low = split3(templates_ref[:, at : at + chunk])
        even = even + (dot(hi, hi, NT) + dot(mid, mid, NT))
        mixed = mixed + (dot(hi, mid, NT) + dot(hi, low, NT))
    gram = (even + (mixed + mixed.T)) * (1.0 / full_width)
    gram_ref[...] = gram
    first_ref[...] = invert_tile(gram[:LANES, :LANES])


def finish_kernel(gram_ref, first_ref, out_ref):
    first = first_ref[...]
    side = gram_ref[:LANES, LANES:]
    half = dot_f32(first, side, NN)
    schur = gram_ref[LANES:, LANES:] - dot_f32(side.T, half, NN)
    last = invert_tile(schur)
    cross = dot_f32(half, last, NN)
    out_ref[:LANES, :LANES] = first + dot_f32(cross, half, NT)
    out_ref[:LANES, LANES:] = -cross
    out_ref[LANES:, :LANES] = -cross.T
    out_ref[LANES:, LANES:] = last


def in_vmem(kernel, shapes, name, *arrays):
    return pl.pallas_call(
        kernel,
        out_shape=shapes,
        compiler_params=pltpu.CompilerParams(vmem_limit_bytes=VMEM_LIMIT),
        name=name,
    )(*arrays)


def window_sums(read, rows, first, begin, span, unroll):
    lines = begin.shape[0]
    sub = lax.broadcasted_iota(jnp.int32, (SUB, LANES), 0)
    spans = [jnp.broadcast_to(span[j : j + 1], (SUB, LANES)).astype(F32) for j in range(lines)]
    offsets = [
        (2 * (first + sub - jnp.broadcast_to(begin[j : j + 1], (SUB, LANES))) + 1).astype(F32) - spans[j]
        for j in range(lines)
    ]

    def add(block, shift, sums):
        size = block.shape[0]
        out = []
        for j in range(lines):
            m = offsets[j][:size] + shift
            masked = jnp.where(jnp.abs(m) < spans[j][:size], block, 0.0)
            weighted = masked * m
            out += [sums[3 * j] + masked, sums[3 * j + 1] + weighted, sums[3 * j + 2] + weighted * m]
        return out

    def step(i, sums):
        for u in range(unroll):
            row = (i * unroll + u) * SUB
            shift = (2 * row) if isinstance(row, int) else (2 * row).astype(F32)
            sums = add(read(row, SUB), shift, sums)
        return sums

    sums = [jnp.zeros((SUB, LANES), F32)] * (3 * lines)
    full = rows // SUB
    if full > unroll:
        sums = lax.fori_loop(0, full // unroll, step, sums)
        done = full // unroll * unroll
    else:
        done = 0
    for i in range(done, full):
        sums = add(read(i * SUB, SUB), 2.0 * i * SUB, sums)
    out = [jnp.sum(x, axis=0, keepdims=True) for x in sums]
    if rows % SUB:
        zero = jnp.zeros((rows % SUB, LANES), F32)
        tail = add(read(full * SUB, rows % SUB), 2.0 * full * SUB, [zero] * (3 * lines))
        out = [x + jnp.sum(y, axis=0, keepdims=True) for x, y in zip(out, tail)]
    return [out[3 * j + k] for k in range(3) for j in range(lines)]


def cube_kernel(device_ref, begin_ref, span_ref, cube_ref, out_ref):
    width = cube_ref.shape[0]
    first = device_ref[0] * width

    def tile(i, carry):
        lanes = pl.ds(pl.multiple_of(i * LANES, LANES), LANES)
        sums = window_sums(
            lambda row, size: cube_ref[pl.ds(row, size), lanes],
            width,
            first,
            begin_ref[:, lanes],
            span_ref[:, lanes],
            28,
        )
        for r, value in enumerate(sums):
            out_ref[r : r + 1, lanes] = value
        return carry

    lax.fori_loop(0, cube_ref.shape[1] // LANES, tile, 0)


def cube_windows(device, begin, span, cube):
    vmem = pl.BlockSpec(memory_space=pltpu.VMEM)
    return pl.pallas_call(
        cube_kernel,
        in_specs=[pl.BlockSpec(memory_space=pltpu.SMEM), vmem, vmem, vmem],
        out_specs=vmem,
        out_shape=jax.ShapeDtypeStruct((3 * begin.shape[0], cube.shape[1]), F32),
        compiler_params=pltpu.CompilerParams(vmem_limit_bytes=VMEM_LIMIT),
        name="cube_windows",
    )(device, begin, span, cube)


def owner_kernel(
    bins_ref, owner_ref, begin_ref, span_ref, projections_ref, inverse_ref, rows_ref,
    weights_ref, out_ref, continuum_ref,
):
    inverse = inverse_ref[...]
    weights_ref[...] = dot_f32(projections_ref[: weights_ref.shape[0], :], inverse, NN)
    member = jnp.where(bins_ref[...] == owner_ref[...], 1.0, 0.0).astype(BF16)
    picked = jnp.zeros((bins_ref.shape[0], inverse.shape[0]), F32)
    for part in split3(projections_ref[...]):
        picked = picked + dot(member, part, NN)
    spaxel_weights = dot_f32(picked, inverse, NN)
    full_width = rows_ref.shape[0]
    step = 512
    for at in range(0, full_width, step):
        continuum_ref[at : at + step, :] = dot_f32(rows_ref[at : at + step, :], spaxel_weights, NT)
    sums = window_sums(
        lambda row, size: continuum_ref[pl.ds(pl.multiple_of(row, SUB), size), :],
        full_width,
        0,
        begin_ref[...],
        span_ref[...],
        28,
    )
    for r, value in enumerate(sums):
        out_ref[r : r + 1, :] = value


def owned(bins, owner, begin, span, projections, inverse, rows, own_slots):
    return pl.pallas_call(
        owner_kernel,
        out_shape=(
            jax.ShapeDtypeStruct((own_slots, inverse.shape[0]), F32),
            jax.ShapeDtypeStruct((3 * begin.shape[0], bins.shape[0]), F32),
        ),
        scratch_shapes=[pltpu.VMEM((rows.shape[0], bins.shape[0]), F32)],
        compiler_params=pltpu.CompilerParams(vmem_limit_bytes=VMEM_LIMIT),
        name="owned",
    )(bins, owner, begin, span, projections, inverse, rows)


def shards(cube, templates, bin_id, owner_bins, line_start, line_width):
    devices = lax.axis_size("spax")
    device = lax.axis_index("spax")
    spaxels = cube.shape[0]
    total_bins = owner_bins.shape[0]
    own_spaxels = spaxels // devices
    own_slots = total_bins // devices
    here = device.reshape(1).astype(jnp.int32)
    columns = cube.T

    partial = project(here, bin_id[None, :], owner_bins[:, None], columns, templates)
    received = lax.all_to_all(partial.reshape(devices, own_slots, -1), "spax", 0, 0)
    mine = jnp.sum(received, axis=0)

    partial_sums = cube_windows(here, line_start, line_width, columns)
    cube_sums = lax.psum_scatter(partial_sums, "spax", scatter_dimension=1, tiled=True)

    count = templates.shape[0]
    gram, first = in_vmem(
        functools.partial(gram_kernel, chunk=512),
        (jax.ShapeDtypeStruct((count, count), F32), jax.ShapeDtypeStruct((LANES, LANES), F32)),
        "gram",
        templates,
    )
    inverse = in_vmem(finish_kernel, jax.ShapeDtypeStruct((count, count), F32), "finish", gram, first)

    blocks = [mine]
    for k in range(1, devices):
        blocks.append(lax.ppermute(mine, "spax", [(d, d ^ k) for d in range(devices)]))
    projections = jnp.concatenate(blocks, axis=0)
    order = device ^ jnp.arange(devices, dtype=jnp.int32)
    owner_row = jnp.take(owner_bins.reshape(devices, own_slots), order, axis=0).reshape(1, total_bins)

    own = lambda x: lax.dynamic_slice_in_dim(x, device * own_spaxels, own_spaxels, x.ndim - 1)
    begin, span = own(line_start), own(line_width)
    weights, continuum_sums = owned(
        own(bin_id)[:, None], owner_row, begin, span, projections, inverse, templates.T, own_slots
    )
    scale = span.astype(F32)
    divisor = jnp.concatenate([scale, scale * scale, scale * scale * scale], axis=0)
    return (weights, (cube_sums - continuum_sums) / divisor)


def solution(mesh):
    placed = (
        P("strips", "spax"),
        P(),
        P("strips"),
        P("strips"),
        P(None, "strips"),
        P(None, "strips"),
    )
    return jax.shard_map(
        shards,
        mesh=mesh,
        in_specs=placed,
        out_specs=(P(("strips", "spax"), None), P(None, ("strips", "spax"))),
        check_vma=False,
    )
```

time: 239 us -> 100 us (0.42)
  other arithmetic: 101 us -> 1.47 us
  waiting for transfers between devices: 51.1 us -> 5.95 us
  Pallas kernels: 0 us -> 35.8 us
  starting transfers between devices: 0.26 us -> 28.3 us
  blocking collectives: 24.6 us -> 0 us
  local copies, waits for them, and re-layouts: 32 us -> 13.9 us
  matrix products: 13.6 us -> 0 us
    another operation x9 -> x0, other arithmetic: 53.9 us -> none  [the longest x6 34.1 us: shards(): factor = jnp.linalg.cholesky(gram)]
    reduce_scatter x1, waiting for transfers between devices: 51 us -> 0.01 us  [shards(): lax.psum_scatter(partial_sums, 'spax', scatter_dimension=1, tiled=True)]
    pallas_call x0 -> x5, Pallas kernels: none -> 35.8 us  [the longest x2 14.2 us: in_vmem(): pl.pallas_call(kernel, out_shape=shapes, compiler_params=pltpu.CompilerPa...]
    scatter-add x2 -> x0, other arithmetic: 27.1 us -> none  [the longest x1 14.7 us: shards(): jax.ops.segment_sum(jnp.ones((spaxels,), jnp.float32), bin_id, total_bins...]
    all_gather x1 -> x0, blocking collectives: 24.6 us -> none  [shards(): lax.all_gather(weights, 'spax', axis=0, tiled=True)]
    ppermute x0 -> x15, starting transfers between devices: none -> 20.9 us  [shards(): lax.ppermute(mine, 'spax', [(d, d ^ k) for d in range(devices)])]
    gather x3 -> x1, local copies, waits for them, and re-layouts: 21.4 us -> 0.56 us  [shards(): jnp.take(owner_bins.reshape(devices, own_slots), order, axis=0)]
    reduce_sum x2 -> x1, other arithmetic: 17.4 us -> 0.04 us  [shards(): mine = jnp.sum(received, axis=0)]
  transfers between devices with their start and end apart: 2 -> 17, of which waited for: 1 -> 3; matrix products, arithmetic and copies ran while one was open for 34% -> 7% of each run, Pallas kernels for 0% -> 30%
where the time goes in v1:
time: 100 us; the launch traced here: 99.6 us
  Pallas kernels  35.8 us (36%)
  starting transfers between devices  28.3 us (28%)
  between operations  14.2 us (14%)
  local copies, waits for them, and re-layouts  13.9 us (14%)
  waiting for transfers between devices  5.95 us (6%)
  other arithmetic  1.47 us (1%)
    ppermute x15, starting transfers between devices, shards(): lax.ppermute(mine, 'spax', [(d, d ^ k) for d in range(devices)])  20.9 us
    pallas_call x2, Pallas kernels, in_vmem(): pl.pallas_call(kernel, out_shape=shapes, compiler_params=pltpu.CompilerPa...  14.2 us
    unnamed x32, local copies, waits for them, and re-layouts  11.5 us
    pallas_call x1, Pallas kernels, owned(): pl.pallas_call(owner_kernel, out_shape=(jax.ShapeDtypeStruct((own_slots,...  8.76 us
    all_to_all x1, starting transfers between devices, shards(): lax.all_to_all(partial.reshape(devices, own_slots, -1), 'spax', 0, 0)  7.36 us
    pallas_call x1, Pallas kernels, cube_windows(): pl.pallas_call(cube_kernel, in_specs=[pl.BlockSpec(memory_space=pltpu.SME...  6.49 us
    pallas_call x1, Pallas kernels, project(): pl.pallas_call(functools.partial(project_kernel, chunk=min(spaxels, 512))...  6.36 us
    ppermute x15, waiting for transfers between devices, shards(): lax.ppermute(mine, 'spax', [(d, d ^ k) for d in range(devices)])  5.93 us
  transfers between devices with their start and end apart: 17, of which 3 were waited for; matrix products, arithmetic and copies ran while one was open for 7% of the time, Pallas kernels for 30%

profile of v1, /device:TPU:0, one launch (start us, length us, event | category | flops | bytes accessed | tf_op | source)
XLA Modules:
  0.0 99.6 jit_solution(6030118759593769554)
XLA Ops:
  7.2 0.8 copy.10.owner_ref
  8.0 1.5 %copy-done.2 = f32[2048,224]{0,1:T(8,128)S(1)} copy-done((f32[2048,224]{0,1:T(8,128)S(1)}, f32[2048,224]{0,1:T(8,128)}, u32[]{:S(2)}) %copy-start.2) | copy-done | bytes 1835032
  9.5 0.7 copy-done.6
  10.2 6.4 %project.1 = f32[512,256]{1,0:T(8,128)} custom-call(s32[1]{0:T(128)} %bitcast.2.device_ref, s32[1,2048]{1,0:T(1,128)S(1)} %bitcast.13, s32[512,1]{1,0:T(8,128)S(1)} %copy.10.owner_ref, f32[224,2048]{1,0:T(8,128)S(1)} %bitcast.11, f32[256,3584]{1,0:T(8,128)} %templates_ref.3), custom_call_target="tpu_custom_call" | custom-call | tf_op jit(solution)/shard_map/project/pallas_call | solution.py:66
  16.6 7.4 %all-to-all-start = ((f32[16,32,256]{2,1,0:T(8,128)}), f32[16,32,256]{2,1,0:T(8,128)S(1)}, u32[]{:S(2)}, u32[]{:S(2)}) async-start(f32[16,32,256]{2,1,0:T(8,128)} %bitcast.6), calls=%async_computation | async-start | bytes 1048576 | tf_op jit(solution)/shard_map/all_to_all | solution.py:298
  24.0 6.5 %cube_windows.1 = f32[24,2048]{1,0:T(8,128)} custom-call(s32[1]{0:T(128)} %bitcast.2.device_ref, s32[8,2048]{1,0:T(8,128)S(1)} %copy-done.4, s32[8,2048]{1,0:T(8,128)S(1)} %copy-done.5, f32[224,2048]{1,0:T(8,128)S(1)} %bitcast.12), custom_call_target="tpu_custom_call" | custom-call | tf_op jit(solution)/shard_map/cube_windows/pallas_call | solution.py:237
  30.6 2.0 %copy-done = f32[256,3584]{1,0:T(8,128)S(1)} copy-done((f32[256,3584]{1,0:T(8,128)S(1)}, f32[256,3584]{1,0:T(8,128)}, u32[]{:S(2)}) %copy-start) | copy-done | bytes 3670040
  32.7 8.6 %gram.1 = (f32[256,256]{1,0:T(8,128)S(1)}, f32[128,128]{1,0:T(8,128)S(1)}) custom-call(f32[256,3584]{1,0:T(8,128)S(1)} %copy-done), custom_call_target="tpu_custom_call" | custom-call | tf_op jit(solution)/shard_map/gram/pallas_call | solution.py:163
  41.3 5.2 %copy.11 = f32[256,3584]{0,1:T(8,128)} copy(f32[256,3584]{1,0:T(8,128)} %templates_ref.3) | data formatting | bytes 7340032 | tf_op args[1]
  46.5 0.8 dynamic-slice_bitcast_fusion
  47.4 0.6 gather_fusion
  48.1 5.5 %finish.1.inverse_ref = f32[256,256]{1,0:T(8,128)S(1)} custom-call(f32[256,256]{1,0:T(8,128)S(1)} %get-tuple-element.6.gram_ref, f32[128,128]{1,0:T(8,128)S(1)} %get-tuple-element.7.first_ref), custom_call_target="tpu_custom_call" | custom-call | tf_op jit(solution)/shard_map/finish/pallas_call | solution.py:163
  54.2 1.7 %collective-permute-start.1 = (f32[32,256]{1,0:T(8,128)S(1)}, f32[32,256]{1,0:T(8,128)S(1)}, u32[]{:S(2)}, u32[]{:S(2)}) collective-permute-start(f32[32,256]{1,0:T(8,128)S(1)} %reduce_sum.9), channel_id=1, source_target_pairs={{0,2},{1,3},{2,0},{3,1},{4,6},{5,7},{6,4},{7,5},{8,10},{9,11},{10,... | collective-permute-start | bytes 98312 | tf_op jit(solution)/shard_map/ppermute | solution.py:315
  55.9 1.7 %collective-permute-start.3 = (f32[32,256]{1,0:T(8,128)S(1)}, f32[32,256]{1,0:T(8,128)S(1)}, u32[]{:S(2)}, u32[]{:S(2)}) collective-permute-start(f32[32,256]{1,0:T(8,128)S(1)} %reduce_sum.9), channel_id=1, source_target_pairs={{0,4},{1,5},{2,6},{3,7},{4,0},{5,1},{6,2},{7,3},{8,12},{9,13},{10,... | collective-permute-start | bytes 98312 | tf_op jit(solution)/shard_map/ppermute | solution.py:315
  57.7 2.6 %collective-permute-start.5 = (f32[32,256]{1,0:T(8,128)S(1)}, f32[32,256]{1,0:T(8,128)S(1)}, u32[]{:S(2)}, u32[]{:S(2)}) collective-permute-start(f32[32,256]{1,0:T(8,128)S(1)} %reduce_sum.9), channel_id=1, source_target_pairs={{0,6},{1,7},{2,4},{3,5},{4,2},{5,3},{6,0},{7,1},{8,14},{9,15},{10,... | collective-permute-start | bytes 98312 | tf_op jit(solution)/shard_map/ppermute | solution.py:315
  60.3 2.5 %collective-permute-start.7 = (f32[32,256]{1,0:T(8,128)S(1)}, f32[32,256]{1,0:T(8,128)S(1)}, u32[]{:S(2)}, u32[]{:S(2)}) collective-permute-start(f32[32,256]{1,0:T(8,128)S(1)} %reduce_sum.9), channel_id=1, source_target_pairs={{0,8},{1,9},{2,10},{3,11},{4,12},{5,13},{6,14},{7,15},{8,0},{9,1},... | collective-permute-start | bytes 98312 | tf_op jit(solution)/shard_map/ppermute | solution.py:315
  63.4 3.1 %collective-permute-start.9 = (f32[32,256]{1,0:T(8,128)S(1)}, f32[32,256]{1,0:T(8,128)S(1)}, u32[]{:S(2)}, u32[]{:S(2)}) collective-permute-start(f32[32,256]{1,0:T(8,128)S(1)} %reduce_sum.9), channel_id=1, source_target_pairs={{0,10},{1,11},{2,8},{3,9},{4,14},{5,15},{6,12},{7,13},{8,2},{9,3},... | collective-permute-start | bytes 98312 | tf_op jit(solution)/shard_map/ppermute | solution.py:315
  66.7 3.4 %collective-permute-start.11 = (f32[32,256]{1,0:T(8,128)S(1)}, f32[32,256]{1,0:T(8,128)S(1)}, u32[]{:S(2)}, u32[]{:S(2)}) collective-permute-start(f32[32,256]{1,0:T(8,128)S(1)} %reduce_sum.9), channel_id=1, source_target_pairs={{0,12},{1,13},{2,14},{3,15},{4,8},{5,9},{6,10},{7,11},{8,4},{9,5},... | collective-permute-start | bytes 98312 | tf_op jit(solution)/shard_map/ppermute | solution.py:315
  70.6 4.0 %collective-permute-start.13 = (f32[32,256]{1,0:T(8,128)S(1)}, f32[32,256]{1,0:T(8,128)S(1)}, u32[]{:S(2)}, u32[]{:S(2)}) collective-permute-start(f32[32,256]{1,0:T(8,128)S(1)} %reduce_sum.9), channel_id=1, source_target_pairs={{0,14},{1,15},{2,12},{3,13},{4,10},{5,11},{6,8},{7,9},{8,6},{9,7},... | collective-permute-start | bytes 98312 | tf_op jit(solution)/shard_map/ppermute | solution.py:315
  75.2 2.0 %collective-permute-done.13 = f32[32,256]{1,0:T(8,128)S(1)} collective-permute-done((f32[32,256]{1,0:T(8,128)S(1)}, f32[32,256]{1,0:T(8,128)S(1)}, u32[]{:S(2)}, u32[]{:S(2)}) %collective-permute-start.13) | collective-permute-done | bytes 32800 | tf_op jit(solution)/shard_map/ppermute | solution.py:315
  77.2 3.4 %collective-permute-done.14 = f32[32,256]{1,0:T(8,128)S(1)} collective-permute-done((f32[32,256]{1,0:T(8,128)S(1)}, f32[32,256]{1,0:T(8,128)S(1)}, u32[]{:S(2)}, u32[]{:S(2)}) %collective-permute-start.14) | collective-permute-done | bytes 32800 | tf_op jit(solution)/shard_map/ppermute | solution.py:315
  80.7 2.0 %copy-done.1 = f32[256,3584]{0,1:T(8,128)S(1)} copy-done((f32[256,3584]{0,1:T(8,128)S(1)}, f32[256,3584]{0,1:T(8,128)}, u32[]{:S(2)}) %copy-start.1) | copy-done | bytes 3670040
  82.7 8.8 %owned.1 = (f32[32,256]{1,0:T(8,128)}, f32[24,128]{1,0:T(8,128)S(1)}) custom-call(s32[128,1]{1,0:T(8,128)S(1)} %copy.12.bins_ref, s32[1,512]{1,0:T(1,128)S(1)} %select_n.39.owner_ref, s32[8,128]{1,0:T(8,128)S(1)} %constant_dynamic-slice_fusion.1.begin_ref, s32[8,128]{1,0:T(8,128)S(1)} %get-tuple-element.11.span_ref, ...), custom_call_target="tpu_custom_call" | custom-call | tf_op jit(solution)/shard_map/owned/pallas_call | solution.py:275
  91.5 1.3 %maximum_divide_fusion = f32[24,128]{1,0:T(8,128)} fusion(f32[8,128]{1,0:T(8,128)S(1)} %get-tuple-element.13, f32[8,128]{1,0:T(8,128)S(1)} %get-tuple-element.12, f32[8,128]{1,0:T(8,128)S(1)} %get-tuple-element.10, f32[24,128]{1,0:T(8,128)} %reduce-scatter.2.cloned.1.call-done, f32[24,128]{1,0:T(8,128)S(1)} %get-tuple-element.9), kind=kLoop, calls=%fused_computation.17 | loop fusion | flops 12288 | bytes 49152 | tf_op jit(solution)/shard_map/div | solution.py:327
  (64 shorter events, 3.1 us)
Async XLA Ops:
  8.0 1.5 %copy-start.2 = (f32[2048,224]{0,1:T(8,128)S(1)}, f32[2048,224]{0,1:T(8,128)}, u32[]{:S(2)}) copy-start(f32[2048,224]{0,1:T(8,128)} %param.6) | copy-start | bytes 5505028
  10.2 13.8 %copy-start.3 = (f32[2048,224]{0,1:T(8,128)S(1)}, f32[2048,224]{0,1:T(8,128)}, u32[]{:S(2)}) copy-start(f32[2048,224]{0,1:T(8,128)} %param.6) | copy-start | bytes 5505028
  10.2 13.8 %copy-start.4 = (s32[8,2048]{1,0:T(8,128)S(1)}, s32[8,2048]{1,0:T(8,128)}, u32[]{:S(2)}) copy-start(s32[8,2048]{1,0:T(8,128)} %begin_ref.1) | copy-start | bytes 196612
  10.2 13.8 %copy-start.5 = (s32[8,2048]{1,0:T(8,128)S(1)}, s32[8,2048]{1,0:T(8,128)}, u32[]{:S(2)}) copy-start(s32[8,2048]{1,0:T(8,128)} %span_ref.1) | copy-start | bytes 196612
  10.2 20.3 %copy-start.7 = (s32[512]{0:T(512)S(1)}, s32[512]{0:T(512)}, u32[]{:S(2)}) copy-start(s32[512]{0:T(512)} %param.9) | copy-start | bytes 6148
  16.6 37.1 %all-to-all-start = ((f32[16,32,256]{2,1,0:T(8,128)}), f32[16,32,256]{2,1,0:T(8,128)S(1)}, u32[]{:S(2)}, u32[]{:S(2)}) async-start(f32[16,32,256]{2,1,0:T(8,128)} %bitcast.6), calls=%async_computation | async-start | bytes 1048576 | tf_op jit(solution)/shard_map/all_to_all | solution.py:298
  23.9 67.5 %reduce-scatter.2.cloned.1.call-start = ((), (), s32[]{:S(2)}) async-start(), calls=%async_computation.2 | async-start | bytes 208896 | tf_op jit(solution)/shard_map/reduce_scatter | solution.py:302
  30.6 2.0 %copy-start = (f32[256,3584]{1,0:T(8,128)S(1)}, f32[256,3584]{1,0:T(8,128)}, u32[]{:S(2)}) copy-start(f32[256,3584]{1,0:T(8,128)} %templates_ref.3) | copy-start | bytes 11010052
  53.7 4.0 %collective-permute-start = (f32[32,256]{1,0:T(8,128)S(1)}, f32[32,256]{1,0:T(8,128)S(1)}, u32[]{:S(2)}, u32[]{:S(2)}) collective-permute-start(f32[32,256]{1,0:T(8,128)S(1)} %reduce_sum.9), channel_id=1, source_target_pairs={{0,1},{1,0},{2,3},{3,2},{4,5},{5,4},{6,7},{7,6},{8,9},{9,8},{10,11... | collective-permute-start | bytes 98312 | tf_op jit(solution)/shard_map/ppermute | solution.py:315
  54.2 6.1 %collective-permute-start.1 = (f32[32,256]{1,0:T(8,128)S(1)}, f32[32,256]{1,0:T(8,128)S(1)}, u32[]{:S(2)}, u32[]{:S(2)}) collective-permute-start(f32[32,256]{1,0:T(8,128)S(1)} %reduce_sum.9), channel_id=1, source_target_pairs={{0,2},{1,3},{2,0},{3,1},{4,6},{5,7},{6,4},{7,5},{8,10},{9,11},{10,... | collective-permute-start | bytes 98312 | tf_op jit(solution)/shard_map/ppermute | solution.py:315
  55.9 4.5 %collective-permute-start.2 = (f32[32,256]{1,0:T(8,128)S(1)}, f32[32,256]{1,0:T(8,128)S(1)}, u32[]{:S(2)}, u32[]{:S(2)}) collective-permute-start(f32[32,256]{1,0:T(8,128)S(1)} %reduce_sum.9), channel_id=1, source_target_pairs={{0,3},{1,2},{2,1},{3,0},{4,7},{5,6},{6,5},{7,4},{8,11},{9,10},{10,... | collective-permute-start | bytes 98312 | tf_op jit(solution)/shard_map/ppermute | solution.py:315
  55.9 7.0 %collective-permute-start.3 = (f32[32,256]{1,0:T(8,128)S(1)}, f32[32,256]{1,0:T(8,128)S(1)}, u32[]{:S(2)}, u32[]{:S(2)}) collective-permute-start(f32[32,256]{1,0:T(8,128)S(1)} %reduce_sum.9), channel_id=1, source_target_pairs={{0,4},{1,5},{2,6},{3,7},{4,0},{5,1},{6,2},{7,3},{8,12},{9,13},{10,... | collective-permute-start | bytes 98312 | tf_op jit(solution)/shard_map/ppermute | solution.py:315
  57.6 5.8 %collective-permute-start.4 = (f32[32,256]{1,0:T(8,128)S(1)}, f32[32,256]{1,0:T(8,128)S(1)}, u32[]{:S(2)}, u32[]{:S(2)}) collective-permute-start(f32[32,256]{1,0:T(8,128)S(1)} %reduce_sum.9), channel_id=1, source_target_pairs={{0,5},{1,4},{2,7},{3,6},{4,1},{5,0},{6,3},{7,2},{8,13},{9,12},{10,... | collective-permute-start | bytes 98312 | tf_op jit(solution)/shard_map/ppermute | solution.py:315
  57.7 8.8 %collective-permute-start.5 = (f32[32,256]{1,0:T(8,128)S(1)}, f32[32,256]{1,0:T(8,128)S(1)}, u32[]{:S(2)}, u32[]{:S(2)}) collective-permute-start(f32[32,256]{1,0:T(8,128)S(1)} %reduce_sum.9), channel_id=1, source_target_pairs={{0,6},{1,7},{2,4},{3,5},{4,2},{5,3},{6,0},{7,1},{8,14},{9,15},{10,... | collective-permute-start | bytes 98312 | tf_op jit(solution)/shard_map/ppermute | solution.py:315
  60.3 6.4 %collective-permute-start.6 = (f32[32,256]{1,0:T(8,128)S(1)}, f32[32,256]{1,0:T(8,128)S(1)}, u32[]{:S(2)}, u32[]{:S(2)}) collective-permute-start(f32[32,256]{1,0:T(8,128)S(1)} %reduce_sum.9), channel_id=1, source_target_pairs={{0,7},{1,6},{2,5},{3,4},{4,3},{5,2},{6,1},{7,0},{8,15},{9,14},{10,... | collective-permute-start | bytes 98312 | tf_op jit(solution)/shard_map/ppermute | solution.py:315
  60.3 9.7 %collective-permute-start.7 = (f32[32,256]{1,0:T(8,128)S(1)}, f32[32,256]{1,0:T(8,128)S(1)}, u32[]{:S(2)}, u32[]{:S(2)}) collective-permute-start(f32[32,256]{1,0:T(8,128)S(1)} %reduce_sum.9), channel_id=1, source_target_pairs={{0,8},{1,9},{2,10},{3,11},{4,12},{5,13},{6,14},{7,15},{8,0},{9,1},... | collective-permute-start | bytes 98312 | tf_op jit(solution)/shard_map/ppermute | solution.py:315
  62.9 7.7 %collective-permute-start.8 = (f32[32,256]{1,0:T(8,128)S(1)}, f32[32,256]{1,0:T(8,128)S(1)}, u32[]{:S(2)}, u32[]{:S(2)}) collective-permute-start(f32[32,256]{1,0:T(8,128)S(1)} %reduce_sum.9), channel_id=1, source_target_pairs={{0,9},{1,8},{2,11},{3,10},{4,13},{5,12},{6,15},{7,14},{8,1},{9,0},... | collective-permute-start | bytes 98312 | tf_op jit(solution)/shard_map/ppermute | solution.py:315
  63.4 11.1 %collective-permute-start.9 = (f32[32,256]{1,0:T(8,128)S(1)}, f32[32,256]{1,0:T(8,128)S(1)}, u32[]{:S(2)}, u32[]{:S(2)}) collective-permute-start(f32[32,256]{1,0:T(8,128)S(1)} %reduce_sum.9), channel_id=1, source_target_pairs={{0,10},{1,11},{2,8},{3,9},{4,14},{5,15},{6,12},{7,13},{8,2},{9,3},... | collective-permute-start | bytes 98312 | tf_op jit(solution)/shard_map/ppermute | solution.py:315
  66.5 8.2 %collective-permute-start.10 = (f32[32,256]{1,0:T(8,128)S(1)}, f32[32,256]{1,0:T(8,128)S(1)}, u32[]{:S(2)}, u32[]{:S(2)}) collective-permute-start(f32[32,256]{1,0:T(8,128)S(1)} %reduce_sum.9), channel_id=1, source_target_pairs={{0,11},{1,10},{2,9},{3,8},{4,15},{5,14},{6,13},{7,12},{8,3},{9,2},... | collective-permute-start | bytes 98312 | tf_op jit(solution)/shard_map/ppermute | solution.py:315
  66.7 8.1 %collective-permute-start.11 = (f32[32,256]{1,0:T(8,128)S(1)}, f32[32,256]{1,0:T(8,128)S(1)}, u32[]{:S(2)}, u32[]{:S(2)}) collective-permute-start(f32[32,256]{1,0:T(8,128)S(1)} %reduce_sum.9), channel_id=1, source_target_pairs={{0,12},{1,13},{2,14},{3,15},{4,8},{5,9},{6,10},{7,11},{8,4},{9,5},... | collective-permute-start | bytes 98312 | tf_op jit(solution)/shard_map/ppermute | solution.py:315
  70.0 5.2 %collective-permute-start.12 = (f32[32,256]{1,0:T(8,128)S(1)}, f32[32,256]{1,0:T(8,128)S(1)}, u32[]{:S(2)}, u32[]{:S(2)}) collective-permute-start(f32[32,256]{1,0:T(8,128)S(1)} %reduce_sum.9), channel_id=1, source_target_pairs={{0,13},{1,12},{2,15},{3,14},{4,9},{5,8},{6,11},{7,10},{8,5},{9,4},... | collective-permute-start | bytes 98312 | tf_op jit(solution)/shard_map/ppermute | solution.py:315
  70.6 6.7 %collective-permute-start.13 = (f32[32,256]{1,0:T(8,128)S(1)}, f32[32,256]{1,0:T(8,128)S(1)}, u32[]{:S(2)}, u32[]{:S(2)}) collective-permute-start(f32[32,256]{1,0:T(8,128)S(1)} %reduce_sum.9), channel_id=1, source_target_pairs={{0,14},{1,15},{2,12},{3,13},{4,10},{5,11},{6,8},{7,9},{8,6},{9,7},... | collective-permute-start | bytes 98312 | tf_op jit(solution)/shard_map/ppermute | solution.py:315
  74.5 6.1 %collective-permute-start.14 = (f32[32,256]{1,0:T(8,128)S(1)}, f32[32,256]{1,0:T(8,128)S(1)}, u32[]{:S(2)}, u32[]{:S(2)}) collective-permute-start(f32[32,256]{1,0:T(8,128)S(1)} %reduce_sum.9), channel_id=1, source_target_pairs={{0,15},{1,14},{2,13},{3,12},{4,11},{5,10},{6,9},{7,8},{8,7},{9,6},... | collective-permute-start | bytes 98312 | tf_op jit(solution)/shard_map/ppermute | solution.py:315
  80.7 2.0 %copy-start.1 = (f32[256,3584]{0,1:T(8,128)S(1)}, f32[256,3584]{0,1:T(8,128)}, u32[]{:S(2)}) copy-start(f32[256,3584]{0,1:T(8,128)} %copy.11) | copy-start | bytes 11010052
  (1 other events, 0.7 us)
Sparse Core Ops, SparseCore 0:
  30.6 55.5 reduce-scatter.1

commit v2 on v1

v2 whole, which is shorter than its diff:
```python
import functools

import jax
import jax.numpy as jnp
from jax import lax
from jax.experimental import pallas as pl
from jax.experimental.pallas import tpu as pltpu
from jax.sharding import PartitionSpec as P

HIGHEST = lax.Precision.HIGHEST
F32 = jnp.float32
BF16 = jnp.bfloat16
LANES = 128
SUB = 8
VMEM_LIMIT = 20 * 1024 * 1024

NT = (((1,), (1,)), ((), ()))
NN = (((1,), (0,)), ((), ()))


def split3(x):
    hi = x.astype(BF16)
    rest = x - hi.astype(F32)
    mid = rest.astype(BF16)
    low = (rest - mid.astype(F32)).astype(BF16)
    return hi, mid, low


def dot(a, b, dims):
    return lax.dot_general(a, b, dims, preferred_element_type=F32)


def dot_f32(a, b, dims):
    return lax.dot_general(a, b, dims, precision=HIGHEST, preferred_element_type=F32)


def template_window(width, full_width):
    return min(full_width, -(-(width + LANES - 1) // LANES) * LANES)


def project_kernel(
    device_ref, bins_ref, owner_ref, cube_ref, templates_ref, out_ref,
    held_ref, window_ref, cube_sem, window_sem, *, chunk,
):
    width, spaxels = cube_ref.shape
    slots = owner_ref.shape[1]
    full_width = templates_ref.shape[1]
    first = device_ref[0] * width
    window = window_ref.shape[1]
    base = pl.multiple_of(jnp.minimum(first // LANES * LANES, full_width - window), LANES)
    chunks = spaxels // chunk

    def cube_copy(i):
        lanes = pl.ds(i * chunk, chunk)
        return pltpu.make_async_copy(cube_ref.at[:, lanes], held_ref.at[:, lanes], cube_sem.at[i])

    window_copy = pltpu.make_async_copy(templates_ref.at[:, pl.ds(base, window)], window_ref, window_sem)

    @pl.when(pl.program_id(0) == 0)
    def _():
        for i in range(chunks):
            cube_copy(i).start()
        window_copy.start()

    owner = jnp.broadcast_to(owner_ref[...], (SUB, slots)).T[:, :1]
    sums = jnp.zeros((slots, width), F32)
    counts = jnp.zeros((slots, LANES), F32)
    for i in range(chunks):
        here = owner == bins_ref[:, i * chunk : (i + 1) * chunk]
        ones = jnp.where(here, 1.0, 0.0)
        for lane in range(0, chunk, LANES):
            counts = counts + ones[:, lane : lane + LANES]
        member = ones.astype(BF16)

        @pl.when(pl.program_id(0) == 0)
        def _(i=i):
            cube_copy(i).wait()

        for part in split3(held_ref[:, i * chunk : (i + 1) * chunk]):
            sums = sums + dot(member, part, NT)
    means = sums / jnp.sum(counts, axis=1, keepdims=True)

    @pl.when(pl.program_id(0) == 0)
    def _():
        window_copy.wait()

    mine = pltpu.roll(window_ref[...], window - (first - base), 1)[:, :width]
    out_ref[...] = dot_f32(means, mine, NT) * (1.0 / full_width)


def project(device, bins, owner, cube, templates):
    width, spaxels = cube.shape
    slots = owner.shape[1]
    block = min(slots, 512)
    chunk = min(spaxels, 512)
    count, full_width = templates.shape
    return pl.pallas_call(
        functools.partial(project_kernel, chunk=chunk),
        grid=(slots // block,),
        in_specs=[
            pl.BlockSpec(memory_space=pltpu.SMEM),
            pl.BlockSpec((1, spaxels), lambda i: (0, 0)),
            pl.BlockSpec((1, block), lambda i: (0, i)),
            pl.BlockSpec(memory_space=pl.ANY),
            pl.BlockSpec(memory_space=pl.ANY),
        ],
        out_specs=pl.BlockSpec((block, count), lambda i: (i, 0)),
        out_shape=jax.ShapeDtypeStruct((slots, count), F32),
        scratch_shapes=[
            pltpu.VMEM((width, spaxels), F32),
            pltpu.VMEM((count, template_window(width, full_width)), F32),
            pltpu.SemaphoreType.DMA((spaxels // chunk,)),
            pltpu.SemaphoreType.DMA,
        ],
        compiler_params=pltpu.CompilerParams(vmem_limit_bytes=VMEM_LIMIT),
        name="project",
    )(device, bins, owner, cube, templates)


def invert_tile(tile):
    size = tile.shape[0]
    count = size // SUB
    lanes = lax.broadcasted_iota(jnp.int32, (SUB, size), 1)
    rows_at = lax.broadcasted_iota(jnp.int32, (SUB, size), 0)
    rows = [tile[i * SUB : (i + 1) * SUB, :] for i in range(count)]
    for k in range(count):
        block = rows[k]
        first = k * SUB
        a = {}
        for i in range(SUB):
            for j in range(i, SUB):
                a[i, j] = jnp.broadcast_to(block[i : i + 1, first + j : first + j + 1], (SUB, size))

        def at(i, j):
            return a[(i, j) if i <= j else (j, i)]

        for p in range(SUB):
            inverse = 1.0 / a[p, p]
            others = [i for i in range(SUB) if i != p]
            scaled = {i: at(i, p) * inverse for i in others}
            old = {i: at(i, p) for i in others}
            for i in others:
                for j in others:
                    if i <= j:
                        a[i, j] = a[i, j] - scaled[i] * old[j]
            for i in others:
                a[(i, p) if i <= p else (p, i)] = scaled[i]
            a[p, p] = -inverse
        columns = []
        for j in range(SUB):
            column = at(0, j)
            for i in range(1, SUB):
                column = jnp.where(rows_at == i, at(i, j), column)
            columns.append(column)
        swept = jnp.zeros((SUB, size), F32)
        for j in range(SUB):
            swept = swept - columns[j] * jnp.broadcast_to(block[j : j + 1, :], (SUB, size))
        for j in range(SUB):
            swept = jnp.where(lanes == first + j, columns[j], swept)
        inside = (lanes >= first) & (lanes < first + SUB)
        for i in range(count):
            if i == k:
                continue
            new = jnp.where(inside, 0.0, rows[i])
            for j in range(SUB):
                spread = jnp.broadcast_to(rows[i][:, first + j : first + j + 1], (SUB, size))
                new = new - spread * jnp.broadcast_to(swept[j : j + 1, :], (SUB, size))
            rows[i] = new
        rows[k] = swept
    return -jnp.concatenate(rows, axis=0)


def gram_kernel(templates_ref, gram_ref, first_ref, *, chunk):
    count, full_width = templates_ref.shape
    even = jnp.zeros((count, count), F32)
    mixed = jnp.zeros((count, count), F32)
    for at in range(0, full_width, chunk):
        hi, mid, low = split3(templates_ref[:, at : at + chunk])
        even = even + (dot(hi, hi, NT) + dot(mid, mid, NT))
        mixed = mixed + (dot(hi, mid, NT) + dot(hi, low, NT))
    gram = (even + (mixed + mixed.T)) * (1.0 / full_width)
    gram_ref[...] = gram
    first_ref[...] = invert_tile(gram[:LANES, :LANES])


def finish_kernel(gram_ref, first_ref, out_ref):
    first = first_ref[...]
    side = gram_ref[:LANES, LANES:]
    half = dot_f32(first, side, NN)
    schur = gram_ref[LANES:, LANES:] - dot_f32(side.T, half, NN)
    last = invert_tile(schur)
    cross = dot_f32(half, last, NN)
    out_ref[:LANES, :LANES] = first + dot_f32(cross, half, NT)
    out_ref[:LANES, LANES:] = -cross
    out_ref[LANES:, :LANES] = -cross.T
    out_ref[LANES:, LANES:] = last


def in_vmem(kernel, shapes, name, *arrays):
    return pl.pallas_call(
        kernel,
        out_shape=shapes,
        compiler_params=pltpu.CompilerParams(vmem_limit_bytes=VMEM_LIMIT),
        name=name,
    )(*arrays)


def window_sums(read, rows, first, begin, span):
    lines = begin.shape[0]
    sub = lax.broadcasted_iota(jnp.int32, (SUB, LANES), 0)
    spans = [jnp.broadcast_to(span[j : j + 1], (SUB, LANES)).astype(F32) for j in range(lines)]
    offsets = [
        (2 * (first + sub - jnp.broadcast_to(begin[j : j + 1], (SUB, LANES))) + 1).astype(F32) - spans[j]
        for j in range(lines)
    ]

    def add(block, shift, sums):
        size = block.shape[0]
        out = []
        for j in range(lines):
            m = offsets[j][:size] + shift
            masked = jnp.where(jnp.abs(m) < spans[j][:size], block, 0.0)
            weighted = masked * m
            out += [sums[3 * j] + masked, sums[3 * j + 1] + weighted, sums[3 * j + 2] + weighted * m]
        return out

    full = rows // SUB
    out = [jnp.zeros((1, LANES), F32)] * (3 * lines)
    if full:
        sums = [jnp.zeros((SUB, LANES), F32)] * (3 * lines)
        for i in range(full):
            sums = add(read(i * SUB, SUB), 2.0 * i * SUB, sums)
        out = [jnp.sum(x, axis=0, keepdims=True) for x in sums]
    if rows % SUB:
        sums = [jnp.zeros((rows % SUB, LANES), F32)] * (3 * lines)
        sums = add(read(full * SUB, rows % SUB), 2.0 * full * SUB, sums)
        out = [x + jnp.sum(y, axis=0, keepdims=True) for x, y in zip(out, sums)]
    return [out[3 * j + k] for k in range(3) for j in range(lines)]


def cube_kernel(device_ref, begin_ref, span_ref, cube_ref, out_ref, *, head):
    width = cube_ref.shape[0]
    own = cube_ref.shape[1] // out_ref.shape[0]
    tiles = own // LANES

    def owner(i, carry):
        for t in range(tiles):
            lanes = pl.ds(pl.multiple_of(i * own + t * LANES, LANES), LANES)
            sums = window_sums(
                lambda row, size: cube_ref[pl.ds(row, size), lanes],
                width,
                device_ref[0] * width,
                begin_ref[:, lanes],
                span_ref[:, lanes],
            )
            for r, value in enumerate(sums):
                out_ref[i, head + t * len(sums) + r : head + t * len(sums) + r + 1, :] = value
        return carry

    lax.fori_loop(0, out_ref.shape[0], owner, 0)


def cube_windows(device, begin, span, cube, devices, head):
    vmem = pl.BlockSpec(memory_space=pltpu.VMEM)
    tail = 3 * begin.shape[0] * (cube.shape[1] // devices // LANES)
    return pl.pallas_call(
        functools.partial(cube_kernel, head=head),
        in_specs=[pl.BlockSpec(memory_space=pltpu.SMEM), vmem, vmem, vmem],
        out_specs=vmem,
        out_shape=jax.ShapeDtypeStruct((devices, head + tail, LANES), F32),
        compiler_params=pltpu.CompilerParams(vmem_limit_bytes=VMEM_LIMIT),
        name="cube_windows",
    )(device, begin, span, cube)


def pack_kernel(received_ref, sums_ref, out_ref):
    total = received_ref[0]
    for i in range(1, received_ref.shape[0]):
        total = total + received_ref[i]
    slots, count = total.shape
    for half in range(count // LANES):
        value = total[:, half * LANES : (half + 1) * LANES]
        for i in range(received_ref.shape[0]):
            out_ref[i, half * slots : (half + 1) * slots, :] = value
    head = slots * (count // LANES)
    out_ref[:, head:, :] = sums_ref[:, head:, :]


def owner_kernel(
    device_ref, starts_ref, bins_ref, owner_ref, begin_ref, span_ref, received_ref, inverse_ref, templates_ref,
    weights_ref, out_ref, continuum_ref,
):
    devices = received_ref.shape[0]
    own_slots, count = weights_ref.shape
    halves = count // LANES
    head = own_slots * halves
    own = begin_ref.shape[1]
    lines = begin_ref.shape[0]
    inverse = inverse_ref[...]
    device = device_ref[0]

    mine = jnp.concatenate(
        [received_ref[device, h * own_slots : (h + 1) * own_slots, :] for h in range(halves)], axis=1
    )
    weights_ref[...] = dot_f32(mine, inverse, NN)

    bins = jnp.broadcast_to(bins_ref[...], (SUB, own)).T[:, :1]
    member = jnp.where(bins == owner_ref[...], 1.0, 0.0).astype(BF16)
    picked = []
    for h in range(halves):
        block = received_ref[:, h * own_slots : (h + 1) * own_slots, :].reshape(devices * own_slots, LANES)
        hi, mid, low = split3(block)
        picked.append(dot(member, hi, NN) + (dot(member, mid, NN) + dot(member, low, NN)))
    spaxel_weights = dot_f32(jnp.concatenate(picked, axis=1), inverse, NN)

    full_width = templates_ref.shape[1]
    step = 512
    for at in range(0, full_width, step):
        value = dot_f32(spaxel_weights, templates_ref[:, at : at + step], NN)
        for t in range(step // LANES):
            continuum_ref[at // LANES + t] = value[:, t * LANES : (t + 1) * LANES]
    continuum_ref[full_width // LANES] = jnp.zeros((own, LANES), F32)

    begin = begin_ref[...]
    span = span_ref[...].astype(F32)
    centre = 2.0 * (begin - begin // LANES * LANES).astype(F32) + span - 1.0
    pad = jnp.zeros((LANES - 2 * lines, own), F32)
    columns = jnp.concatenate([centre, span, pad], axis=0).T
    continuum_lanes = lax.broadcasted_iota(jnp.int32, (SUB, LANES), 1)
    twice = (2 * continuum_lanes).astype(F32)
    rows_at = lax.broadcasted_iota(jnp.int32, (SUB, LANES), 0)
    found = []
    for g in range(own // SUB):
        rows = slice(g * SUB, (g + 1) * SUB)
        result = jnp.zeros((SUB, LANES), F32)
        for j in range(lines):
            left = right = None
            for r in range(SUB):
                tile = starts_ref[j, g * SUB + r] // LANES
                a = continuum_ref[tile, rows, :]
                b = continuum_ref[tile + 1, rows, :]
                left = a if left is None else jnp.where(rows_at == r, a, left)
                right = b if right is None else jnp.where(rows_at == r, b, right)
            width = jnp.broadcast_to(columns[rows, lines + j : lines + j + 1], (SUB, LANES))
            m = twice - jnp.broadcast_to(columns[rows, j : j + 1], (SUB, LANES))
            n = m + 2.0 * LANES
            left = jnp.where(jnp.abs(m) < width, left, 0.0)
            right = jnp.where(jnp.abs(n) < width, right, 0.0)
            left_m = left * m
            right_n = right * n
            for k, term in enumerate((left + right, left_m + right_n, left_m * m + right_n * n)):
                total = jnp.sum(term, axis=1, keepdims=True)
                result = jnp.where(continuum_lanes == k * lines + j, total, result)
        found.append(result)
    continuum_sums = jnp.concatenate(found, axis=0).T[: 3 * lines, :]

    cube_sums = received_ref[0, head:, :]
    for i in range(1, devices):
        cube_sums = cube_sums + received_ref[i, head:, :]
    scale = jnp.concatenate([span, span * span, span * span * span], axis=0)
    out_ref[...] = (cube_sums - continuum_sums) / scale


def owned(device, starts, bins, owner, begin, span, received, inverse, templates, own_slots):
    vmem = pl.BlockSpec(memory_space=pltpu.VMEM)
    smem = pl.BlockSpec(memory_space=pltpu.SMEM)
    own = begin.shape[1]
    return pl.pallas_call(
        owner_kernel,
        in_specs=[smem, smem] + [vmem] * 7,
        out_shape=(
            jax.ShapeDtypeStruct((own_slots, inverse.shape[0]), F32),
            jax.ShapeDtypeStruct((3 * begin.shape[0], own), F32),
        ),
        scratch_shapes=[pltpu.VMEM((templates.shape[1] // LANES + 1, own, LANES), F32)],
        compiler_params=pltpu.CompilerParams(vmem_limit_bytes=VMEM_LIMIT),
        name="owned",
    )(device, starts, bins, owner, begin, span, received, inverse, templates)


def shards(cube, templates, bin_id, owner_bins, line_start, line_width):
    devices = lax.axis_size("spax")
    device = lax.axis_index("spax")
    spaxels = cube.shape[0]
    total_bins = owner_bins.shape[0]
    count = templates.shape[0]
    own_spaxels = spaxels // devices
    own_slots = total_bins // devices
    here = device.reshape(1).astype(jnp.int32)
    columns = cube.T
    bins = bin_id[None, :]
    owner = owner_bins[None, :]

    partial = project(here, bins, owner, columns, templates)
    received = lax.all_to_all(partial.reshape(devices, own_slots, count), "spax", 0, 0)

    head = own_slots * (count // LANES)
    sums = cube_windows(here, line_start, line_width, columns, devices, head)
    gram, first = in_vmem(
        functools.partial(gram_kernel, chunk=512),
        (jax.ShapeDtypeStruct((count, count), F32), jax.ShapeDtypeStruct((LANES, LANES), F32)),
        "gram",
        templates,
    )
    received, sums, gram, first = lax.optimization_barrier((received, sums, gram, first))
    parcel = in_vmem(pack_kernel, jax.ShapeDtypeStruct(sums.shape, F32), "pack", received, sums)
    parcel, gram, first = lax.optimization_barrier((parcel, gram, first))
    arrived = lax.all_to_all(parcel, "spax", 0, 0)
    inverse = in_vmem(finish_kernel, jax.ShapeDtypeStruct((count, count), F32), "finish", gram, first)

    own = lambda x: lax.dynamic_slice_in_dim(x, device * own_spaxels, own_spaxels, 1)
    begin, span = own(line_start), own(line_width)
    return owned(here, begin, own(bins), owner, begin, span, arrived, inverse, templates, own_slots)


def solution(mesh):
    placed = (
        P("strips", "spax"),
        P(),
        P("strips"),
        P("strips"),
        P(None, "strips"),
        P(None, "strips"),
    )
    return jax.shard_map(
        shards,
        mesh=mesh,
        in_specs=placed,
        out_specs=(P(("strips", "spax"), None), P(None, ("strips", "spax"))),
        check_vma=False,
    )
```

time: 100 us -> 74.1 us (0.74)
  starting transfers between devices: 28.3 us -> 13.7 us
  between operations: 14.2 us -> 0.75 us
  waiting for transfers between devices: 5.95 us -> 11.2 us
  local copies, waits for them, and re-layouts: 13.9 us -> 9.77 us
  Pallas kernels: 35.8 us -> 38.2 us
  other arithmetic: 1.47 us -> 0 us
    ppermute x15 -> x0, starting transfers between devices: 20.9 us -> none  [shards(): lax.ppermute(mine, 'spax', [(d, d ^ k) for d in range(devices)])]
    all_to_all x1 -> x2, waiting for transfers between devices: 0.01 us -> 11.2 us  [the longest x1 11.2 us: shards(): arrived = lax.all_to_all(parcel, 'spax', 0, 0)]
    all_to_all x1 -> x2, starting transfers between devices: 7.36 us -> 13.7 us  [the longest x1 7.5 us: shards(): lax.all_to_all(partial.reshape(devices, own_slots, count), 'spax', 0, 0)]
    ppermute x15 -> x0, waiting for transfers between devices: 5.93 us -> none  [shards(): lax.ppermute(mine, 'spax', [(d, d ^ k) for d in range(devices)])]
    unnamed x32 -> x20, local copies, waits for them, and re-layouts: 11.5 us -> 9.01 us
    broadcast_in_dim x3 -> x0, local copies, waits for them, and re-layouts: 1.7 us -> none  [the longest x2 0.87 us: shards(): own(bin_id)[:, None]]
    pallas_call x3, Pallas kernels: 21.6 us -> 23.1 us  [the longest x1 11.1 us: owned(): pl.pallas_call(owner_kernel, in_specs=[smem, smem] + [vmem] * 7, out_shap...]
    div x1 -> x0, other arithmetic: 1.32 us -> none  [shards(): return (weights, (cube_sums - continuum_sums) / divisor)]
  transfers between devices with their start and end apart: 17 -> 2, of which waited for: 3 -> 1; matrix products, arithmetic and copies ran while one was open for 7% -> 1% of each run, Pallas kernels for 30% -> 27%
where the time goes in v2:
time: 74.1 us; the launch traced here: 73.5 us
  Pallas kernels  38.2 us (52%)
  starting transfers between devices  13.7 us (18%)
  waiting for transfers between devices  11.2 us (15%)
  local copies, waits for them, and re-layouts  9.77 us (13%)
  between operations  0.75 us (1%)
    pallas_call x3, Pallas kernels, in_vmem(): pl.pallas_call(kernel, out_shape=shapes, compiler_params=pltpu.CompilerPa...  15.1 us
    all_to_all x1, waiting for transfers between devices, shards(): arrived = lax.all_to_all(parcel, 'spax', 0, 0)  11.2 us
    pallas_call x1, Pallas kernels, owned(): pl.pallas_call(owner_kernel, in_specs=[smem, smem] + [vmem] * 7, out_shap...  11.1 us
    unnamed x20, local copies, waits for them, and re-layouts  9.01 us
    all_to_all x1, starting transfers between devices, shards(): lax.all_to_all(partial.reshape(devices, own_slots, count), 'spax', 0, 0)  7.5 us
    all_to_all x1, starting transfers between devices, shards(): arrived = lax.all_to_all(parcel, 'spax', 0, 0)  6.19 us
    pallas_call x1, Pallas kernels, project(): pl.pallas_call(functools.partial(project_kernel, chunk=chunk), grid=(slot...  6.13 us
    pallas_call x1, Pallas kernels, cube_windows(): pl.pallas_call(functools.partial(cube_kernel, head=head), in_specs=[pl.Bl...  5.82 us
  transfers between devices with their start and end apart: 2, of which 1 were waited for; matrix products, arithmetic and copies ran while one was open for 1% of the time, Pallas kernels for 27%

profile of v2, /device:TPU:0, one launch (start us, length us, event | category | flops | bytes accessed | tf_op | source)
XLA Modules:
  0.0 73.5 jit_solution(7674894297755470394)
XLA Ops:
  0.6 0.0 copy-start
  0.6 2.0 %copy-done = f32[256,3584]{1,0:T(8,128)S(1)} copy-done((f32[256,3584]{1,0:T(8,128)S(1)}, f32[256,3584]{1,0:T(8,128)}, u32[]{:S(2)}) %copy-start) | copy-done | bytes 3670040
  2.7 1.5 %copy-done.3 = f32[2048,224]{0,1:T(8,128)S(1)} copy-done((f32[2048,224]{0,1:T(8,128)S(1)}, f32[2048,224]{0,1:T(8,128)}, u32[]{:S(2)}) %copy-start.3) | copy-done | bytes 1835032
  4.2 0.7 copy-done.7
  4.9 0.7 copy-done.8
  5.6 6.1 %project.1 = f32[512,256]{1,0:T(8,128)} custom-call(s32[1]{0:T(128)} %bitcast.device_ref, s32[1,2048]{1,0:T(1,128)S(1)} %bitcast.9, s32[1,512]{1,0:T(1,128)S(1)} %bitcast.10, f32[224,2048]{1,0:T(8,128)S(1)} %bitcast.7, f32[256,3584]{1,0:T(8,128)S(1)} %copy-done), custom_call_target="tpu_custom_call" | custom-call | tf_op jit(solution)/shard_map/project/pallas_call | solution.py:97
  11.7 0.0 copy-start.5
  11.7 0.0 copy-start.6
  11.7 7.5 %all-to-all-start = ((f32[16,32,256]{2,1,0:T(8,128)}), f32[16,32,256]{2,1,0:T(8,128)S(1)}, u32[]{:S(2)}, u32[]{:S(2)}) async-start(f32[16,32,256]{2,1,0:T(8,128)} %bitcast.5), calls=%async_computation | async-start | bytes 1048576 | tf_op jit(solution)/shard_map/all_to_all | solution.py:395
  19.2 0.0 copy-start.1
  19.2 2.0 %copy-done.1 = f32[256,3584]{1,0:T(8,128)S(1)} copy-done((f32[256,3584]{1,0:T(8,128)S(1)}, f32[256,3584]{1,0:T(8,128)}, u32[]{:S(2)}) %copy-start.1) | copy-done | bytes 3670040
  21.3 8.6 %gram.1 = (f32[256,256]{1,0:T(8,128)S(1)}, f32[128,128]{1,0:T(8,128)S(1)}) custom-call(f32[256,3584]{1,0:T(8,128)S(1)} %copy-done.1), custom_call_target="tpu_custom_call" | custom-call | tf_op jit(solution)/shard_map/gram/pallas_call | solution.py:200
  29.9 0.0 copy-done.4
  29.9 0.0 copy-done.5
  29.9 0.0 copy-start.9
  30.0 5.8 %cube_windows.1.sums_ref = f32[16,88,128]{2,1,0:T(8,128)S(1)} custom-call(s32[1]{0:T(128)} %bitcast.device_ref, s32[8,2048]{1,0:T(8,128)S(1)} %copy-done.6, s32[8,2048]{1,0:T(8,128)S(1)} %copy-done.5, f32[224,2048]{1,0:T(8,128)S(1)} %bitcast.8), custom_call_target="tpu_custom_call" | custom-call | tf_op jit(solution)/shard_map/cube_windows/pallas_call | solution.py:266
  35.8 0.0 all-to-all-done.received_ref
  35.8 0.9 %pack.1 = f32[16,88,128]{2,1,0:T(8,128)} custom-call(f32[16,32,256]{2,1,0:T(8,128)S(1)} %all-to-all-done.received_ref, f32[16,88,128]{2,1,0:T(8,128)S(1)} %cube_windows.1.sums_ref), custom_call_target="tpu_custom_call" | custom-call | tf_op jit(solution)/shard_map/pack/pallas_call | solution.py:200
  36.7 6.2 %all-to-all-start.1 = ((f32[16,88,128]{2,1,0:T(8,128)}), f32[16,88,128]{2,1,0:T(8,128)S(1)}, u32[]{:S(2)}, u32[]{:S(2)}) async-start(f32[16,88,128]{2,1,0:T(8,128)} %pack.1), calls=%async_computation.1 | async-start | bytes 1441792 | tf_op jit(solution)/shard_map/all_to_all | solution.py:408
  42.9 0.8 %dynamic-slice_bitcast_fusion.bins_ref = s32[1,128]{1,0:T(1,128)S(1)} fusion(s32[2048]{0:T(1024)} %param.8, s32[]{:T(128)S(6)} %select_n.2), kind=kLoop, calls=%fused_computation | loop fusion | bytes 1028 | tf_op jit(solution)/shard_map/dynamic_slice | solution.py:411
  43.7 5.5 %finish.1.inverse_ref = f32[256,256]{1,0:T(8,128)S(1)} custom-call(f32[256,256]{1,0:T(8,128)S(1)} %get-tuple-element.18.gram_ref, f32[128,128]{1,0:T(8,128)S(1)} %get-tuple-element.19.first_ref), custom_call_target="tpu_custom_call" | custom-call | tf_op jit(solution)/shard_map/finish/pallas_call | solution.py:200
  49.2 11.2 %all-to-all-done.1.received_ref = f32[16,88,128]{2,1,0:T(8,128)S(1)} async-done(((f32[16,88,128]{2,1,0:T(8,128)}), f32[16,88,128]{2,1,0:T(8,128)S(1)}, u32[]{:S(2)}, u32[]{:S(2)}) %all-to-all-start.1) | async-done | bytes 720928 | tf_op jit(solution)/shard_map/all_to_all | solution.py:408
  60.4 2.0 %copy-done.2 = f32[256,3584]{1,0:T(8,128)S(1)} copy-done((f32[256,3584]{1,0:T(8,128)S(1)}, f32[256,3584]{1,0:T(8,128)}, u32[]{:S(2)}) %copy-start.2) | copy-done | bytes 3670040
  62.4 11.1 %owned.1 = (f32[32,256]{1,0:T(8,128)}, f32[24,128]{1,0:T(8,128)}) custom-call(s32[1]{0:T(128)} %bitcast.device_ref, s32[8,128]{1,0:T(8,128)S(1)} %get-tuple-element.21.starts_ref.begin_ref, s32[1,128]{1,0:T(1,128)S(1)} %dynamic-slice_bitcast_fusion.bins_ref, s32[1,512]{1,0:T(1,128)S(1)} %bitcast.11, s32[8,128]{1,0:T(8,128)S(1)} %get-tuple-element.21.starts_ref.begin_ref, ...), custom_call_target="tpu_custom_call" | custom-call | tf_op jit(solution)/shard_map/owned/pallas_call | solution.py:368
  (8 shorter events, 0.0 us)
Async XLA Ops:
  0.6 2.0 %copy-start = (f32[256,3584]{1,0:T(8,128)S(1)}, f32[256,3584]{1,0:T(8,128)}, u32[]{:S(2)}) copy-start(f32[256,3584]{1,0:T(8,128)} %templates_ref.5) | copy-start | bytes 11010052
  2.7 1.5 %copy-start.3 = (f32[2048,224]{0,1:T(8,128)S(1)}, f32[2048,224]{0,1:T(8,128)}, u32[]{:S(2)}) copy-start(f32[2048,224]{0,1:T(8,128)} %param.6) | copy-start | bytes 5505028
  4.2 0.7 copy-start.7
  4.9 0.7 copy-start.8
  5.6 24.4 %copy-start.4 = (f32[2048,224]{0,1:T(8,128)S(1)}, f32[2048,224]{0,1:T(8,128)}, u32[]{:S(2)}) copy-start(f32[2048,224]{0,1:T(8,128)} %param.6) | copy-start | bytes 5505028
  11.7 18.2 %copy-start.5 = (s32[8,2048]{1,0:T(8,128)S(1)}, s32[8,2048]{1,0:T(8,128)}, u32[]{:S(2)}) copy-start(s32[8,2048]{1,0:T(8,128)} %span_ref.1) | copy-start | bytes 196612
  11.7 18.2 %copy-start.6 = (s32[8,2048]{1,0:T(8,128)S(1)}, s32[8,2048]{1,0:T(8,128)}, u32[]{:S(2)}) copy-start(s32[8,2048]{1,0:T(8,128)} %begin_ref.1) | copy-start | bytes 196612
  11.7 24.1 %all-to-all-start = ((f32[16,32,256]{2,1,0:T(8,128)}), f32[16,32,256]{2,1,0:T(8,128)S(1)}, u32[]{:S(2)}, u32[]{:S(2)}) async-start(f32[16,32,256]{2,1,0:T(8,128)} %bitcast.5), calls=%async_computation | async-start | bytes 1048576 | tf_op jit(solution)/shard_map/all_to_all | solution.py:395
  19.2 2.0 %copy-start.1 = (f32[256,3584]{1,0:T(8,128)S(1)}, f32[256,3584]{1,0:T(8,128)}, u32[]{:S(2)}) copy-start(f32[256,3584]{1,0:T(8,128)} %templates_ref.5) | copy-start | bytes 11010052
  29.9 30.5 %copy-start.9 = (s32[512]{0:T(512)S(1)}, s32[512]{0:T(512)}, u32[]{:S(2)}) copy-start(s32[512]{0:T(512)} %param.9) | copy-start | bytes 6148
  36.7 23.7 %all-to-all-start.1 = ((f32[16,88,128]{2,1,0:T(8,128)}), f32[16,88,128]{2,1,0:T(8,128)S(1)}, u32[]{:S(2)}, u32[]{:S(2)}) async-start(f32[16,88,128]{2,1,0:T(8,128)} %pack.1), calls=%async_computation.1 | async-start | bytes 1441792 | tf_op jit(solution)/shard_map/all_to_all | solution.py:408
  60.4 2.0 %copy-start.2 = (f32[256,3584]{1,0:T(8,128)S(1)}, f32[256,3584]{1,0:T(8,128)}, u32[]{:S(2)}) copy-start(f32[256,3584]{1,0:T(8,128)} %templates_ref.5) | copy-start | bytes 11010052

commit v3 on v2

v3 whole, which is shorter than its diff:
```python
import functools

import jax
import jax.numpy as jnp
from jax import lax
from jax.experimental import pallas as pl
from jax.experimental.pallas import tpu as pltpu
from jax.sharding import PartitionSpec as P

HIGHEST = lax.Precision.HIGHEST
F32 = jnp.float32
BF16 = jnp.bfloat16
LANES = 128
SUB = 8
VMEM_LIMIT = 20 * 1024 * 1024

NT = (((1,), (1,)), ((), ()))
NN = (((1,), (0,)), ((), ()))


def split3(x):
    hi = x.astype(BF16)
    rest = x - hi.astype(F32)
    mid = rest.astype(BF16)
    low = (rest - mid.astype(F32)).astype(BF16)
    return hi, mid, low


def dot(a, b, dims):
    return lax.dot_general(a, b, dims, preferred_element_type=F32)


def dot_f32(a, b, dims):
    return lax.dot_general(a, b, dims, precision=HIGHEST, preferred_element_type=F32)


def template_window(width, full_width):
    return min(full_width, -(-(width + LANES - 1) // LANES) * LANES)


def project_kernel(
    device_ref, bins_ref, owner_ref, cube_ref, templates_ref, out_ref,
    held_ref, window_ref, bins_held_ref, owner_held_ref, cube_sem, window_sem, small_sem, *, chunk,
):
    width, spaxels = cube_ref.shape
    slots = out_ref.shape[0]
    full_width = templates_ref.shape[1]
    first = device_ref[0] * width
    window = window_ref.shape[1]
    base = pl.multiple_of(jnp.minimum(first // LANES * LANES, full_width - window), LANES)
    chunks = spaxels // chunk

    def cube_copy(i):
        lanes = pl.ds(i * chunk, chunk)
        return pltpu.make_async_copy(cube_ref.at[:, lanes], held_ref.at[:, lanes], cube_sem.at[i])

    window_copy = pltpu.make_async_copy(templates_ref.at[:, pl.ds(base, window)], window_ref, window_sem)

    small_copies = [
        pltpu.make_async_copy(bins_ref, bins_held_ref, small_sem.at[0]),
        pltpu.make_async_copy(owner_ref, owner_held_ref, small_sem.at[1]),
    ]

    @pl.when(pl.program_id(0) == 0)
    def _():
        for copy in small_copies:
            copy.start()
        for i in range(chunks):
            cube_copy(i).start()
        window_copy.start()
        for copy in small_copies:
            copy.wait()

    owner = owner_held_ref[:, pl.ds(pl.multiple_of(pl.program_id(0) * slots, LANES), slots)]
    owner = jnp.broadcast_to(owner, (SUB, slots)).T[:, :1]
    sums = jnp.zeros((slots, width), F32)
    counts = jnp.zeros((slots, LANES), F32)
    for i in range(chunks):
        here = owner == bins_held_ref[:, i * chunk : (i + 1) * chunk]
        ones = jnp.where(here, 1.0, 0.0)
        for lane in range(0, chunk, LANES):
            counts = counts + ones[:, lane : lane + LANES]
        member = ones.astype(BF16)

        @pl.when(pl.program_id(0) == 0)
        def _(i=i):
            cube_copy(i).wait()

        for part in split3(held_ref[:, i * chunk : (i + 1) * chunk]):
            sums = sums + dot(member, part, NT)
    means = sums / jnp.sum(counts, axis=1, keepdims=True)

    @pl.when(pl.program_id(0) == 0)
    def _():
        window_copy.wait()

    mine = pltpu.roll(window_ref[...], window - (first - base), 1)[:, :width]
    out_ref[...] = dot_f32(means, mine, NT) * (1.0 / full_width)


def project(device, bins, owner, cube, templates):
    width, spaxels = cube.shape
    slots = owner.shape[1]
    block = min(slots, 512)
    chunk = min(spaxels, 512)
    count, full_width = templates.shape
    return pl.pallas_call(
        functools.partial(project_kernel, chunk=chunk),
        grid=(slots // block,),
        in_specs=[
            pl.BlockSpec(memory_space=pltpu.SMEM),
            pl.BlockSpec(memory_space=pltpu.HBM),
            pl.BlockSpec(memory_space=pltpu.HBM),
            pl.BlockSpec(memory_space=pltpu.HBM),
            pl.BlockSpec(memory_space=pltpu.HBM),
        ],
        out_specs=pl.BlockSpec((block, count), lambda i: (i, 0)),
        out_shape=jax.ShapeDtypeStruct((slots, count), F32),
        scratch_shapes=[
            pltpu.VMEM((width, spaxels), F32),
            pltpu.VMEM((count, template_window(width, full_width)), F32),
            pltpu.VMEM(bins.shape, jnp.int32),
            pltpu.VMEM(owner.shape, jnp.int32),
            pltpu.SemaphoreType.DMA((spaxels // chunk,)),
            pltpu.SemaphoreType.DMA,
            pltpu.SemaphoreType.DMA((2,)),
        ],
        compiler_params=pltpu.CompilerParams(vmem_limit_bytes=VMEM_LIMIT),
        name="project",
    )(device, bins, owner, cube, templates)


def reciprocal(x):
    r = pl.reciprocal(x, approx=True)
    r = r * (2.0 - x * r)
    return r * (2.0 - x * r)


def invert_tile(tile):
    size = tile.shape[0]
    count = size // SUB
    lanes = lax.broadcasted_iota(jnp.int32, (SUB, size), 1)
    rows_at = lax.broadcasted_iota(jnp.int32, (SUB, size), 0)
    rows = [tile[i * SUB : (i + 1) * SUB, :] for i in range(count)]
    for k in range(count):
        block = rows[k]
        first = k * SUB
        a = {}
        for i in range(SUB):
            for j in range(i, SUB):
                a[i, j] = jnp.broadcast_to(block[i : i + 1, first + j : first + j + 1], (SUB, size))

        def at(i, j):
            return (i, j) if i <= j else (j, i)

        for p in range(0, SUB, 2):
            q = p + 1
            pp, pq, qq = a[p, p], a[p, q], a[q, q]
            inverse = reciprocal(pp * qq - pq * pq)
            others = [i for i in range(SUB) if i not in (p, q)]
            old = {i: (a[at(i, p)], a[at(i, q)]) for i in others}
            new = {
                i: ((u * qq - v * pq) * inverse, (v * pp - u * pq) * inverse) for i, (u, v) in old.items()
            }
            for i in others:
                for j in others:
                    if i <= j:
                        a[i, j] = a[i, j] - new[i][0] * old[j][0] - new[i][1] * old[j][1]
            for i in others:
                a[at(i, p)], a[at(i, q)] = new[i]
            a[p, p], a[p, q], a[q, q] = -(qq * inverse), pq * inverse, -(pp * inverse)
        columns = []
        for j in range(SUB):
            column = a[at(0, j)]
            for i in range(1, SUB):
                column = jnp.where(rows_at == i, a[at(i, j)], column)
            columns.append(column)
        terms = [columns[j] * jnp.broadcast_to(block[j : j + 1, :], (SUB, size)) for j in range(SUB)]
        while len(terms) > 1:
            terms = [x + y for x, y in zip(terms[::2], terms[1::2])]
        swept = -terms[0]
        for j in range(SUB):
            swept = jnp.where(lanes == first + j, columns[j], swept)
        inside = (lanes >= first) & (lanes < first + SUB)
        spread_rows = [jnp.broadcast_to(swept[j : j + 1, :], (SUB, size)) for j in range(SUB)]
        order = list(range(k + 1, count)) + list(range(k))
        for i in order:
            terms = [
                jnp.broadcast_to(rows[i][:, first + j : first + j + 1], (SUB, size)) * spread_rows[j]
                for j in range(SUB)
            ]
            while len(terms) > 1:
                terms = [x + y for x, y in zip(terms[::2], terms[1::2])]
            rows[i] = jnp.where(inside, 0.0, rows[i]) - terms[0]
        rows[k] = swept
    return -jnp.concatenate(rows, axis=0)


def gram_kernel(templates_ref, gram_ref, first_ref, scale_ref, held_ref, sem, *, chunk):
    count, full_width = templates_ref.shape

    def copy(i):
        lanes = pl.ds(i * chunk, chunk)
        return pltpu.make_async_copy(templates_ref.at[:, lanes], held_ref.at[:, lanes], sem.at[i])

    for i in range(full_width // chunk):
        copy(i).start()
    even = jnp.zeros((count, count), F32)
    mixed = jnp.zeros((count, count), F32)
    for i in range(full_width // chunk):
        copy(i).wait()
        hi, mid, low = split3(held_ref[:, i * chunk : (i + 1) * chunk])
        even = even + (dot(hi, hi, NT) + dot(mid, mid, NT))
        mixed = mixed + (dot(hi, mid, NT) + dot(hi, low, NT))
    gram = (even + (mixed + mixed.T)) * (1.0 / full_width)
    same = lax.broadcasted_iota(jnp.int32, gram.shape, 0) == lax.broadcasted_iota(jnp.int32, gram.shape, 1)
    diagonal = jnp.where(same, gram, 0.0)
    row = lax.rsqrt(jnp.sum(diagonal, axis=0, keepdims=True))
    column = lax.rsqrt(jnp.sum(diagonal, axis=1, keepdims=True))
    gram = gram * row * column
    scale_ref[...] = row
    gram_ref[...] = gram
    first_ref[...] = invert_tile(gram[:LANES, :LANES])


def gram_inverse(templates, chunk):
    count, full_width = templates.shape
    return pl.pallas_call(
        functools.partial(gram_kernel, chunk=chunk),
        in_specs=[pl.BlockSpec(memory_space=pltpu.HBM)],
        out_shape=(
            jax.ShapeDtypeStruct((count, count), F32),
            jax.ShapeDtypeStruct((LANES, LANES), F32),
            jax.ShapeDtypeStruct((1, count), F32),
        ),
        scratch_shapes=[
            pltpu.VMEM((count, full_width), F32),
            pltpu.SemaphoreType.DMA((full_width // chunk,)),
        ],
        compiler_params=pltpu.CompilerParams(vmem_limit_bytes=VMEM_LIMIT),
        name="gram",
    )(templates)


def finish_kernel(gram_ref, first_ref, scale_ref, out_ref):
    first = first_ref[...]
    side = gram_ref[:LANES, LANES:]
    half = dot_f32(first, side, NN)
    schur = gram_ref[LANES:, LANES:] - dot_f32(side.T, half, NN)
    last = invert_tile(schur)
    cross = dot_f32(half, last, NN)
    row = scale_ref[...]
    column = jnp.broadcast_to(row, (SUB, row.shape[1])).T[:, :1]
    near, far = row[:, :LANES], row[:, LANES:]
    out_ref[:LANES, :LANES] = (first + dot_f32(cross, half, NT)) * near * column[:LANES]
    out_ref[:LANES, LANES:] = -cross * far * column[:LANES]
    out_ref[LANES:, :LANES] = -cross.T * near * column[LANES:]
    out_ref[LANES:, LANES:] = last * far * column[LANES:]


def in_vmem(kernel, shapes, name, *arrays):
    return pl.pallas_call(
        kernel,
        out_shape=shapes,
        compiler_params=pltpu.CompilerParams(vmem_limit_bytes=VMEM_LIMIT),
        name=name,
    )(*arrays)


def window_sums(read, rows, first, begin, span):
    lines = begin.shape[0]
    sub = lax.broadcasted_iota(jnp.int32, (SUB, LANES), 0)
    spans = [jnp.broadcast_to(span[j : j + 1], (SUB, LANES)).astype(F32) for j in range(lines)]
    offsets = [
        (2 * (first + sub - jnp.broadcast_to(begin[j : j + 1], (SUB, LANES))) + 1).astype(F32) - spans[j]
        for j in range(lines)
    ]

    def add(block, shift, sums):
        size = block.shape[0]
        out = []
        for j in range(lines):
            m = offsets[j][:size] + shift
            masked = jnp.where(jnp.abs(m) < spans[j][:size], block, 0.0)
            weighted = masked * m
            out += [sums[3 * j] + masked, sums[3 * j + 1] + weighted, sums[3 * j + 2] + weighted * m]
        return out

    full = rows // SUB
    out = [jnp.zeros((1, LANES), F32)] * (3 * lines)
    if full:
        sums = [jnp.zeros((SUB, LANES), F32)] * (3 * lines)
        for i in range(full):
            sums = add(read(i * SUB, SUB), 2.0 * i * SUB, sums)
        out = [jnp.sum(x, axis=0, keepdims=True) for x in sums]
    if rows % SUB:
        sums = [jnp.zeros((rows % SUB, LANES), F32)] * (3 * lines)
        sums = add(read(full * SUB, rows % SUB), 2.0 * full * SUB, sums)
        out = [x + jnp.sum(y, axis=0, keepdims=True) for x, y in zip(out, sums)]
    return [out[3 * j + k] for k in range(3) for j in range(lines)]


def cube_kernel(
    device_ref, begin_ref, span_ref, cube_ref, same_ref, other_ref,
    begins_ref, spans_ref, held_ref, lines_sem, cube_sem,
):
    width = cube_ref.shape[0]
    owners = 2 * same_ref.shape[0]
    device = device_ref[0]

    def tile_copy(i):
        lanes = pl.ds(pl.multiple_of(i * LANES, LANES), LANES)
        return pltpu.make_async_copy(cube_ref.at[:, lanes], held_ref.at[i], cube_sem.at[i])

    line_copies = [
        pltpu.make_async_copy(begin_ref, begins_ref, lines_sem.at[0]),
        pltpu.make_async_copy(span_ref, spans_ref, lines_sem.at[1]),
    ]
    for copy in line_copies:
        copy.start()
    for i in range(owners):
        tile_copy(i).start()
    for copy in line_copies:
        copy.wait()

    def owner(i, carry):
        tile_copy(i).wait()
        lanes = pl.ds(pl.multiple_of(i * LANES, LANES), LANES)
        sums = window_sums(
            lambda row, size: held_ref[i, row : row + size, :],
            width,
            device * width,
            begins_ref[:, lanes],
            spans_ref[:, lanes],
        )
        value = jnp.concatenate(sums, axis=0)
        same = i % 2 == device % 2

        @pl.when(same)
        def _():
            same_ref[i // 2] = value

        @pl.when(jnp.logical_not(same))
        def _():
            other_ref[i // 2] = value

        return carry

    lax.fori_loop(0, owners, owner, 0)


def cube_windows(device, begin, span, cube, devices):
    hbm = pl.BlockSpec(memory_space=pltpu.HBM)
    width, spaxels = cube.shape
    half = jax.ShapeDtypeStruct((devices // 2, 3 * begin.shape[0], LANES), F32)
    return pl.pallas_call(
        cube_kernel,
        in_specs=[pl.BlockSpec(memory_space=pltpu.SMEM), hbm, hbm, hbm],
        out_shape=(half, half),
        scratch_shapes=[
            pltpu.VMEM(begin.shape, jnp.int32),
            pltpu.VMEM(span.shape, jnp.int32),
            pltpu.VMEM((devices, width, LANES), F32),
            pltpu.SemaphoreType.DMA((2,)),
            pltpu.SemaphoreType.DMA((devices,)),
        ],
        compiler_params=pltpu.CompilerParams(vmem_limit_bytes=VMEM_LIMIT),
        name="cube_windows",
    )(device, begin, span, cube)


def pack_kernel(received_ref, same_ref, other_ref, out_ref):
    total = received_ref[0]
    for i in range(1, received_ref.shape[0]):
        total = total + received_ref[i]
    slots, count = total.shape
    for half in range(count // LANES):
        value = total[:, half * LANES : (half + 1) * LANES]
        for i in range(out_ref.shape[0]):
            out_ref[i, half * slots : (half + 1) * slots, :] = value
    head = slots * (count // LANES)
    out_ref[:, head:, :] = same_ref[...] + other_ref[...]


def owner_kernel(
    device_ref, starts_ref, bins_ref, owner_ref, begin_ref, span_ref, near_ref, far_ref, inverse_ref, templates_ref,
    weights_ref, out_ref, held_ref, continuum_ref, bins_held_ref, owner_held_ref, sem, small_sem, *, chunk,
):
    chips = near_ref.shape[0]
    own_slots, count = weights_ref.shape
    halves = count // LANES
    head = own_slots * halves
    own = begin_ref.shape[1]
    lines = begin_ref.shape[0]
    full_width = templates_ref.shape[1]
    device = device_ref[0]

    def copy(i):
        lanes = pl.ds(i * chunk, chunk)
        return pltpu.make_async_copy(templates_ref.at[:, lanes], held_ref.at[:, lanes], sem.at[i])

    own_bins = bins_ref.at[:, pl.ds(pl.multiple_of(device * own, LANES), own)]
    small_copies = [
        pltpu.make_async_copy(own_bins, bins_held_ref, small_sem.at[0]),
        pltpu.make_async_copy(owner_ref, owner_held_ref, small_sem.at[1]),
    ]
    for small in small_copies:
        small.start()
    for i in range(full_width // chunk):
        copy(i).start()

    inverse = inverse_ref[...]
    chip, core = device // 2, device % 2
    mine = jnp.concatenate([near_ref[chip, h * own_slots : (h + 1) * own_slots, :] for h in range(halves)], axis=1)
    weights_ref[...] = dot_f32(mine, inverse, NN)

    for small in small_copies:
        small.wait()
    bins = jnp.broadcast_to(bins_held_ref[...], (SUB, own)).T[:, :1]
    member = jnp.where(bins == owner_held_ref[...], 1.0, 0.0).astype(BF16)
    picked = []
    for h in range(halves):
        rows = slice(h * own_slots, (h + 1) * own_slots)
        blocks = []
        for i in range(chips):
            near, far = near_ref[i, rows, :], far_ref[i, rows, :]
            blocks += [jnp.where(core == 0, near, far), jnp.where(core == 0, far, near)]
        hi, mid, low = split3(jnp.concatenate(blocks, axis=0))
        picked.append(dot(member, hi, NN) + (dot(member, mid, NN) + dot(member, low, NN)))
    spaxel_weights = dot_f32(jnp.concatenate(picked, axis=1), inverse, NN)

    hi, mid, low = split3(spaxel_weights)
    all_parts = jnp.concatenate([hi, mid, low], axis=0)
    for i in range(full_width // chunk):
        copy(i).wait()
        first, second, third = split3(held_ref[:, i * chunk : (i + 1) * chunk])
        by_first = dot(all_parts, first, NN)
        by_second = dot(all_parts[: 2 * own], second, NN)
        by_third = dot(hi, third, NN)
        value = by_first[:own] + (
            (by_first[own : 2 * own] + by_second[:own]) + (by_first[2 * own :] + by_second[own:] + by_third)
        )
        for t in range(chunk // LANES):
            continuum_ref[i * (chunk // LANES) + t] = value[:, t * LANES : (t + 1) * LANES]
    continuum_ref[full_width // LANES] = jnp.zeros((own, LANES), F32)

    begin = begin_ref[...]
    span = span_ref[...].astype(F32)
    centre = 2.0 * (begin & (LANES - 1)).astype(F32) + span - 1.0
    pad = jnp.zeros((LANES - 2 * lines, own), F32)
    columns = jnp.concatenate([centre, span, pad], axis=0).T
    lanes = lax.broadcasted_iota(jnp.int32, (SUB, LANES), 1)
    twice = (2 * lanes).astype(F32)
    rows_at = lax.broadcasted_iota(jnp.int32, (SUB, LANES), 0)
    at_row = [rows_at == r for r in range(SUB)]
    found = []
    for g in range(own // SUB):
        rows = slice(g * SUB, (g + 1) * SUB)
        result = jnp.zeros((SUB, LANES), F32)
        for j in range(lines):
            left = right = None
            for r in range(SUB):
                tile = lax.shift_right_logical(starts_ref[j, g * SUB + r], 7)
                a = continuum_ref[tile, rows, :]
                b = continuum_ref[tile + 1, rows, :]
                left = a if left is None else jnp.where(at_row[r], a, left)
                right = b if right is None else jnp.where(at_row[r], b, right)
            width = jnp.broadcast_to(columns[rows, lines + j : lines + j + 1], (SUB, LANES))
            m = twice - jnp.broadcast_to(columns[rows, j : j + 1], (SUB, LANES))
            n = m + 2.0 * LANES
            left = jnp.where(jnp.abs(m) < width, left, 0.0)
            right = jnp.where(jnp.abs(n) < width, right, 0.0)
            left_m = left * m
            right_n = right * n
            for k, term in enumerate((left + right, left_m + right_n, left_m * m + right_n * n)):
                total = jnp.sum(term, axis=1, keepdims=True)
                result = jnp.where(lanes == k * lines + j, total, result)
        found.append(result)
    continuum_sums = jnp.concatenate(found, axis=0).T[: 3 * lines, :]

    cube_sums = near_ref[0, head:, :]
    for i in range(1, chips):
        cube_sums = cube_sums + near_ref[i, head:, :]
    scale = jnp.concatenate([span, span * span, span * span * span], axis=0)
    out_ref[...] = (cube_sums - continuum_sums) / scale


def owned(device, bins, owner, begin, span, near, far, inverse, templates, own_slots, chunk):
    vmem = pl.BlockSpec(memory_space=pltpu.VMEM)
    smem = pl.BlockSpec(memory_space=pltpu.SMEM)
    hbm = pl.BlockSpec(memory_space=pltpu.HBM)
    own = begin.shape[1]
    count, full_width = templates.shape
    return pl.pallas_call(
        functools.partial(owner_kernel, chunk=chunk),
        in_specs=[smem, smem, hbm, hbm] + [vmem] * 5 + [hbm],
        out_shape=(
            jax.ShapeDtypeStruct((own_slots, count), F32),
            jax.ShapeDtypeStruct((3 * begin.shape[0], own), F32),
        ),
        scratch_shapes=[
            pltpu.VMEM((count, full_width), F32),
            pltpu.VMEM((full_width // LANES + 1, own, LANES), F32),
            pltpu.VMEM((1, own), jnp.int32),
            pltpu.VMEM(owner.shape, jnp.int32),
            pltpu.SemaphoreType.DMA((full_width // chunk,)),
            pltpu.SemaphoreType.DMA((2,)),
        ],
        compiler_params=pltpu.CompilerParams(vmem_limit_bytes=VMEM_LIMIT),
        name="owned",
    )(device, begin, bins, owner, begin, span, near, far, inverse, templates)


def shards(cube, templates, bin_id, owner_bins, line_start, line_width):
    devices = lax.axis_size("spax")
    device = lax.axis_index("spax")
    spaxels = cube.shape[0]
    total_bins = owner_bins.shape[0]
    count = templates.shape[0]
    own_spaxels = spaxels // devices
    own_slots = total_bins // devices
    here = device.reshape(1).astype(jnp.int32)
    templates = pltpu.with_memory_space_constraint(templates, pltpu.HBM)
    columns = pltpu.with_memory_space_constraint(cube.T, pltpu.HBM)
    begins = pltpu.with_memory_space_constraint(line_start, pltpu.HBM)
    spans = pltpu.with_memory_space_constraint(line_width, pltpu.HBM)
    bins = pltpu.with_memory_space_constraint(bin_id[None, :], pltpu.HBM)
    owner = pltpu.with_memory_space_constraint(owner_bins[None, :], pltpu.HBM)
    cores = [list(range(core, devices, 2)) for core in range(2)]
    swap = [(d, d ^ 1) for d in range(devices)]

    partial = project(here, bins, owner, columns, templates)
    partial, here_after = lax.optimization_barrier((partial, here))
    received = lax.all_to_all(partial.reshape(devices, own_slots, count), "spax", 0, 0)

    same, other = cube_windows(here_after, begins, spans, columns, devices)
    other = lax.ppermute(other, "spax", swap)
    gram, first, scale = gram_inverse(templates, 512)
    received, same, other, gram, first, scale = lax.optimization_barrier(
        (received, same, other, gram, first, scale)
    )
    head = own_slots * (count // LANES)
    parcel = in_vmem(
        pack_kernel,
        jax.ShapeDtypeStruct((devices // 2, head + same.shape[1], LANES), F32),
        "pack",
        received,
        same,
        other,
    )
    parcel, gram, first, scale = lax.optimization_barrier((parcel, gram, first, scale))
    near = lax.all_to_all(parcel, "spax", 0, 0, axis_index_groups=cores)
    inverse = in_vmem(finish_kernel, jax.ShapeDtypeStruct((count, count), F32), "finish", gram, first, scale)
    far = lax.ppermute(near, "spax", swap)

    own = lambda x: lax.dynamic_slice_in_dim(x, device * own_spaxels, own_spaxels, 1)
    return owned(here, bins, owner, own(line_start), own(line_width), near, far, inverse, templates, own_slots, 512)


def solution(mesh):
    placed = (
        P("strips", "spax"),
        P(),
        P("strips"),
        P("strips"),
        P(None, "strips"),
        P(None, "strips"),
    )
    return jax.shard_map(
        shards,
        mesh=mesh,
        in_specs=placed,
        out_specs=(P(("strips", "spax"), None), P(None, ("strips", "spax"))),
        check_vma=False,
    )
```

time: 74.1 us -> 74.9 us (1.011)
  blocking collectives: 0 us -> 17.5 us
  waiting for transfers between devices: 11.2 us -> 0.01 us
  Pallas kernels: 38.2 us -> 47.6 us
  local copies, waits for them, and re-layouts: 9.77 us -> 0.71 us
  starting transfers between devices: 13.7 us -> 7.84 us
    all_to_all x0 -> x1, blocking collectives: none -> 17.5 us  [shards(): near = lax.all_to_all(parcel, 'spax', 0, 0, axis_index_groups=cores)]
    pallas_call x2 -> x3, Pallas kernels: 16.9 us -> 34.3 us  [the longest x1 17.1 us: owned(): pl.pallas_call(functools.partial(owner_kernel, chunk=chunk), in_specs=[sm...]
    all_to_all x1 -> x0, waiting for transfers between devices: 11.2 us -> none  [shards(): arrived = lax.all_to_all(parcel, 'spax', 0, 0)]
    pallas_call x3 -> x2, Pallas kernels: 15.1 us -> 5.67 us  [in_vmem(): pl.pallas_call(kernel, out_shape=shapes, compiler_params=pltpu.CompilerPa...]
    unnamed x20 -> x0, local copies, waits for them, and re-layouts: 9.01 us -> none
    all_to_all x1 -> x0, starting transfers between devices: 6.19 us -> none  [shards(): arrived = lax.all_to_all(parcel, 'spax', 0, 0)]
    pallas_call x1, Pallas kernels: 6.13 us -> 7.56 us  [project(): pl.pallas_call(functools.partial(project_kernel, chunk=chunk), grid=(slot...]
  transfers between devices with their start and end apart: 2 -> 3, of which waited for: 1 -> 0; matrix products, arithmetic and copies ran while one was open for 1% -> 1% of each run, Pallas kernels for 27% -> 31%
where the time goes in v3:
time: 74.9 us; the launch traced here: 74.4 us
  Pallas kernels  47.6 us (64%)
  blocking collectives  17.5 us (23%)
  starting transfers between devices  7.84 us (10%)
  between operations  0.87 us (1%)
    all_to_all x1, blocking collectives, shards(): near = lax.all_to_all(parcel, 'spax', 0, 0, axis_index_groups=cores)  17.5 us
    pallas_call x1, Pallas kernels, owned(): pl.pallas_call(functools.partial(owner_kernel, chunk=chunk), in_specs=[sm...  17.1 us
    pallas_call x1, Pallas kernels, gram_inverse(): pl.pallas_call(functools.partial(gram_kernel, chunk=chunk), in_specs=[pl....  10.6 us
    pallas_call x1, Pallas kernels, project(): pl.pallas_call(functools.partial(project_kernel, chunk=chunk), grid=(slot...  7.56 us
    all_to_all x1, starting transfers between devices, shards(): lax.all_to_all(partial.reshape(devices, own_slots, count), 'spax', 0, 0)  7.37 us
    pallas_call x1, Pallas kernels, cube_windows(): pl.pallas_call(cube_kernel, in_specs=[pl.BlockSpec(memory_space=pltpu.SME...  6.67 us
    pallas_call x2, Pallas kernels, in_vmem(): pl.pallas_call(kernel, out_shape=shapes, compiler_params=pltpu.CompilerPa...  5.67 us
  transfers between devices with their start and end apart: 3, of which 0 were waited for; matrix products, arithmetic and copies ran while one was open for 1% of the time, Pallas kernels for 31%

profile of v3, /device:TPU:0, one launch (start us, length us, event | category | flops | bytes accessed | tf_op | source)
XLA Modules:
  0.0 74.4 jit_solution(14136132695591743427)
XLA Ops:
  0.6 7.6 %project.1 = f32[512,256]{1,0:T(8,128)} custom-call(s32[1]{0:T(128)} %bitcast.device_ref, s32[1,2048]{1,0:T(1,128)} %bitcast.7, s32[1,512]{1,0:T(1,128)} %bitcast.9, f32[224,2048]{1,0:T(8,128)} %bitcast.5, f32[256,3584]{1,0:T(8,128)} %templates_ref.5), custom_call_target="tpu_custom_call" | custom-call | tf_op jit(solution)/shard_map/project/pallas_call | solution.py:107
  8.2 7.4 %all-to-all-start = ((f32[16,32,256]{2,1,0:T(8,128)}), f32[16,32,256]{2,1,0:T(8,128)S(1)}, u32[]{:S(2)}, u32[]{:S(2)}) async-start(f32[16,32,256]{2,1,0:T(8,128)} %bitcast.4), calls=%async_computation | async-start | bytes 1048576 | tf_op jit(solution)/shard_map/all_to_all | solution.py:534
  15.6 6.7 %cube_windows.1 = (f32[8,24,128]{2,1,0:T(8,128)S(1)}, f32[8,24,128]{2,1,0:T(8,128)S(1)}) custom-call(s32[1]{0:T(128)} %bitcast.device_ref, s32[8,2048]{1,0:T(8,128)} %begin_ref.1, s32[8,2048]{1,0:T(8,128)} %span_ref.1, f32[224,2048]{1,0:T(8,128)} %bitcast.6), custom_call_target="tpu_custom_call" | custom-call | tf_op jit(solution)/shard_map/cube_windows/pallas_call | solution.py:356
  22.3 0.5 collective-permute-start
  22.7 10.6 %gram.1 = (f32[256,256]{1,0:T(8,128)S(1)}, f32[128,128]{1,0:T(8,128)S(1)}, f32[1,256]{1,0:T(1,128)S(1)}) custom-call(f32[256,3584]{1,0:T(8,128)} %templates_ref.5), custom_call_target="tpu_custom_call" | custom-call | tf_op jit(solution)/shard_map/gram/pallas_call | solution.py:228
  33.3 0.0 collective-permute-done.other_ref
  33.3 0.0 all-to-all-done.received_ref
  33.4 17.5 %all_to_all.10.near_ref = f32[8,88,128]{2,1,0:T(8,128)S(1)} all-to-all(f32[8,88,128]{2,1,0:T(8,128)S(1)} %pack.1), channel_id=1, replica_groups={{0,2,4,6,8,10,12,14},{1,3,5,7,9,11,13,15},{16,18,20,22,24,26,28,30},{17..., dimensions={0} | all-to-all | bytes 720896 | tf_op jit(solution)/shard_map/all_to_all | solution.py:552
  50.9 0.0 collective-permute-start.1
  50.9 0.7 constant_dynamic-slice_fusion
  51.6 5.6 %finish.1.inverse_ref = f32[256,256]{1,0:T(8,128)S(1)} custom-call(f32[256,256]{1,0:T(8,128)S(1)} %get-tuple-element.33.gram_ref, f32[128,128]{1,0:T(8,128)S(1)} %get-tuple-element.34.first_ref, f32[1,256]{1,0:T(1,128)S(1)} %get-tuple-element.35.scale_ref), custom_call_target="tpu_custom_call" | custom-call | tf_op jit(solution)/shard_map/finish/pallas_call | solution.py:262
  57.2 0.0 collective-permute-done.1.far_ref
  57.2 17.1 %owned.1 = (f32[32,256]{1,0:T(8,128)}, f32[24,128]{1,0:T(8,128)}) custom-call(s32[1]{0:T(128)} %bitcast.device_ref, s32[8,128]{1,0:T(8,128)S(1)} %get-tuple-element.37.starts_ref.begin_ref, s32[1,2048]{1,0:T(1,128)} %bitcast.8, s32[1,512]{1,0:T(1,128)} %bitcast.10, s32[8,128]{1,0:T(8,128)S(1)} %get-tuple-element.37.starts_ref.begin_ref, ...), custom_call_target="tpu_custom_call" | custom-call | tf_op jit(solution)/shard_map/owned/pallas_call | solution.py:494
  (1 shorter events, 0.0 us)
Async XLA Ops:
  8.2 25.1 %all-to-all-start = ((f32[16,32,256]{2,1,0:T(8,128)}), f32[16,32,256]{2,1,0:T(8,128)S(1)}, u32[]{:S(2)}, u32[]{:S(2)}) async-start(f32[16,32,256]{2,1,0:T(8,128)} %bitcast.4), calls=%async_computation | async-start | bytes 1048576 | tf_op jit(solution)/shard_map/all_to_all | solution.py:534
  22.3 11.1 %collective-permute-start = (f32[8,24,128]{2,1,0:T(8,128)S(1)}, f32[8,24,128]{2,1,0:T(8,128)S(1)}, u32[]{:S(2)}, u32[]{:S(2)}) collective-permute-start(f32[8,24,128]{2,1,0:T(8,128)S(1)} %get-tuple-element.22), channel_id=1, source_target_pairs={{0,1},{1,0},{2,3},{3,2},{4,5},{5,4},{6,7},{7,6},{8,9},{9,8},{10,11... | collective-permute-start | bytes 294920 | tf_op jit(solution)/shard_map/ppermute | solution.py:537
  50.9 6.3 %collective-permute-start.1 = (f32[8,88,128]{2,1,0:T(8,128)S(1)}, f32[8,88,128]{2,1,0:T(8,128)S(1)}, u32[]{:S(2)}, u32[]{:S(2)}) collective-permute-start(f32[8,88,128]{2,1,0:T(8,128)S(1)} %all_to_all.10.near_ref), channel_id=1, source_target_pairs={{0,1},{1,0},{2,3},{3,2},{4,5},{5,4},{6,7},{7,6},{8,9},{9,8},{10,11... | collective-permute-start | bytes 1081352 | tf_op jit(solution)/shard_map/ppermute | solution.py:554

commit v4 on v3

--- a/solution.py
+++ b/solution.py
@@ -196,7 +196,7 @@
     return -jnp.concatenate(rows, axis=0)
 
 
-def gram_kernel(templates_ref, gram_ref, first_ref, scale_ref, held_ref, sem, *, chunk):
+def gram_kernel(templates_ref, gram_ref, scale_ref, held_ref, sem, *, chunk):
     count, full_width = templates_ref.shape
 
     def copy(i):
@@ -220,17 +220,15 @@
     gram = gram * row * column
     scale_ref[...] = row
     gram_ref[...] = gram
-    first_ref[...] = invert_tile(gram[:LANES, :LANES])
-
-
-def gram_inverse(templates, chunk):
+
+
+def scaled_gram(templates, chunk):
     count, full_width = templates.shape
     return pl.pallas_call(
         functools.partial(gram_kernel, chunk=chunk),
         in_specs=[pl.BlockSpec(memory_space=pltpu.HBM)],
         out_shape=(
             jax.ShapeDtypeStruct((count, count), F32),
-            jax.ShapeDtypeStruct((LANES, LANES), F32),
             jax.ShapeDtypeStruct((1, count), F32),
         ),
         scratch_shapes=[
@@ -242,8 +240,8 @@
     )(templates)
 
 
-def finish_kernel(gram_ref, first_ref, scale_ref, out_ref):
-    first = first_ref[...]
+def invert_kernel(gram_ref, scale_ref, out_ref):
+    first = invert_tile(gram_ref[:LANES, :LANES])
     side = gram_ref[:LANES, LANES:]
     half = dot_f32(first, side, NN)
     schur = gram_ref[LANES:, LANES:] - dot_f32(side.T, half, NN)
@@ -301,11 +299,10 @@
 
 
 def cube_kernel(
-    device_ref, begin_ref, span_ref, cube_ref, same_ref, other_ref,
-    begins_ref, spans_ref, held_ref, lines_sem, cube_sem,
+    device_ref, begin_ref, span_ref, cube_ref, out_ref, begins_ref, spans_ref, held_ref, lines_sem, cube_sem,
 ):
     width = cube_ref.shape[0]
-    owners = 2 * same_ref.shape[0]
+    owners = out_ref.shape[0]
     device = device_ref[0]
 
     def tile_copy(i):
@@ -333,17 +330,8 @@
             begins_ref[:, lanes],
             spans_ref[:, lanes],
         )
-        value = jnp.concatenate(sums, axis=0)
-        same = i % 2 == device % 2
-
-        @pl.when(same)
-        def _():
-            same_ref[i // 2] = value
-
-        @pl.when(jnp.logical_not(same))
-        def _():
-            other_ref[i // 2] = value
-
+        for r, value in enumerate(sums):
+            out_ref[i, r : r + 1, :] = value
         return carry
 
     lax.fori_loop(0, owners, owner, 0)
@@ -351,16 +339,14 @@
 
 def cube_windows(device, begin, span, cube, devices):
     hbm = pl.BlockSpec(memory_space=pltpu.HBM)
-    width, spaxels = cube.shape
-    half = jax.ShapeDtypeStruct((devices // 2, 3 * begin.shape[0], LANES), F32)
     return pl.pallas_call(
         cube_kernel,
         in_specs=[pl.BlockSpec(memory_space=pltpu.SMEM), hbm, hbm, hbm],
-        out_shape=(half, half),
+        out_shape=jax.ShapeDtypeStruct((devices, 3 * begin.shape[0], LANES), F32),
         scratch_shapes=[
             pltpu.VMEM(begin.shape, jnp.int32),
             pltpu.VMEM(span.shape, jnp.int32),
-            pltpu.VMEM((devices, width, LANES), F32),
+            pltpu.VMEM((devices, cube.shape[0], LANES), F32),
             pltpu.SemaphoreType.DMA((2,)),
             pltpu.SemaphoreType.DMA((devices,)),
         ],
@@ -369,40 +355,41 @@
     )(device, begin, span, cube)
 
 
-def pack_kernel(received_ref, same_ref, other_ref, out_ref):
+def pack_kernel(received_ref, sums_ref, out_ref):
     total = received_ref[0]
     for i in range(1, received_ref.shape[0]):
         total = total + received_ref[i]
-    slots, count = total.shape
-    for half in range(count // LANES):
-        value = total[:, half * LANES : (half + 1) * LANES]
-        for i in range(out_ref.shape[0]):
-            out_ref[i, half * slots : (half + 1) * slots, :] = value
-    head = slots * (count // LANES)
-    out_ref[:, head:, :] = same_ref[...] + other_ref[...]
+    slots = total.shape[0]
+    for i in range(out_ref.shape[0]):
+        half = i % 2
+        out_ref[i, :slots, :] = total[:, half * LANES : (half + 1) * LANES]
+    out_ref[:, slots:, :] = sums_ref[...]
 
 
 def owner_kernel(
-    device_ref, starts_ref, bins_ref, owner_ref, begin_ref, span_ref, near_ref, far_ref, inverse_ref, templates_ref,
-    weights_ref, out_ref, held_ref, continuum_ref, bins_held_ref, owner_held_ref, sem, small_sem, *, chunk,
+    device_ref, bins_ref, owner_ref, begin_ref, span_ref, near_ref, far_ref, inverse_ref, templates_ref,
+    weights_ref, out_ref,
+    held_ref, continuum_ref, bins_held_ref, owner_held_ref, begins_ref, spans_ref, starts_ref, sem, small_sem,
+    *, chunk,
 ):
-    chips = near_ref.shape[0]
-    own_slots, count = weights_ref.shape
-    halves = count // LANES
-    head = own_slots * halves
-    own = begin_ref.shape[1]
+    devices = near_ref.shape[0]
+    slots = weights_ref.shape[0]
+    own = bins_held_ref.shape[1]
     lines = begin_ref.shape[0]
     full_width = templates_ref.shape[1]
     device = device_ref[0]
+    own_lanes = pl.ds(pl.multiple_of(device * own, LANES), own)
 
     def copy(i):
         lanes = pl.ds(i * chunk, chunk)
         return pltpu.make_async_copy(templates_ref.at[:, lanes], held_ref.at[:, lanes], sem.at[i])
 
-    own_bins = bins_ref.at[:, pl.ds(pl.multiple_of(device * own, LANES), own)]
     small_copies = [
-        pltpu.make_async_copy(own_bins, bins_held_ref, small_sem.at[0]),
+        pltpu.make_async_copy(bins_ref.at[:, own_lanes], bins_held_ref, small_sem.at[0]),
         pltpu.make_async_copy(owner_ref, owner_held_ref, small_sem.at[1]),
+        pltpu.make_async_copy(begin_ref.at[:, own_lanes], begins_ref, small_sem.at[2]),
+        pltpu.make_async_copy(span_ref.at[:, own_lanes], spans_ref, small_sem.at[3]),
+        pltpu.make_async_copy(begin_ref.at[:, own_lanes], starts_ref, small_sem.at[4]),
     ]
     for small in small_copies:
         small.start()
@@ -410,8 +397,12 @@
         copy(i).start()
 
     inverse = inverse_ref[...]
-    chip, core = device // 2, device % 2
-    mine = jnp.concatenate([near_ref[chip, h * own_slots : (h + 1) * own_slots, :] for h in range(halves)], axis=1)
+    low_first = device % 2 == 0
+
+    def halves(near, far):
+        return jnp.where(low_first, near, far), jnp.where(low_first, far, near)
+
+    mine = jnp.concatenate(halves(near_ref[device, :slots, :], far_ref[device, :slots, :]), axis=1)
     weights_ref[...] = dot_f32(mine, inverse, NN)
 
     for small in small_copies:
@@ -419,45 +410,29 @@
     bins = jnp.broadcast_to(bins_held_ref[...], (SUB, own)).T[:, :1]
     member = jnp.where(bins == owner_held_ref[...], 1.0, 0.0).astype(BF16)
     picked = []
-    for h in range(halves):
-        rows = slice(h * own_slots, (h + 1) * own_slots)
-        blocks = []
-        for i in range(chips):
-            near, far = near_ref[i, rows, :], far_ref[i, rows, :]
-            blocks += [jnp.where(core == 0, near, far), jnp.where(core == 0, far, near)]
-        hi, mid, low = split3(jnp.concatenate(blocks, axis=0))
+    for half in (near_ref, far_ref):
+        hi, mid, low = split3(half[:, :slots, :].reshape(devices * slots, LANES))
         picked.append(dot(member, hi, NN) + (dot(member, mid, NN) + dot(member, low, NN)))
-    spaxel_weights = dot_f32(jnp.concatenate(picked, axis=1), inverse, NN)
-
-    hi, mid, low = split3(spaxel_weights)
-    all_parts = jnp.concatenate([hi, mid, low], axis=0)
+    spaxel_weights = dot_f32(jnp.concatenate(halves(*picked), axis=1), inverse, NN)
+
     for i in range(full_width // chunk):
         copy(i).wait()
-        first, second, third = split3(held_ref[:, i * chunk : (i + 1) * chunk])
-        by_first = dot(all_parts, first, NN)
-        by_second = dot(all_parts[: 2 * own], second, NN)
-        by_third = dot(hi, third, NN)
-        value = by_first[:own] + (
-            (by_first[own : 2 * own] + by_second[:own]) + (by_first[2 * own :] + by_second[own:] + by_third)
-        )
+        value = dot_f32(spaxel_weights, held_ref[:, i * chunk : (i + 1) * chunk], NN)
         for t in range(chunk // LANES):
             continuum_ref[i * (chunk // LANES) + t] = value[:, t * LANES : (t + 1) * LANES]
     continuum_ref[full_width // LANES] = jnp.zeros((own, LANES), F32)
 
-    begin = begin_ref[...]
-    span = span_ref[...].astype(F32)
+    begin = begins_ref[...]
+    span = spans_ref[...].astype(F32)
     centre = 2.0 * (begin & (LANES - 1)).astype(F32) + span - 1.0
-    pad = jnp.zeros((LANES - 2 * lines, own), F32)
-    columns = jnp.concatenate([centre, span, pad], axis=0).T
-    lanes = lax.broadcasted_iota(jnp.int32, (SUB, LANES), 1)
-    twice = (2 * lanes).astype(F32)
     rows_at = lax.broadcasted_iota(jnp.int32, (SUB, LANES), 0)
     at_row = [rows_at == r for r in range(SUB)]
-    found = []
-    for g in range(own // SUB):
-        rows = slice(g * SUB, (g + 1) * SUB)
-        result = jnp.zeros((SUB, LANES), F32)
-        for j in range(lines):
+    twice = 2.0 * lax.broadcasted_iota(jnp.int32, (LANES, own), 0).astype(F32)
+    sums = [None] * (3 * lines)
+    for j in range(lines):
+        picks = ([], [])
+        for g in range(own // SUB):
+            rows = slice(g * SUB, (g + 1) * SUB)
             left = right = None
             for r in range(SUB):
                 tile = lax.shift_right_logical(starts_ref[j, g * SUB + r], 7)
@@ -465,50 +440,53 @@
                 b = continuum_ref[tile + 1, rows, :]
                 left = a if left is None else jnp.where(at_row[r], a, left)
                 right = b if right is None else jnp.where(at_row[r], b, right)
-            width = jnp.broadcast_to(columns[rows, lines + j : lines + j + 1], (SUB, LANES))
-            m = twice - jnp.broadcast_to(columns[rows, j : j + 1], (SUB, LANES))
-            n = m + 2.0 * LANES
-            left = jnp.where(jnp.abs(m) < width, left, 0.0)
-            right = jnp.where(jnp.abs(n) < width, right, 0.0)
-            left_m = left * m
-            right_n = right * n
-            for k, term in enumerate((left + right, left_m + right_n, left_m * m + right_n * n)):
-                total = jnp.sum(term, axis=1, keepdims=True)
-                result = jnp.where(lanes == k * lines + j, total, result)
-        found.append(result)
-    continuum_sums = jnp.concatenate(found, axis=0).T[: 3 * lines, :]
-
-    cube_sums = near_ref[0, head:, :]
-    for i in range(1, chips):
-        cube_sums = cube_sums + near_ref[i, head:, :]
+            picks[0].append(left)
+            picks[1].append(right)
+        terms = None
+        for side in range(2):
+            block = jnp.concatenate(picks[side], axis=0).T
+            m = twice + (2.0 * LANES * side - centre[j : j + 1])
+            masked = jnp.where(jnp.abs(m) < span[j : j + 1], block, 0.0)
+            weighted = masked * m
+            new = [masked, weighted, weighted * m]
+            terms = new if terms is None else [x + y for x, y in zip(terms, new)]
+        for k in range(3):
+            sums[k * lines + j] = jnp.sum(terms[k], axis=0, keepdims=True)
+    continuum_sums = jnp.concatenate(sums, axis=0)
+
+    cube_sums = near_ref[0, slots:, :]
+    for i in range(1, devices):
+        cube_sums = cube_sums + near_ref[i, slots:, :]
     scale = jnp.concatenate([span, span * span, span * span * span], axis=0)
     out_ref[...] = (cube_sums - continuum_sums) / scale
 
 
-def owned(device, bins, owner, begin, span, near, far, inverse, templates, own_slots, chunk):
+def owned(device, bins, owner, begin, span, near, far, inverse, templates, own_slots, own, chunk):
     vmem = pl.BlockSpec(memory_space=pltpu.VMEM)
-    smem = pl.BlockSpec(memory_space=pltpu.SMEM)
     hbm = pl.BlockSpec(memory_space=pltpu.HBM)
-    own = begin.shape[1]
     count, full_width = templates.shape
+    lines = begin.shape[0]
     return pl.pallas_call(
         functools.partial(owner_kernel, chunk=chunk),
-        in_specs=[smem, smem, hbm, hbm] + [vmem] * 5 + [hbm],
+        in_specs=[pl.BlockSpec(memory_space=pltpu.SMEM)] + [hbm] * 4 + [vmem] * 3 + [hbm],
         out_shape=(
             jax.ShapeDtypeStruct((own_slots, count), F32),
-            jax.ShapeDtypeStruct((3 * begin.shape[0], own), F32),
+            jax.ShapeDtypeStruct((3 * lines, own), F32),
         ),
         scratch_shapes=[
             pltpu.VMEM((count, full_width), F32),
             pltpu.VMEM((full_width // LANES + 1, own, LANES), F32),
             pltpu.VMEM((1, own), jnp.int32),
             pltpu.VMEM(owner.shape, jnp.int32),
+            pltpu.VMEM((lines, own), jnp.int32),
+            pltpu.VMEM((lines, own), jnp.int32),
+            pltpu.SMEM((lines, own), jnp.int32),
             pltpu.SemaphoreType.DMA((full_width // chunk,)),
-            pltpu.SemaphoreType.DMA((2,)),
+            pltpu.SemaphoreType.DMA((5,)),
         ],
         compiler_params=pltpu.CompilerParams(vmem_limit_bytes=VMEM_LIMIT),
         name="owned",
-    )(device, begin, bins, owner, begin, span, near, far, inverse, templates)
+    )(device, bins, owner, begin, span, near, far, inverse, templates)
 
 
 def shards(cube, templates, bin_id, owner_bins, line_start, line_width):
@@ -520,41 +498,32 @@
     own_spaxels = spaxels // devices
     own_slots = total_bins // devices
     here = device.reshape(1).astype(jnp.int32)
-    templates = pltpu.with_memory_space_constraint(templates, pltpu.HBM)
-    columns = pltpu.with_memory_space_constraint(cube.T, pltpu.HBM)
-    begins = pltpu.with_memory_space_constraint(line_start, pltpu.HBM)
-    spans = pltpu.with_memory_space_constraint(line_width, pltpu.HBM)
-    bins = pltpu.with_memory_space_constraint(bin_id[None, :], pltpu.HBM)
-    owner = pltpu.with_memory_space_constraint(owner_bins[None, :], pltpu.HBM)
-    cores = [list(range(core, devices, 2)) for core in range(2)]
-    swap = [(d, d ^ 1) for d in range(devices)]
+    pin = lambda x: pltpu.with_memory_space_constraint(x, pltpu.HBM)
+    templates, columns = pin(templates), pin(cube.T)
+    begin, span = pin(line_start), pin(line_width)
+    bins, owner = pin(bin_id[None, :]), pin(owner_bins[None, :])
 
     partial = project(here, bins, owner, columns, templates)
     partial, here_after = lax.optimization_barrier((partial, here))
     received = lax.all_to_all(partial.reshape(devices, own_slots, count), "spax", 0, 0)
 
-    same, other = cube_windows(here_after, begins, spans, columns, devices)
-    other = lax.ppermute(other, "spax", swap)
-    gram, first, scale = gram_inverse(templates, 512)
-    received, same, other, gram, first, scale = lax.optimization_barrier(
-        (received, same, other, gram, first, scale)
-    )
-    head = own_slots * (count // LANES)
+    sums = cube_windows(here_after, begin, span, columns, devices)
+    gram, scale = scaled_gram(templates, 512)
+    received, sums, gram, scale = lax.optimization_barrier((received, sums, gram, scale))
     parcel = in_vmem(
         pack_kernel,
-        jax.ShapeDtypeStruct((devices // 2, head + same.shape[1], LANES), F32),
+        jax.ShapeDtypeStruct((devices, own_slots + sums.shape[1], LANES), F32),
         "pack",
         received,
-        same,
-        other,
+        sums,
     )
-    parcel, gram, first, scale = lax.optimization_barrier((parcel, gram, first, scale))
-    near = lax.all_to_all(parcel, "spax", 0, 0, axis_index_groups=cores)
-    inverse = in_vmem(finish_kernel, jax.ShapeDtypeStruct((count, count), F32), "finish", gram, first, scale)
-    far = lax.ppermute(near, "spax", swap)
-
-    own = lambda x: lax.dynamic_slice_in_dim(x, device * own_spaxels, own_spaxels, 1)
-    return owned(here, bins, owner, own(line_start), own(line_width), near, far, inverse, templates, own_slots, 512)
+    parcel, gram, scale = lax.optimization_barrier((parcel, gram, scale))
+    near = lax.all_to_all(parcel, "spax", 0, 0)
+    inverse = in_vmem(invert_kernel, jax.ShapeDtypeStruct((count, count), F32), "invert", gram, scale)
+    far = lax.ppermute(near, "spax", [(d, d ^ 1) for d in range(devices)])
+    return owned(
+        here, bins, owner, begin, span, near, far, inverse, templates, own_slots, own_spaxels, 512
+    )
 
 
 def solution(mesh):

time: 74.9 us -> 65.3 us (0.87)
  Pallas kernels: 47.6 us -> 36.5 us
  waiting for transfers between devices: 0.01 us -> 2.97 us
    pallas_call x2, Pallas kernels: 27.7 us -> 11.3 us  [the longest x1 7.37 us: owned(): pl.pallas_call(functools.partial(owner_kernel, chunk=chunk), in_specs=[pl...]
    pallas_call x2, Pallas kernels: 5.67 us -> 10.1 us  [in_vmem(): pl.pallas_call(kernel, out_shape=shapes, compiler_params=pltpu.CompilerPa...]
    all_to_all x1, waiting for transfers between devices: 0.01 us -> 2.97 us  [shards(): lax.all_to_all(partial.reshape(devices, own_slots, count), 'spax', 0, 0)]
    pallas_call x1, Pallas kernels: 6.67 us -> 7.54 us  [cube_windows(): pl.pallas_call(cube_kernel, in_specs=[pl.BlockSpec(memory_space=pltpu.SME...]
  transfers between devices with their start and end apart: 3 -> 2, of which waited for: 0 -> 1; matrix products, arithmetic and copies ran while one was open for 1% -> 0% of each run, Pallas kernels for 31% -> 33%
where the time goes in v4:
time: 65.3 us; the launch traced here: 65 us
  Pallas kernels  36.5 us (56%)
  blocking collectives  17.1 us (26%)
  starting transfers between devices  7.48 us (11%)
  waiting for transfers between devices  2.97 us (5%)
  between operations  0.85 us (1%)
    all_to_all x1, blocking collectives, shards(): near = lax.all_to_all(parcel, 'spax', 0, 0)  17.1 us
    pallas_call x2, Pallas kernels, in_vmem(): pl.pallas_call(kernel, out_shape=shapes, compiler_params=pltpu.CompilerPa...  10.1 us
    pallas_call x1, Pallas kernels, project(): pl.pallas_call(functools.partial(project_kernel, chunk=chunk), grid=(slot...  7.56 us
    pallas_call x1, Pallas kernels, cube_windows(): pl.pallas_call(cube_kernel, in_specs=[pl.BlockSpec(memory_space=pltpu.SME...  7.54 us
    all_to_all x1, starting transfers between devices, shards(): lax.all_to_all(partial.reshape(devices, own_slots, count), 'spax', 0, 0)  7.37 us
    pallas_call x1, Pallas kernels, owned(): pl.pallas_call(functools.partial(owner_kernel, chunk=chunk), in_specs=[pl...  7.37 us
    pallas_call x1, Pallas kernels, scaled_gram(): pl.pallas_call(functools.partial(gram_kernel, chunk=chunk), in_specs=[pl....  3.95 us
    all_to_all x1, waiting for transfers between devices, shards(): lax.all_to_all(partial.reshape(devices, own_slots, count), 'spax', 0, 0)  2.97 us
  transfers between devices with their start and end apart: 2, of which 1 were waited for; matrix products, arithmetic and copies ran while one was open for 0% of the time, Pallas kernels for 33%

profile of v4, /device:TPU:0, one launch (start us, length us, event | category | flops | bytes accessed | tf_op | source)
XLA Modules:
  0.0 65.0 jit_solution(13343448270032678824)
XLA Ops:
  0.6 7.6 %project.1 = f32[512,256]{1,0:T(8,128)} custom-call(s32[1]{0:T(128)} %bitcast.device_ref, s32[1,2048]{1,0:T(1,128)} %bitcast.7, s32[1,512]{1,0:T(1,128)} %bitcast.9, f32[224,2048]{1,0:T(8,128)} %bitcast.5, f32[256,3584]{1,0:T(8,128)} %templates_ref.5), custom_call_target="tpu_custom_call" | custom-call | tf_op jit(solution)/shard_map/project/pallas_call | solution.py:107
  8.2 7.4 %all-to-all-start = ((f32[16,32,256]{2,1,0:T(8,128)}), f32[16,32,256]{2,1,0:T(8,128)S(1)}, u32[]{:S(2)}, u32[]{:S(2)}) async-start(f32[16,32,256]{2,1,0:T(8,128)} %bitcast.4), calls=%async_computation | async-start | bytes 1048576 | tf_op jit(solution)/shard_map/all_to_all | solution.py:508
  15.6 3.9 %gram.1 = (f32[256,256]{1,0:T(8,128)S(1)}, f32[1,256]{1,0:T(1,128)S(1)}) custom-call(f32[256,3584]{1,0:T(8,128)} %templates_ref.5), custom_call_target="tpu_custom_call" | custom-call | tf_op jit(solution)/shard_map/gram/pallas_call | solution.py:227
  19.5 7.5 %cube_windows.1.sums_ref = f32[16,24,128]{2,1,0:T(8,128)S(1)} custom-call(s32[1]{0:T(128)} %bitcast.device_ref, s32[8,2048]{1,0:T(8,128)} %begin_ref.3, s32[8,2048]{1,0:T(8,128)} %span_ref.3, f32[224,2048]{1,0:T(8,128)} %bitcast.6), custom_call_target="tpu_custom_call" | custom-call | tf_op jit(solution)/shard_map/cube_windows/pallas_call | solution.py:342
  27.1 3.0 %all-to-all-done.received_ref = f32[16,32,256]{2,1,0:T(8,128)S(1)} async-done(((f32[16,32,256]{2,1,0:T(8,128)}), f32[16,32,256]{2,1,0:T(8,128)S(1)}, u32[]{:S(2)}, u32[]{:S(2)}) %all-to-all-start) | async-done | bytes 524320 | tf_op jit(solution)/shard_map/all_to_all | solution.py:508
  30.1 17.1 %all_to_all.10.near_ref = f32[16,56,128]{2,1,0:T(8,128)S(1)} all-to-all(f32[16,56,128]{2,1,0:T(8,128)S(1)} %pack.1), channel_id=1, replica_groups=mesh['strips'=2,'spax'=16] {'spax'}, dimensions={0} | all-to-all | bytes 917504 | tf_op jit(solution)/shard_map/all_to_all | solution.py:521
  47.2 0.1 collective-permute-start
  47.4 10.1 %invert.1.inverse_ref = f32[256,256]{1,0:T(8,128)S(1)} custom-call(f32[256,256]{1,0:T(8,128)S(1)} %get-tuple-element.22.gram_ref, f32[1,256]{1,0:T(1,128)S(1)} %get-tuple-element.23.scale_ref), custom_call_target="tpu_custom_call" | custom-call | tf_op jit(solution)/shard_map/invert/pallas_call | solution.py:260
  57.4 0.0 collective-permute-done.far_ref
  57.4 7.4 %owned.1 = (f32[32,256]{1,0:T(8,128)}, f32[24,128]{1,0:T(8,128)}) custom-call(s32[1]{0:T(128)} %bitcast.device_ref, s32[1,2048]{1,0:T(1,128)} %bitcast.8, s32[1,512]{1,0:T(1,128)} %bitcast.10, s32[8,2048]{1,0:T(8,128)} %begin_ref.3, s32[8,2048]{1,0:T(8,128)} %span_ref.3, f32[16,56,128]{2,1,0:T(8,128)S(1)} %all_to_all.10.near_ref, ...), custom_call_target="tpu_custom_call" | custom-call | tf_op jit(solution)/shard_map/owned/pallas_call | solution.py:469
  (1 shorter events, 0.0 us)
Async XLA Ops:
  8.2 21.8 %all-to-all-start = ((f32[16,32,256]{2,1,0:T(8,128)}), f32[16,32,256]{2,1,0:T(8,128)S(1)}, u32[]{:S(2)}, u32[]{:S(2)}) async-start(f32[16,32,256]{2,1,0:T(8,128)} %bitcast.4), calls=%async_computation | async-start | bytes 1048576 | tf_op jit(solution)/shard_map/all_to_all | solution.py:508
  47.2 10.2 %collective-permute-start = (f32[16,56,128]{2,1,0:T(8,128)S(1)}, f32[16,56,128]{2,1,0:T(8,128)S(1)}, u32[]{:S(2)}, u32[]{:S(2)}) collective-permute-start(f32[16,56,128]{2,1,0:T(8,128)S(1)} %all_to_all.10.near_ref), channel_id=1, source_target_pairs={{0,1},{1,0},{2,3},{3,2},{4,5},{5,4},{6,7},{7,6},{8,9},{9,8},{10,11... | collective-permute-start | bytes 1376264 | tf_op jit(solution)/shard_map/ppermute | solution.py:523

commit v5 on v4

--- a/solution.py
+++ b/solution.py
@@ -39,11 +39,11 @@
 
 
 def project_kernel(
-    device_ref, bins_ref, owner_ref, cube_ref, templates_ref, out_ref,
+    device_ref, bins_ref, owner_ref, cube_ref, templates_ref, keep_ref, send_ref,
     held_ref, window_ref, bins_held_ref, owner_held_ref, cube_sem, window_sem, small_sem, *, chunk,
 ):
     width, spaxels = cube_ref.shape
-    slots = out_ref.shape[0]
+    slots = keep_ref.shape[0]
     full_width = templates_ref.shape[1]
     first = device_ref[0] * width
     window = window_ref.shape[1]
@@ -95,7 +95,11 @@
         window_copy.wait()
 
     mine = pltpu.roll(window_ref[...], window - (first - base), 1)[:, :width]
-    out_ref[...] = dot_f32(means, mine, NT) * (1.0 / full_width)
+    projections = dot_f32(means, mine, NT) * (1.0 / full_width)
+    low, high = projections[:, :LANES], projections[:, LANES:]
+    low_kept = device_ref[0] % 2 == 0
+    keep_ref[...] = jnp.where(low_kept, low, high)
+    send_ref[...] = jnp.where(low_kept, high, low)
 
 
 def project(device, bins, owner, cube, templates):
@@ -114,8 +118,8 @@
             pl.BlockSpec(memory_space=pltpu.HBM),
             pl.BlockSpec(memory_space=pltpu.HBM),
         ],
-        out_specs=pl.BlockSpec((block, count), lambda i: (i, 0)),
-        out_shape=jax.ShapeDtypeStruct((slots, count), F32),
+        out_specs=[pl.BlockSpec((block, LANES), lambda i: (i, 0))] * 2,
+        out_shape=[jax.ShapeDtypeStruct((slots, LANES), F32)] * 2,
         scratch_shapes=[
             pltpu.VMEM((width, spaxels), F32),
             pltpu.VMEM((count, template_window(width, full_width)), F32),
@@ -355,14 +359,18 @@
     )(device, begin, span, cube)
 
 
+def add_kernel(x_ref, y_ref, out_ref):
+    out_ref[...] = x_ref[...] + y_ref[...]
+
+
 def pack_kernel(received_ref, sums_ref, out_ref):
-    total = received_ref[0]
-    for i in range(1, received_ref.shape[0]):
-        total = total + received_ref[i]
-    slots = total.shape[0]
-    for i in range(out_ref.shape[0]):
-        half = i % 2
-        out_ref[i, :slots, :] = total[:, half * LANES : (half + 1) * LANES]
+    slots = received_ref.shape[1]
+    for half in range(2):
+        total = received_ref[half]
+        for i in range(half + 2, received_ref.shape[0], 2):
+            total = total + received_ref[i]
+        for i in range(half, out_ref.shape[0], 2):
+            out_ref[i, :slots, :] = total
     out_ref[:, slots:, :] = sums_ref[...]
 
 
@@ -499,16 +507,21 @@
     own_slots = total_bins // devices
     here = device.reshape(1).astype(jnp.int32)
     pin = lambda x: pltpu.with_memory_space_constraint(x, pltpu.HBM)
+    raw_templates = templates
     templates, columns = pin(templates), pin(cube.T)
     begin, span = pin(line_start), pin(line_width)
     bins, owner = pin(bin_id[None, :]), pin(owner_bins[None, :])
 
-    partial = project(here, bins, owner, columns, templates)
-    partial, here_after = lax.optimization_barrier((partial, here))
-    received = lax.all_to_all(partial.reshape(devices, own_slots, count), "spax", 0, 0)
+    swap = [(d, d ^ 1) for d in range(devices)]
+    keep, send = project(here, bins, owner, columns, templates)
+    swapped = lax.ppermute(send, "spax", swap)
+    partial = in_vmem(add_kernel, jax.ShapeDtypeStruct(keep.shape, F32), "add", keep, swapped)
+    partial, here_after, later = lax.optimization_barrier((partial, here, raw_templates))
+    later = pin(later)
+    received = lax.all_to_all(partial.reshape(devices, own_slots, LANES), "spax", 0, 0)
 
     sums = cube_windows(here_after, begin, span, columns, devices)
-    gram, scale = scaled_gram(templates, 512)
+    gram, scale = scaled_gram(later, 512)
     received, sums, gram, scale = lax.optimization_barrier((received, sums, gram, scale))
     parcel = in_vmem(
         pack_kernel,
@@ -520,9 +533,10 @@
     parcel, gram, scale = lax.optimization_barrier((parcel, gram, scale))
     near = lax.all_to_all(parcel, "spax", 0, 0)
     inverse = in_vmem(invert_kernel, jax.ShapeDtypeStruct((count, count), F32), "invert", gram, scale)
-    far = lax.ppermute(near, "spax", [(d, d ^ 1) for d in range(devices)])
+    near, inverse = lax.optimization_barrier((near, inverse))
+    far = lax.ppermute(near, "spax", swap)
     return owned(
-        here, bins, owner, begin, span, near, far, inverse, templates, own_slots, own_spaxels, 512
+        here, bins, owner, begin, span, near, far, inverse, later, own_slots, own_spaxels, 512
     )
 
 

time: 65.3 us -> 58.4 us (0.89)
  blocking collectives: 17.1 us -> 0 us
  starting transfers between devices: 7.48 us -> 14.1 us
  waiting for transfers between devices: 2.97 us -> 5.87 us
  Pallas kernels: 36.5 us -> 37.2 us
    all_to_all x1 -> x0, blocking collectives: 17.1 us -> none  [shards(): near = lax.all_to_all(parcel, 'spax', 0, 0)]
    all_to_all x1 -> x2, starting transfers between devices: 7.37 us -> 13.4 us  [the longest x1 7.28 us: shards(): lax.all_to_all(partial.reshape(devices, own_slots, LANES), 'spax', 0, 0)]
    ppermute x1 -> x2, waiting for transfers between devices: 0.01 us -> 2.86 us  [the longest x1 1.7 us: shards(): far = lax.ppermute(near, 'spax', swap)]
    pallas_call x2 -> x3, Pallas kernels: 10.1 us -> 11.6 us  [in_vmem(): pl.pallas_call(kernel, out_shape=shapes, compiler_params=pltpu.CompilerPa...]
    pallas_call x1, Pallas kernels: 7.56 us -> 6.77 us  [project(): pl.pallas_call(functools.partial(project_kernel, chunk=chunk), grid=(slot...]
    all_to_all x1 -> x2, waiting for transfers between devices: 2.97 us -> 3 us  [the longest x1 3 us: shards(): near = lax.all_to_all(parcel, 'spax', 0, 0)]
  transfers between devices with their start and end apart: 2 -> 4, of which waited for: 1 -> 3; matrix products, arithmetic and copies ran while one was open for 0% -> 0% of each run, Pallas kernels for 33% -> 37%
where the time goes in v5:
time: 58.4 us; the launch traced here: 58 us
  Pallas kernels  37.2 us (64%)
  starting transfers between devices  14.1 us (24%)
  waiting for transfers between devices  5.87 us (10%)
  between operations  0.85 us (1%)
    pallas_call x3, Pallas kernels, in_vmem(): pl.pallas_call(kernel, out_shape=shapes, compiler_params=pltpu.CompilerPa...  11.6 us
    pallas_call x1, Pallas kernels, cube_windows(): pl.pallas_call(cube_kernel, in_specs=[pl.BlockSpec(memory_space=pltpu.SME...  7.54 us
    pallas_call x1, Pallas kernels, owned(): pl.pallas_call(functools.partial(owner_kernel, chunk=chunk), in_specs=[pl...  7.36 us
    all_to_all x1, starting transfers between devices, shards(): lax.all_to_all(partial.reshape(devices, own_slots, LANES), 'spax', 0, 0)  7.28 us
    pallas_call x1, Pallas kernels, project(): pl.pallas_call(functools.partial(project_kernel, chunk=chunk), grid=(slot...  6.77 us
    all_to_all x1, starting transfers between devices, shards(): near = lax.all_to_all(parcel, 'spax', 0, 0)  6.17 us
    pallas_call x1, Pallas kernels, scaled_gram(): pl.pallas_call(functools.partial(gram_kernel, chunk=chunk), in_specs=[pl....  3.96 us
    all_to_all x1, waiting for transfers between devices, shards(): near = lax.all_to_all(parcel, 'spax', 0, 0)  3 us
  transfers between devices with their start and end apart: 4, of which 3 were waited for; matrix products, arithmetic and copies ran while one was open for 0% of the time, Pallas kernels for 37%

profile of v5, /device:TPU:0, one launch (start us, length us, event | category | flops | bytes accessed | tf_op | source)
XLA Modules:
  0.0 58.0 jit_solution(7489187604096212703)
XLA Ops:
  0.6 6.8 %project.1 = (f32[512,128]{1,0:T(8,128)S(1)}, f32[512,128]{1,0:T(8,128)S(1)}) custom-call(s32[1]{0:T(128)} %bitcast.device_ref, s32[1,2048]{1,0:T(1,128)} %bitcast.7, s32[1,512]{1,0:T(1,128)} %bitcast.9, f32[224,2048]{1,0:T(8,128)} %bitcast.5, f32[256,3584]{1,0:T(8,128)} %templates_ref.3), custom_call_target="tpu_custom_call" | custom-call | tf_op jit(solution)/shard_map/project/pallas_call | solution.py:111
  7.4 0.5 collective-permute-start
  7.9 1.2 %collective-permute-done.y_ref = f32[512,128]{1,0:T(8,128)S(1)} collective-permute-done((f32[512,128]{1,0:T(8,128)S(1)}, f32[512,128]{1,0:T(8,128)S(1)}, u32[]{:S(2)}, u32[]{:S(2)}) %collective-permute-start) | collective-permute-done | bytes 262176 | tf_op jit(solution)/shard_map/ppermute | solution.py:517
  9.1 0.7 %add.1 = f32[512,128]{1,0:T(8,128)} custom-call(f32[512,128]{1,0:T(8,128)S(1)} %get-tuple-element.18.x_ref, f32[512,128]{1,0:T(8,128)S(1)} %collective-permute-done.y_ref), custom_call_target="tpu_custom_call" | custom-call | tf_op jit(solution)/shard_map/add/pallas_call | solution.py:264
  9.8 7.3 %all-to-all-start = ((f32[16,32,128]{2,1,0:T(8,128)}), f32[16,32,128]{2,1,0:T(8,128)S(1)}, u32[]{:S(2)}, u32[]{:S(2)}) async-start(f32[16,32,128]{2,1,0:T(8,128)} %bitcast.4), calls=%async_computation | async-start | bytes 524288 | tf_op jit(solution)/shard_map/all_to_all | solution.py:521
  17.1 4.0 %gram.1 = (f32[256,256]{1,0:T(8,128)S(1)}, f32[1,256]{1,0:T(1,128)S(1)}) custom-call(f32[256,3584]{1,0:T(8,128)} %templates_ref.3), custom_call_target="tpu_custom_call" | custom-call | tf_op jit(solution)/shard_map/gram/pallas_call | solution.py:231
  21.1 7.5 %cube_windows.1.sums_ref = f32[16,24,128]{2,1,0:T(8,128)S(1)} custom-call(s32[1]{0:T(128)} %bitcast.device_ref, s32[8,2048]{1,0:T(8,128)} %begin_ref.3, s32[8,2048]{1,0:T(8,128)} %span_ref.3, f32[224,2048]{1,0:T(8,128)} %bitcast.6), custom_call_target="tpu_custom_call" | custom-call | tf_op jit(solution)/shard_map/cube_windows/pallas_call | solution.py:346
  28.6 0.0 all-to-all-done.received_ref
  28.6 0.8 %pack.1 = f32[16,56,128]{2,1,0:T(8,128)} custom-call(f32[16,32,128]{2,1,0:T(8,128)S(1)} %all-to-all-done.received_ref, f32[16,24,128]{2,1,0:T(8,128)S(1)} %cube_windows.1.sums_ref), custom_call_target="tpu_custom_call" | custom-call | tf_op jit(solution)/shard_map/pack/pallas_call | solution.py:264
  29.4 6.2 %all-to-all-start.1 = ((f32[16,56,128]{2,1,0:T(8,128)}), f32[16,56,128]{2,1,0:T(8,128)S(1)}, u32[]{:S(2)}, u32[]{:S(2)}) async-start(f32[16,56,128]{2,1,0:T(8,128)} %pack.1), calls=%async_computation.1 | async-start | bytes 917504 | tf_op jit(solution)/shard_map/all_to_all | solution.py:534
  35.6 10.1 %invert.1.inverse_ref = f32[256,256]{1,0:T(8,128)S(1)} custom-call(f32[256,256]{1,0:T(8,128)S(1)} %get-tuple-element.30.gram_ref, f32[1,256]{1,0:T(1,128)S(1)} %get-tuple-element.31.scale_ref), custom_call_target="tpu_custom_call" | custom-call | tf_op jit(solution)/shard_map/invert/pallas_call | solution.py:264
  45.7 3.0 %all-to-all-done.1.near_ref = f32[16,56,128]{2,1,0:T(8,128)S(1)} async-done(((f32[16,56,128]{2,1,0:T(8,128)}), f32[16,56,128]{2,1,0:T(8,128)S(1)}, u32[]{:S(2)}, u32[]{:S(2)}) %all-to-all-start.1) | async-done | bytes 458784 | tf_op jit(solution)/shard_map/all_to_all | solution.py:534
  48.7 0.1 collective-permute-start.1
  48.8 1.7 %collective-permute-done.1.far_ref = f32[16,56,128]{2,1,0:T(8,128)S(1)} collective-permute-done((f32[16,56,128]{2,1,0:T(8,128)S(1)}, f32[16,56,128]{2,1,0:T(8,128)S(1)}, u32[]{:S(2)}, u32[]{:S(2)}) %collective-permute-start.1) | collective-permute-done | bytes 458784 | tf_op jit(solution)/shard_map/ppermute | solution.py:537
  50.5 7.4 %owned.1 = (f32[32,256]{1,0:T(8,128)}, f32[24,128]{1,0:T(8,128)}) custom-call(s32[1]{0:T(128)} %bitcast.device_ref, s32[1,2048]{1,0:T(1,128)} %bitcast.8, s32[1,512]{1,0:T(1,128)} %bitcast.10, s32[8,2048]{1,0:T(8,128)} %begin_ref.3, s32[8,2048]{1,0:T(8,128)} %span_ref.3, f32[16,56,128]{2,1,0:T(8,128)S(1)} %all-to-all-done.1.near_ref, ...), custom_call_target="tpu_custom_call" | custom-call | tf_op jit(solution)/shard_map/owned/pallas_call | solution.py:477
Async XLA Ops:
  7.4 1.7 %collective-permute-start = (f32[512,128]{1,0:T(8,128)S(1)}, f32[512,128]{1,0:T(8,128)S(1)}, u32[]{:S(2)}, u32[]{:S(2)}) collective-permute-start(f32[512,128]{1,0:T(8,128)S(1)} %get-tuple-element.19), channel_id=1, source_target_pairs={{0,1},{1,0},{2,3},{3,2},{4,5},{5,4},{6,7},{7,6},{8,9},{9,8},{10,11... | collective-permute-start | bytes 786440 | tf_op jit(solution)/shard_map/ppermute | solution.py:517
  9.8 18.8 %all-to-all-start = ((f32[16,32,128]{2,1,0:T(8,128)}), f32[16,32,128]{2,1,0:T(8,128)S(1)}, u32[]{:S(2)}, u32[]{:S(2)}) async-start(f32[16,32,128]{2,1,0:T(8,128)} %bitcast.4), calls=%async_computation | async-start | bytes 524288 | tf_op jit(solution)/shard_map/all_to_all | solution.py:521
  29.4 19.3 %all-to-all-start.1 = ((f32[16,56,128]{2,1,0:T(8,128)}), f32[16,56,128]{2,1,0:T(8,128)S(1)}, u32[]{:S(2)}, u32[]{:S(2)}) async-start(f32[16,56,128]{2,1,0:T(8,128)} %pack.1), calls=%async_computation.1 | async-start | bytes 917504 | tf_op jit(solution)/shard_map/all_to_all | solution.py:534
  48.7 1.8 %collective-permute-start.1 = (f32[16,56,128]{2,1,0:T(8,128)S(1)}, f32[16,56,128]{2,1,0:T(8,128)S(1)}, u32[]{:S(2)}, u32[]{:S(2)}) collective-permute-start(f32[16,56,128]{2,1,0:T(8,128)S(1)} %all-to-all-done.1.near_ref), channel_id=1, source_target_pairs={{0,1},{1,0},{2,3},{3,2},{4,5},{5,4},{6,7},{7,6},{8,9},{9,8},{10,11... | collective-permute-start | bytes 1376264 | tf_op jit(solution)/shard_map/ppermute | solution.py:537

commit v6 on v5

--- a/solution.py
+++ b/solution.py
@@ -149,36 +149,27 @@
     for k in range(count):
         block = rows[k]
         first = k * SUB
-        a = {}
-        for i in range(SUB):
-            for j in range(i, SUB):
-                a[i, j] = jnp.broadcast_to(block[i : i + 1, first + j : first + j + 1], (SUB, size))
-
-        def at(i, j):
-            return (i, j) if i <= j else (j, i)
+        columns = [
+            jnp.broadcast_to(block[:, first + j : first + j + 1], (SUB, size)) for j in range(SUB)
+        ]
 
         for p in range(0, SUB, 2):
             q = p + 1
-            pp, pq, qq = a[p, p], a[p, q], a[q, q]
+            of_p = [jnp.broadcast_to(column[p : p + 1, :], (SUB, size)) for column in columns]
+            of_q = [jnp.broadcast_to(column[q : q + 1, :], (SUB, size)) for column in columns]
+            pp, pq, qq = of_p[p], of_p[q], of_q[q]
             inverse = reciprocal(pp * qq - pq * pq)
-            others = [i for i in range(SUB) if i not in (p, q)]
-            old = {i: (a[at(i, p)], a[at(i, q)]) for i in others}
-            new = {
-                i: ((u * qq - v * pq) * inverse, (v * pp - u * pq) * inverse) for i, (u, v) in old.items()
-            }
-            for i in others:
-                for j in others:
-                    if i <= j:
-                        a[i, j] = a[i, j] - new[i][0] * old[j][0] - new[i][1] * old[j][1]
-            for i in others:
-                a[at(i, p)], a[at(i, q)] = new[i]
-            a[p, p], a[p, q], a[q, q] = -(qq * inverse), pq * inverse, -(pp * inverse)
-        columns = []
-        for j in range(SUB):
-            column = a[at(0, j)]
-            for i in range(1, SUB):
-                column = jnp.where(rows_at == i, a[at(i, j)], column)
-            columns.append(column)
+            x, y, z = qq * inverse, -(pq * inverse), pp * inverse
+            by_p = (columns[p] * qq - columns[q] * pq) * inverse
+            by_q = (columns[q] * pp - columns[p] * pq) * inverse
+            at_p, at_q = rows_at == p, rows_at == q
+            take_p = jnp.where(at_p, 1.0 - x, jnp.where(at_q, -y, by_p))
+            take_q = jnp.where(at_q, 1.0 - z, jnp.where(at_p, -y, by_q))
+            for j in range(SUB):
+                if j not in (p, q):
+                    columns[j] = (columns[j] - take_p * of_p[j]) - take_q * of_q[j]
+            columns[p] = jnp.where(at_p, -x, jnp.where(at_q, -y, by_p))
+            columns[q] = jnp.where(at_q, -z, jnp.where(at_p, -y, by_q))
         terms = [columns[j] * jnp.broadcast_to(block[j : j + 1, :], (SUB, size)) for j in range(SUB)]
         while len(terms) > 1:
             terms = [x + y for x, y in zip(terms[::2], terms[1::2])]
@@ -244,7 +235,17 @@
     )(templates)
 
 
-def invert_kernel(gram_ref, scale_ref, out_ref):
+def invert_kernel(
+    gram_ref, scale_ref, templates_ref, out_ref, hi_ref, mid_ref, low_ref, held_ref, sem, *, chunk,
+):
+    full_width = templates_ref.shape[1]
+
+    def copy(i):
+        lanes = pl.ds(i * chunk, chunk)
+        return pltpu.make_async_copy(templates_ref.at[:, lanes], held_ref.at[:, lanes], sem.at[i])
+
+    for i in range(full_width // chunk):
+        copy(i).start()
     first = invert_tile(gram_ref[:LANES, :LANES])
     side = gram_ref[:LANES, LANES:]
     half = dot_f32(first, side, NN)
@@ -258,6 +259,29 @@
     out_ref[:LANES, LANES:] = -cross * far * column[:LANES]
     out_ref[LANES:, :LANES] = -cross.T * near * column[LANES:]
     out_ref[LANES:, LANES:] = last * far * column[LANES:]
+
+    inverse = out_ref[...]
+    for i in range(full_width // chunk):
+        copy(i).wait()
+        lanes = slice(i * chunk, (i + 1) * chunk)
+        hi_ref[:, lanes], mid_ref[:, lanes], low_ref[:, lanes] = split3(dot_f32(inverse, held_ref[:, lanes], NN))
+
+
+def invert(gram, scale, templates, chunk):
+    vmem = pl.BlockSpec(memory_space=pltpu.VMEM)
+    count, full_width = templates.shape
+    part = jax.ShapeDtypeStruct((count, full_width), BF16)
+    return pl.pallas_call(
+        functools.partial(invert_kernel, chunk=chunk),
+        in_specs=[vmem, vmem, pl.BlockSpec(memory_space=pltpu.HBM)],
+        out_shape=(jax.ShapeDtypeStruct((count, count), F32), part, part, part),
+        scratch_shapes=[
+            pltpu.VMEM((count, full_width), F32),
+            pltpu.SemaphoreType.DMA((full_width // chunk,)),
+        ],
+        compiler_params=pltpu.CompilerParams(vmem_limit_bytes=VMEM_LIMIT),
+        name="invert",
+    )(gram, scale, templates)
 
 
 def in_vmem(kernel, shapes, name, *arrays):
@@ -375,22 +399,18 @@
 
 
 def owner_kernel(
-    device_ref, bins_ref, owner_ref, begin_ref, span_ref, near_ref, far_ref, inverse_ref, templates_ref,
+    device_ref, bins_ref, owner_ref, begin_ref, span_ref, near_ref, far_ref, inverse_ref, hi_ref, mid_ref, low_ref,
     weights_ref, out_ref,
-    held_ref, continuum_ref, bins_held_ref, owner_held_ref, begins_ref, spans_ref, starts_ref, sem, small_sem,
+    continuum_ref, bins_held_ref, owner_held_ref, begins_ref, spans_ref, starts_ref, small_sem,
     *, chunk,
 ):
     devices = near_ref.shape[0]
     slots = weights_ref.shape[0]
     own = bins_held_ref.shape[1]
     lines = begin_ref.shape[0]
-    full_width = templates_ref.shape[1]
+    full_width = hi_ref.shape[1]
     device = device_ref[0]
     own_lanes = pl.ds(pl.multiple_of(device * own, LANES), own)
-
-    def copy(i):
-        lanes = pl.ds(i * chunk, chunk)
-        return pltpu.make_async_copy(templates_ref.at[:, lanes], held_ref.at[:, lanes], sem.at[i])
 
     small_copies = [
         pltpu.make_async_copy(bins_ref.at[:, own_lanes], bins_held_ref, small_sem.at[0]),
@@ -401,17 +421,14 @@
     ]
     for small in small_copies:
         small.start()
-    for i in range(full_width // chunk):
-        copy(i).start()
-
-    inverse = inverse_ref[...]
+
     low_first = device % 2 == 0
 
     def halves(near, far):
         return jnp.where(low_first, near, far), jnp.where(low_first, far, near)
 
     mine = jnp.concatenate(halves(near_ref[device, :slots, :], far_ref[device, :slots, :]), axis=1)
-    weights_ref[...] = dot_f32(mine, inverse, NN)
+    weights_ref[...] = dot_f32(mine, inverse_ref[...], NN)
 
     for small in small_copies:
         small.wait()
@@ -421,11 +438,15 @@
     for half in (near_ref, far_ref):
         hi, mid, low = split3(half[:, :slots, :].reshape(devices * slots, LANES))
         picked.append(dot(member, hi, NN) + (dot(member, mid, NN) + dot(member, low, NN)))
-    spaxel_weights = dot_f32(jnp.concatenate(halves(*picked), axis=1), inverse, NN)
+    hi, mid, low = split3(jnp.concatenate(halves(*picked), axis=1))
 
     for i in range(full_width // chunk):
-        copy(i).wait()
-        value = dot_f32(spaxel_weights, held_ref[:, i * chunk : (i + 1) * chunk], NN)
+        lanes = slice(i * chunk, (i + 1) * chunk)
+        first, second, third = hi_ref[:, lanes], mid_ref[:, lanes], low_ref[:, lanes]
+        value = dot(hi, first, NN) + (
+            (dot(mid, first, NN) + dot(hi, second, NN))
+            + (dot(low, first, NN) + dot(mid, second, NN) + dot(hi, third, NN))
+        )
         for t in range(chunk // LANES):
             continuum_ref[i * (chunk // LANES) + t] = value[:, t * LANES : (t + 1) * LANES]
     continuum_ref[full_width // LANES] = jnp.zeros((own, LANES), F32)
@@ -469,32 +490,30 @@
     out_ref[...] = (cube_sums - continuum_sums) / scale
 
 
-def owned(device, bins, owner, begin, span, near, far, inverse, templates, own_slots, own, chunk):
+def owned(device, bins, owner, begin, span, near, far, inverse, parts, own_slots, own, chunk):
     vmem = pl.BlockSpec(memory_space=pltpu.VMEM)
     hbm = pl.BlockSpec(memory_space=pltpu.HBM)
-    count, full_width = templates.shape
+    count, full_width = parts[0].shape
     lines = begin.shape[0]
     return pl.pallas_call(
         functools.partial(owner_kernel, chunk=chunk),
-        in_specs=[pl.BlockSpec(memory_space=pltpu.SMEM)] + [hbm] * 4 + [vmem] * 3 + [hbm],
+        in_specs=[pl.BlockSpec(memory_space=pltpu.SMEM)] + [hbm] * 4 + [vmem] * 6,
         out_shape=(
             jax.ShapeDtypeStruct((own_slots, count), F32),
             jax.ShapeDtypeStruct((3 * lines, own), F32),
         ),
         scratch_shapes=[
-            pltpu.VMEM((count, full_width), F32),
             pltpu.VMEM((full_width // LANES + 1, own, LANES), F32),
             pltpu.VMEM((1, own), jnp.int32),
             pltpu.VMEM(owner.shape, jnp.int32),
             pltpu.VMEM((lines, own), jnp.int32),
             pltpu.VMEM((lines, own), jnp.int32),
             pltpu.SMEM((lines, own), jnp.int32),
-            pltpu.SemaphoreType.DMA((full_width // chunk,)),
             pltpu.SemaphoreType.DMA((5,)),
         ],
         compiler_params=pltpu.CompilerParams(vmem_limit_bytes=VMEM_LIMIT),
         name="owned",
-    )(device, bins, owner, begin, span, near, far, inverse, templates)
+    )(device, bins, owner, begin, span, near, far, inverse, *parts)
 
 
 def shards(cube, templates, bin_id, owner_bins, line_start, line_width):
@@ -532,11 +551,11 @@
     )
     parcel, gram, scale = lax.optimization_barrier((parcel, gram, scale))
     near = lax.all_to_all(parcel, "spax", 0, 0)
-    inverse = in_vmem(invert_kernel, jax.ShapeDtypeStruct((count, count), F32), "invert", gram, scale)
+    inverse, *parts = invert(gram, scale, later, 512)
     near, inverse = lax.optimization_barrier((near, inverse))
     far = lax.ppermute(near, "spax", swap)
     return owned(
-        here, bins, owner, begin, span, near, far, inverse, later, own_slots, own_spaxels, 512
+        here, bins, owner, begin, span, near, far, inverse, parts, own_slots, own_spaxels, 512
     )
 
 

time: 58.4 us -> 64.8 us (1.11)
  local copies, waits for them, and re-layouts: 0 us -> 5.48 us
  Pallas kernels: 37.2 us -> 41 us
  waiting for transfers between devices: 5.87 us -> 2.75 us
    pallas_call x0 -> x1, Pallas kernels: none -> 16.4 us  [invert(): pl.pallas_call(functools.partial(invert_kernel, chunk=chunk), in_specs=[v...]
    pallas_call x3 -> x2, Pallas kernels: 11.6 us -> 1.53 us  [in_vmem(): pl.pallas_call(kernel, out_shape=shapes, compiler_params=pltpu.CompilerPa...]
    unnamed x0 -> x8, local copies, waits for them, and re-layouts: none -> 5.48 us
    all_to_all x1, waiting for transfers between devices: 3 us -> 0.01 us  [shards(): near = lax.all_to_all(parcel, 'spax', 0, 0)]
    pallas_call x1, Pallas kernels: 7.36 us -> 4.84 us  [owned(): pl.pallas_call(functools.partial(owner_kernel, chunk=chunk), in_specs=[pl...]
  transfers between devices with their start and end apart: 4 -> 4, of which waited for: 3 -> 2; matrix products, arithmetic and copies ran while one was open for 0% -> 0% of each run, Pallas kernels for 37% -> 43%
where the time goes in v6:
time: 64.8 us; the launch traced here: 64.4 us
  Pallas kernels  41 us (63%)
  starting transfers between devices  14.2 us (22%)
  local copies, waits for them, and re-layouts  5.48 us (8%)
  waiting for transfers between devices  2.75 us (4%)
  between operations  0.88 us (1%)
    pallas_call x1, Pallas kernels, invert(): pl.pallas_call(functools.partial(invert_kernel, chunk=chunk), in_specs=[v...  16.4 us
    pallas_call x1, Pallas kernels, cube_windows(): pl.pallas_call(cube_kernel, in_specs=[pl.BlockSpec(memory_space=pltpu.SME...  7.54 us
    all_to_all x1, starting transfers between devices, shards(): lax.all_to_all(partial.reshape(devices, own_slots, LANES), 'spax', 0, 0)  7.28 us
    pallas_call x1, Pallas kernels, project(): pl.pallas_call(functools.partial(project_kernel, chunk=chunk), grid=(slot...  6.72 us
    all_to_all x1, starting transfers between devices, shards(): near = lax.all_to_all(parcel, 'spax', 0, 0)  6.19 us
    unnamed x8, local copies, waits for them, and re-layouts  5.48 us
    pallas_call x1, Pallas kernels, owned(): pl.pallas_call(functools.partial(owner_kernel, chunk=chunk), in_specs=[pl...  4.84 us
    pallas_call x1, Pallas kernels, scaled_gram(): pl.pallas_call(functools.partial(gram_kernel, chunk=chunk), in_specs=[pl....  3.96 us
  transfers between devices with their start and end apart: 4, of which 2 were waited for; matrix products, arithmetic and copies ran while one was open for 0% of the time, Pallas kernels for 43%

profile of v6, /device:TPU:0, one launch (start us, length us, event | category | flops | bytes accessed | tf_op | source)
XLA Modules:
  0.0 64.4 jit_solution(10638024638542760483)
XLA Ops:
  0.6 6.7 %project.1 = (f32[512,128]{1,0:T(8,128)S(1)}, f32[512,128]{1,0:T(8,128)S(1)}) custom-call(s32[1]{0:T(128)} %bitcast.device_ref, s32[1,2048]{1,0:T(1,128)} %bitcast.7, s32[1,512]{1,0:T(1,128)} %bitcast.9, f32[224,2048]{1,0:T(8,128)} %bitcast.5, f32[256,3584]{1,0:T(8,128)} %templates_ref.3), custom_call_target="tpu_custom_call" | custom-call | tf_op jit(solution)/shard_map/project/pallas_call | solution.py:111
  7.4 0.5 collective-permute-start
  7.9 1.2 %collective-permute-done.y_ref = f32[512,128]{1,0:T(8,128)S(1)} collective-permute-done((f32[512,128]{1,0:T(8,128)S(1)}, f32[512,128]{1,0:T(8,128)S(1)}, u32[]{:S(2)}, u32[]{:S(2)}) %collective-permute-start) | collective-permute-done | bytes 262176 | tf_op jit(solution)/shard_map/ppermute | solution.py:536
  9.0 0.7 %add.1 = f32[512,128]{1,0:T(8,128)} custom-call(f32[512,128]{1,0:T(8,128)S(1)} %get-tuple-element.22.x_ref, f32[512,128]{1,0:T(8,128)S(1)} %collective-permute-done.y_ref), custom_call_target="tpu_custom_call" | custom-call | tf_op jit(solution)/shard_map/add/pallas_call | solution.py:288
  9.8 7.3 %all-to-all-start = ((f32[16,32,128]{2,1,0:T(8,128)}), f32[16,32,128]{2,1,0:T(8,128)S(1)}, u32[]{:S(2)}, u32[]{:S(2)}) async-start(f32[16,32,128]{2,1,0:T(8,128)} %bitcast.4), calls=%async_computation | async-start | bytes 524288 | tf_op jit(solution)/shard_map/all_to_all | solution.py:540
  17.1 4.0 %gram.1 = (f32[256,256]{1,0:T(8,128)S(1)}, f32[1,256]{1,0:T(1,128)S(1)}) custom-call(f32[256,3584]{1,0:T(8,128)} %templates_ref.3), custom_call_target="tpu_custom_call" | custom-call | tf_op jit(solution)/shard_map/gram/pallas_call | solution.py:222
  21.0 7.5 %cube_windows.1.sums_ref = f32[16,24,128]{2,1,0:T(8,128)S(1)} custom-call(s32[1]{0:T(128)} %bitcast.device_ref, s32[8,2048]{1,0:T(8,128)} %begin_ref.3, s32[8,2048]{1,0:T(8,128)} %span_ref.3, f32[224,2048]{1,0:T(8,128)} %bitcast.6), custom_call_target="tpu_custom_call" | custom-call | tf_op jit(solution)/shard_map/cube_windows/pallas_call | solution.py:370
  28.6 0.0 all-to-all-done.received_ref
  28.6 0.8 %pack.1 = f32[16,56,128]{2,1,0:T(8,128)} custom-call(f32[16,32,128]{2,1,0:T(8,128)S(1)} %all-to-all-done.received_ref, f32[16,24,128]{2,1,0:T(8,128)S(1)} %cube_windows.1.sums_ref), custom_call_target="tpu_custom_call" | custom-call | tf_op jit(solution)/shard_map/pack/pallas_call | solution.py:288
  29.4 6.2 %all-to-all-start.1 = ((f32[16,56,128]{2,1,0:T(8,128)}), f32[16,56,128]{2,1,0:T(8,128)S(1)}, u32[]{:S(2)}, u32[]{:S(2)}) async-start(f32[16,56,128]{2,1,0:T(8,128)} %pack.1), calls=%async_computation.1 | async-start | bytes 917504 | tf_op jit(solution)/shard_map/all_to_all | solution.py:553
  35.6 16.4 %invert.1 = (f32[256,256]{1,0:T(8,128)S(1)}, bf16[256,3584]{1,0:T(8,128)(2,1)S(1)}, bf16[256,3584]{1,0:T(8,128)(2,1)S(1)}, bf16[256,3584]{1,0:T(8,128)(2,1)S(1)}) custom-call(f32[256,256]{1,0:T(8,128)S(1)} %get-tuple-element.34.gram_ref, f32[1,256]{1,0:T(1,128)S(1)} %get-tuple-element.35.scale_ref, f32[256,3584]{1,0:T(8,128)} %templates_ref.3), custom_call_target="tpu_custom_call" | custom-call | tf_op jit(solution)/shard_map/invert/pallas_call | solution.py:274
  52.0 0.0 copy-start
  52.0 1.2 %copy-done = bf16[256,3584]{1,0:T(8,128)(2,1)} copy-done((bf16[256,3584]{1,0:T(8,128)(2,1)}, bf16[256,3584]{1,0:T(8,128)(2,1)S(1)}, u32[]{:S(2)}) %copy-start) | copy-done | bytes 1835032
  53.3 0.0 copy-start.2
  53.3 1.2 %copy-done.2 = bf16[256,3584]{1,0:T(8,128)(2,1)} copy-done((bf16[256,3584]{1,0:T(8,128)(2,1)}, bf16[256,3584]{1,0:T(8,128)(2,1)S(1)}, u32[]{:S(2)}) %copy-start.2) | copy-done | bytes 1835032
  54.5 0.0 all-to-all-done.1.near_ref
  54.5 0.2 collective-permute-start.1
  54.7 1.6 %collective-permute-done.1.far_ref = f32[16,56,128]{2,1,0:T(8,128)S(1)} collective-permute-done((f32[16,56,128]{2,1,0:T(8,128)S(1)}, f32[16,56,128]{2,1,0:T(8,128)S(1)}, u32[]{:S(2)}, u32[]{:S(2)}) %collective-permute-start.1) | collective-permute-done | bytes 458784 | tf_op jit(solution)/shard_map/ppermute | solution.py:556
  56.3 0.0 copy-start.1
  56.3 1.5 %copy-done.1 = bf16[256,3584]{1,0:T(8,128)(2,1)S(1)} copy-done((bf16[256,3584]{1,0:T(8,128)(2,1)S(1)}, bf16[256,3584]{1,0:T(8,128)(2,1)}, u32[]{:S(2)}) %copy-start.1) | copy-done | bytes 1835032
  57.8 0.0 copy-start.3
  57.8 1.5 %copy-done.3 = bf16[256,3584]{1,0:T(8,128)(2,1)S(1)} copy-done((bf16[256,3584]{1,0:T(8,128)(2,1)S(1)}, bf16[256,3584]{1,0:T(8,128)(2,1)}, u32[]{:S(2)}) %copy-start.3) | copy-done | bytes 1835032
  59.3 4.8 %owned.1 = (f32[32,256]{1,0:T(8,128)}, f32[24,128]{1,0:T(8,128)}) custom-call(s32[1]{0:T(128)} %bitcast.device_ref, s32[1,2048]{1,0:T(1,128)} %bitcast.8, s32[1,512]{1,0:T(1,128)} %bitcast.10, s32[8,2048]{1,0:T(8,128)} %begin_ref.3, s32[8,2048]{1,0:T(8,128)} %span_ref.3, f32[16,56,128]{2,1,0:T(8,128)S(1)} %all-to-all-done.1.near_ref, ...), custom_call_target="tpu_custom_call" | custom-call | tf_op jit(solution)/shard_map/owned/pallas_call | solution.py:498
Async XLA Ops:
  7.4 1.7 %collective-permute-start = (f32[512,128]{1,0:T(8,128)S(1)}, f32[512,128]{1,0:T(8,128)S(1)}, u32[]{:S(2)}, u32[]{:S(2)}) collective-permute-start(f32[512,128]{1,0:T(8,128)S(1)} %get-tuple-element.23), channel_id=1, source_target_pairs={{0,1},{1,0},{2,3},{3,2},{4,5},{5,4},{6,7},{7,6},{8,9},{9,8},{10,11... | collective-permute-start | bytes 786440 | tf_op jit(solution)/shard_map/ppermute | solution.py:536
  9.8 18.8 %all-to-all-start = ((f32[16,32,128]{2,1,0:T(8,128)}), f32[16,32,128]{2,1,0:T(8,128)S(1)}, u32[]{:S(2)}, u32[]{:S(2)}) async-start(f32[16,32,128]{2,1,0:T(8,128)} %bitcast.4), calls=%async_computation | async-start | bytes 524288 | tf_op jit(solution)/shard_map/all_to_all | solution.py:540
  29.4 25.1 %all-to-all-start.1 = ((f32[16,56,128]{2,1,0:T(8,128)}), f32[16,56,128]{2,1,0:T(8,128)S(1)}, u32[]{:S(2)}, u32[]{:S(2)}) async-start(f32[16,56,128]{2,1,0:T(8,128)} %pack.1), calls=%async_computation.1 | async-start | bytes 917504 | tf_op jit(solution)/shard_map/all_to_all | solution.py:553
  52.0 1.3 %copy-start = (bf16[256,3584]{1,0:T(8,128)(2,1)}, bf16[256,3584]{1,0:T(8,128)(2,1)S(1)}, u32[]{:S(2)}) copy-start(bf16[256,3584]{1,0:T(8,128)(2,1)S(1)} %get-tuple-element.40.mid_ref) | copy-start | bytes 5505028
  53.3 1.2 %copy-start.2 = (bf16[256,3584]{1,0:T(8,128)(2,1)}, bf16[256,3584]{1,0:T(8,128)(2,1)S(1)}, u32[]{:S(2)}) copy-start(bf16[256,3584]{1,0:T(8,128)(2,1)S(1)} %get-tuple-element.41.low_ref) | copy-start | bytes 5505028
  54.5 1.8 %collective-permute-start.1 = (f32[16,56,128]{2,1,0:T(8,128)S(1)}, f32[16,56,128]{2,1,0:T(8,128)S(1)}, u32[]{:S(2)}, u32[]{:S(2)}) collective-permute-start(f32[16,56,128]{2,1,0:T(8,128)S(1)} %all-to-all-done.1.near_ref), channel_id=1, source_target_pairs={{0,1},{1,0},{2,3},{3,2},{4,5},{5,4},{6,7},{7,6},{8,9},{9,8},{10,11... | collective-permute-start | bytes 1376264 | tf_op jit(solution)/shard_map/ppermute | solution.py:556
  56.3 1.5 %copy-start.1 = (bf16[256,3584]{1,0:T(8,128)(2,1)S(1)}, bf16[256,3584]{1,0:T(8,128)(2,1)}, u32[]{:S(2)}) copy-start(bf16[256,3584]{1,0:T(8,128)(2,1)} %copy-done) | copy-start | bytes 5505028
  57.8 1.5 %copy-start.3 = (bf16[256,3584]{1,0:T(8,128)(2,1)S(1)}, bf16[256,3584]{1,0:T(8,128)(2,1)}, u32[]{:S(2)}) copy-start(bf16[256,3584]{1,0:T(8,128)(2,1)} %copy-done.2) | copy-start | bytes 5505028

commit v7 on v5

--- a/solution.py
+++ b/solution.py
@@ -40,7 +40,7 @@
 
 def project_kernel(
     device_ref, bins_ref, owner_ref, cube_ref, templates_ref, keep_ref, send_ref,
-    held_ref, window_ref, bins_held_ref, owner_held_ref, cube_sem, window_sem, small_sem, *, chunk,
+    held_ref, window_ref, member_ref, bins_held_ref, owner_held_ref, cube_sem, window_sem, small_sem, *, chunk,
 ):
     width, spaxels = cube_ref.shape
     slots = keep_ref.shape[0]
@@ -61,40 +61,48 @@
         pltpu.make_async_copy(owner_ref, owner_held_ref, small_sem.at[1]),
     ]
 
-    @pl.when(pl.program_id(0) == 0)
+    def at_first(action):
+        pl.when(pl.program_id(0) == 0)(action)
+
+    @at_first
     def _():
         for copy in small_copies:
             copy.start()
+        window_copy.start()
         for i in range(chunks):
             cube_copy(i).start()
-        window_copy.start()
         for copy in small_copies:
             copy.wait()
 
     owner = owner_held_ref[:, pl.ds(pl.multiple_of(pl.program_id(0) * slots, LANES), slots)]
     owner = jnp.broadcast_to(owner, (SUB, slots)).T[:, :1]
-    sums = jnp.zeros((slots, width), F32)
     counts = jnp.zeros((slots, LANES), F32)
     for i in range(chunks):
-        here = owner == bins_held_ref[:, i * chunk : (i + 1) * chunk]
-        ones = jnp.where(here, 1.0, 0.0)
+        lanes = slice(i * chunk, (i + 1) * chunk)
+        ones = jnp.where(owner == bins_held_ref[:, lanes], 1.0, 0.0)
         for lane in range(0, chunk, LANES):
             counts = counts + ones[:, lane : lane + LANES]
-        member = ones.astype(BF16)
-
-        @pl.when(pl.program_id(0) == 0)
+        member_ref[:, lanes] = ones.astype(BF16)
+    counts = jnp.sum(counts, axis=1, keepdims=True)
+
+    @at_first
+    def _():
+        window_copy.wait()
+
+    mine = pltpu.roll(window_ref[...], window - (first - base), 1)[:, :width]
+
+    sums = jnp.zeros((slots, width), F32)
+    for i in range(chunks):
+
+        @at_first
         def _(i=i):
             cube_copy(i).wait()
 
-        for part in split3(held_ref[:, i * chunk : (i + 1) * chunk]):
+        lanes = slice(i * chunk, (i + 1) * chunk)
+        member = member_ref[:, lanes]
+        for part in split3(held_ref[:, lanes]):
             sums = sums + dot(member, part, NT)
-    means = sums / jnp.sum(counts, axis=1, keepdims=True)
-
-    @pl.when(pl.program_id(0) == 0)
-    def _():
-        window_copy.wait()
-
-    mine = pltpu.roll(window_ref[...], window - (first - base), 1)[:, :width]
+    means = sums / counts
     projections = dot_f32(means, mine, NT) * (1.0 / full_width)
     low, high = projections[:, :LANES], projections[:, LANES:]
     low_kept = device_ref[0] % 2 == 0
@@ -105,7 +113,7 @@
 def project(device, bins, owner, cube, templates):
     width, spaxels = cube.shape
     slots = owner.shape[1]
-    block = min(slots, 512)
+    block = min(slots, 512, max(LANES, 2**20 // spaxels))
     chunk = min(spaxels, 512)
     count, full_width = templates.shape
     return pl.pallas_call(
@@ -123,6 +131,7 @@
         scratch_shapes=[
             pltpu.VMEM((width, spaxels), F32),
             pltpu.VMEM((count, template_window(width, full_width)), F32),
+            pltpu.VMEM((block, spaxels), BF16),
             pltpu.VMEM(bins.shape, jnp.int32),
             pltpu.VMEM(owner.shape, jnp.int32),
             pltpu.SemaphoreType.DMA((spaxels // chunk,)),
@@ -200,7 +209,7 @@
     return -jnp.concatenate(rows, axis=0)
 
 
-def gram_kernel(templates_ref, gram_ref, scale_ref, held_ref, sem, *, chunk):
+def gram_kernel(templates_ref, gram_ref, scale_ref, hi_ref, mid_ref, low_ref, held_ref, sem, *, chunk):
     count, full_width = templates_ref.shape
 
     def copy(i):
@@ -213,7 +222,9 @@
     mixed = jnp.zeros((count, count), F32)
     for i in range(full_width // chunk):
         copy(i).wait()
-        hi, mid, low = split3(held_ref[:, i * chunk : (i + 1) * chunk])
+        lanes = slice(i * chunk, (i + 1) * chunk)
+        hi, mid, low = split3(held_ref[:, lanes])
+        hi_ref[:, lanes], mid_ref[:, lanes], low_ref[:, lanes] = hi, mid, low
         even = even + (dot(hi, hi, NT) + dot(mid, mid, NT))
         mixed = mixed + (dot(hi, mid, NT) + dot(hi, low, NT))
     gram = (even + (mixed + mixed.T)) * (1.0 / full_width)
@@ -228,12 +239,16 @@
 
 def scaled_gram(templates, chunk):
     count, full_width = templates.shape
+    part = pltpu.VMEM((count, full_width), BF16)
     return pl.pallas_call(
         functools.partial(gram_kernel, chunk=chunk),
         in_specs=[pl.BlockSpec(memory_space=pltpu.HBM)],
         out_shape=(
             jax.ShapeDtypeStruct((count, count), F32),
             jax.ShapeDtypeStruct((1, count), F32),
+            part,
+            part,
+            part,
         ),
         scratch_shapes=[
             pltpu.VMEM((count, full_width), F32),
@@ -375,22 +390,18 @@
 
 
 def owner_kernel(
-    device_ref, bins_ref, owner_ref, begin_ref, span_ref, near_ref, far_ref, inverse_ref, templates_ref,
+    device_ref, bins_ref, owner_ref, begin_ref, span_ref, near_ref, far_ref, inverse_ref, hi_ref, mid_ref, low_ref,
     weights_ref, out_ref,
-    held_ref, continuum_ref, bins_held_ref, owner_held_ref, begins_ref, spans_ref, starts_ref, sem, small_sem,
+    continuum_ref, bins_held_ref, owner_held_ref, begins_ref, spans_ref, starts_ref, small_sem,
     *, chunk,
 ):
     devices = near_ref.shape[0]
     slots = weights_ref.shape[0]
     own = bins_held_ref.shape[1]
     lines = begin_ref.shape[0]
-    full_width = templates_ref.shape[1]
+    full_width = hi_ref.shape[1]
     device = device_ref[0]
     own_lanes = pl.ds(pl.multiple_of(device * own, LANES), own)
-
-    def copy(i):
-        lanes = pl.ds(i * chunk, chunk)
-        return pltpu.make_async_copy(templates_ref.at[:, lanes], held_ref.at[:, lanes], sem.at[i])
 
     small_copies = [
         pltpu.make_async_copy(bins_ref.at[:, own_lanes], bins_held_ref, small_sem.at[0]),
@@ -401,16 +412,14 @@
     ]
     for small in small_copies:
         small.start()
-    for i in range(full_width // chunk):
-        copy(i).start()
-
-    inverse = inverse_ref[...]
+
     low_first = device % 2 == 0
 
     def halves(near, far):
         return jnp.where(low_first, near, far), jnp.where(low_first, far, near)
 
     mine = jnp.concatenate(halves(near_ref[device, :slots, :], far_ref[device, :slots, :]), axis=1)
+    inverse = inverse_ref[...]
     weights_ref[...] = dot_f32(mine, inverse, NN)
 
     for small in small_copies:
@@ -422,10 +431,15 @@
         hi, mid, low = split3(half[:, :slots, :].reshape(devices * slots, LANES))
         picked.append(dot(member, hi, NN) + (dot(member, mid, NN) + dot(member, low, NN)))
     spaxel_weights = dot_f32(jnp.concatenate(halves(*picked), axis=1), inverse, NN)
+    hi, mid, low = split3(spaxel_weights)
 
     for i in range(full_width // chunk):
-        copy(i).wait()
-        value = dot_f32(spaxel_weights, held_ref[:, i * chunk : (i + 1) * chunk], NN)
+        lanes = slice(i * chunk, (i + 1) * chunk)
+        first, second, third = hi_ref[:, lanes], mid_ref[:, lanes], low_ref[:, lanes]
+        value = dot(hi, first, NN) + (
+            (dot(mid, first, NN) + dot(hi, second, NN))
+            + (dot(low, first, NN) + dot(mid, second, NN) + dot(hi, third, NN))
+        )
         for t in range(chunk // LANES):
             continuum_ref[i * (chunk // LANES) + t] = value[:, t * LANES : (t + 1) * LANES]
     continuum_ref[full_width // LANES] = jnp.zeros((own, LANES), F32)
@@ -469,32 +483,30 @@
     out_ref[...] = (cube_sums - continuum_sums) / scale
 
 
-def owned(device, bins, owner, begin, span, near, far, inverse, templates, own_slots, own, chunk):
+def owned(device, bins, owner, begin, span, near, far, inverse, parts, own_slots, own, chunk):
     vmem = pl.BlockSpec(memory_space=pltpu.VMEM)
     hbm = pl.BlockSpec(memory_space=pltpu.HBM)
-    count, full_width = templates.shape
+    count, full_width = parts[0].shape
     lines = begin.shape[0]
     return pl.pallas_call(
         functools.partial(owner_kernel, chunk=chunk),
-        in_specs=[pl.BlockSpec(memory_space=pltpu.SMEM)] + [hbm] * 4 + [vmem] * 3 + [hbm],
+        in_specs=[pl.BlockSpec(memory_space=pltpu.SMEM)] + [hbm] * 4 + [vmem] * 6,
         out_shape=(
             jax.ShapeDtypeStruct((own_slots, count), F32),
             jax.ShapeDtypeStruct((3 * lines, own), F32),
         ),
         scratch_shapes=[
-            pltpu.VMEM((count, full_width), F32),
             pltpu.VMEM((full_width // LANES + 1, own, LANES), F32),
             pltpu.VMEM((1, own), jnp.int32),
             pltpu.VMEM(owner.shape, jnp.int32),
             pltpu.VMEM((lines, own), jnp.int32),
             pltpu.VMEM((lines, own), jnp.int32),
             pltpu.SMEM((lines, own), jnp.int32),
-            pltpu.SemaphoreType.DMA((full_width // chunk,)),
             pltpu.SemaphoreType.DMA((5,)),
         ],
         compiler_params=pltpu.CompilerParams(vmem_limit_bytes=VMEM_LIMIT),
         name="owned",
-    )(device, bins, owner, begin, span, near, far, inverse, templates)
+    )(device, bins, owner, begin, span, near, far, inverse, *parts)
 
 
 def shards(cube, templates, bin_id, owner_bins, line_start, line_width):
@@ -521,7 +533,7 @@
     received = lax.all_to_all(partial.reshape(devices, own_slots, LANES), "spax", 0, 0)
 
     sums = cube_windows(here_after, begin, span, columns, devices)
-    gram, scale = scaled_gram(later, 512)
+    gram, scale, *parts = scaled_gram(later, 512)
     received, sums, gram, scale = lax.optimization_barrier((received, sums, gram, scale))
     parcel = in_vmem(
         pack_kernel,
@@ -536,7 +548,7 @@
     near, inverse = lax.optimization_barrier((near, inverse))
     far = lax.ppermute(near, "spax", swap)
     return owned(
-        here, bins, owner, begin, span, near, far, inverse, later, own_slots, own_spaxels, 512
+        here, bins, owner, begin, span, near, far, inverse, parts, own_slots, own_spaxels, 512
     )
 
 

time: 58.4 us -> 61.5 us (1.053)
  local copies, waits for them, and re-layouts: 0 us -> 5.49 us
  Pallas kernels: 37.2 us -> 34.7 us
    unnamed x0 -> x8, local copies, waits for them, and re-layouts: none -> 5.49 us
    pallas_call x1, Pallas kernels: 7.36 us -> 5.21 us  [owned(): pl.pallas_call(functools.partial(owner_kernel, chunk=chunk), in_specs=[pl...]
  transfers between devices with their start and end apart: 4 -> 4, of which waited for: 3 -> 3; matrix products, arithmetic and copies ran while one was open for 0% -> 0% of each run, Pallas kernels for 37% -> 35%
where the time goes in v7:
time: 61.5 us; the launch traced here: 61 us
  Pallas kernels  34.7 us (56%)
  starting transfers between devices  14.1 us (23%)
  waiting for transfers between devices  5.87 us (10%)
  local copies, waits for them, and re-layouts  5.49 us (9%)
  between operations  0.86 us (1%)
    pallas_call x3, Pallas kernels, in_vmem(): pl.pallas_call(kernel, out_shape=shapes, compiler_params=pltpu.CompilerPa...  11.6 us
    pallas_call x1, Pallas kernels, cube_windows(): pl.pallas_call(cube_kernel, in_specs=[pl.BlockSpec(memory_space=pltpu.SME...  7.53 us
    all_to_all x1, starting transfers between devices, shards(): lax.all_to_all(partial.reshape(devices, own_slots, LANES), 'spax', 0, 0)  7.28 us
    pallas_call x1, Pallas kernels, project(): pl.pallas_call(functools.partial(project_kernel, chunk=chunk), grid=(slot...  6.4 us
    all_to_all x1, starting transfers between devices, shards(): near = lax.all_to_all(parcel, 'spax', 0, 0)  6.18 us
    unnamed x8, local copies, waits for them, and re-layouts  5.49 us
    pallas_call x1, Pallas kernels, owned(): pl.pallas_call(functools.partial(owner_kernel, chunk=chunk), in_specs=[pl...  5.21 us
    pallas_call x1, Pallas kernels, scaled_gram(): pl.pallas_call(functools.partial(gram_kernel, chunk=chunk), in_specs=[pl....  3.98 us
  transfers between devices with their start and end apart: 4, of which 3 were waited for; matrix products, arithmetic and copies ran while one was open for 0% of the time, Pallas kernels for 35%

profile of v7, /device:TPU:0, one launch (start us, length us, event | category | flops | bytes accessed | tf_op | source)
XLA Modules:
  0.0 61.0 jit_solution(18099654842936860378)
XLA Ops:
  0.6 6.4 %project.1 = (f32[512,128]{1,0:T(8,128)S(1)}, f32[512,128]{1,0:T(8,128)S(1)}) custom-call(s32[1]{0:T(128)} %bitcast.device_ref, s32[1,2048]{1,0:T(1,128)} %bitcast.7, s32[1,512]{1,0:T(1,128)} %bitcast.9, f32[224,2048]{1,0:T(8,128)} %bitcast.5, f32[256,3584]{1,0:T(8,128)} %templates_ref.2), custom_call_target="tpu_custom_call" | custom-call | tf_op jit(solution)/shard_map/project/pallas_call | solution.py:119
  7.0 0.5 collective-permute-start
  7.6 1.2 %collective-permute-done.y_ref = f32[512,128]{1,0:T(8,128)S(1)} collective-permute-done((f32[512,128]{1,0:T(8,128)S(1)}, f32[512,128]{1,0:T(8,128)S(1)}, u32[]{:S(2)}, u32[]{:S(2)}) %collective-permute-start) | collective-permute-done | bytes 262176 | tf_op jit(solution)/shard_map/ppermute | solution.py:529
  8.7 0.7 %add.1 = f32[512,128]{1,0:T(8,128)} custom-call(f32[512,128]{1,0:T(8,128)S(1)} %get-tuple-element.21.x_ref, f32[512,128]{1,0:T(8,128)S(1)} %collective-permute-done.y_ref), custom_call_target="tpu_custom_call" | custom-call | tf_op jit(solution)/shard_map/add/pallas_call | solution.py:279
  9.5 7.3 %all-to-all-start = ((f32[16,32,128]{2,1,0:T(8,128)}), f32[16,32,128]{2,1,0:T(8,128)S(1)}, u32[]{:S(2)}, u32[]{:S(2)}) async-start(f32[16,32,128]{2,1,0:T(8,128)} %bitcast.4), calls=%async_computation | async-start | bytes 524288 | tf_op jit(solution)/shard_map/all_to_all | solution.py:533
  16.7 4.0 %gram.1 = (f32[256,256]{1,0:T(8,128)S(1)}, f32[1,256]{1,0:T(1,128)S(1)}, bf16[256,3584]{1,0:T(8,128)(2,1)S(1)}, bf16[256,3584]{1,0:T(8,128)(2,1)S(1)}, bf16[256,3584]{1,0:T(8,128)(2,1)S(1)}) custom-call(f32[256,3584]{1,0:T(8,128)} %templates_ref.2), custom_call_target="tpu_custom_call" | custom-call | tf_op jit(solution)/shard_map/gram/pallas_call | solution.py:243
  20.7 0.0 copy-start
  20.7 1.2 %copy-done = bf16[256,3584]{1,0:T(8,128)(2,1)} copy-done((bf16[256,3584]{1,0:T(8,128)(2,1)}, bf16[256,3584]{1,0:T(8,128)(2,1)S(1)}, u32[]{:S(2)}) %copy-start) | copy-done | bytes 1835032
  22.0 0.0 copy-start.2
  22.0 1.2 %copy-done.2 = bf16[256,3584]{1,0:T(8,128)(2,1)} copy-done((bf16[256,3584]{1,0:T(8,128)(2,1)}, bf16[256,3584]{1,0:T(8,128)(2,1)S(1)}, u32[]{:S(2)}) %copy-start.2) | copy-done | bytes 1835032
  23.2 7.5 %cube_windows.1.sums_ref = f32[16,24,128]{2,1,0:T(8,128)S(1)} custom-call(s32[1]{0:T(128)} %bitcast.device_ref, s32[8,2048]{1,0:T(8,128)} %begin_ref.3, s32[8,2048]{1,0:T(8,128)} %span_ref.3, f32[224,2048]{1,0:T(8,128)} %bitcast.6), custom_call_target="tpu_custom_call" | custom-call | tf_op jit(solution)/shard_map/cube_windows/pallas_call | solution.py:361
  30.8 0.0 all-to-all-done.received_ref
  30.8 0.8 %pack.1 = f32[16,56,128]{2,1,0:T(8,128)} custom-call(f32[16,32,128]{2,1,0:T(8,128)S(1)} %all-to-all-done.received_ref, f32[16,24,128]{2,1,0:T(8,128)S(1)} %cube_windows.1.sums_ref), custom_call_target="tpu_custom_call" | custom-call | tf_op jit(solution)/shard_map/pack/pallas_call | solution.py:279
  31.6 6.2 %all-to-all-start.1 = ((f32[16,56,128]{2,1,0:T(8,128)}), f32[16,56,128]{2,1,0:T(8,128)S(1)}, u32[]{:S(2)}, u32[]{:S(2)}) async-start(f32[16,56,128]{2,1,0:T(8,128)} %pack.1), calls=%async_computation.1 | async-start | bytes 917504 | tf_op jit(solution)/shard_map/all_to_all | solution.py:546
  37.8 10.1 %invert.1.inverse_ref = f32[256,256]{1,0:T(8,128)S(1)} custom-call(f32[256,256]{1,0:T(8,128)S(1)} %get-tuple-element.33.gram_ref, f32[1,256]{1,0:T(1,128)S(1)} %get-tuple-element.34.scale_ref), custom_call_target="tpu_custom_call" | custom-call | tf_op jit(solution)/shard_map/invert/pallas_call | solution.py:279
  47.8 3.0 %all-to-all-done.1.near_ref = f32[16,56,128]{2,1,0:T(8,128)S(1)} async-done(((f32[16,56,128]{2,1,0:T(8,128)}), f32[16,56,128]{2,1,0:T(8,128)S(1)}, u32[]{:S(2)}, u32[]{:S(2)}) %all-to-all-start.1) | async-done | bytes 458784 | tf_op jit(solution)/shard_map/all_to_all | solution.py:546
  50.8 0.1 collective-permute-start.1
  51.0 1.7 %collective-permute-done.1.far_ref = f32[16,56,128]{2,1,0:T(8,128)S(1)} collective-permute-done((f32[16,56,128]{2,1,0:T(8,128)S(1)}, f32[16,56,128]{2,1,0:T(8,128)S(1)}, u32[]{:S(2)}, u32[]{:S(2)}) %collective-permute-start.1) | collective-permute-done | bytes 458784 | tf_op jit(solution)/shard_map/ppermute | solution.py:549
  52.7 0.0 copy-start.1
  52.7 1.5 %copy-done.1 = bf16[256,3584]{1,0:T(8,128)(2,1)S(1)} copy-done((bf16[256,3584]{1,0:T(8,128)(2,1)S(1)}, bf16[256,3584]{1,0:T(8,128)(2,1)}, u32[]{:S(2)}) %copy-start.1) | copy-done | bytes 1835032
  54.2 0.0 copy-start.3
  54.2 1.5 %copy-done.3 = bf16[256,3584]{1,0:T(8,128)(2,1)S(1)} copy-done((bf16[256,3584]{1,0:T(8,128)(2,1)S(1)}, bf16[256,3584]{1,0:T(8,128)(2,1)}, u32[]{:S(2)}) %copy-start.3) | copy-done | bytes 1835032
  55.7 5.2 %owned.1 = (f32[32,256]{1,0:T(8,128)}, f32[24,128]{1,0:T(8,128)}) custom-call(s32[1]{0:T(128)} %bitcast.device_ref, s32[1,2048]{1,0:T(1,128)} %bitcast.8, s32[1,512]{1,0:T(1,128)} %bitcast.10, s32[8,2048]{1,0:T(8,128)} %begin_ref.3, s32[8,2048]{1,0:T(8,128)} %span_ref.3, f32[16,56,128]{2,1,0:T(8,128)S(1)} %all-to-all-done.1.near_ref, ...), custom_call_target="tpu_custom_call" | custom-call | tf_op jit(solution)/shard_map/owned/pallas_call | solution.py:491
Async XLA Ops:
  7.0 1.7 %collective-permute-start = (f32[512,128]{1,0:T(8,128)S(1)}, f32[512,128]{1,0:T(8,128)S(1)}, u32[]{:S(2)}, u32[]{:S(2)}) collective-permute-start(f32[512,128]{1,0:T(8,128)S(1)} %get-tuple-element.22), channel_id=1, source_target_pairs={{0,1},{1,0},{2,3},{3,2},{4,5},{5,4},{6,7},{7,6},{8,9},{9,8},{10,11... | collective-permute-start | bytes 786440 | tf_op jit(solution)/shard_map/ppermute | solution.py:529
  9.5 21.3 %all-to-all-start = ((f32[16,32,128]{2,1,0:T(8,128)}), f32[16,32,128]{2,1,0:T(8,128)S(1)}, u32[]{:S(2)}, u32[]{:S(2)}) async-start(f32[16,32,128]{2,1,0:T(8,128)} %bitcast.4), calls=%async_computation | async-start | bytes 524288 | tf_op jit(solution)/shard_map/all_to_all | solution.py:533
  20.7 1.3 %copy-start = (bf16[256,3584]{1,0:T(8,128)(2,1)}, bf16[256,3584]{1,0:T(8,128)(2,1)S(1)}, u32[]{:S(2)}) copy-start(bf16[256,3584]{1,0:T(8,128)(2,1)S(1)} %get-tuple-element.38.mid_ref) | copy-start | bytes 5505028
  22.0 1.2 %copy-start.2 = (bf16[256,3584]{1,0:T(8,128)(2,1)}, bf16[256,3584]{1,0:T(8,128)(2,1)S(1)}, u32[]{:S(2)}) copy-start(bf16[256,3584]{1,0:T(8,128)(2,1)S(1)} %get-tuple-element.39.low_ref) | copy-start | bytes 5505028
  31.6 19.3 %all-to-all-start.1 = ((f32[16,56,128]{2,1,0:T(8,128)}), f32[16,56,128]{2,1,0:T(8,128)S(1)}, u32[]{:S(2)}, u32[]{:S(2)}) async-start(f32[16,56,128]{2,1,0:T(8,128)} %pack.1), calls=%async_computation.1 | async-start | bytes 917504 | tf_op jit(solution)/shard_map/all_to_all | solution.py:546
  50.8 1.8 %collective-permute-start.1 = (f32[16,56,128]{2,1,0:T(8,128)S(1)}, f32[16,56,128]{2,1,0:T(8,128)S(1)}, u32[]{:S(2)}, u32[]{:S(2)}) collective-permute-start(f32[16,56,128]{2,1,0:T(8,128)S(1)} %all-to-all-done.1.near_ref), channel_id=1, source_target_pairs={{0,1},{1,0},{2,3},{3,2},{4,5},{5,4},{6,7},{7,6},{8,9},{9,8},{10,11... | collective-permute-start | bytes 1376264 | tf_op jit(solution)/shard_map/ppermute | solution.py:549
  52.7 1.5 %copy-start.1 = (bf16[256,3584]{1,0:T(8,128)(2,1)S(1)}, bf16[256,3584]{1,0:T(8,128)(2,1)}, u32[]{:S(2)}) copy-start(bf16[256,3584]{1,0:T(8,128)(2,1)} %copy-done) | copy-start | bytes 5505028
  54.2 1.5 %copy-start.3 = (bf16[256,3584]{1,0:T(8,128)(2,1)S(1)}, bf16[256,3584]{1,0:T(8,128)(2,1)}, u32[]{:S(2)}) copy-start(bf16[256,3584]{1,0:T(8,128)(2,1)} %copy-done.2) | copy-start | bytes 5505028

commit v8 on v7

--- a/solution.py
+++ b/solution.py
@@ -209,12 +209,22 @@
     return -jnp.concatenate(rows, axis=0)
 
 
-def gram_kernel(templates_ref, gram_ref, scale_ref, hi_ref, mid_ref, low_ref, held_ref, sem, *, chunk):
+def gram_kernel(
+    templates_ref, gram_ref, scale_ref, hi_ref, mid_ref, low_ref, held_ref, mid_held_ref, low_held_ref, sem, out_sem,
+    *, chunk,
+):
     count, full_width = templates_ref.shape
 
     def copy(i):
         lanes = pl.ds(i * chunk, chunk)
         return pltpu.make_async_copy(templates_ref.at[:, lanes], held_ref.at[:, lanes], sem.at[i])
+
+    def out_copies(i):
+        lanes = pl.ds(i * chunk, chunk)
+        return [
+            pltpu.make_async_copy(mid_held_ref.at[:, lanes], mid_ref.at[:, lanes], out_sem.at[0, i]),
+            pltpu.make_async_copy(low_held_ref.at[:, lanes], low_ref.at[:, lanes], out_sem.at[1, i]),
+        ]
 
     for i in range(full_width // chunk):
         copy(i).start()
@@ -224,7 +234,9 @@
         copy(i).wait()
         lanes = slice(i * chunk, (i + 1) * chunk)
         hi, mid, low = split3(held_ref[:, lanes])
-        hi_ref[:, lanes], mid_ref[:, lanes], low_ref[:, lanes] = hi, mid, low
+        hi_ref[:, lanes], mid_held_ref[:, lanes], low_held_ref[:, lanes] = hi, mid, low
+        for out in out_copies(i):
+            out.start()
         even = even + (dot(hi, hi, NT) + dot(mid, mid, NT))
         mixed = mixed + (dot(hi, mid, NT) + dot(hi, low, NT))
     gram = (even + (mixed + mixed.T)) * (1.0 / full_width)
@@ -235,32 +247,43 @@
     gram = gram * row * column
     scale_ref[...] = row
     gram_ref[...] = gram
+    for i in range(full_width // chunk):
+        for out in out_copies(i):
+            out.wait()
 
 
 def scaled_gram(templates, chunk):
     count, full_width = templates.shape
-    part = pltpu.VMEM((count, full_width), BF16)
+    vmem, hbm = (pl.BlockSpec(memory_space=space) for space in (pltpu.VMEM, pltpu.HBM))
     return pl.pallas_call(
         functools.partial(gram_kernel, chunk=chunk),
-        in_specs=[pl.BlockSpec(memory_space=pltpu.HBM)],
+        in_specs=[hbm],
+        out_specs=(vmem, vmem, vmem, hbm, hbm),
         out_shape=(
             jax.ShapeDtypeStruct((count, count), F32),
             jax.ShapeDtypeStruct((1, count), F32),
-            part,
-            part,
-            part,
+            pltpu.VMEM((count, full_width), BF16),
+            pltpu.HBM((count, full_width), BF16),
+            pltpu.HBM((count, full_width), BF16),
         ),
         scratch_shapes=[
             pltpu.VMEM((count, full_width), F32),
+            pltpu.VMEM((count, full_width), BF16),
+            pltpu.VMEM((count, full_width), BF16),
             pltpu.SemaphoreType.DMA((full_width // chunk,)),
+            pltpu.SemaphoreType.DMA((2, full_width // chunk)),
         ],
         compiler_params=pltpu.CompilerParams(vmem_limit_bytes=VMEM_LIMIT),
         name="gram",
     )(templates)
 
 
-def invert_kernel(gram_ref, scale_ref, out_ref):
-    first = invert_tile(gram_ref[:LANES, :LANES])
+def first_kernel(gram_ref, out_ref):
+    out_ref[...] = invert_tile(gram_ref[:LANES, :LANES])
+
+
+def finish_kernel(gram_ref, first_ref, scale_ref, out_ref):
+    first = first_ref[...]
     side = gram_ref[:LANES, LANES:]
     half = dot_f32(first, side, NN)
     schur = gram_ref[LANES:, LANES:] - dot_f32(side.T, half, NN)
@@ -317,6 +340,16 @@
     return [out[3 * j + k] for k in range(3) for j in range(lines)]
 
 
+def halving_order(devices):
+    bits = devices.bit_length() - 1
+    return list(range(2, bits)) + [1, 0]
+
+
+def flips(position, devices):
+    order = halving_order(devices)
+    return sum(((position >> (len(order) - 1 - t)) & 1) << bit for t, bit in enumerate(order))
+
+
 def cube_kernel(
     device_ref, begin_ref, span_ref, cube_ref, out_ref, begins_ref, spans_ref, held_ref, lines_sem, cube_sem,
 ):
@@ -324,9 +357,11 @@
     owners = out_ref.shape[0]
     device = device_ref[0]
 
+    def owner_lanes(i):
+        return pl.ds(pl.multiple_of((device ^ flips(i, owners)) * LANES, LANES), LANES)
+
     def tile_copy(i):
-        lanes = pl.ds(pl.multiple_of(i * LANES, LANES), LANES)
-        return pltpu.make_async_copy(cube_ref.at[:, lanes], held_ref.at[i], cube_sem.at[i])
+        return pltpu.make_async_copy(cube_ref.at[:, owner_lanes(i)], held_ref.at[i], cube_sem.at[i])
 
     line_copies = [
         pltpu.make_async_copy(begin_ref, begins_ref, lines_sem.at[0]),
@@ -341,7 +376,7 @@
 
     def owner(i, carry):
         tile_copy(i).wait()
-        lanes = pl.ds(pl.multiple_of(i * LANES, LANES), LANES)
+        lanes = owner_lanes(i)
         sums = window_sums(
             lambda row, size: held_ref[i, row : row + size, :],
             width,
@@ -374,32 +409,61 @@
     )(device, begin, span, cube)
 
 
-def add_kernel(x_ref, y_ref, out_ref):
-    out_ref[...] = x_ref[...] + y_ref[...]
-
-
-def pack_kernel(received_ref, sums_ref, out_ref):
-    slots = received_ref.shape[1]
-    for half in range(2):
-        total = received_ref[half]
-        for i in range(half + 2, received_ref.shape[0], 2):
-            total = total + received_ref[i]
-        for i in range(half, out_ref.shape[0], 2):
-            out_ref[i, :slots, :] = total
-    out_ref[:, slots:, :] = sums_ref[...]
+def split_kernel(device_ref, x_ref, y_ref, keep_ref, send_ref):
+    half = keep_ref.shape[0]
+    total = x_ref[...] + y_ref[...]
+    low_kept = (device_ref[0] >> 1) % 2 == 0
+    keep_ref[...] = jnp.where(low_kept, total[:half], total[half:])
+    send_ref[...] = jnp.where(low_kept, total[half:], total[:half])
+
+
+def join_kernel(x_ref, y_ref, sums_ref, keep_ref, send_ref):
+    slots = x_ref.shape[0]
+    half = sums_ref.shape[0] // 2
+    total = x_ref[...] + y_ref[...]
+    for out_ref, first in ((keep_ref, 0), (send_ref, half)):
+        out_ref[:slots, :] = total
+        out_ref[slots:, :] = sums_ref[first : first + half, :]
+
+
+def step_kernel(x_ref, y_ref, keep_ref, send_ref):
+    rows = x_ref.shape[0]
+    half = rows - keep_ref.shape[0]
+    slots = rows - 2 * half
+    total = x_ref[:slots, :] + y_ref[:slots, :]
+    for out_ref, first in ((keep_ref, slots), (send_ref, slots + half)):
+        out_ref[:slots, :] = total
+        out_ref[slots:, :] = x_ref[first : first + half, :] + y_ref[first : first + half, :]
+
+
+def rows_of(count):
+    return jax.ShapeDtypeStruct((count, LANES), F32)
+
+
+def split_slots(device, x, y):
+    vmem = pl.BlockSpec(memory_space=pltpu.VMEM)
+    half = rows_of(x.shape[0] // 2)
+    return pl.pallas_call(
+        split_kernel,
+        in_specs=[pl.BlockSpec(memory_space=pltpu.SMEM), vmem, vmem],
+        out_shape=(half, half),
+        compiler_params=pltpu.CompilerParams(vmem_limit_bytes=VMEM_LIMIT),
+        name="split_slots",
+    )(device, x, y)
 
 
 def owner_kernel(
-    device_ref, bins_ref, owner_ref, begin_ref, span_ref, near_ref, far_ref, inverse_ref, hi_ref, mid_ref, low_ref,
+    device_ref, bins_ref, owner_ref, begin_ref, span_ref,
+    kept_ref, by_x_ref, by_core_ref, by_both_ref, inverse_ref, hi_ref, mid_ref, low_ref,
     weights_ref, out_ref,
-    continuum_ref, bins_held_ref, owner_held_ref, begins_ref, spans_ref, starts_ref, small_sem,
-    *, chunk,
+    continuum_ref, mid_held_ref, low_held_ref, bins_held_ref, owner_held_ref, begins_ref, spans_ref, starts_ref,
+    parts_sem, small_sem, *, chunk,
 ):
-    devices = near_ref.shape[0]
-    slots = weights_ref.shape[0]
+    own_slots = weights_ref.shape[0]
     own = bins_held_ref.shape[1]
     lines = begin_ref.shape[0]
     full_width = hi_ref.shape[1]
+    half = owner_held_ref.shape[1] // 2
     device = device_ref[0]
     own_lanes = pl.ds(pl.multiple_of(device * own, LANES), own)
 
@@ -410,38 +474,62 @@
         pltpu.make_async_copy(span_ref.at[:, own_lanes], spans_ref, small_sem.at[3]),
         pltpu.make_async_copy(begin_ref.at[:, own_lanes], starts_ref, small_sem.at[4]),
     ]
-    for small in small_copies:
-        small.start()
-
-    low_first = device % 2 == 0
-
-    def halves(near, far):
-        return jnp.where(low_first, near, far), jnp.where(low_first, far, near)
-
-    mine = jnp.concatenate(halves(near_ref[device, :slots, :], far_ref[device, :slots, :]), axis=1)
+    part_copies = [
+        pltpu.make_async_copy(mid_ref, mid_held_ref, parts_sem.at[0]),
+        pltpu.make_async_copy(low_ref, low_held_ref, parts_sem.at[1]),
+    ]
+    for copy in small_copies + part_copies:
+        copy.start()
+
     inverse = inverse_ref[...]
+    core_low = device % 2 == 0
+    low_kept = (device >> 1) % 2 == 0
+
+    def by_lanes(near, far):
+        return jnp.concatenate([jnp.where(core_low, near, far), jnp.where(core_low, far, near)], axis=1)
+
+    slot = device * own_slots
+    in_kept = (slot // half) == ((device >> 1) % 2)
+    rows = pl.ds(pl.multiple_of(slot % half, own_slots), own_slots)
+    mine = by_lanes(
+        jnp.where(in_kept, kept_ref[rows, :], by_x_ref[rows, :]),
+        jnp.where(in_kept, by_core_ref[rows, :], by_both_ref[rows, :]),
+    )
     weights_ref[...] = dot_f32(mine, inverse, NN)
 
-    for small in small_copies:
-        small.wait()
+    for copy in small_copies:
+        copy.wait()
     bins = jnp.broadcast_to(bins_held_ref[...], (SUB, own)).T[:, :1]
-    member = jnp.where(bins == owner_held_ref[...], 1.0, 0.0).astype(BF16)
+    low_slots, high_slots = owner_held_ref[:, :half], owner_held_ref[:, half:]
+    members = [
+        jnp.where(bins == jnp.where(low_kept, a, b), 1.0, 0.0).astype(BF16)
+        for a, b in ((low_slots, high_slots), (high_slots, low_slots))
+    ]
     picked = []
-    for half in (near_ref, far_ref):
-        hi, mid, low = split3(half[:, :slots, :].reshape(devices * slots, LANES))
-        picked.append(dot(member, hi, NN) + (dot(member, mid, NN) + dot(member, low, NN)))
-    spaxel_weights = dot_f32(jnp.concatenate(halves(*picked), axis=1), inverse, NN)
+    for kept_half, other_half in ((kept_ref, by_x_ref), (by_core_ref, by_both_ref)):
+        value = None
+        for member, block in zip(members, (kept_half, other_half)):
+            hi, mid, low = split3(block[:half, :])
+            new = dot(member, hi, NN) + (dot(member, mid, NN) + dot(member, low, NN))
+            value = new if value is None else value + new
+        picked.append(value)
+    spaxel_weights = dot_f32(by_lanes(*picked), inverse, NN)
+
     hi, mid, low = split3(spaxel_weights)
-
+    tiles = chunk // LANES
+    for i in range(full_width // chunk):
+        first = hi_ref[:, i * chunk : (i + 1) * chunk]
+        value = dot(hi, first, NN) + (dot(mid, first, NN) + dot(low, first, NN))
+        for t in range(tiles):
+            continuum_ref[i * tiles + t] = value[:, t * LANES : (t + 1) * LANES]
+    for copy in part_copies:
+        copy.wait()
     for i in range(full_width // chunk):
         lanes = slice(i * chunk, (i + 1) * chunk)
-        first, second, third = hi_ref[:, lanes], mid_ref[:, lanes], low_ref[:, lanes]
-        value = dot(hi, first, NN) + (
-            (dot(mid, first, NN) + dot(hi, second, NN))
-            + (dot(low, first, NN) + dot(mid, second, NN) + dot(hi, third, NN))
-        )
-        for t in range(chunk // LANES):
-            continuum_ref[i * (chunk // LANES) + t] = value[:, t * LANES : (t + 1) * LANES]
+        second, third = mid_held_ref[:, lanes], low_held_ref[:, lanes]
+        value = dot(hi, second, NN) + (dot(mid, second, NN) + dot(hi, third, NN))
+        for t in range(tiles):
+            continuum_ref[i * tiles + t] += value[:, t * LANES : (t + 1) * LANES]
     continuum_ref[full_width // LANES] = jnp.zeros((own, LANES), F32)
 
     begin = begins_ref[...]
@@ -476,37 +564,42 @@
             sums[k * lines + j] = jnp.sum(terms[k], axis=0, keepdims=True)
     continuum_sums = jnp.concatenate(sums, axis=0)
 
-    cube_sums = near_ref[0, slots:, :]
-    for i in range(1, devices):
-        cube_sums = cube_sums + near_ref[i, slots:, :]
+    own_rows = slice(half, half + 3 * lines)
+    other_rows = slice(half + 3 * lines, half + 6 * lines)
+    cube_sums = (kept_ref[own_rows, :] + by_x_ref[own_rows, :]) + (
+        by_core_ref[other_rows, :] + by_both_ref[other_rows, :]
+    )
     scale = jnp.concatenate([span, span * span, span * span * span], axis=0)
     out_ref[...] = (cube_sums - continuum_sums) / scale
 
 
-def owned(device, bins, owner, begin, span, near, far, inverse, parts, own_slots, own, chunk):
+def owned(device, bins, owner, begin, span, messages, inverse, parts, own_slots, own, chunk):
     vmem = pl.BlockSpec(memory_space=pltpu.VMEM)
     hbm = pl.BlockSpec(memory_space=pltpu.HBM)
     count, full_width = parts[0].shape
     lines = begin.shape[0]
     return pl.pallas_call(
         functools.partial(owner_kernel, chunk=chunk),
-        in_specs=[pl.BlockSpec(memory_space=pltpu.SMEM)] + [hbm] * 4 + [vmem] * 6,
+        in_specs=[pl.BlockSpec(memory_space=pltpu.SMEM)] + [hbm] * 4 + [vmem] * 6 + [hbm] * 2,
         out_shape=(
             jax.ShapeDtypeStruct((own_slots, count), F32),
             jax.ShapeDtypeStruct((3 * lines, own), F32),
         ),
         scratch_shapes=[
             pltpu.VMEM((full_width // LANES + 1, own, LANES), F32),
+            pltpu.VMEM((count, full_width), BF16),
+            pltpu.VMEM((count, full_width), BF16),
             pltpu.VMEM((1, own), jnp.int32),
             pltpu.VMEM(owner.shape, jnp.int32),
             pltpu.VMEM((lines, own), jnp.int32),
             pltpu.VMEM((lines, own), jnp.int32),
             pltpu.SMEM((lines, own), jnp.int32),
+            pltpu.SemaphoreType.DMA((2,)),
             pltpu.SemaphoreType.DMA((5,)),
         ],
         compiler_params=pltpu.CompilerParams(vmem_limit_bytes=VMEM_LIMIT),
         name="owned",
-    )(device, bins, owner, begin, span, near, far, inverse, *parts)
+    )(device, bins, owner, begin, span, *messages, inverse, *parts)
 
 
 def shards(cube, templates, bin_id, owner_bins, line_start, line_width):
@@ -515,41 +608,56 @@
     spaxels = cube.shape[0]
     total_bins = owner_bins.shape[0]
     count = templates.shape[0]
+    lines = line_start.shape[0]
     own_spaxels = spaxels // devices
     own_slots = total_bins // devices
     here = device.reshape(1).astype(jnp.int32)
     pin = lambda x: pltpu.with_memory_space_constraint(x, pltpu.HBM)
-    raw_templates = templates
-    templates, columns = pin(templates), pin(cube.T)
+    columns = pin(cube.T)
     begin, span = pin(line_start), pin(line_width)
     bins, owner = pin(bin_id[None, :]), pin(owner_bins[None, :])
-
-    swap = [(d, d ^ 1) for d in range(devices)]
-    keep, send = project(here, bins, owner, columns, templates)
-    swapped = lax.ppermute(send, "spax", swap)
-    partial = in_vmem(add_kernel, jax.ShapeDtypeStruct(keep.shape, F32), "add", keep, swapped)
-    partial, here_after, later = lax.optimization_barrier((partial, here, raw_templates))
-    later = pin(later)
-    received = lax.all_to_all(partial.reshape(devices, own_slots, LANES), "spax", 0, 0)
-
-    sums = cube_windows(here_after, begin, span, columns, devices)
-    gram, scale, *parts = scaled_gram(later, 512)
-    received, sums, gram, scale = lax.optimization_barrier((received, sums, gram, scale))
-    parcel = in_vmem(
-        pack_kernel,
-        jax.ShapeDtypeStruct((devices, own_slots + sums.shape[1], LANES), F32),
-        "pack",
-        received,
-        sums,
-    )
-    parcel, gram, scale = lax.optimization_barrier((parcel, gram, scale))
-    near = lax.all_to_all(parcel, "spax", 0, 0)
-    inverse = in_vmem(invert_kernel, jax.ShapeDtypeStruct((count, count), F32), "invert", gram, scale)
-    near, inverse = lax.optimization_barrier((near, inverse))
-    far = lax.ppermute(near, "spax", swap)
-    return owned(
-        here, bins, owner, begin, span, near, far, inverse, parts, own_slots, own_spaxels, 512
-    )
+    after = lax.optimization_barrier
+
+    def swap(x, bit):
+        return lax.ppermute(x, "spax", [(d, d ^ (1 << bit)) for d in range(devices)])
+
+    keep, send = project(here, bins, owner, columns, pin(templates))
+    keep, send = split_slots(here, keep, swap(send, 0))
+    keep, send, now = after((keep, send, here))
+    arrived = swap(send, 1)
+    sums = cube_windows(now, begin, span, columns, devices)
+    sums = sums.reshape(devices * 3 * lines, LANES)
+    keep, arrived, sums, templates = after((keep, arrived, sums, templates))
+    slots, extra = total_bins // 2, devices * 3 * lines // 2
+    message = rows_of(slots + extra)
+    keep, send = in_vmem(join_kernel, (message, message), "join", keep, arrived, sums)
+
+    keep, send, templates = after((keep, send, templates))
+    gram = scale = first = None
+    for bit in range(2, devices.bit_length() - 1):
+        arrived = swap(send, bit)
+        if gram is None:
+            gram, scale, *parts = scaled_gram(pin(templates), 512)
+            arrived, gram = after((arrived, gram))
+        elif first is None:
+            first = in_vmem(first_kernel, jax.ShapeDtypeStruct((LANES, LANES), F32), "first", gram)
+            arrived, first = after((arrived, first))
+        extra //= 2
+        message = rows_of(slots + extra)
+        keep, send = in_vmem(step_kernel, (message, message), "step", keep, arrived)
+        if first is None:
+            keep, send, gram = after((keep, send, gram))
+        else:
+            keep, send, first = after((keep, send, first))
+
+    by_x = swap(send, 1)
+    by_core = swap(keep, 0)
+    inverse = in_vmem(finish_kernel, jax.ShapeDtypeStruct((count, count), F32), "finish", gram, first, scale)
+    by_x, by_core, inverse = after((by_x, by_core, inverse))
+    by_both = swap(by_x, 0)
+    messages = (keep, by_x, by_core, by_both)
+    parts = [parts[0], pin(parts[1]), pin(parts[2])]
+    return owned(here, bins, owner, begin, span, messages, inverse, parts, own_slots, own_spaxels, 512)
 
 
 def solution(mesh):

time: 61.5 us -> 51.1 us (0.83)
  local copies, waits for them, and re-layouts: 5.49 us -> 0 us
  starting transfers between devices: 14.1 us -> 9.07 us
  waiting for transfers between devices: 5.87 us -> 6.77 us
    all_to_all x2 -> x0, starting transfers between devices: 13.5 us -> none  [the longest x1 7.28 us: shards(): lax.all_to_all(partial.reshape(devices, own_slots, LANES), 'spax', 0, 0)]
    ppermute x2 -> x7, starting transfers between devices: 0.63 us -> 9.07 us  [swap(): return lax.ppermute(x, 'spax', [(d, d ^ 1 << bit) for d in range(devices)])]
    unnamed x8 -> x0, local copies, waits for them, and re-layouts: 5.49 us -> none
    ppermute x2 -> x7, waiting for transfers between devices: 2.86 us -> 6.77 us  [swap(): return lax.ppermute(x, 'spax', [(d, d ^ 1 << bit) for d in range(devices)])]
    all_to_all x2 -> x0, waiting for transfers between devices: 3 us -> none  [the longest x1 3 us: shards(): near = lax.all_to_all(parcel, 'spax', 0, 0)]
    pallas_call x3 -> x5, Pallas kernels: 11.6 us -> 10.1 us  [in_vmem(): pl.pallas_call(kernel, out_shape=shapes, compiler_params=pltpu.CompilerPa...]
    pallas_call x1 -> x2, Pallas kernels: 3.98 us -> 4.47 us  [the longest x1 4.44 us: scaled_gram(): pl.pallas_call(functools.partial(gram_kernel, chunk=chunk), in_specs=[hbm...]
  transfers between devices with their start and end apart: 4 -> 7, of which waited for: 3 -> 4; matrix products, arithmetic and copies ran while one was open for 0% -> 0% of each run, Pallas kernels for 35% -> 43%
where the time goes in v8:
time: 51.1 us; the launch traced here: 51 us
  Pallas kernels  34.2 us (67%)
  starting transfers between devices  9.07 us (18%)
  waiting for transfers between devices  6.77 us (13%)
  between operations  0.89 us (2%)
    pallas_call x5, Pallas kernels, in_vmem(): pl.pallas_call(kernel, out_shape=shapes, compiler_params=pltpu.CompilerPa...  10.1 us
    ppermute x7, starting transfers between devices, swap(): return lax.ppermute(x, 'spax', [(d, d ^ 1 << bit) for d in range(devices)])  9.07 us
    pallas_call x1, Pallas kernels, cube_windows(): pl.pallas_call(cube_kernel, in_specs=[pl.BlockSpec(memory_space=pltpu.SME...  7.73 us
    ppermute x7, waiting for transfers between devices, swap(): return lax.ppermute(x, 'spax', [(d, d ^ 1 << bit) for d in range(devices)])  6.77 us
    pallas_call x1, Pallas kernels, project(): pl.pallas_call(functools.partial(project_kernel, chunk=chunk), grid=(slot...  6.4 us
    pallas_call x1, Pallas kernels, owned(): pl.pallas_call(functools.partial(owner_kernel, chunk=chunk), in_specs=[pl...  5.53 us
    pallas_call x1, Pallas kernels, scaled_gram(): pl.pallas_call(functools.partial(gram_kernel, chunk=chunk), in_specs=[hbm...  4.44 us
  transfers between devices with their start and end apart: 7, of which 4 were waited for; matrix products, arithmetic and copies ran while one was open for 0% of the time, Pallas kernels for 43%

profile of v8, /device:TPU:0, one launch (start us, length us, event | category | flops | bytes accessed | tf_op | source)
XLA Modules:
  0.0 51.0 jit_solution(6468956178717733863)
XLA Ops:
  0.6 6.4 %project.1 = (f32[512,128]{1,0:T(8,128)S(1)}, f32[512,128]{1,0:T(8,128)S(1)}) custom-call(s32[1]{0:T(128)} %bitcast.device_ref, s32[1,2048]{1,0:T(1,128)} %bitcast.8, s32[1,512]{1,0:T(1,128)} %bitcast.10, f32[224,2048]{1,0:T(8,128)} %bitcast.6, f32[256,3584]{1,0:T(8,128)} %templates_ref.2), custom_call_target="tpu_custom_call" | custom-call | tf_op jit(solution)/shard_map/project/pallas_call | solution.py:119
  7.0 0.5 %collective-permute-start = (f32[512,128]{1,0:T(8,128)S(1)}, f32[512,128]{1,0:T(8,128)S(1)}, u32[]{:S(2)}, u32[]{:S(2)}) collective-permute-start(f32[512,128]{1,0:T(8,128)S(1)} %get-tuple-element.41), channel_id=1, source_target_pairs={{0,1},{1,0},{2,3},{3,2},{4,5},{5,4},{6,7},{7,6},{8,9},{9,8},{10,11... | collective-permute-start | bytes 786440 | tf_op jit(solution)/shard_map/ppermute | solution.py:622
  7.6 1.2 %collective-permute-done.y_ref = f32[512,128]{1,0:T(8,128)S(1)} collective-permute-done((f32[512,128]{1,0:T(8,128)S(1)}, f32[512,128]{1,0:T(8,128)S(1)}, u32[]{:S(2)}, u32[]{:S(2)}) %collective-permute-start) | collective-permute-done | bytes 262176 | tf_op jit(solution)/shard_map/ppermute | solution.py:622
  8.8 2.9 %collective-permute-start.1 = (f32[256,128]{1,0:T(8,128)S(1)}, f32[256,128]{1,0:T(8,128)S(1)}, u32[]{:S(2)}, u32[]{:S(2)}) collective-permute-start(f32[256,128]{1,0:T(8,128)S(1)} %get-tuple-element.45), channel_id=1, source_target_pairs={{0,2},{1,3},{2,0},{3,1},{4,6},{5,7},{6,4},{7,5},{8,10},{9,11},{10,... | collective-permute-start | bytes 393224 | tf_op jit(solution)/shard_map/ppermute | solution.py:622
  11.7 7.7 %cube_windows.1 = f32[16,24,128]{2,1,0:T(8,128)S(1)} custom-call(s32[1]{0:T(128)} %bitcast.device_ref, s32[8,2048]{1,0:T(8,128)} %begin_ref.3, s32[8,2048]{1,0:T(8,128)} %span_ref.3, f32[224,2048]{1,0:T(8,128)} %bitcast.7), custom_call_target="tpu_custom_call" | custom-call | tf_op jit(solution)/shard_map/cube_windows/pallas_call | solution.py:396
  19.4 0.0 collective-permute-done.1.y_ref
  19.5 1.6 %collective-permute-start.2 = (f32[448,128]{1,0:T(8,128)S(1)}, f32[448,128]{1,0:T(8,128)S(1)}, u32[]{:S(2)}, u32[]{:S(2)}) collective-permute-start(f32[448,128]{1,0:T(8,128)S(1)} %get-tuple-element.54), channel_id=1, source_target_pairs={{0,4},{1,5},{2,6},{3,7},{4,0},{5,1},{6,2},{7,3},{8,12},{9,13},{10,... | collective-permute-start | bytes 688136 | tf_op jit(solution)/shard_map/ppermute | solution.py:622
  21.1 4.4 %gram.1 = (f32[256,256]{1,0:T(8,128)S(1)}, f32[1,256]{1,0:T(1,128)S(1)}, bf16[256,3584]{1,0:T(8,128)(2,1)S(1)}, bf16[256,3584]{1,0:T(8,128)(2,1)}, bf16[256,3584]{1,0:T(8,128)(2,1)}) custom-call(f32[256,3584]{1,0:T(8,128)} %templates_ref.2), custom_call_target="tpu_custom_call" | custom-call | tf_op jit(solution)/shard_map/gram/pallas_call | solution.py:258
  25.6 1.3 %collective-permute-done.2.y_ref = f32[448,128]{1,0:T(8,128)S(1)} collective-permute-done((f32[448,128]{1,0:T(8,128)S(1)}, f32[448,128]{1,0:T(8,128)S(1)}, u32[]{:S(2)}, u32[]{:S(2)}) %collective-permute-start.2) | collective-permute-done | bytes 229408 | tf_op jit(solution)/shard_map/ppermute | solution.py:622
  26.9 2.7 %collective-permute-start.3 = (f32[352,128]{1,0:T(8,128)S(1)}, f32[352,128]{1,0:T(8,128)S(1)}, u32[]{:S(2)}, u32[]{:S(2)}) collective-permute-start(f32[352,128]{1,0:T(8,128)S(1)} %get-tuple-element.62), channel_id=1, source_target_pairs={{0,8},{1,9},{2,10},{3,11},{4,12},{5,13},{6,14},{7,15},{8,0},{9,1},... | collective-permute-start | bytes 540680 | tf_op jit(solution)/shard_map/ppermute | solution.py:622
  29.6 4.4 %first.1.first_ref = f32[128,128]{1,0:T(8,128)S(1)} custom-call(f32[256,256]{1,0:T(8,128)S(1)} %get-tuple-element.63.gram_ref), custom_call_target="tpu_custom_call" | custom-call | tf_op jit(solution)/shard_map/first/pallas_call | solution.py:302
  34.0 3.2 %collective-permute-done.3.y_ref = f32[352,128]{1,0:T(8,128)S(1)} collective-permute-done((f32[352,128]{1,0:T(8,128)S(1)}, f32[352,128]{1,0:T(8,128)S(1)}, u32[]{:S(2)}, u32[]{:S(2)}) %collective-permute-start.3) | collective-permute-done | bytes 180256 | tf_op jit(solution)/shard_map/ppermute | solution.py:622
  37.2 0.8 %collective-permute-start.4 = (f32[304,128]{1,0:T(8,128)S(1)}, f32[304,128]{1,0:T(8,128)S(1)}, u32[]{:S(2)}, u32[]{:S(2)}) collective-permute-start(f32[304,128]{1,0:T(8,128)S(1)} %get-tuple-element.69), channel_id=1, source_target_pairs={{0,2},{1,3},{2,0},{3,1},{4,6},{5,7},{6,4},{7,5},{8,10},{9,11},{10,... | collective-permute-start | bytes 466952 | tf_op jit(solution)/shard_map/ppermute | solution.py:622
  38.0 0.0 collective-permute-start.5
  38.0 5.6 %finish.1.inverse_ref = f32[256,256]{1,0:T(8,128)S(1)} custom-call(f32[256,256]{1,0:T(8,128)S(1)} %get-tuple-element.63.gram_ref, f32[128,128]{1,0:T(8,128)S(1)} %first.1.first_ref, f32[1,256]{1,0:T(1,128)S(1)} %get-tuple-element.71.scale_ref), custom_call_target="tpu_custom_call" | custom-call | tf_op jit(solution)/shard_map/finish/pallas_call | solution.py:302
  43.6 0.0 collective-permute-done.4.by_x_ref
  43.6 0.0 collective-permute-done.5.by_core_ref
  43.7 0.6 %collective-permute-start.6 = (f32[304,128]{1,0:T(8,128)S(1)}, f32[304,128]{1,0:T(8,128)S(1)}, u32[]{:S(2)}, u32[]{:S(2)}) collective-permute-start(f32[304,128]{1,0:T(8,128)S(1)} %collective-permute-done.4.by_x_ref), channel_id=1, source_target_pairs={{0,1},{1,0},{2,3},{3,2},{4,5},{5,4},{6,7},{7,6},{8,9},{9,8},{10,11... | collective-permute-start | bytes 466952 | tf_op jit(solution)/shard_map/ppermute | solution.py:622
  44.2 1.0 %collective-permute-done.6.by_both_ref = f32[304,128]{1,0:T(8,128)S(1)} collective-permute-done((f32[304,128]{1,0:T(8,128)S(1)}, f32[304,128]{1,0:T(8,128)S(1)}, u32[]{:S(2)}, u32[]{:S(2)}) %collective-permute-start.6) | collective-permute-done | bytes 155680 | tf_op jit(solution)/shard_map/ppermute | solution.py:622
  45.2 5.5 %owned.1 = (f32[32,256]{1,0:T(8,128)}, f32[24,128]{1,0:T(8,128)}) custom-call(s32[1]{0:T(128)} %bitcast.device_ref, s32[1,2048]{1,0:T(1,128)} %bitcast.9, s32[1,512]{1,0:T(1,128)} %bitcast.11, s32[8,2048]{1,0:T(8,128)} %begin_ref.3, s32[8,2048]{1,0:T(8,128)} %span_ref.3, f32[304,128]{1,0:T(8,128)S(1)} %get-tuple-element.68.kept_ref, ...), custom_call_target="tpu_custom_call" | custom-call | tf_op jit(solution)/shard_map/owned/pallas_call | solution.py:581
  (4 shorter events, 0.1 us)
Async XLA Ops:
  7.0 1.7 %collective-permute-start = (f32[512,128]{1,0:T(8,128)S(1)}, f32[512,128]{1,0:T(8,128)S(1)}, u32[]{:S(2)}, u32[]{:S(2)}) collective-permute-start(f32[512,128]{1,0:T(8,128)S(1)} %get-tuple-element.41), channel_id=1, source_target_pairs={{0,1},{1,0},{2,3},{3,2},{4,5},{5,4},{6,7},{7,6},{8,9},{9,8},{10,11... | collective-permute-start | bytes 786440 | tf_op jit(solution)/shard_map/ppermute | solution.py:622
  8.8 10.7 %collective-permute-start.1 = (f32[256,128]{1,0:T(8,128)S(1)}, f32[256,128]{1,0:T(8,128)S(1)}, u32[]{:S(2)}, u32[]{:S(2)}) collective-permute-start(f32[256,128]{1,0:T(8,128)S(1)} %get-tuple-element.45), channel_id=1, source_target_pairs={{0,2},{1,3},{2,0},{3,1},{4,6},{5,7},{6,4},{7,5},{8,10},{9,11},{10,... | collective-permute-start | bytes 393224 | tf_op jit(solution)/shard_map/ppermute | solution.py:622
  19.5 7.4 %collective-permute-start.2 = (f32[448,128]{1,0:T(8,128)S(1)}, f32[448,128]{1,0:T(8,128)S(1)}, u32[]{:S(2)}, u32[]{:S(2)}) collective-permute-start(f32[448,128]{1,0:T(8,128)S(1)} %get-tuple-element.54), channel_id=1, source_target_pairs={{0,4},{1,5},{2,6},{3,7},{4,0},{5,1},{6,2},{7,3},{8,12},{9,13},{10,... | collective-permute-start | bytes 688136 | tf_op jit(solution)/shard_map/ppermute | solution.py:622
  26.9 10.3 %collective-permute-start.3 = (f32[352,128]{1,0:T(8,128)S(1)}, f32[352,128]{1,0:T(8,128)S(1)}, u32[]{:S(2)}, u32[]{:S(2)}) collective-permute-start(f32[352,128]{1,0:T(8,128)S(1)} %get-tuple-element.62), channel_id=1, source_target_pairs={{0,8},{1,9},{2,10},{3,11},{4,12},{5,13},{6,14},{7,15},{8,0},{9,1},... | collective-permute-start | bytes 540680 | tf_op jit(solution)/shard_map/ppermute | solution.py:622
  37.2 6.4 %collective-permute-start.4 = (f32[304,128]{1,0:T(8,128)S(1)}, f32[304,128]{1,0:T(8,128)S(1)}, u32[]{:S(2)}, u32[]{:S(2)}) collective-permute-start(f32[304,128]{1,0:T(8,128)S(1)} %get-tuple-element.69), channel_id=1, source_target_pairs={{0,2},{1,3},{2,0},{3,1},{4,6},{5,7},{6,4},{7,5},{8,10},{9,11},{10,... | collective-permute-start | bytes 466952 | tf_op jit(solution)/shard_map/ppermute | solution.py:622
  38.0 5.7 %collective-permute-start.5 = (f32[304,128]{1,0:T(8,128)S(1)}, f32[304,128]{1,0:T(8,128)S(1)}, u32[]{:S(2)}, u32[]{:S(2)}) collective-permute-start(f32[304,128]{1,0:T(8,128)S(1)} %get-tuple-element.68.kept_ref), channel_id=1, source_target_pairs={{0,1},{1,0},{2,3},{3,2},{4,5},{5,4},{6,7},{7,6},{8,9},{9,8},{10,11... | collective-permute-start | bytes 466952 | tf_op jit(solution)/shard_map/ppermute | solution.py:622
  43.7 1.6 %collective-permute-start.6 = (f32[304,128]{1,0:T(8,128)S(1)}, f32[304,128]{1,0:T(8,128)S(1)}, u32[]{:S(2)}, u32[]{:S(2)}) collective-permute-start(f32[304,128]{1,0:T(8,128)S(1)} %collective-permute-done.4.by_x_ref), channel_id=1, source_target_pairs={{0,1},{1,0},{2,3},{3,2},{4,5},{5,4},{6,7},{7,6},{8,9},{9,8},{10,11... | collective-permute-start | bytes 466952 | tf_op jit(solution)/shard_map/ppermute | solution.py:622

commit v9 on v8

--- a/solution.py
+++ b/solution.py
@@ -39,8 +39,9 @@
 
 
 def project_kernel(
-    device_ref, bins_ref, owner_ref, cube_ref, templates_ref, keep_ref, send_ref,
-    held_ref, window_ref, member_ref, bins_held_ref, owner_held_ref, cube_sem, window_sem, small_sem, *, chunk,
+    device_ref, bins_ref, owner_ref, begin_ref, span_ref, cube_ref, templates_ref,
+    keep_ref, send_ref, begins_ref, spans_ref, held_ref,
+    window_ref, member_ref, bins_held_ref, owner_held_ref, cube_sem, window_sem, small_sem, *, chunk,
 ):
     width, spaxels = cube_ref.shape
     slots = keep_ref.shape[0]
@@ -61,6 +62,11 @@
         pltpu.make_async_copy(owner_ref, owner_held_ref, small_sem.at[1]),
     ]
 
+    line_copies = [
+        pltpu.make_async_copy(begin_ref, begins_ref, small_sem.at[2]),
+        pltpu.make_async_copy(span_ref, spans_ref, small_sem.at[3]),
+    ]
+
     def at_first(action):
         pl.when(pl.program_id(0) == 0)(action)
 
@@ -71,6 +77,8 @@
         window_copy.start()
         for i in range(chunks):
             cube_copy(i).start()
+        for copy in line_copies:
+            copy.start()
         for copy in small_copies:
             copy.wait()
 
@@ -103,6 +111,12 @@
         for part in split3(held_ref[:, lanes]):
             sums = sums + dot(member, part, NT)
     means = sums / counts
+
+    @at_first
+    def _():
+        for copy in line_copies:
+            copy.wait()
+
     projections = dot_f32(means, mine, NT) * (1.0 / full_width)
     low, high = projections[:, :LANES], projections[:, LANES:]
     low_kept = device_ref[0] % 2 == 0
@@ -110,7 +124,7 @@
     send_ref[...] = jnp.where(low_kept, high, low)
 
 
-def project(device, bins, owner, cube, templates):
+def project(device, bins, owner, begin, span, cube, templates):
     width, spaxels = cube.shape
     slots = owner.shape[1]
     block = min(slots, 512, max(LANES, 2**20 // spaxels))
@@ -121,26 +135,28 @@
         grid=(slots // block,),
         in_specs=[
             pl.BlockSpec(memory_space=pltpu.SMEM),
-            pl.BlockSpec(memory_space=pltpu.HBM),
-            pl.BlockSpec(memory_space=pltpu.HBM),
-            pl.BlockSpec(memory_space=pltpu.HBM),
-            pl.BlockSpec(memory_space=pltpu.HBM),
+        ]
+        + [pl.BlockSpec(memory_space=pltpu.HBM)] * 6,
+        out_specs=[pl.BlockSpec((block, LANES), lambda i: (i, 0))] * 2 + [pl.BlockSpec(memory_space=pltpu.VMEM)] * 3,
+        out_shape=[
+            jax.ShapeDtypeStruct((slots, LANES), F32),
+            jax.ShapeDtypeStruct((slots, LANES), F32),
+            pltpu.VMEM(begin.shape, jnp.int32),
+            pltpu.VMEM(span.shape, jnp.int32),
+            pltpu.VMEM((width, spaxels), F32),
         ],
-        out_specs=[pl.BlockSpec((block, LANES), lambda i: (i, 0))] * 2,
-        out_shape=[jax.ShapeDtypeStruct((slots, LANES), F32)] * 2,
         scratch_shapes=[
-            pltpu.VMEM((width, spaxels), F32),
             pltpu.VMEM((count, template_window(width, full_width)), F32),
             pltpu.VMEM((block, spaxels), BF16),
             pltpu.VMEM(bins.shape, jnp.int32),
             pltpu.VMEM(owner.shape, jnp.int32),
             pltpu.SemaphoreType.DMA((spaxels // chunk,)),
             pltpu.SemaphoreType.DMA,
-            pltpu.SemaphoreType.DMA((2,)),
+            pltpu.SemaphoreType.DMA((4,)),
         ],
         compiler_params=pltpu.CompilerParams(vmem_limit_bytes=VMEM_LIMIT),
         name="project",
-    )(device, bins, owner, cube, templates)
+    )(device, bins, owner, begin, span, cube, templates)
 
 
 def reciprocal(x):
@@ -149,13 +165,13 @@
     return r * (2.0 - x * r)
 
 
-def invert_tile(tile):
+def eliminate(tile, start, stop):
     size = tile.shape[0]
     count = size // SUB
     lanes = lax.broadcasted_iota(jnp.int32, (SUB, size), 1)
     rows_at = lax.broadcasted_iota(jnp.int32, (SUB, size), 0)
     rows = [tile[i * SUB : (i + 1) * SUB, :] for i in range(count)]
-    for k in range(count):
+    for k in range(start, stop):
         block = rows[k]
         first = k * SUB
         a = {}
@@ -206,7 +222,7 @@
                 terms = [x + y for x, y in zip(terms[::2], terms[1::2])]
             rows[i] = jnp.where(inside, 0.0, rows[i]) - terms[0]
         rows[k] = swept
-    return -jnp.concatenate(rows, axis=0)
+    return jnp.concatenate(rows, axis=0)
 
 
 def gram_kernel(
@@ -278,16 +294,22 @@
     )(templates)
 
 
-def first_kernel(gram_ref, out_ref):
-    out_ref[...] = invert_tile(gram_ref[:LANES, :LANES])
-
-
-def finish_kernel(gram_ref, first_ref, scale_ref, out_ref):
-    first = first_ref[...]
+STEPS = LANES // SUB
+EARLY = 10
+
+
+def first_kernel(gram_ref, first_ref, half_ref, second_ref):
+    first = -eliminate(gram_ref[:LANES, :LANES], 0, STEPS)
     side = gram_ref[:LANES, LANES:]
     half = dot_f32(first, side, NN)
-    schur = gram_ref[LANES:, LANES:] - dot_f32(side.T, half, NN)
-    last = invert_tile(schur)
+    first_ref[...] = first
+    half_ref[...] = half
+    second_ref[...] = eliminate(gram_ref[LANES:, LANES:] - dot_f32(side.T, half, NN), 0, EARLY)
+
+
+def finish_kernel(first_ref, half_ref, second_ref, scale_ref, out_ref):
+    first, half = first_ref[...], half_ref[...]
+    last = -eliminate(second_ref[...], EARLY, STEPS)
     cross = dot_f32(half, last, NN)
     row = scale_ref[...]
     column = jnp.broadcast_to(row, (SUB, row.shape[1])).T[:, :1]
@@ -350,60 +372,32 @@
     return sum(((position >> (len(order) - 1 - t)) & 1) << bit for t, bit in enumerate(order))
 
 
-def cube_kernel(
-    device_ref, begin_ref, span_ref, cube_ref, out_ref, begins_ref, spans_ref, held_ref, lines_sem, cube_sem,
-):
+def cube_kernel(device_ref, begin_ref, span_ref, cube_ref, out_ref, *, devices, start):
     width = cube_ref.shape[0]
-    owners = out_ref.shape[0]
     device = device_ref[0]
-
-    def owner_lanes(i):
-        return pl.ds(pl.multiple_of((device ^ flips(i, owners)) * LANES, LANES), LANES)
-
-    def tile_copy(i):
-        return pltpu.make_async_copy(cube_ref.at[:, owner_lanes(i)], held_ref.at[i], cube_sem.at[i])
-
-    line_copies = [
-        pltpu.make_async_copy(begin_ref, begins_ref, lines_sem.at[0]),
-        pltpu.make_async_copy(span_ref, spans_ref, lines_sem.at[1]),
-    ]
-    for copy in line_copies:
-        copy.start()
-    for i in range(owners):
-        tile_copy(i).start()
-    for copy in line_copies:
-        copy.wait()
+    rows = 3 * begin_ref.shape[0]
 
     def owner(i, carry):
-        tile_copy(i).wait()
-        lanes = owner_lanes(i)
+        lanes = pl.ds(pl.multiple_of((device ^ flips(start + i, devices)) * LANES, LANES), LANES)
         sums = window_sums(
-            lambda row, size: held_ref[i, row : row + size, :],
+            lambda row, size: cube_ref[row : row + size, lanes],
             width,
             device * width,
-            begins_ref[:, lanes],
-            spans_ref[:, lanes],
+            begin_ref[:, lanes],
+            span_ref[:, lanes],
         )
-        for r, value in enumerate(sums):
-            out_ref[i, r : r + 1, :] = value
+        out_ref[pl.ds(pl.multiple_of(i * rows, SUB), rows), :] = jnp.concatenate(sums, axis=0)
         return carry
 
-    lax.fori_loop(0, owners, owner, 0)
-
-
-def cube_windows(device, begin, span, cube, devices):
-    hbm = pl.BlockSpec(memory_space=pltpu.HBM)
+    lax.fori_loop(0, out_ref.shape[0] // rows, owner, 0)
+
+
+def cube_windows(device, begin, span, cube, devices, start, stop):
+    vmem = pl.BlockSpec(memory_space=pltpu.VMEM)
     return pl.pallas_call(
-        cube_kernel,
-        in_specs=[pl.BlockSpec(memory_space=pltpu.SMEM), hbm, hbm, hbm],
-        out_shape=jax.ShapeDtypeStruct((devices, 3 * begin.shape[0], LANES), F32),
-        scratch_shapes=[
-            pltpu.VMEM(begin.shape, jnp.int32),
-            pltpu.VMEM(span.shape, jnp.int32),
-            pltpu.VMEM((devices, cube.shape[0], LANES), F32),
-            pltpu.SemaphoreType.DMA((2,)),
-            pltpu.SemaphoreType.DMA((devices,)),
-        ],
+        functools.partial(cube_kernel, devices=devices, start=start),
+        in_specs=[pl.BlockSpec(memory_space=pltpu.SMEM), vmem, vmem, vmem],
+        out_shape=rows_of((stop - start) * 3 * begin.shape[0]),
         compiler_params=pltpu.CompilerParams(vmem_limit_bytes=VMEM_LIMIT),
         name="cube_windows",
     )(device, begin, span, cube)
@@ -417,13 +411,16 @@
     send_ref[...] = jnp.where(low_kept, total[half:], total[:half])
 
 
-def join_kernel(x_ref, y_ref, sums_ref, keep_ref, send_ref):
+def join_kernel(x_ref, y_ref, early_ref, late_ref, keep_ref, send_ref):
     slots = x_ref.shape[0]
-    half = sums_ref.shape[0] // 2
+    early = early_ref.shape[0]
+    rest = keep_ref.shape[0] - slots - early
     total = x_ref[...] + y_ref[...]
-    for out_ref, first in ((keep_ref, 0), (send_ref, half)):
-        out_ref[:slots, :] = total
-        out_ref[slots:, :] = sums_ref[first : first + half, :]
+    keep_ref[:slots, :] = total
+    keep_ref[slots : slots + early, :] = early_ref[...]
+    keep_ref[slots + early :, :] = late_ref[:rest, :]
+    send_ref[:slots, :] = total
+    send_ref[slots:, :] = late_ref[rest:, :]
 
 
 def step_kernel(x_ref, y_ref, keep_ref, send_ref):
@@ -621,16 +618,19 @@
     def swap(x, bit):
         return lax.ppermute(x, "spax", [(d, d ^ (1 << bit)) for d in range(devices)])
 
-    keep, send = project(here, bins, owner, columns, pin(templates))
-    keep, send = split_slots(here, keep, swap(send, 0))
+    keep, send, begins, spans, held = project(here, bins, owner, begin, span, columns, pin(templates))
+    arrived = swap(send, 0)
+    cut = devices * 3 // 16
+    early = cube_windows(here, begins, spans, held, devices, 0, cut)
+    keep, arrived, early = after((keep, arrived, early))
+    keep, send = split_slots(here, keep, arrived)
     keep, send, now = after((keep, send, here))
     arrived = swap(send, 1)
-    sums = cube_windows(now, begin, span, columns, devices)
-    sums = sums.reshape(devices * 3 * lines, LANES)
-    keep, arrived, sums, templates = after((keep, arrived, sums, templates))
+    late = cube_windows(now, begins, spans, held, devices, cut, devices)
+    keep, arrived, early, late, templates = after((keep, arrived, early, late, templates))
     slots, extra = total_bins // 2, devices * 3 * lines // 2
     message = rows_of(slots + extra)
-    keep, send = in_vmem(join_kernel, (message, message), "join", keep, arrived, sums)
+    keep, send = in_vmem(join_kernel, (message, message), "join", keep, arrived, early, late)
 
     keep, send, templates = after((keep, send, templates))
     gram = scale = first = None
@@ -640,7 +640,7 @@
             gram, scale, *parts = scaled_gram(pin(templates), 512)
             arrived, gram = after((arrived, gram))
         elif first is None:
-            first = in_vmem(first_kernel, jax.ShapeDtypeStruct((LANES, LANES), F32), "first", gram)
+            first = in_vmem(first_kernel, [rows_of(LANES)] * 3, "first", gram)
             arrived, first = after((arrived, first))
         extra //= 2
         message = rows_of(slots + extra)
@@ -652,7 +652,7 @@
 
     by_x = swap(send, 1)
     by_core = swap(keep, 0)
-    inverse = in_vmem(finish_kernel, jax.ShapeDtypeStruct((count, count), F32), "finish", gram, first, scale)
+    inverse = in_vmem(finish_kernel, jax.ShapeDtypeStruct((count, count), F32), "finish", *first, scale)
     by_x, by_core, inverse = after((by_x, by_core, inverse))
     by_both = swap(by_x, 0)
     messages = (keep, by_x, by_core, by_both)

time: 51.1 us -> 47 us (0.920)
  Pallas kernels: 34.2 us -> 32.5 us
  waiting for transfers between devices: 6.77 us -> 5.08 us
  starting transfers between devices: 9.07 us -> 8.35 us
    pallas_call x1 -> x2, Pallas kernels: 7.73 us -> 5.97 us  [cube_windows(): pl.pallas_call(functools.partial(cube_kernel, devices=devices, start=star...]
    ppermute x7, waiting for transfers between devices: 6.77 us -> 5.08 us  [swap(): return lax.ppermute(x, 'spax', [(d, d ^ 1 << bit) for d in range(devices)])]
    ppermute x7, starting transfers between devices: 9.07 us -> 8.35 us  [swap(): return lax.ppermute(x, 'spax', [(d, d ^ 1 << bit) for d in range(devices)])]
  transfers between devices with their start and end apart: 7 -> 7, of which waited for: 4 -> 4; matrix products, arithmetic and copies ran while one was open for 0% -> 0% of each run, Pallas kernels for 43% -> 44%
where the time goes in v9:
time: 47 us; the launch traced here: 46.8 us
  Pallas kernels  32.5 us (69%)
  starting transfers between devices  8.35 us (18%)
  waiting for transfers between devices  5.08 us (11%)
  between operations  0.89 us (2%)
    pallas_call x5, Pallas kernels, in_vmem(): pl.pallas_call(kernel, out_shape=shapes, compiler_params=pltpu.CompilerPa...  10.2 us
    ppermute x7, starting transfers between devices, swap(): return lax.ppermute(x, 'spax', [(d, d ^ 1 << bit) for d in range(devices)])  8.35 us
    pallas_call x1, Pallas kernels, project(): pl.pallas_call(functools.partial(project_kernel, chunk=chunk), grid=(slot...  6.33 us
    pallas_call x2, Pallas kernels, cube_windows(): pl.pallas_call(functools.partial(cube_kernel, devices=devices, start=star...  5.97 us
    pallas_call x1, Pallas kernels, owned(): pl.pallas_call(functools.partial(owner_kernel, chunk=chunk), in_specs=[pl...  5.53 us
    ppermute x7, waiting for transfers between devices, swap(): return lax.ppermute(x, 'spax', [(d, d ^ 1 << bit) for d in range(devices)])  5.08 us
    pallas_call x1, Pallas kernels, scaled_gram(): pl.pallas_call(functools.partial(gram_kernel, chunk=chunk), in_specs=[hbm...  4.46 us
  transfers between devices with their start and end apart: 7, of which 4 were waited for; matrix products, arithmetic and copies ran while one was open for 0% of the time, Pallas kernels for 44%

profile of v9, /device:TPU:0, one launch (start us, length us, event | category | flops | bytes accessed | tf_op | source)
XLA Modules:
  0.0 46.8 jit_solution(5973041715005268063)
XLA Ops:
  0.6 6.3 %project.1 = (f32[512,128]{1,0:T(8,128)S(1)}, f32[512,128]{1,0:T(8,128)S(1)}, s32[8,2048]{1,0:T(8,128)S(1)}, s32[8,2048]{1,0:T(8,128)S(1)}, f32[224,2048]{1,0:T(8,128)S(1)}) custom-call(s32[1]{0:T(128)} %bitcast.device_ref, s32[1,2048]{1,0:T(1,128)} %bitcast.5, s32[1,512]{1,0:T(1,128)} %bitcast.7, s32[8,2048]{1,0:T(8,128)} %begin_ref.3, s32[8,2048]{1,0:T(8,128)} %span_ref.3, ...), custom_call_target="tpu_custom_call" | custom-call | tf_op jit(solution)/shard_map/project/pallas_call | solution.py:133
  7.0 0.5 %collective-permute-start = (f32[512,128]{1,0:T(8,128)S(1)}, f32[512,128]{1,0:T(8,128)S(1)}, u32[]{:S(2)}, u32[]{:S(2)}) collective-permute-start(f32[512,128]{1,0:T(8,128)S(1)} %get-tuple-element.55), channel_id=1, source_target_pairs={{0,1},{1,0},{2,3},{3,2},{4,5},{5,4},{6,7},{7,6},{8,9},{9,8},{10,11... | collective-permute-start | bytes 786440 | tf_op jit(solution)/shard_map/ppermute | solution.py:619
  7.5 1.1 %cube_windows.2.early_ref = f32[72,128]{1,0:T(8,128)S(1)} custom-call(s32[1]{0:T(128)} %bitcast.device_ref, s32[8,2048]{1,0:T(8,128)S(1)} %get-tuple-element.56.begin_ref, s32[8,2048]{1,0:T(8,128)S(1)} %get-tuple-element.57.span_ref, f32[224,2048]{1,0:T(8,128)S(1)} %get-tuple-element.58.cube_ref), custom_call_target="tpu_custom_call" | custom-call | tf_op jit(solution)/shard_map/cube_windows/pallas_call | solution.py:397
  8.6 0.1 collective-permute-done.y_ref
  8.7 2.9 %collective-permute-start.1 = (f32[256,128]{1,0:T(8,128)S(1)}, f32[256,128]{1,0:T(8,128)S(1)}, u32[]{:S(2)}, u32[]{:S(2)}) collective-permute-start(f32[256,128]{1,0:T(8,128)S(1)} %get-tuple-element.64), channel_id=1, source_target_pairs={{0,2},{1,3},{2,0},{3,1},{4,6},{5,7},{6,4},{7,5},{8,10},{9,11},{10,... | collective-permute-start | bytes 393224 | tf_op jit(solution)/shard_map/ppermute | solution.py:619
  11.6 4.9 %cube_windows.3.late_ref = f32[312,128]{1,0:T(8,128)S(1)} custom-call(s32[1]{0:T(128)} %bitcast.device_ref, s32[8,2048]{1,0:T(8,128)S(1)} %get-tuple-element.56.begin_ref, s32[8,2048]{1,0:T(8,128)S(1)} %get-tuple-element.57.span_ref, f32[224,2048]{1,0:T(8,128)S(1)} %get-tuple-element.58.cube_ref), custom_call_target="tpu_custom_call" | custom-call | tf_op jit(solution)/shard_map/cube_windows/pallas_call | solution.py:397
  16.5 0.0 collective-permute-done.1.y_ref
  16.6 1.6 %collective-permute-start.2 = (f32[448,128]{1,0:T(8,128)S(1)}, f32[448,128]{1,0:T(8,128)S(1)}, u32[]{:S(2)}, u32[]{:S(2)}) collective-permute-start(f32[448,128]{1,0:T(8,128)S(1)} %get-tuple-element.75), channel_id=1, source_target_pairs={{0,4},{1,5},{2,6},{3,7},{4,0},{5,1},{6,2},{7,3},{8,12},{9,13},{10,... | collective-permute-start | bytes 688136 | tf_op jit(solution)/shard_map/ppermute | solution.py:619
  18.2 4.5 %gram.1 = (f32[256,256]{1,0:T(8,128)S(1)}, f32[1,256]{1,0:T(1,128)S(1)}, bf16[256,3584]{1,0:T(8,128)(2,1)S(1)}, bf16[256,3584]{1,0:T(8,128)(2,1)}, bf16[256,3584]{1,0:T(8,128)(2,1)}) custom-call(f32[256,3584]{1,0:T(8,128)} %templates_ref.2), custom_call_target="tpu_custom_call" | custom-call | tf_op jit(solution)/shard_map/gram/pallas_call | solution.py:274
  22.7 1.3 %collective-permute-done.2.y_ref = f32[448,128]{1,0:T(8,128)S(1)} collective-permute-done((f32[448,128]{1,0:T(8,128)S(1)}, f32[448,128]{1,0:T(8,128)S(1)}, u32[]{:S(2)}, u32[]{:S(2)}) %collective-permute-start.2) | collective-permute-done | bytes 229408 | tf_op jit(solution)/shard_map/ppermute | solution.py:619
  24.0 2.7 %collective-permute-start.3 = (f32[352,128]{1,0:T(8,128)S(1)}, f32[352,128]{1,0:T(8,128)S(1)}, u32[]{:S(2)}, u32[]{:S(2)}) collective-permute-start(f32[352,128]{1,0:T(8,128)S(1)} %get-tuple-element.83), channel_id=1, source_target_pairs={{0,8},{1,9},{2,10},{3,11},{4,12},{5,13},{6,14},{7,15},{8,0},{9,1},... | collective-permute-start | bytes 540680 | tf_op jit(solution)/shard_map/ppermute | solution.py:619
  26.7 7.7 %first.1 = (f32[128,128]{1,0:T(8,128)S(1)}, f32[128,128]{1,0:T(8,128)S(1)}, f32[128,128]{1,0:T(8,128)S(1)}) custom-call(f32[256,256]{1,0:T(8,128)S(1)} %get-tuple-element.84.gram_ref), custom_call_target="tpu_custom_call" | custom-call | tf_op jit(solution)/shard_map/first/pallas_call | solution.py:324
  34.4 0.0 collective-permute-done.3.y_ref
  34.4 0.6 %collective-permute-start.4 = (f32[304,128]{1,0:T(8,128)S(1)}, f32[304,128]{1,0:T(8,128)S(1)}, u32[]{:S(2)}, u32[]{:S(2)}) collective-permute-start(f32[304,128]{1,0:T(8,128)S(1)} %get-tuple-element.95), channel_id=1, source_target_pairs={{0,2},{1,3},{2,0},{3,1},{4,6},{5,7},{6,4},{7,5},{8,10},{9,11},{10,... | collective-permute-start | bytes 466952 | tf_op jit(solution)/shard_map/ppermute | solution.py:619
  35.0 0.0 collective-permute-start.5
  35.0 2.4 %finish.1.inverse_ref = f32[256,256]{1,0:T(8,128)S(1)} custom-call(f32[128,128]{1,0:T(8,128)S(1)} %get-tuple-element.96.first_ref, f32[128,128]{1,0:T(8,128)S(1)} %get-tuple-element.97.half_ref, f32[128,128]{1,0:T(8,128)S(1)} %get-tuple-element.98.second_ref, f32[1,256]{1,0:T(1,128)S(1)} %get-tuple-element.99.scale_ref), custom_call_target="tpu_custom_call" | custom-call | tf_op jit(solution)/shard_map/finish/pallas_call | solution.py:324
  37.4 2.3 %collective-permute-done.4.by_x_ref = f32[304,128]{1,0:T(8,128)S(1)} collective-permute-done((f32[304,128]{1,0:T(8,128)S(1)}, f32[304,128]{1,0:T(8,128)S(1)}, u32[]{:S(2)}, u32[]{:S(2)}) %collective-permute-start.4) | collective-permute-done | bytes 155680 | tf_op jit(solution)/shard_map/ppermute | solution.py:619
  39.7 0.0 collective-permute-done.5.by_core_ref
  39.7 0.0 collective-permute-start.6
  39.7 1.4 %collective-permute-done.6.by_both_ref = f32[304,128]{1,0:T(8,128)S(1)} collective-permute-done((f32[304,128]{1,0:T(8,128)S(1)}, f32[304,128]{1,0:T(8,128)S(1)}, u32[]{:S(2)}, u32[]{:S(2)}) %collective-permute-start.6) | collective-permute-done | bytes 155680 | tf_op jit(solution)/shard_map/ppermute | solution.py:619
  41.1 5.5 %owned.1 = (f32[32,256]{1,0:T(8,128)}, f32[24,128]{1,0:T(8,128)}) custom-call(s32[1]{0:T(128)} %bitcast.device_ref, s32[1,2048]{1,0:T(1,128)} %bitcast.6, s32[1,512]{1,0:T(1,128)} %bitcast.8, s32[8,2048]{1,0:T(8,128)} %begin_ref.3, s32[8,2048]{1,0:T(8,128)} %span_ref.3, f32[304,128]{1,0:T(8,128)S(1)} %get-tuple-element.94.kept_ref, ...), custom_call_target="tpu_custom_call" | custom-call | tf_op jit(solution)/shard_map/owned/pallas_call | solution.py:578
  (4 shorter events, 0.1 us)
Async XLA Ops:
  7.0 1.7 %collective-permute-start = (f32[512,128]{1,0:T(8,128)S(1)}, f32[512,128]{1,0:T(8,128)S(1)}, u32[]{:S(2)}, u32[]{:S(2)}) collective-permute-start(f32[512,128]{1,0:T(8,128)S(1)} %get-tuple-element.55), channel_id=1, source_target_pairs={{0,1},{1,0},{2,3},{3,2},{4,5},{5,4},{6,7},{7,6},{8,9},{9,8},{10,11... | collective-permute-start | bytes 786440 | tf_op jit(solution)/shard_map/ppermute | solution.py:619
  8.7 7.8 %collective-permute-start.1 = (f32[256,128]{1,0:T(8,128)S(1)}, f32[256,128]{1,0:T(8,128)S(1)}, u32[]{:S(2)}, u32[]{:S(2)}) collective-permute-start(f32[256,128]{1,0:T(8,128)S(1)} %get-tuple-element.64), channel_id=1, source_target_pairs={{0,2},{1,3},{2,0},{3,1},{4,6},{5,7},{6,4},{7,5},{8,10},{9,11},{10,... | collective-permute-start | bytes 393224 | tf_op jit(solution)/shard_map/ppermute | solution.py:619
  16.6 7.4 %collective-permute-start.2 = (f32[448,128]{1,0:T(8,128)S(1)}, f32[448,128]{1,0:T(8,128)S(1)}, u32[]{:S(2)}, u32[]{:S(2)}) collective-permute-start(f32[448,128]{1,0:T(8,128)S(1)} %get-tuple-element.75), channel_id=1, source_target_pairs={{0,4},{1,5},{2,6},{3,7},{4,0},{5,1},{6,2},{7,3},{8,12},{9,13},{10,... | collective-permute-start | bytes 688136 | tf_op jit(solution)/shard_map/ppermute | solution.py:619
  24.0 10.4 %collective-permute-start.3 = (f32[352,128]{1,0:T(8,128)S(1)}, f32[352,128]{1,0:T(8,128)S(1)}, u32[]{:S(2)}, u32[]{:S(2)}) collective-permute-start(f32[352,128]{1,0:T(8,128)S(1)} %get-tuple-element.83), channel_id=1, source_target_pairs={{0,8},{1,9},{2,10},{3,11},{4,12},{5,13},{6,14},{7,15},{8,0},{9,1},... | collective-permute-start | bytes 540680 | tf_op jit(solution)/shard_map/ppermute | solution.py:619
  34.4 5.3 %collective-permute-start.4 = (f32[304,128]{1,0:T(8,128)S(1)}, f32[304,128]{1,0:T(8,128)S(1)}, u32[]{:S(2)}, u32[]{:S(2)}) collective-permute-start(f32[304,128]{1,0:T(8,128)S(1)} %get-tuple-element.95), channel_id=1, source_target_pairs={{0,2},{1,3},{2,0},{3,1},{4,6},{5,7},{6,4},{7,5},{8,10},{9,11},{10,... | collective-permute-start | bytes 466952 | tf_op jit(solution)/shard_map/ppermute | solution.py:619
  35.0 4.7 %collective-permute-start.5 = (f32[304,128]{1,0:T(8,128)S(1)}, f32[304,128]{1,0:T(8,128)S(1)}, u32[]{:S(2)}, u32[]{:S(2)}) collective-permute-start(f32[304,128]{1,0:T(8,128)S(1)} %get-tuple-element.94.kept_ref), channel_id=1, source_target_pairs={{0,1},{1,0},{2,3},{3,2},{4,5},{5,4},{6,7},{7,6},{8,9},{9,8},{10,11... | collective-permute-start | bytes 466952 | tf_op jit(solution)/shard_map/ppermute | solution.py:619
  39.7 1.4 %collective-permute-start.6 = (f32[304,128]{1,0:T(8,128)S(1)}, f32[304,128]{1,0:T(8,128)S(1)}, u32[]{:S(2)}, u32[]{:S(2)}) collective-permute-start(f32[304,128]{1,0:T(8,128)S(1)} %collective-permute-done.4.by_x_ref), channel_id=1, source_target_pairs={{0,1},{1,0},{2,3},{3,2},{4,5},{5,4},{6,7},{7,6},{8,9},{9,8},{10,11... | collective-permute-start | bytes 466952 | tf_op jit(solution)/shard_map/ppermute | solution.py:619

commit v10 on v9

--- a/solution.py
+++ b/solution.py
@@ -39,124 +39,94 @@
 
 
 def project_kernel(
-    device_ref, bins_ref, owner_ref, begin_ref, span_ref, cube_ref, templates_ref,
+    device_ref, bins_ref, begin_ref, span_ref, cube_ref, templates_ref,
     keep_ref, send_ref, begins_ref, spans_ref, held_ref,
-    window_ref, member_ref, bins_held_ref, owner_held_ref, cube_sem, window_sem, small_sem, *, chunk,
+    sums_ref, counts_ref, window_ref, bins_held_ref, firsts_ref, cube_sem, small_sem, *, chunk,
 ):
     width, spaxels = cube_ref.shape
-    slots = keep_ref.shape[0]
+    total_bins = keep_ref.shape[0]
     full_width = templates_ref.shape[1]
     first = device_ref[0] * width
     window = window_ref.shape[1]
     base = pl.multiple_of(jnp.minimum(first // LANES * LANES, full_width - window), LANES)
     chunks = spaxels // chunk
+    reach = chunk + SUB
 
     def cube_copy(i):
         lanes = pl.ds(i * chunk, chunk)
         return pltpu.make_async_copy(cube_ref.at[:, lanes], held_ref.at[:, lanes], cube_sem.at[i])
 
-    window_copy = pltpu.make_async_copy(templates_ref.at[:, pl.ds(base, window)], window_ref, window_sem)
-
-    small_copies = [
-        pltpu.make_async_copy(bins_ref, bins_held_ref, small_sem.at[0]),
-        pltpu.make_async_copy(owner_ref, owner_held_ref, small_sem.at[1]),
+    bins_copy = pltpu.make_async_copy(bins_ref, bins_held_ref, small_sem.at[0])
+    firsts_copy = pltpu.make_async_copy(bins_ref, firsts_ref, small_sem.at[1])
+    window_copy = pltpu.make_async_copy(templates_ref.at[:, pl.ds(base, window)], window_ref, small_sem.at[2])
+    line_copies = [
+        pltpu.make_async_copy(begin_ref, begins_ref, small_sem.at[3]),
+        pltpu.make_async_copy(span_ref, spans_ref, small_sem.at[4]),
     ]
-
-    line_copies = [
-        pltpu.make_async_copy(begin_ref, begins_ref, small_sem.at[2]),
-        pltpu.make_async_copy(span_ref, spans_ref, small_sem.at[3]),
-    ]
-
-    def at_first(action):
-        pl.when(pl.program_id(0) == 0)(action)
-
-    @at_first
-    def _():
-        for copy in small_copies:
-            copy.start()
-        window_copy.start()
-        for i in range(chunks):
-            cube_copy(i).start()
-        for copy in line_copies:
-            copy.start()
-        for copy in small_copies:
-            copy.wait()
-
-    owner = owner_held_ref[:, pl.ds(pl.multiple_of(pl.program_id(0) * slots, LANES), slots)]
-    owner = jnp.broadcast_to(owner, (SUB, slots)).T[:, :1]
-    counts = jnp.zeros((slots, LANES), F32)
+    for copy in [bins_copy, firsts_copy] + [cube_copy(i) for i in range(chunks)] + [window_copy] + line_copies:
+        copy.start()
+    sums_ref[...] = jnp.zeros(sums_ref.shape, F32)
+    counts_ref[...] = jnp.zeros(counts_ref.shape, F32)
+    rows_at = lax.broadcasted_iota(jnp.int32, (reach, chunk), 0)
+    bins_copy.wait()
+    firsts_copy.wait()
+
     for i in range(chunks):
         lanes = slice(i * chunk, (i + 1) * chunk)
-        ones = jnp.where(owner == bins_held_ref[:, lanes], 1.0, 0.0)
-        for lane in range(0, chunk, LANES):
+        low_bin = pl.multiple_of(firsts_ref[0, i * chunk] // SUB * SUB, SUB)
+        rows = pl.ds(low_bin, reach)
+        ones = jnp.where(rows_at == bins_held_ref[:, lanes] - low_bin, 1.0, 0.0)
+        counts = ones[:, :LANES]
+        for lane in range(LANES, chunk, LANES):
             counts = counts + ones[:, lane : lane + LANES]
-        member_ref[:, lanes] = ones.astype(BF16)
-    counts = jnp.sum(counts, axis=1, keepdims=True)
-
-    @at_first
-    def _():
-        window_copy.wait()
-
+        counts_ref[rows, :] += counts
+        member = ones.astype(BF16)
+        cube_copy(i).wait()
+        hi, mid, low = split3(held_ref[:, lanes])
+        sums_ref[rows, :] += dot(member, hi, NT) + (dot(member, mid, NT) + dot(member, low, NT))
+
+    window_copy.wait()
     mine = pltpu.roll(window_ref[...], window - (first - base), 1)[:, :width]
-
-    sums = jnp.zeros((slots, width), F32)
-    for i in range(chunks):
-
-        @at_first
-        def _(i=i):
-            cube_copy(i).wait()
-
-        lanes = slice(i * chunk, (i + 1) * chunk)
-        member = member_ref[:, lanes]
-        for part in split3(held_ref[:, lanes]):
-            sums = sums + dot(member, part, NT)
-    means = sums / counts
-
-    @at_first
-    def _():
-        for copy in line_copies:
-            copy.wait()
-
-    projections = dot_f32(means, mine, NT) * (1.0 / full_width)
-    low, high = projections[:, :LANES], projections[:, LANES:]
     low_kept = device_ref[0] % 2 == 0
-    keep_ref[...] = jnp.where(low_kept, low, high)
-    send_ref[...] = jnp.where(low_kept, high, low)
-
-
-def project(device, bins, owner, begin, span, cube, templates):
+    block = min(total_bins, 512)
+    for at in range(0, total_bins, block):
+        rows = slice(at, at + block)
+        means = sums_ref[rows, :] / jnp.sum(counts_ref[rows, :], axis=1, keepdims=True)
+        projections = dot_f32(means, mine, NT) * (1.0 / full_width)
+        low, high = projections[:, :LANES], projections[:, LANES:]
+        keep_ref[rows, :] = jnp.where(low_kept, low, high)
+        send_ref[rows, :] = jnp.where(low_kept, high, low)
+    for copy in line_copies:
+        copy.wait()
+
+
+def project(device, bins, begin, span, cube, templates, total_bins):
     width, spaxels = cube.shape
-    slots = owner.shape[1]
-    block = min(slots, 512, max(LANES, 2**20 // spaxels))
-    chunk = min(spaxels, 512)
+    chunk = min(spaxels, 256)
     count, full_width = templates.shape
     return pl.pallas_call(
         functools.partial(project_kernel, chunk=chunk),
-        grid=(slots // block,),
-        in_specs=[
-            pl.BlockSpec(memory_space=pltpu.SMEM),
-        ]
-        + [pl.BlockSpec(memory_space=pltpu.HBM)] * 6,
-        out_specs=[pl.BlockSpec((block, LANES), lambda i: (i, 0))] * 2 + [pl.BlockSpec(memory_space=pltpu.VMEM)] * 3,
+        in_specs=[pl.BlockSpec(memory_space=pltpu.SMEM)] + [pl.BlockSpec(memory_space=pltpu.HBM)] * 5,
+        out_specs=[pl.BlockSpec(memory_space=pltpu.VMEM)] * 5,
         out_shape=[
-            jax.ShapeDtypeStruct((slots, LANES), F32),
-            jax.ShapeDtypeStruct((slots, LANES), F32),
+            rows_of(total_bins),
+            rows_of(total_bins),
             pltpu.VMEM(begin.shape, jnp.int32),
             pltpu.VMEM(span.shape, jnp.int32),
             pltpu.VMEM((width, spaxels), F32),
         ],
         scratch_shapes=[
+            pltpu.VMEM((total_bins + chunk + SUB, width), F32),
+            pltpu.VMEM((total_bins + chunk + SUB, LANES), F32),
             pltpu.VMEM((count, template_window(width, full_width)), F32),
-            pltpu.VMEM((block, spaxels), BF16),
             pltpu.VMEM(bins.shape, jnp.int32),
-            pltpu.VMEM(owner.shape, jnp.int32),
+            pltpu.SMEM(bins.shape, jnp.int32),
             pltpu.SemaphoreType.DMA((spaxels // chunk,)),
-            pltpu.SemaphoreType.DMA,
-            pltpu.SemaphoreType.DMA((4,)),
+            pltpu.SemaphoreType.DMA((5,)),
         ],
         compiler_params=pltpu.CompilerParams(vmem_limit_bytes=VMEM_LIMIT),
         name="project",
-    )(device, bins, owner, begin, span, cube, templates)
+    )(device, bins, begin, span, cube, templates)
 
 
 def reciprocal(x):
@@ -295,7 +265,7 @@
 
 
 STEPS = LANES // SUB
-EARLY = 10
+EARLY = 5
 
 
 def first_kernel(gram_ref, first_ref, half_ref, second_ref):
@@ -412,25 +382,32 @@
 
 
 def join_kernel(x_ref, y_ref, early_ref, late_ref, keep_ref, send_ref):
-    slots = x_ref.shape[0]
-    early = early_ref.shape[0]
-    rest = keep_ref.shape[0] - slots - early
+    slots, early = x_ref.shape[0], early_ref.shape[0]
     total = x_ref[...] + y_ref[...]
+    keep_ref[...] = total
+    send_ref[:slots, :] = total
+    send_ref[slots : slots + early, :] = early_ref[...]
+    send_ref[slots + early :, :] = late_ref[...]
+
+
+def step_kernel(x_ref, y_ref, sums_ref, keep_ref, send_ref, *, slots):
+    half = (y_ref.shape[0] - slots) // 2
+    own = sums_ref.shape[0]
+    total = x_ref[:slots, :] + y_ref[:slots, :]
+
+    def gathered(first):
+        value = y_ref[slots + first : slots + first + half, :]
+        if x_ref.shape[0] > slots:
+            value = value + x_ref[slots + first : slots + first + half, :]
+        return value
+
+    kept, sent = gathered(0), gathered(half) + sums_ref[own - half :, :]
+    if own > half:
+        kept = kept + sums_ref[:half, :]
     keep_ref[:slots, :] = total
-    keep_ref[slots : slots + early, :] = early_ref[...]
-    keep_ref[slots + early :, :] = late_ref[:rest, :]
+    keep_ref[slots:, :] = kept
     send_ref[:slots, :] = total
-    send_ref[slots:, :] = late_ref[rest:, :]
-
-
-def step_kernel(x_ref, y_ref, keep_ref, send_ref):
-    rows = x_ref.shape[0]
-    half = rows - keep_ref.shape[0]
-    slots = rows - 2 * half
-    total = x_ref[:slots, :] + y_ref[:slots, :]
-    for out_ref, first in ((keep_ref, slots), (send_ref, slots + half)):
-        out_ref[:slots, :] = total
-        out_ref[slots:, :] = x_ref[first : first + half, :] + y_ref[first : first + half, :]
+    send_ref[slots:, :] = sent
 
 
 def rows_of(count):
@@ -453,7 +430,7 @@
     device_ref, bins_ref, owner_ref, begin_ref, span_ref,
     kept_ref, by_x_ref, by_core_ref, by_both_ref, inverse_ref, hi_ref, mid_ref, low_ref,
     weights_ref, out_ref,
-    continuum_ref, mid_held_ref, low_held_ref, bins_held_ref, owner_held_ref, begins_ref, spans_ref, starts_ref,
+    continuum_ref, mine_ref, mid_held_ref, low_held_ref, bins_held_ref, owner_held_ref, begins_ref, spans_ref, starts_ref,
     parts_sem, small_sem, *, chunk,
 ):
     own_slots = weights_ref.shape[0]
@@ -461,6 +438,7 @@
     lines = begin_ref.shape[0]
     full_width = hi_ref.shape[1]
     half = owner_held_ref.shape[1] // 2
+    inverse = inverse_ref[...]
     device = device_ref[0]
     own_lanes = pl.ds(pl.multiple_of(device * own, LANES), own)
 
@@ -478,29 +456,35 @@
     for copy in small_copies + part_copies:
         copy.start()
 
-    inverse = inverse_ref[...]
     core_low = device % 2 == 0
     low_kept = (device >> 1) % 2 == 0
 
+    def lane_halves(near, far):
+        return jnp.where(core_low, near, far), jnp.where(core_low, far, near)
+
     def by_lanes(near, far):
-        return jnp.concatenate([jnp.where(core_low, near, far), jnp.where(core_low, far, near)], axis=1)
-
-    slot = device * own_slots
-    in_kept = (slot // half) == ((device >> 1) % 2)
-    rows = pl.ds(pl.multiple_of(slot % half, own_slots), own_slots)
-    mine = by_lanes(
-        jnp.where(in_kept, kept_ref[rows, :], by_x_ref[rows, :]),
-        jnp.where(in_kept, by_core_ref[rows, :], by_both_ref[rows, :]),
-    )
-    weights_ref[...] = dot_f32(mine, inverse, NN)
+        return jnp.concatenate(lane_halves(near, far), axis=1)
 
     for copy in small_copies:
         copy.wait()
+
+    kept_first = jnp.where(low_kept, 0, half)
+    for i in range(own_slots):
+        picked_bin = owner_held_ref[0, device * own_slots + i]
+        in_kept = (picked_bin >= half) == (kept_first > 0)
+        row = pl.ds(picked_bin - jnp.where(picked_bin >= half, half, 0), 1)
+        low, high = lane_halves(
+            jnp.where(in_kept, kept_ref[row, :], by_x_ref[row, :]),
+            jnp.where(in_kept, by_core_ref[row, :], by_both_ref[row, :]),
+        )
+        mine_ref[i : i + 1, :LANES] = low
+        mine_ref[i : i + 1, LANES:] = high
+    weights_ref[...] = dot_f32(mine_ref[...], inverse, NN)
+
     bins = jnp.broadcast_to(bins_held_ref[...], (SUB, own)).T[:, :1]
-    low_slots, high_slots = owner_held_ref[:, :half], owner_held_ref[:, half:]
+    bins_at = lax.broadcasted_iota(jnp.int32, (own, half), 1)
     members = [
-        jnp.where(bins == jnp.where(low_kept, a, b), 1.0, 0.0).astype(BF16)
-        for a, b in ((low_slots, high_slots), (high_slots, low_slots))
+        jnp.where(bins_at == bins - low, 1.0, 0.0).astype(BF16) for low in (kept_first, half - kept_first)
     ]
     picked = []
     for kept_half, other_half in ((kept_ref, by_x_ref), (by_core_ref, by_both_ref)):
@@ -584,10 +568,11 @@
         ),
         scratch_shapes=[
             pltpu.VMEM((full_width // LANES + 1, own, LANES), F32),
+            pltpu.VMEM((own_slots, count), F32),
             pltpu.VMEM((count, full_width), BF16),
             pltpu.VMEM((count, full_width), BF16),
             pltpu.VMEM((1, own), jnp.int32),
-            pltpu.VMEM(owner.shape, jnp.int32),
+            pltpu.SMEM(owner.shape, jnp.int32),
             pltpu.VMEM((lines, own), jnp.int32),
             pltpu.VMEM((lines, own), jnp.int32),
             pltpu.SMEM((lines, own), jnp.int32),
@@ -618,37 +603,43 @@
     def swap(x, bit):
         return lax.ppermute(x, "spax", [(d, d ^ (1 << bit)) for d in range(devices)])
 
-    keep, send, begins, spans, held = project(here, bins, owner, begin, span, columns, pin(templates))
+    keep, send, begins, spans, held = project(here, bins, begin, span, columns, pin(templates), total_bins)
+    windows = lambda start, stop, now: cube_windows(now, begins, spans, held, devices, start, stop)
     arrived = swap(send, 0)
-    cut = devices * 3 // 16
-    early = cube_windows(here, begins, spans, held, devices, 0, cut)
+    left = devices // 2
+    cut = left + devices * 3 // 16
+    early = windows(left, cut, here)
     keep, arrived, early = after((keep, arrived, early))
     keep, send = split_slots(here, keep, arrived)
     keep, send, now = after((keep, send, here))
     arrived = swap(send, 1)
-    late = cube_windows(now, begins, spans, held, devices, cut, devices)
+    late = windows(cut, devices, now)
     keep, arrived, early, late, templates = after((keep, arrived, early, late, templates))
-    slots, extra = total_bins // 2, devices * 3 * lines // 2
-    message = rows_of(slots + extra)
-    keep, send = in_vmem(join_kernel, (message, message), "join", keep, arrived, early, late)
-
-    keep, send, templates = after((keep, send, templates))
-    gram = scale = first = None
+    slots = total_bins // 2
+    message = rows_of(slots + left * 3 * lines)
+    keep, send = in_vmem(join_kernel, (rows_of(slots), message), "join", keep, arrived, early, late)
+
+    keep, send, now, templates = after((keep, send, here, templates))
+    gram = first = None
     for bit in range(2, devices.bit_length() - 1):
         arrived = swap(send, bit)
+        left //= 2
+        last_step = bit == devices.bit_length() - 2
+        sums = windows(0 if last_step else left, 2 * left, now)
         if gram is None:
             gram, scale, *parts = scaled_gram(pin(templates), 512)
-            arrived, gram = after((arrived, gram))
+            arrived, sums, gram = after((arrived, sums, gram))
         elif first is None:
             first = in_vmem(first_kernel, [rows_of(LANES)] * 3, "first", gram)
-            arrived, first = after((arrived, first))
-        extra //= 2
-        message = rows_of(slots + extra)
-        keep, send = in_vmem(step_kernel, (message, message), "step", keep, arrived)
+            arrived, sums, first = after((arrived, sums, first))
+        message = rows_of(slots + left * 3 * lines)
+        keep, send = in_vmem(
+            functools.partial(step_kernel, slots=slots), (message, message), "step", keep, arrived, sums
+        )
         if first is None:
-            keep, send, gram = after((keep, send, gram))
+            keep, send, now, gram = after((keep, send, here, gram))
         else:
-            keep, send, first = after((keep, send, first))
+            keep, send, now, first = after((keep, send, here, first))
 
     by_x = swap(send, 1)
     by_core = swap(keep, 0)

time: 47 us -> 46.1 us (0.981)
  waiting for transfers between devices: 5.08 us -> 3.7 us
  starting transfers between devices: 8.35 us -> 9.72 us
  Pallas kernels: 32.5 us -> 31.6 us
    ppermute x7, waiting for transfers between devices: 5.08 us -> 3.7 us  [swap(): return lax.ppermute(x, 'spax', [(d, d ^ 1 << bit) for d in range(devices)])]
    ppermute x7, starting transfers between devices: 8.35 us -> 9.72 us  [swap(): return lax.ppermute(x, 'spax', [(d, d ^ 1 << bit) for d in range(devices)])]
    pallas_call x1, Pallas kernels: 6.33 us -> 5.63 us  [project(): pl.pallas_call(functools.partial(project_kernel, chunk=chunk), in_specs=[...]
    pallas_call x2 -> x4, Pallas kernels: 5.97 us -> 5.96 us  [cube_windows(): pl.pallas_call(functools.partial(cube_kernel, devices=devices, start=star...]
where the time goes in v10:
time: 46.1 us; the launch traced here: 45.9 us
  Pallas kernels  31.6 us (69%)
  starting transfers between devices  9.72 us (21%)
  waiting for transfers between devices  3.7 us (8%)
  between operations  0.89 us (2%)
    pallas_call x5, Pallas kernels, in_vmem(): pl.pallas_call(kernel, out_shape=shapes, compiler_params=pltpu.CompilerPa...  10.1 us
    ppermute x7, starting transfers between devices, swap(): return lax.ppermute(x, 'spax', [(d, d ^ 1 << bit) for d in range(devices)])  9.72 us
    pallas_call x4, Pallas kernels, cube_windows(): pl.pallas_call(functools.partial(cube_kernel, devices=devices, start=star...  5.96 us
    pallas_call x1, Pallas kernels, project(): pl.pallas_call(functools.partial(project_kernel, chunk=chunk), in_specs=[...  5.63 us
    pallas_call x1, Pallas kernels, owned(): pl.pallas_call(functools.partial(owner_kernel, chunk=chunk), in_specs=[pl...  5.45 us
    pallas_call x1, Pallas kernels, scaled_gram(): pl.pallas_call(functools.partial(gram_kernel, chunk=chunk), in_specs=[hbm...  4.46 us
    ppermute x7, waiting for transfers between devices, swap(): return lax.ppermute(x, 'spax', [(d, d ^ 1 << bit) for d in range(devices)])  3.7 us
  transfers between devices with their start and end apart: 7, of which 4 were waited for; matrix products, arithmetic and copies ran while one was open for 0% of the time, Pallas kernels for 44%

profile of v10, /device:TPU:0, one launch (start us, length us, event | category | flops | bytes accessed | tf_op | source)
XLA Modules:
  0.0 45.9 jit_solution(9728945213903418502)
XLA Ops:
  0.6 5.6 %project.1 = (f32[512,128]{1,0:T(8,128)S(1)}, f32[512,128]{1,0:T(8,128)S(1)}, s32[8,2048]{1,0:T(8,128)S(1)}, s32[8,2048]{1,0:T(8,128)S(1)}, f32[224,2048]{1,0:T(8,128)S(1)}) custom-call(s32[1]{0:T(128)} %bitcast.device_ref, s32[1,2048]{1,0:T(1,128)} %bitcast.5, s32[8,2048]{1,0:T(8,128)} %begin_ref.3, s32[8,2048]{1,0:T(8,128)} %span_ref.3, ...), custom_call_target="tpu_custom_call" | custom-call | tf_op jit(solution)/shard_map/project/pallas_call | solution.py:107
  6.3 0.5 %collective-permute-start = (f32[512,128]{1,0:T(8,128)S(1)}, f32[512,128]{1,0:T(8,128)S(1)}, u32[]{:S(2)}, u32[]{:S(2)}) collective-permute-start(f32[512,128]{1,0:T(8,128)S(1)} %get-tuple-element.59), channel_id=1, source_target_pairs={{0,1},{1,0},{2,3},{3,2},{4,5},{5,4},{6,7},{7,6},{8,9},{9,8},{10,11... | collective-permute-start | bytes 786440 | tf_op jit(solution)/shard_map/ppermute | solution.py:604
  6.8 1.1 %cube_windows.4.early_ref = f32[72,128]{1,0:T(8,128)S(1)} custom-call(s32[1]{0:T(128)} %bitcast.device_ref, s32[8,2048]{1,0:T(8,128)S(1)} %get-tuple-element.60.begin_ref, s32[8,2048]{1,0:T(8,128)S(1)} %get-tuple-element.61.span_ref, f32[224,2048]{1,0:T(8,128)S(1)} %get-tuple-element.62.cube_ref), custom_call_target="tpu_custom_call" | custom-call | tf_op jit(solution)/shard_map/cube_windows/pallas_call | solution.py:367
  7.9 0.1 collective-permute-done.y_ref
  8.0 2.9 %collective-permute-start.1 = (f32[256,128]{1,0:T(8,128)S(1)}, f32[256,128]{1,0:T(8,128)S(1)}, u32[]{:S(2)}, u32[]{:S(2)}) collective-permute-start(f32[256,128]{1,0:T(8,128)S(1)} %get-tuple-element.68), channel_id=1, source_target_pairs={{0,2},{1,3},{2,0},{3,1},{4,6},{5,7},{6,4},{7,5},{8,10},{9,11},{10,... | collective-permute-start | bytes 393224 | tf_op jit(solution)/shard_map/ppermute | solution.py:604
  10.9 1.8 %cube_windows.5.late_ref = f32[120,128]{1,0:T(8,128)S(1)} custom-call(s32[1]{0:T(128)} %bitcast.device_ref, s32[8,2048]{1,0:T(8,128)S(1)} %get-tuple-element.60.begin_ref, s32[8,2048]{1,0:T(8,128)S(1)} %get-tuple-element.61.span_ref, f32[224,2048]{1,0:T(8,128)S(1)} %get-tuple-element.62.cube_ref), custom_call_target="tpu_custom_call" | custom-call | tf_op jit(solution)/shard_map/cube_windows/pallas_call | solution.py:367
  12.7 2.0 %collective-permute-done.1.y_ref = f32[256,128]{1,0:T(8,128)S(1)} collective-permute-done((f32[256,128]{1,0:T(8,128)S(1)}, f32[256,128]{1,0:T(8,128)S(1)}, u32[]{:S(2)}, u32[]{:S(2)}) %collective-permute-start.1) | collective-permute-done | bytes 131104 | tf_op jit(solution)/shard_map/ppermute | solution.py:604
  14.7 1.9 %collective-permute-start.2 = (f32[448,128]{1,0:T(8,128)S(1)}, f32[448,128]{1,0:T(8,128)S(1)}, u32[]{:S(2)}, u32[]{:S(2)}) collective-permute-start(f32[448,128]{1,0:T(8,128)S(1)} %get-tuple-element.79), channel_id=1, source_target_pairs={{0,4},{1,5},{2,6},{3,7},{4,0},{5,1},{6,2},{7,3},{8,12},{9,13},{10,... | collective-permute-start | bytes 688136 | tf_op jit(solution)/shard_map/ppermute | solution.py:604
  16.6 1.4 %cube_windows.6.sums_ref = f32[96,128]{1,0:T(8,128)S(1)} custom-call(s32[1]{0:T(128)} %bitcast.device_ref, s32[8,2048]{1,0:T(8,128)S(1)} %get-tuple-element.60.begin_ref, s32[8,2048]{1,0:T(8,128)S(1)} %get-tuple-element.61.span_ref, f32[224,2048]{1,0:T(8,128)S(1)} %get-tuple-element.62.cube_ref), custom_call_target="tpu_custom_call" | custom-call | tf_op jit(solution)/shard_map/cube_windows/pallas_call | solution.py:367
  18.1 4.5 %gram.1 = (f32[256,256]{1,0:T(8,128)S(1)}, f32[1,256]{1,0:T(1,128)S(1)}, bf16[256,3584]{1,0:T(8,128)(2,1)S(1)}, bf16[256,3584]{1,0:T(8,128)(2,1)}, bf16[256,3584]{1,0:T(8,128)(2,1)}) custom-call(f32[256,3584]{1,0:T(8,128)} %templates_ref.2), custom_call_target="tpu_custom_call" | custom-call | tf_op jit(solution)/shard_map/gram/pallas_call | solution.py:244
  22.6 0.0 collective-permute-done.2.y_ref
  22.6 2.6 %collective-permute-start.3 = (f32[352,128]{1,0:T(8,128)S(1)}, f32[352,128]{1,0:T(8,128)S(1)}, u32[]{:S(2)}, u32[]{:S(2)}) collective-permute-start(f32[352,128]{1,0:T(8,128)S(1)} %get-tuple-element.89), channel_id=1, source_target_pairs={{0,8},{1,9},{2,10},{3,11},{4,12},{5,13},{6,14},{7,15},{8,0},{9,1},... | collective-permute-start | bytes 540680 | tf_op jit(solution)/shard_map/ppermute | solution.py:604
  25.3 1.6 %cube_windows.7.sums_ref = f32[96,128]{1,0:T(8,128)S(1)} custom-call(s32[1]{0:T(128)} %bitcast.device_ref, s32[8,2048]{1,0:T(8,128)S(1)} %get-tuple-element.60.begin_ref, s32[8,2048]{1,0:T(8,128)S(1)} %get-tuple-element.61.span_ref, f32[224,2048]{1,0:T(8,128)S(1)} %get-tuple-element.62.cube_ref), custom_call_target="tpu_custom_call" | custom-call | tf_op jit(solution)/shard_map/cube_windows/pallas_call | solution.py:367
  26.9 6.2 %first.1 = (f32[128,128]{1,0:T(8,128)S(1)}, f32[128,128]{1,0:T(8,128)S(1)}, f32[128,128]{1,0:T(8,128)S(1)}) custom-call(f32[256,256]{1,0:T(8,128)S(1)} %get-tuple-element.91.gram_ref), custom_call_target="tpu_custom_call" | custom-call | tf_op jit(solution)/shard_map/first/pallas_call | solution.py:294
  33.1 0.0 collective-permute-done.3.y_ref
  33.2 1.6 %collective-permute-start.4 = (f32[304,128]{1,0:T(8,128)S(1)}, f32[304,128]{1,0:T(8,128)S(1)}, u32[]{:S(2)}, u32[]{:S(2)}) collective-permute-start(f32[304,128]{1,0:T(8,128)S(1)} %get-tuple-element.103), channel_id=1, source_target_pairs={{0,2},{1,3},{2,0},{3,1},{4,6},{5,7},{6,4},{7,5},{8,10},{9,11},{10,... | collective-permute-start | bytes 466952 | tf_op jit(solution)/shard_map/ppermute | solution.py:604
  34.7 0.0 collective-permute-start.5
  34.7 3.8 %finish.1.inverse_ref = f32[256,256]{1,0:T(8,128)S(1)} custom-call(f32[128,128]{1,0:T(8,128)S(1)} %get-tuple-element.104.first_ref, f32[128,128]{1,0:T(8,128)S(1)} %get-tuple-element.105.half_ref, f32[128,128]{1,0:T(8,128)S(1)} %get-tuple-element.106.second_ref, f32[1,256]{1,0:T(1,128)S(1)} %get-tuple-element.107.scale_ref), custom_call_target="tpu_custom_call" | custom-call | tf_op jit(solution)/shard_map/finish/pallas_call | solution.py:294
  38.5 0.4 collective-permute-done.4.by_x_ref
  38.9 0.0 collective-permute-done.5.by_core_ref
  38.9 0.2 collective-permute-start.6
  39.1 1.2 %collective-permute-done.6.by_both_ref = f32[304,128]{1,0:T(8,128)S(1)} collective-permute-done((f32[304,128]{1,0:T(8,128)S(1)}, f32[304,128]{1,0:T(8,128)S(1)}, u32[]{:S(2)}, u32[]{:S(2)}) %collective-permute-start.6) | collective-permute-done | bytes 155680 | tf_op jit(solution)/shard_map/ppermute | solution.py:604
  40.3 5.4 %owned.1 = (f32[32,256]{1,0:T(8,128)}, f32[24,128]{1,0:T(8,128)}) custom-call(s32[1]{0:T(128)} %bitcast.device_ref, s32[1,2048]{1,0:T(1,128)} %bitcast.6, s32[1,512]{1,0:T(1,128)} %bitcast.7, s32[8,2048]{1,0:T(8,128)} %begin_ref.3, s32[8,2048]{1,0:T(8,128)} %span_ref.3, f32[304,128]{1,0:T(8,128)S(1)} %get-tuple-element.102.kept_ref, ...), custom_call_target="tpu_custom_call" | custom-call | tf_op jit(solution)/shard_map/owned/pallas_call | solution.py:562
  (4 shorter events, 0.1 us)
Async XLA Ops:
  6.3 1.7 %collective-permute-start = (f32[512,128]{1,0:T(8,128)S(1)}, f32[512,128]{1,0:T(8,128)S(1)}, u32[]{:S(2)}, u32[]{:S(2)}) collective-permute-start(f32[512,128]{1,0:T(8,128)S(1)} %get-tuple-element.59), channel_id=1, source_target_pairs={{0,1},{1,0},{2,3},{3,2},{4,5},{5,4},{6,7},{7,6},{8,9},{9,8},{10,11... | collective-permute-start | bytes 786440 | tf_op jit(solution)/shard_map/ppermute | solution.py:604
  8.0 6.7 %collective-permute-start.1 = (f32[256,128]{1,0:T(8,128)S(1)}, f32[256,128]{1,0:T(8,128)S(1)}, u32[]{:S(2)}, u32[]{:S(2)}) collective-permute-start(f32[256,128]{1,0:T(8,128)S(1)} %get-tuple-element.68), channel_id=1, source_target_pairs={{0,2},{1,3},{2,0},{3,1},{4,6},{5,7},{6,4},{7,5},{8,10},{9,11},{10,... | collective-permute-start | bytes 393224 | tf_op jit(solution)/shard_map/ppermute | solution.py:604
  14.7 7.8 %collective-permute-start.2 = (f32[448,128]{1,0:T(8,128)S(1)}, f32[448,128]{1,0:T(8,128)S(1)}, u32[]{:S(2)}, u32[]{:S(2)}) collective-permute-start(f32[448,128]{1,0:T(8,128)S(1)} %get-tuple-element.79), channel_id=1, source_target_pairs={{0,4},{1,5},{2,6},{3,7},{4,0},{5,1},{6,2},{7,3},{8,12},{9,13},{10,... | collective-permute-start | bytes 688136 | tf_op jit(solution)/shard_map/ppermute | solution.py:604
  22.6 10.5 %collective-permute-start.3 = (f32[352,128]{1,0:T(8,128)S(1)}, f32[352,128]{1,0:T(8,128)S(1)}, u32[]{:S(2)}, u32[]{:S(2)}) collective-permute-start(f32[352,128]{1,0:T(8,128)S(1)} %get-tuple-element.89), channel_id=1, source_target_pairs={{0,8},{1,9},{2,10},{3,11},{4,12},{5,13},{6,14},{7,15},{8,0},{9,1},... | collective-permute-start | bytes 540680 | tf_op jit(solution)/shard_map/ppermute | solution.py:604
  33.2 5.8 %collective-permute-start.4 = (f32[304,128]{1,0:T(8,128)S(1)}, f32[304,128]{1,0:T(8,128)S(1)}, u32[]{:S(2)}, u32[]{:S(2)}) collective-permute-start(f32[304,128]{1,0:T(8,128)S(1)} %get-tuple-element.103), channel_id=1, source_target_pairs={{0,2},{1,3},{2,0},{3,1},{4,6},{5,7},{6,4},{7,5},{8,10},{9,11},{10,... | collective-permute-start | bytes 466952 | tf_op jit(solution)/shard_map/ppermute | solution.py:604
  34.7 4.2 %collective-permute-start.5 = (f32[304,128]{1,0:T(8,128)S(1)}, f32[304,128]{1,0:T(8,128)S(1)}, u32[]{:S(2)}, u32[]{:S(2)}) collective-permute-start(f32[304,128]{1,0:T(8,128)S(1)} %get-tuple-element.102.kept_ref), channel_id=1, source_target_pairs={{0,1},{1,0},{2,3},{3,2},{4,5},{5,4},{6,7},{7,6},{8,9},{9,8},{10,11... | collective-permute-start | bytes 466952 | tf_op jit(solution)/shard_map/ppermute | solution.py:604
  38.9 1.4 %collective-permute-start.6 = (f32[304,128]{1,0:T(8,128)S(1)}, f32[304,128]{1,0:T(8,128)S(1)}, u32[]{:S(2)}, u32[]{:S(2)}) collective-permute-start(f32[304,128]{1,0:T(8,128)S(1)} %collective-permute-done.4.by_x_ref), channel_id=1, source_target_pairs={{0,1},{1,0},{2,3},{3,2},{4,5},{5,4},{6,7},{7,6},{8,9},{9,8},{10,11... | collective-permute-start | bytes 466952 | tf_op jit(solution)/shard_map/ppermute | solution.py:604

commit v11 on v10

--- a/solution.py
+++ b/solution.py
@@ -41,7 +41,7 @@
 def project_kernel(
     device_ref, bins_ref, begin_ref, span_ref, cube_ref, templates_ref,
     keep_ref, send_ref, begins_ref, spans_ref, held_ref,
-    sums_ref, counts_ref, window_ref, bins_held_ref, firsts_ref, cube_sem, small_sem, *, chunk,
+    bins_held_ref, sums_ref, window_ref, firsts_ref, cube_sem, small_sem, *, chunk,
 ):
     width, spaxels = cube_ref.shape
     total_bins = keep_ref.shape[0]
@@ -54,7 +54,7 @@
 
     def cube_copy(i):
         lanes = pl.ds(i * chunk, chunk)
-        return pltpu.make_async_copy(cube_ref.at[:, lanes], held_ref.at[:, lanes], cube_sem.at[i])
+        return pltpu.make_async_copy(cube_ref.at[:, lanes], held_ref.at[pl.ds(0, width), lanes], cube_sem.at[i])
 
     bins_copy = pltpu.make_async_copy(bins_ref, bins_held_ref, small_sem.at[0])
     firsts_copy = pltpu.make_async_copy(bins_ref, firsts_ref, small_sem.at[1])
@@ -63,35 +63,38 @@
         pltpu.make_async_copy(begin_ref, begins_ref, small_sem.at[3]),
         pltpu.make_async_copy(span_ref, spans_ref, small_sem.at[4]),
     ]
-    for copy in [bins_copy, firsts_copy] + [cube_copy(i) for i in range(chunks)] + [window_copy] + line_copies:
+    for copy in [bins_copy, firsts_copy, window_copy] + [cube_copy(i) for i in range(chunks)] + line_copies:
         copy.start()
     sums_ref[...] = jnp.zeros(sums_ref.shape, F32)
-    counts_ref[...] = jnp.zeros(counts_ref.shape, F32)
+    joined = held_ref.shape[0] > width
+    counted = sums_ref.shape[1] - COUNT_ROWS
+    if joined:
+        held_ref[width:, :] = jnp.ones((COUNT_ROWS, spaxels), F32)
     rows_at = lax.broadcasted_iota(jnp.int32, (reach, chunk), 0)
     bins_copy.wait()
     firsts_copy.wait()
+    window_copy.wait()
+    mine = pltpu.roll(window_ref[...], window - (first - base), 1)[:, :width]
 
     for i in range(chunks):
         lanes = slice(i * chunk, (i + 1) * chunk)
         low_bin = pl.multiple_of(firsts_ref[0, i * chunk] // SUB * SUB, SUB)
         rows = pl.ds(low_bin, reach)
-        ones = jnp.where(rows_at == bins_held_ref[:, lanes] - low_bin, 1.0, 0.0)
-        counts = ones[:, :LANES]
-        for lane in range(LANES, chunk, LANES):
-            counts = counts + ones[:, lane : lane + LANES]
-        counts_ref[rows, :] += counts
-        member = ones.astype(BF16)
+        member = jnp.where(rows_at == bins_held_ref[:, lanes] - low_bin, 1.0, 0.0).astype(BF16)
         cube_copy(i).wait()
         hi, mid, low = split3(held_ref[:, lanes])
-        sums_ref[rows, :] += dot(member, hi, NT) + (dot(member, mid, NT) + dot(member, low, NT))
-
-    window_copy.wait()
-    mine = pltpu.roll(window_ref[...], window - (first - base), 1)[:, :width]
+        new = dot(member, hi, NT) + (dot(member, mid, NT) + dot(member, low, NT))
+        if joined:
+            sums_ref[rows, :] += new
+        else:
+            sums_ref[rows, :width] += new
+            sums_ref[rows, counted:] += dot(member, jnp.ones((COUNT_ROWS, chunk), BF16), NT)
+
     low_kept = device_ref[0] % 2 == 0
     block = min(total_bins, 512)
     for at in range(0, total_bins, block):
         rows = slice(at, at + block)
-        means = sums_ref[rows, :] / jnp.sum(counts_ref[rows, :], axis=1, keepdims=True)
+        means = sums_ref[rows, :width] / sums_ref[rows, counted : counted + 1]
         projections = dot_f32(means, mine, NT) * (1.0 / full_width)
         low, high = projections[:, :LANES], projections[:, LANES:]
         keep_ref[rows, :] = jnp.where(low_kept, low, high)
@@ -100,26 +103,30 @@
         copy.wait()
 
 
+COUNT_ROWS = 16
+
+
 def project(device, bins, begin, span, cube, templates, total_bins):
     width, spaxels = cube.shape
     chunk = min(spaxels, 256)
+    wide = -(-width // COUNT_ROWS) * COUNT_ROWS + COUNT_ROWS
+    held = width if width % COUNT_ROWS else wide
     count, full_width = templates.shape
     return pl.pallas_call(
         functools.partial(project_kernel, chunk=chunk),
         in_specs=[pl.BlockSpec(memory_space=pltpu.SMEM)] + [pl.BlockSpec(memory_space=pltpu.HBM)] * 5,
-        out_specs=[pl.BlockSpec(memory_space=pltpu.VMEM)] * 5,
+        out_specs=[pl.BlockSpec(memory_space=pltpu.VMEM)] * 6,
         out_shape=[
             rows_of(total_bins),
             rows_of(total_bins),
             pltpu.VMEM(begin.shape, jnp.int32),
             pltpu.VMEM(span.shape, jnp.int32),
-            pltpu.VMEM((width, spaxels), F32),
+            pltpu.VMEM((held, spaxels), F32),
+            pltpu.VMEM(bins.shape, jnp.int32),
         ],
         scratch_shapes=[
-            pltpu.VMEM((total_bins + chunk + SUB, width), F32),
-            pltpu.VMEM((total_bins + chunk + SUB, LANES), F32),
+            pltpu.VMEM((total_bins + chunk + SUB, wide), F32),
             pltpu.VMEM((count, template_window(width, full_width)), F32),
-            pltpu.VMEM(bins.shape, jnp.int32),
             pltpu.SMEM(bins.shape, jnp.int32),
             pltpu.SemaphoreType.DMA((spaxels // chunk,)),
             pltpu.SemaphoreType.DMA((5,)),
@@ -265,7 +272,7 @@
 
 
 STEPS = LANES // SUB
-EARLY = 5
+EARLY = 4
 
 
 def first_kernel(gram_ref, first_ref, half_ref, second_ref):
@@ -342,8 +349,7 @@
     return sum(((position >> (len(order) - 1 - t)) & 1) << bit for t, bit in enumerate(order))
 
 
-def cube_kernel(device_ref, begin_ref, span_ref, cube_ref, out_ref, *, devices, start):
-    width = cube_ref.shape[0]
+def cube_kernel(device_ref, begin_ref, span_ref, cube_ref, out_ref, *, devices, start, width):
     device = device_ref[0]
     rows = 3 * begin_ref.shape[0]
 
@@ -362,10 +368,10 @@
     lax.fori_loop(0, out_ref.shape[0] // rows, owner, 0)
 
 
-def cube_windows(device, begin, span, cube, devices, start, stop):
+def cube_windows(device, begin, span, cube, devices, start, stop, width):
     vmem = pl.BlockSpec(memory_space=pltpu.VMEM)
     return pl.pallas_call(
-        functools.partial(cube_kernel, devices=devices, start=start),
+        functools.partial(cube_kernel, devices=devices, start=start, width=width),
         in_specs=[pl.BlockSpec(memory_space=pltpu.SMEM), vmem, vmem, vmem],
         out_shape=rows_of((stop - start) * 3 * begin.shape[0]),
         compiler_params=pltpu.CompilerParams(vmem_limit_bytes=VMEM_LIMIT),
@@ -426,15 +432,48 @@
     )(device, x, y)
 
 
+def pick(bins_ref, device, lows, blocks, own, half):
+    bins = bins_ref[:, pl.ds(pl.multiple_of(device * own, LANES), own)]
+    bins = jnp.broadcast_to(bins, (SUB, own)).T[:, :1]
+    total = None
+    for low_bin, block in zip(lows, blocks):
+        at = lax.broadcasted_iota(jnp.int32, (own, half), 1)
+        member = jnp.where(at == bins - low_bin, 1.0, 0.0).astype(BF16)
+        hi, mid, low = split3(block[:half, :])
+        value = dot(member, hi, NN) + (dot(member, mid, NN) + dot(member, low, NN))
+        total = value if total is None else total + value
+    return total
+
+
+def pick_kernel(device_ref, bins_ref, kept_ref, by_x_ref, by_core_ref, near_ref, far_ref, *, half):
+    device = device_ref[0]
+    own = near_ref.shape[0]
+    kept_first = jnp.where((device >> 1) % 2 == 0, 0, half)
+    lows = (kept_first, half - kept_first)
+    near_ref[...] = pick(bins_ref, device, lows, (kept_ref, by_x_ref), own, half)
+    far_ref[...] = pick(bins_ref, device, lows[:1], (by_core_ref,), own, half)
+
+
+def pick_early(device, bins, kept, by_x, by_core, own, half):
+    vmem = pl.BlockSpec(memory_space=pltpu.VMEM)
+    return pl.pallas_call(
+        functools.partial(pick_kernel, half=half),
+        in_specs=[pl.BlockSpec(memory_space=pltpu.SMEM)] + [vmem] * 4,
+        out_shape=(rows_of(own), rows_of(own)),
+        compiler_params=pltpu.CompilerParams(vmem_limit_bytes=VMEM_LIMIT),
+        name="pick_early",
+    )(device, bins, kept, by_x, by_core)
+
+
 def owner_kernel(
     device_ref, bins_ref, owner_ref, begin_ref, span_ref,
-    kept_ref, by_x_ref, by_core_ref, by_both_ref, inverse_ref, hi_ref, mid_ref, low_ref,
+    kept_ref, by_x_ref, by_core_ref, by_both_ref, near_ref, far_ref, inverse_ref, hi_ref, mid_ref, low_ref,
     weights_ref, out_ref,
-    continuum_ref, mine_ref, mid_held_ref, low_held_ref, bins_held_ref, owner_held_ref, begins_ref, spans_ref, starts_ref,
+    continuum_ref, mine_ref, mid_held_ref, low_held_ref, owner_held_ref, begins_ref, spans_ref, starts_ref,
     parts_sem, small_sem, *, chunk,
 ):
     own_slots = weights_ref.shape[0]
-    own = bins_held_ref.shape[1]
+    own = begins_ref.shape[1]
     lines = begin_ref.shape[0]
     full_width = hi_ref.shape[1]
     half = owner_held_ref.shape[1] // 2
@@ -443,7 +482,6 @@
     own_lanes = pl.ds(pl.multiple_of(device * own, LANES), own)
 
     small_copies = [
-        pltpu.make_async_copy(bins_ref.at[:, own_lanes], bins_held_ref, small_sem.at[0]),
         pltpu.make_async_copy(owner_ref, owner_held_ref, small_sem.at[1]),
         pltpu.make_async_copy(begin_ref.at[:, own_lanes], begins_ref, small_sem.at[2]),
         pltpu.make_async_copy(span_ref.at[:, own_lanes], spans_ref, small_sem.at[3]),
@@ -481,20 +519,8 @@
         mine_ref[i : i + 1, LANES:] = high
     weights_ref[...] = dot_f32(mine_ref[...], inverse, NN)
 
-    bins = jnp.broadcast_to(bins_held_ref[...], (SUB, own)).T[:, :1]
-    bins_at = lax.broadcasted_iota(jnp.int32, (own, half), 1)
-    members = [
-        jnp.where(bins_at == bins - low, 1.0, 0.0).astype(BF16) for low in (kept_first, half - kept_first)
-    ]
-    picked = []
-    for kept_half, other_half in ((kept_ref, by_x_ref), (by_core_ref, by_both_ref)):
-        value = None
-        for member, block in zip(members, (kept_half, other_half)):
-            hi, mid, low = split3(block[:half, :])
-            new = dot(member, hi, NN) + (dot(member, mid, NN) + dot(member, low, NN))
-            value = new if value is None else value + new
-        picked.append(value)
-    spaxel_weights = dot_f32(by_lanes(*picked), inverse, NN)
+    far = far_ref[...] + pick(bins_ref, device, (half - kept_first,), (by_both_ref,), own, half)
+    spaxel_weights = dot_f32(by_lanes(near_ref[...], far), inverse, NN)
 
     hi, mid, low = split3(spaxel_weights)
     tiles = chunk // LANES
@@ -502,47 +528,46 @@
         first = hi_ref[:, i * chunk : (i + 1) * chunk]
         value = dot(hi, first, NN) + (dot(mid, first, NN) + dot(low, first, NN))
         for t in range(tiles):
-            continuum_ref[i * tiles + t] = value[:, t * LANES : (t + 1) * LANES]
+            continuum_ref[2 * (i * tiles + t)] = value[:, t * LANES : (t + 1) * LANES]
     for copy in part_copies:
         copy.wait()
+    left_half = lax.broadcasted_iota(jnp.int32, (own, LANES), 1) < LANES // 2
+    before = None
     for i in range(full_width // chunk):
         lanes = slice(i * chunk, (i + 1) * chunk)
         second, third = mid_held_ref[:, lanes], low_held_ref[:, lanes]
         value = dot(hi, second, NN) + (dot(mid, second, NN) + dot(hi, third, NN))
         for t in range(tiles):
-            continuum_ref[i * tiles + t] += value[:, t * LANES : (t + 1) * LANES]
-    continuum_ref[full_width // LANES] = jnp.zeros((own, LANES), F32)
+            at = 2 * (i * tiles + t)
+            tile = continuum_ref[at] + value[:, t * LANES : (t + 1) * LANES]
+            continuum_ref[at] = tile
+            turned = pltpu.roll(tile, LANES // 2, 1)
+            if at:
+                continuum_ref[at - 1] = jnp.where(left_half, before, turned)
+            before = turned
+    continuum_ref[2 * (full_width // LANES) - 1] = jnp.where(left_half, before, 0.0)
 
     begin = begins_ref[...]
     span = spans_ref[...].astype(F32)
-    centre = 2.0 * (begin & (LANES - 1)).astype(F32) + span - 1.0
+    centre = 2.0 * (begin & (LANES // 2 - 1)).astype(F32) + span - 1.0
     rows_at = lax.broadcasted_iota(jnp.int32, (SUB, LANES), 0)
     at_row = [rows_at == r for r in range(SUB)]
     twice = 2.0 * lax.broadcasted_iota(jnp.int32, (LANES, own), 0).astype(F32)
     sums = [None] * (3 * lines)
     for j in range(lines):
-        picks = ([], [])
+        picks = []
         for g in range(own // SUB):
             rows = slice(g * SUB, (g + 1) * SUB)
-            left = right = None
+            block = None
             for r in range(SUB):
-                tile = lax.shift_right_logical(starts_ref[j, g * SUB + r], 7)
-                a = continuum_ref[tile, rows, :]
-                b = continuum_ref[tile + 1, rows, :]
-                left = a if left is None else jnp.where(at_row[r], a, left)
-                right = b if right is None else jnp.where(at_row[r], b, right)
-            picks[0].append(left)
-            picks[1].append(right)
-        terms = None
-        for side in range(2):
-            block = jnp.concatenate(picks[side], axis=0).T
-            m = twice + (2.0 * LANES * side - centre[j : j + 1])
-            masked = jnp.where(jnp.abs(m) < span[j : j + 1], block, 0.0)
-            weighted = masked * m
-            new = [masked, weighted, weighted * m]
-            terms = new if terms is None else [x + y for x, y in zip(terms, new)]
-        for k in range(3):
-            sums[k * lines + j] = jnp.sum(terms[k], axis=0, keepdims=True)
+                tile = continuum_ref[lax.shift_right_logical(starts_ref[j, g * SUB + r], 6), rows, :]
+                block = tile if block is None else jnp.where(at_row[r], tile, block)
+            picks.append(block)
+        m = twice - centre[j : j + 1]
+        masked = jnp.where(jnp.abs(m) < span[j : j + 1], jnp.concatenate(picks, axis=0).T, 0.0)
+        weighted = masked * m
+        for k, term in enumerate((masked, weighted, weighted * m)):
+            sums[k * lines + j] = jnp.sum(term, axis=0, keepdims=True)
     continuum_sums = jnp.concatenate(sums, axis=0)
 
     own_rows = slice(half, half + 3 * lines)
@@ -561,17 +586,16 @@
     lines = begin.shape[0]
     return pl.pallas_call(
         functools.partial(owner_kernel, chunk=chunk),
-        in_specs=[pl.BlockSpec(memory_space=pltpu.SMEM)] + [hbm] * 4 + [vmem] * 6 + [hbm] * 2,
+        in_specs=[pl.BlockSpec(memory_space=pltpu.SMEM)] + [vmem] + [hbm] * 3 + [vmem] * 8 + [hbm] * 2,
         out_shape=(
             jax.ShapeDtypeStruct((own_slots, count), F32),
             jax.ShapeDtypeStruct((3 * lines, own), F32),
         ),
         scratch_shapes=[
-            pltpu.VMEM((full_width // LANES + 1, own, LANES), F32),
+            pltpu.VMEM((2 * (full_width // LANES), own, LANES), F32),
             pltpu.VMEM((own_slots, count), F32),
             pltpu.VMEM((count, full_width), BF16),
             pltpu.VMEM((count, full_width), BF16),
-            pltpu.VMEM((1, own), jnp.int32),
             pltpu.SMEM(owner.shape, jnp.int32),
             pltpu.VMEM((lines, own), jnp.int32),
             pltpu.VMEM((lines, own), jnp.int32),
@@ -603,8 +627,10 @@
     def swap(x, bit):
         return lax.ppermute(x, "spax", [(d, d ^ (1 << bit)) for d in range(devices)])
 
-    keep, send, begins, spans, held = project(here, bins, begin, span, columns, pin(templates), total_bins)
-    windows = lambda start, stop, now: cube_windows(now, begins, spans, held, devices, start, stop)
+    keep, send, begins, spans, held, bins_held = project(here, bins, begin, span, columns, pin(templates), total_bins)
+    windows = lambda start, stop, now: cube_windows(
+        now, begins, spans, held, devices, start, stop, cube.shape[1]
+    )
     arrived = swap(send, 0)
     left = devices // 2
     cut = left + devices * 3 // 16
@@ -613,8 +639,8 @@
     keep, send = split_slots(here, keep, arrived)
     keep, send, now = after((keep, send, here))
     arrived = swap(send, 1)
-    late = windows(cut, devices, now)
-    keep, arrived, early, late, templates = after((keep, arrived, early, late, templates))
+    late, next_sums = windows(cut, devices, now), windows(left // 2, left, now)
+    keep, arrived, early, late, next_sums, templates = after((keep, arrived, early, late, next_sums, templates))
     slots = total_bins // 2
     message = rows_of(slots + left * 3 * lines)
     keep, send = in_vmem(join_kernel, (rows_of(slots), message), "join", keep, arrived, early, late)
@@ -625,7 +651,7 @@
         arrived = swap(send, bit)
         left //= 2
         last_step = bit == devices.bit_length() - 2
-        sums = windows(0 if last_step else left, 2 * left, now)
+        sums = next_sums if gram is None else windows(0 if last_step else left, 2 * left, now)
         if gram is None:
             gram, scale, *parts = scaled_gram(pin(templates), 512)
             arrived, sums, gram = after((arrived, sums, gram))
@@ -646,9 +672,11 @@
     inverse = in_vmem(finish_kernel, jax.ShapeDtypeStruct((count, count), F32), "finish", *first, scale)
     by_x, by_core, inverse = after((by_x, by_core, inverse))
     by_both = swap(by_x, 0)
-    messages = (keep, by_x, by_core, by_both)
+    near, far = pick_early(here, bins_held, keep, by_x, by_core, own_spaxels, slots)
+    by_both, near, far = after((by_both, near, far))
+    messages = (keep, by_x, by_core, by_both, near, far)
     parts = [parts[0], pin(parts[1]), pin(parts[2])]
-    return owned(here, bins, owner, begin, span, messages, inverse, parts, own_slots, own_spaxels, 512)
+    return owned(here, bins_held, owner, begin, span, messages, inverse, parts, own_slots, own_spaxels, 512)
 
 
 def solution(mesh):

time: 46.1 us -> 45.5 us (0.987)
  waiting for transfers between devices: 3.7 us -> 2.01 us
  Pallas kernels: 31.6 us -> 32.4 us
    ppermute x7, waiting for transfers between devices: 3.7 us -> 2.01 us  [swap(): return lax.ppermute(x, 'spax', [(d, d ^ 1 << bit) for d in range(devices)])]
    pallas_call x0 -> x1, Pallas kernels: none -> 0.48 us  [pick_early(): pl.pallas_call(functools.partial(pick_kernel, half=half), in_specs=[pl.Bl...]
  transfers between devices with their start and end apart: 7 -> 7, of which waited for: 4 -> 4; matrix products, arithmetic and copies ran while one was open for 0% -> 0% of each run, Pallas kernels for 44% -> 46%
where the time goes in v11:
time: 45.5 us; the launch traced here: 45.3 us
  Pallas kernels  32.4 us (71%)
  starting transfers between devices  10.1 us (22%)
  waiting for transfers between devices  2.01 us (4%)
  between operations  0.9 us (2%)
    pallas_call x5, Pallas kernels, in_vmem(): pl.pallas_call(kernel, out_shape=shapes, compiler_params=pltpu.CompilerPa...  10.1 us
    ppermute x7, starting transfers between devices, swap(): return lax.ppermute(x, 'spax', [(d, d ^ 1 << bit) for d in range(devices)])  10.1 us
    pallas_call x1, Pallas kernels, project(): pl.pallas_call(functools.partial(project_kernel, chunk=chunk), in_specs=[...  6.05 us
    pallas_call x4, Pallas kernels, cube_windows(): pl.pallas_call(functools.partial(cube_kernel, devices=devices, start=star...  5.97 us
    pallas_call x1, Pallas kernels, owned(): pl.pallas_call(functools.partial(owner_kernel, chunk=chunk), in_specs=[pl...  5.34 us
    pallas_call x1, Pallas kernels, scaled_gram(): pl.pallas_call(functools.partial(gram_kernel, chunk=chunk), in_specs=[hbm...  4.43 us
    ppermute x7, waiting for transfers between devices, swap(): return lax.ppermute(x, 'spax', [(d, d ^ 1 << bit) for d in range(devices)])  2.01 us
  transfers between devices with their start and end apart: 7, of which 4 were waited for; matrix products, arithmetic and copies ran while one was open for 0% of the time, Pallas kernels for 46%

profile of v11, /device:TPU:0, one launch (start us, length us, event | category | flops | bytes accessed | tf_op | source)
XLA Modules:
  0.0 45.3 jit_solution(8470136771437807192)
XLA Ops:
  0.6 6.0 %project.1 = (f32[512,128]{1,0:T(8,128)S(1)}, f32[512,128]{1,0:T(8,128)S(1)}, s32[8,2048]{1,0:T(8,128)S(1)}, s32[8,2048]{1,0:T(8,128)S(1)}, f32[240,2048]{1,0:T(8,128)S(1)}, /*index=5*/s32[1,2048]{1,0:T(1,128)S(1)}) custom-call(s32[1]{0:T(128)} %bitcast.device_ref, s32[1,2048]{1,0:T(1,128)} %bitcast.5, s32[8,2048]{1,0:T(8,128)} %begin_ref.3, ...), custom_call_target="tpu_custom_call" | custom-call | tf_op jit(solution)/shard_map/project/pallas_call | solution.py:115
  6.7 0.5 %collective-permute-start = (f32[512,128]{1,0:T(8,128)S(1)}, f32[512,128]{1,0:T(8,128)S(1)}, u32[]{:S(2)}, u32[]{:S(2)}) collective-permute-start(f32[512,128]{1,0:T(8,128)S(1)} %get-tuple-element.66), channel_id=1, source_target_pairs={{0,1},{1,0},{2,3},{3,2},{4,5},{5,4},{6,7},{7,6},{8,9},{9,8},{10,11... | collective-permute-start | bytes 786440 | tf_op jit(solution)/shard_map/ppermute | solution.py:628
  7.2 1.1 %cube_windows.4.early_ref = f32[72,128]{1,0:T(8,128)S(1)} custom-call(s32[1]{0:T(128)} %bitcast.device_ref, s32[8,2048]{1,0:T(8,128)S(1)} %get-tuple-element.67.begin_ref, s32[8,2048]{1,0:T(8,128)S(1)} %get-tuple-element.68.span_ref, f32[240,2048]{1,0:T(8,128)S(1)} %get-tuple-element.69.cube_ref), custom_call_target="tpu_custom_call" | custom-call | tf_op jit(solution)/shard_map/cube_windows/pallas_call | solution.py:373
  8.3 0.1 collective-permute-done.y_ref
  8.4 2.9 %collective-permute-start.1 = (f32[256,128]{1,0:T(8,128)S(1)}, f32[256,128]{1,0:T(8,128)S(1)}, u32[]{:S(2)}, u32[]{:S(2)}) collective-permute-start(f32[256,128]{1,0:T(8,128)S(1)} %get-tuple-element.75), channel_id=1, source_target_pairs={{0,2},{1,3},{2,0},{3,1},{4,6},{5,7},{6,4},{7,5},{8,10},{9,11},{10,... | collective-permute-start | bytes 393224 | tf_op jit(solution)/shard_map/ppermute | solution.py:628
  11.3 1.4 %cube_windows.6.sums_ref = f32[96,128]{1,0:T(8,128)S(1)} custom-call(s32[1]{0:T(128)} %bitcast.device_ref, s32[8,2048]{1,0:T(8,128)S(1)} %get-tuple-element.67.begin_ref, s32[8,2048]{1,0:T(8,128)S(1)} %get-tuple-element.68.span_ref, f32[240,2048]{1,0:T(8,128)S(1)} %get-tuple-element.69.cube_ref), custom_call_target="tpu_custom_call" | custom-call | tf_op jit(solution)/shard_map/cube_windows/pallas_call | solution.py:373
  12.8 1.8 %cube_windows.5.late_ref = f32[120,128]{1,0:T(8,128)S(1)} custom-call(s32[1]{0:T(128)} %bitcast.device_ref, s32[8,2048]{1,0:T(8,128)S(1)} %get-tuple-element.67.begin_ref, s32[8,2048]{1,0:T(8,128)S(1)} %get-tuple-element.68.span_ref, f32[240,2048]{1,0:T(8,128)S(1)} %get-tuple-element.69.cube_ref), custom_call_target="tpu_custom_call" | custom-call | tf_op jit(solution)/shard_map/cube_windows/pallas_call | solution.py:373
  14.6 0.5 %collective-permute-done.1.y_ref = f32[256,128]{1,0:T(8,128)S(1)} collective-permute-done((f32[256,128]{1,0:T(8,128)S(1)}, f32[256,128]{1,0:T(8,128)S(1)}, u32[]{:S(2)}, u32[]{:S(2)}) %collective-permute-start.1) | collective-permute-done | bytes 131104 | tf_op jit(solution)/shard_map/ppermute | solution.py:628
  15.2 1.9 %collective-permute-start.2 = (f32[448,128]{1,0:T(8,128)S(1)}, f32[448,128]{1,0:T(8,128)S(1)}, u32[]{:S(2)}, u32[]{:S(2)}) collective-permute-start(f32[448,128]{1,0:T(8,128)S(1)} %get-tuple-element.86), channel_id=1, source_target_pairs={{0,4},{1,5},{2,6},{3,7},{4,0},{5,1},{6,2},{7,3},{8,12},{9,13},{10,... | collective-permute-start | bytes 688136 | tf_op jit(solution)/shard_map/ppermute | solution.py:628
  17.0 4.4 %gram.1 = (f32[256,256]{1,0:T(8,128)S(1)}, f32[1,256]{1,0:T(1,128)S(1)}, bf16[256,3584]{1,0:T(8,128)(2,1)S(1)}, bf16[256,3584]{1,0:T(8,128)(2,1)}, bf16[256,3584]{1,0:T(8,128)(2,1)}) custom-call(f32[256,3584]{1,0:T(8,128)} %templates_ref.2), custom_call_target="tpu_custom_call" | custom-call | tf_op jit(solution)/shard_map/gram/pallas_call | solution.py:251
  21.5 0.9 %collective-permute-done.2.y_ref = f32[448,128]{1,0:T(8,128)S(1)} collective-permute-done((f32[448,128]{1,0:T(8,128)S(1)}, f32[448,128]{1,0:T(8,128)S(1)}, u32[]{:S(2)}, u32[]{:S(2)}) %collective-permute-start.2) | collective-permute-done | bytes 229408 | tf_op jit(solution)/shard_map/ppermute | solution.py:628
  22.4 2.6 %collective-permute-start.3 = (f32[352,128]{1,0:T(8,128)S(1)}, f32[352,128]{1,0:T(8,128)S(1)}, u32[]{:S(2)}, u32[]{:S(2)}) collective-permute-start(f32[352,128]{1,0:T(8,128)S(1)} %get-tuple-element.96), channel_id=1, source_target_pairs={{0,8},{1,9},{2,10},{3,11},{4,12},{5,13},{6,14},{7,15},{8,0},{9,1},... | collective-permute-start | bytes 540680 | tf_op jit(solution)/shard_map/ppermute | solution.py:628
  25.0 1.6 %cube_windows.7.sums_ref = f32[96,128]{1,0:T(8,128)S(1)} custom-call(s32[1]{0:T(128)} %bitcast.device_ref, s32[8,2048]{1,0:T(8,128)S(1)} %get-tuple-element.67.begin_ref, s32[8,2048]{1,0:T(8,128)S(1)} %get-tuple-element.68.span_ref, f32[240,2048]{1,0:T(8,128)S(1)} %get-tuple-element.69.cube_ref), custom_call_target="tpu_custom_call" | custom-call | tf_op jit(solution)/shard_map/cube_windows/pallas_call | solution.py:373
  26.6 6.0 %first.1 = (f32[128,128]{1,0:T(8,128)S(1)}, f32[128,128]{1,0:T(8,128)S(1)}, f32[128,128]{1,0:T(8,128)S(1)}) custom-call(f32[256,256]{1,0:T(8,128)S(1)} %get-tuple-element.98.gram_ref), custom_call_target="tpu_custom_call" | custom-call | tf_op jit(solution)/shard_map/first/pallas_call | solution.py:301
  32.6 0.0 collective-permute-done.3.y_ref
  32.6 1.6 %collective-permute-start.4 = (f32[304,128]{1,0:T(8,128)S(1)}, f32[304,128]{1,0:T(8,128)S(1)}, u32[]{:S(2)}, u32[]{:S(2)}) collective-permute-start(f32[304,128]{1,0:T(8,128)S(1)} %get-tuple-element.110), channel_id=1, source_target_pairs={{0,2},{1,3},{2,0},{3,1},{4,6},{5,7},{6,4},{7,5},{8,10},{9,11},{10,... | collective-permute-start | bytes 466952 | tf_op jit(solution)/shard_map/ppermute | solution.py:628
  34.2 0.0 collective-permute-start.5
  34.2 4.0 %finish.1.inverse_ref = f32[256,256]{1,0:T(8,128)S(1)} custom-call(f32[128,128]{1,0:T(8,128)S(1)} %get-tuple-element.111.first_ref, f32[128,128]{1,0:T(8,128)S(1)} %get-tuple-element.112.half_ref, f32[128,128]{1,0:T(8,128)S(1)} %get-tuple-element.113.second_ref, f32[1,256]{1,0:T(1,128)S(1)} %get-tuple-element.114.scale_ref), custom_call_target="tpu_custom_call" | custom-call | tf_op jit(solution)/shard_map/finish/pallas_call | solution.py:301
  38.2 0.0 collective-permute-done.4.by_x_ref
  38.2 0.0 collective-permute-done.5.by_core_ref
  38.2 0.6 %collective-permute-start.6 = (f32[304,128]{1,0:T(8,128)S(1)}, f32[304,128]{1,0:T(8,128)S(1)}, u32[]{:S(2)}, u32[]{:S(2)}) collective-permute-start(f32[304,128]{1,0:T(8,128)S(1)} %collective-permute-done.4.by_x_ref), channel_id=1, source_target_pairs={{0,1},{1,0},{2,3},{3,2},{4,5},{5,4},{6,7},{7,6},{8,9},{9,8},{10,11... | collective-permute-start | bytes 466952 | tf_op jit(solution)/shard_map/ppermute | solution.py:628
  38.8 0.5 %pick_early.1 = (f32[128,128]{1,0:T(8,128)S(1)}, f32[128,128]{1,0:T(8,128)S(1)}) custom-call(s32[1]{0:T(128)} %bitcast.device_ref, s32[1,2048]{1,0:T(1,128)S(1)} %get-tuple-element.64.bins_ref, f32[304,128]{1,0:T(8,128)S(1)} %get-tuple-element.109.kept_ref, f32[304,128]{1,0:T(8,128)S(1)} %collective-permute-done.4.by_x_ref, ...), custom_call_target="tpu_custom_call" | custom-call | tf_op jit(solution)/shard_map/pick_early/pallas_call | solution.py:459
  39.3 0.5 %collective-permute-done.6.by_both_ref = f32[304,128]{1,0:T(8,128)S(1)} collective-permute-done((f32[304,128]{1,0:T(8,128)S(1)}, f32[304,128]{1,0:T(8,128)S(1)}, u32[]{:S(2)}, u32[]{:S(2)}) %collective-permute-start.6) | collective-permute-done | bytes 155680 | tf_op jit(solution)/shard_map/ppermute | solution.py:628
  39.8 5.3 %owned.1 = (f32[32,256]{1,0:T(8,128)}, f32[24,128]{1,0:T(8,128)}) custom-call(s32[1]{0:T(128)} %bitcast.device_ref, s32[1,2048]{1,0:T(1,128)S(1)} %get-tuple-element.64.bins_ref, s32[1,512]{1,0:T(1,128)} %bitcast.6, s32[8,2048]{1,0:T(8,128)} %begin_ref.3, s32[8,2048]{1,0:T(8,128)} %span_ref.3, f32[304,128]{1,0:T(8,128)S(1)} %get-tuple-element.109.kept_ref, ...), custom_call_target="tpu_custom_call" | custom-call | tf_op jit(solution)/shard_map/owned/pallas_call | solution.py:587
  (4 shorter events, 0.1 us)
Async XLA Ops:
  6.7 1.7 %collective-permute-start = (f32[512,128]{1,0:T(8,128)S(1)}, f32[512,128]{1,0:T(8,128)S(1)}, u32[]{:S(2)}, u32[]{:S(2)}) collective-permute-start(f32[512,128]{1,0:T(8,128)S(1)} %get-tuple-element.66), channel_id=1, source_target_pairs={{0,1},{1,0},{2,3},{3,2},{4,5},{5,4},{6,7},{7,6},{8,9},{9,8},{10,11... | collective-permute-start | bytes 786440 | tf_op jit(solution)/shard_map/ppermute | solution.py:628
  8.4 6.7 %collective-permute-start.1 = (f32[256,128]{1,0:T(8,128)S(1)}, f32[256,128]{1,0:T(8,128)S(1)}, u32[]{:S(2)}, u32[]{:S(2)}) collective-permute-start(f32[256,128]{1,0:T(8,128)S(1)} %get-tuple-element.75), channel_id=1, source_target_pairs={{0,2},{1,3},{2,0},{3,1},{4,6},{5,7},{6,4},{7,5},{8,10},{9,11},{10,... | collective-permute-start | bytes 393224 | tf_op jit(solution)/shard_map/ppermute | solution.py:628
  15.2 7.2 %collective-permute-start.2 = (f32[448,128]{1,0:T(8,128)S(1)}, f32[448,128]{1,0:T(8,128)S(1)}, u32[]{:S(2)}, u32[]{:S(2)}) collective-permute-start(f32[448,128]{1,0:T(8,128)S(1)} %get-tuple-element.86), channel_id=1, source_target_pairs={{0,4},{1,5},{2,6},{3,7},{4,0},{5,1},{6,2},{7,3},{8,12},{9,13},{10,... | collective-permute-start | bytes 688136 | tf_op jit(solution)/shard_map/ppermute | solution.py:628
  22.4 10.2 %collective-permute-start.3 = (f32[352,128]{1,0:T(8,128)S(1)}, f32[352,128]{1,0:T(8,128)S(1)}, u32[]{:S(2)}, u32[]{:S(2)}) collective-permute-start(f32[352,128]{1,0:T(8,128)S(1)} %get-tuple-element.96), channel_id=1, source_target_pairs={{0,8},{1,9},{2,10},{3,11},{4,12},{5,13},{6,14},{7,15},{8,0},{9,1},... | collective-permute-start | bytes 540680 | tf_op jit(solution)/shard_map/ppermute | solution.py:628
  32.6 5.6 %collective-permute-start.4 = (f32[304,128]{1,0:T(8,128)S(1)}, f32[304,128]{1,0:T(8,128)S(1)}, u32[]{:S(2)}, u32[]{:S(2)}) collective-permute-start(f32[304,128]{1,0:T(8,128)S(1)} %get-tuple-element.110), channel_id=1, source_target_pairs={{0,2},{1,3},{2,0},{3,1},{4,6},{5,7},{6,4},{7,5},{8,10},{9,11},{10,... | collective-permute-start | bytes 466952 | tf_op jit(solution)/shard_map/ppermute | solution.py:628
  34.2 4.1 %collective-permute-start.5 = (f32[304,128]{1,0:T(8,128)S(1)}, f32[304,128]{1,0:T(8,128)S(1)}, u32[]{:S(2)}, u32[]{:S(2)}) collective-permute-start(f32[304,128]{1,0:T(8,128)S(1)} %get-tuple-element.109.kept_ref), channel_id=1, source_target_pairs={{0,1},{1,0},{2,3},{3,2},{4,5},{5,4},{6,7},{7,6},{8,9},{9,8},{10,11... | collective-permute-start | bytes 466952 | tf_op jit(solution)/shard_map/ppermute | solution.py:628
  38.2 1.6 %collective-permute-start.6 = (f32[304,128]{1,0:T(8,128)S(1)}, f32[304,128]{1,0:T(8,128)S(1)}, u32[]{:S(2)}, u32[]{:S(2)}) collective-permute-start(f32[304,128]{1,0:T(8,128)S(1)} %collective-permute-done.4.by_x_ref), channel_id=1, source_target_pairs={{0,1},{1,0},{2,3},{3,2},{4,5},{5,4},{6,7},{7,6},{8,9},{9,8},{10,11... | collective-permute-start | bytes 466952 | tf_op jit(solution)/shard_map/ppermute | solution.py:628

commit v12 on v11

--- a/solution.py
+++ b/solution.py
@@ -41,7 +41,7 @@
 def project_kernel(
     device_ref, bins_ref, begin_ref, span_ref, cube_ref, templates_ref,
     keep_ref, send_ref, begins_ref, spans_ref, held_ref,
-    bins_held_ref, sums_ref, window_ref, firsts_ref, cube_sem, small_sem, *, chunk,
+    bins_held_ref, sums_ref, parts_ref, window_ref, firsts_ref, cube_sem, small_sem, *, chunk,
 ):
     width, spaxels = cube_ref.shape
     total_bins = keep_ref.shape[0]
@@ -51,9 +51,10 @@
     base = pl.multiple_of(jnp.minimum(first // LANES * LANES, full_width - window), LANES)
     chunks = spaxels // chunk
     reach = chunk + SUB
+    pieces = cube_sem.shape[0]
 
     def cube_copy(i):
-        lanes = pl.ds(i * chunk, chunk)
+        lanes = pl.ds(i * (spaxels // pieces), spaxels // pieces)
         return pltpu.make_async_copy(cube_ref.at[:, lanes], held_ref.at[pl.ds(0, width), lanes], cube_sem.at[i])
 
     bins_copy = pltpu.make_async_copy(bins_ref, bins_held_ref, small_sem.at[0])
@@ -63,7 +64,7 @@
         pltpu.make_async_copy(begin_ref, begins_ref, small_sem.at[3]),
         pltpu.make_async_copy(span_ref, spans_ref, small_sem.at[4]),
     ]
-    for copy in [bins_copy, firsts_copy, window_copy] + [cube_copy(i) for i in range(chunks)] + line_copies:
+    for copy in [bins_copy, firsts_copy] + [cube_copy(i) for i in range(pieces)] + [window_copy] + line_copies:
         copy.start()
     sums_ref[...] = jnp.zeros(sums_ref.shape, F32)
     joined = held_ref.shape[0] > width
@@ -73,23 +74,27 @@
     rows_at = lax.broadcasted_iota(jnp.int32, (reach, chunk), 0)
     bins_copy.wait()
     firsts_copy.wait()
-    window_copy.wait()
-    mine = pltpu.roll(window_ref[...], window - (first - base), 1)[:, :width]
+
+    def low_bin(i):
+        return pl.multiple_of(firsts_ref[0, i * chunk] // SUB * SUB, SUB)
 
     for i in range(chunks):
+        if i % (chunks // pieces) == 0:
+            cube_copy(i // (chunks // pieces)).wait()
         lanes = slice(i * chunk, (i + 1) * chunk)
-        low_bin = pl.multiple_of(firsts_ref[0, i * chunk] // SUB * SUB, SUB)
-        rows = pl.ds(low_bin, reach)
-        member = jnp.where(rows_at == bins_held_ref[:, lanes] - low_bin, 1.0, 0.0).astype(BF16)
-        cube_copy(i).wait()
+        member = jnp.where(rows_at == bins_held_ref[:, lanes] - low_bin(i), 1.0, 0.0).astype(BF16)
         hi, mid, low = split3(held_ref[:, lanes])
         new = dot(member, hi, NT) + (dot(member, mid, NT) + dot(member, low, NT))
         if joined:
-            sums_ref[rows, :] += new
+            parts_ref[i] = new
         else:
-            sums_ref[rows, :width] += new
-            sums_ref[rows, counted:] += dot(member, jnp.ones((COUNT_ROWS, chunk), BF16), NT)
-
+            parts_ref[i] = jnp.zeros(parts_ref.shape[1:], F32)
+            parts_ref[i, :, :width] = new
+            parts_ref[i, :, counted:] = dot(member, jnp.ones((COUNT_ROWS, chunk), BF16), NT)
+    for i in range(chunks):
+        sums_ref[pl.ds(low_bin(i), reach), :] += parts_ref[i]
+    window_copy.wait()
+    mine = pltpu.roll(window_ref[...], window - (first - base), 1)[:, :width]
     low_kept = device_ref[0] % 2 == 0
     block = min(total_bins, 512)
     for at in range(0, total_bins, block):
@@ -126,9 +131,10 @@
         ],
         scratch_shapes=[
             pltpu.VMEM((total_bins + chunk + SUB, wide), F32),
+            pltpu.VMEM((spaxels // chunk, chunk + SUB, wide), F32),
             pltpu.VMEM((count, template_window(width, full_width)), F32),
             pltpu.SMEM(bins.shape, jnp.int32),
-            pltpu.SemaphoreType.DMA((spaxels // chunk,)),
+            pltpu.SemaphoreType.DMA((min(spaxels // chunk, 2),)),
             pltpu.SemaphoreType.DMA((5,)),
         ],
         compiler_params=pltpu.CompilerParams(vmem_limit_bytes=VMEM_LIMIT),
@@ -487,11 +493,15 @@
         pltpu.make_async_copy(span_ref.at[:, own_lanes], spans_ref, small_sem.at[3]),
         pltpu.make_async_copy(begin_ref.at[:, own_lanes], starts_ref, small_sem.at[4]),
     ]
-    part_copies = [
-        pltpu.make_async_copy(mid_ref, mid_held_ref, parts_sem.at[0]),
-        pltpu.make_async_copy(low_ref, low_held_ref, parts_sem.at[1]),
-    ]
-    for copy in small_copies + part_copies:
+
+    def part_copies(i):
+        lanes = pl.ds(i * chunk, chunk)
+        return [
+            pltpu.make_async_copy(mid_ref.at[:, lanes], mid_held_ref.at[:, lanes], parts_sem.at[0, i]),
+            pltpu.make_async_copy(low_ref.at[:, lanes], low_held_ref.at[:, lanes], parts_sem.at[1, i]),
+        ]
+
+    for copy in small_copies + [copy for i in range(full_width // chunk) for copy in part_copies(i)]:
         copy.start()
 
     core_low = device % 2 == 0
@@ -529,11 +539,11 @@
         value = dot(hi, first, NN) + (dot(mid, first, NN) + dot(low, first, NN))
         for t in range(tiles):
             continuum_ref[2 * (i * tiles + t)] = value[:, t * LANES : (t + 1) * LANES]
-    for copy in part_copies:
-        copy.wait()
     left_half = lax.broadcasted_iota(jnp.int32, (own, LANES), 1) < LANES // 2
     before = None
     for i in range(full_width // chunk):
+        for copy in part_copies(i):
+            copy.wait()
         lanes = slice(i * chunk, (i + 1) * chunk)
         second, third = mid_held_ref[:, lanes], low_held_ref[:, lanes]
         value = dot(hi, second, NN) + (dot(mid, second, NN) + dot(hi, third, NN))
@@ -600,7 +610,7 @@
             pltpu.VMEM((lines, own), jnp.int32),
             pltpu.VMEM((lines, own), jnp.int32),
             pltpu.SMEM((lines, own), jnp.int32),
-            pltpu.SemaphoreType.DMA((2,)),
+            pltpu.SemaphoreType.DMA((2, full_width // chunk)),
             pltpu.SemaphoreType.DMA((5,)),
         ],
         compiler_params=pltpu.CompilerParams(vmem_limit_bytes=VMEM_LIMIT),

time: 45.5 us -> 45.9 us (level)
    pallas_call x1, Pallas kernels: 5.34 us -> 8.17 us  [owned(): pl.pallas_call(functools.partial(owner_kernel, chunk=chunk), in_specs=[pl...]
    pallas_call x1, Pallas kernels: 6.05 us -> 3.59 us  [project(): pl.pallas_call(functools.partial(project_kernel, chunk=chunk), in_specs=[...]
where the time goes in v12:
time: 45.9 us; the launch traced here: 45.7 us
  Pallas kernels  32.7 us (71%)
  starting transfers between devices  10.1 us (22%)
  waiting for transfers between devices  2 us (4%)
  between operations  0.9 us (2%)
    pallas_call x5, Pallas kernels, in_vmem(): pl.pallas_call(kernel, out_shape=shapes, compiler_params=pltpu.CompilerPa...  10.1 us
    ppermute x7, starting transfers between devices, swap(): return lax.ppermute(x, 'spax', [(d, d ^ 1 << bit) for d in range(devices)])  10.1 us
    pallas_call x1, Pallas kernels, owned(): pl.pallas_call(functools.partial(owner_kernel, chunk=chunk), in_specs=[pl...  8.17 us
    pallas_call x4, Pallas kernels, cube_windows(): pl.pallas_call(functools.partial(cube_kernel, devices=devices, start=star...  5.97 us
    pallas_call x1, Pallas kernels, scaled_gram(): pl.pallas_call(functools.partial(gram_kernel, chunk=chunk), in_specs=[hbm...  4.44 us
    pallas_call x1, Pallas kernels, project(): pl.pallas_call(functools.partial(project_kernel, chunk=chunk), in_specs=[...  3.59 us
    ppermute x7, waiting for transfers between devices, swap(): return lax.ppermute(x, 'spax', [(d, d ^ 1 << bit) for d in range(devices)])  2 us
  transfers between devices with their start and end apart: 7, of which 4 were waited for; matrix products, arithmetic and copies ran while one was open for 0% of the time, Pallas kernels for 46%

profile of v12, /device:TPU:0, one launch (start us, length us, event | category | flops | bytes accessed | tf_op | source)
XLA Modules:
  0.0 45.7 jit_solution(1965787723685808403)
XLA Ops:
  0.6 3.6 %project.1 = (f32[512,128]{1,0:T(8,128)S(1)}, f32[512,128]{1,0:T(8,128)S(1)}, s32[8,2048]{1,0:T(8,128)S(1)}, s32[8,2048]{1,0:T(8,128)S(1)}, f32[240,2048]{1,0:T(8,128)S(1)}, /*index=5*/s32[1,2048]{1,0:T(1,128)S(1)}) custom-call(s32[1]{0:T(128)} %bitcast.device_ref, s32[1,2048]{1,0:T(1,128)} %bitcast.5, s32[8,2048]{1,0:T(8,128)} %begin_ref.3, ...), custom_call_target="tpu_custom_call" | custom-call | tf_op jit(solution)/shard_map/project/pallas_call | solution.py:120
  4.2 0.5 %collective-permute-start = (f32[512,128]{1,0:T(8,128)S(1)}, f32[512,128]{1,0:T(8,128)S(1)}, u32[]{:S(2)}, u32[]{:S(2)}) collective-permute-start(f32[512,128]{1,0:T(8,128)S(1)} %get-tuple-element.66), channel_id=1, source_target_pairs={{0,1},{1,0},{2,3},{3,2},{4,5},{5,4},{6,7},{7,6},{8,9},{9,8},{10,11... | collective-permute-start | bytes 786440 | tf_op jit(solution)/shard_map/ppermute | solution.py:638
  4.8 1.1 %cube_windows.4.early_ref = f32[72,128]{1,0:T(8,128)S(1)} custom-call(s32[1]{0:T(128)} %bitcast.device_ref, s32[8,2048]{1,0:T(8,128)S(1)} %get-tuple-element.67.begin_ref, s32[8,2048]{1,0:T(8,128)S(1)} %get-tuple-element.68.span_ref, f32[240,2048]{1,0:T(8,128)S(1)} %get-tuple-element.69.cube_ref), custom_call_target="tpu_custom_call" | custom-call | tf_op jit(solution)/shard_map/cube_windows/pallas_call | solution.py:379
  5.8 0.1 collective-permute-done.y_ref
  5.9 2.9 %collective-permute-start.1 = (f32[256,128]{1,0:T(8,128)S(1)}, f32[256,128]{1,0:T(8,128)S(1)}, u32[]{:S(2)}, u32[]{:S(2)}) collective-permute-start(f32[256,128]{1,0:T(8,128)S(1)} %get-tuple-element.75), channel_id=1, source_target_pairs={{0,2},{1,3},{2,0},{3,1},{4,6},{5,7},{6,4},{7,5},{8,10},{9,11},{10,... | collective-permute-start | bytes 393224 | tf_op jit(solution)/shard_map/ppermute | solution.py:638
  8.9 1.4 %cube_windows.6.sums_ref = f32[96,128]{1,0:T(8,128)S(1)} custom-call(s32[1]{0:T(128)} %bitcast.device_ref, s32[8,2048]{1,0:T(8,128)S(1)} %get-tuple-element.67.begin_ref, s32[8,2048]{1,0:T(8,128)S(1)} %get-tuple-element.68.span_ref, f32[240,2048]{1,0:T(8,128)S(1)} %get-tuple-element.69.cube_ref), custom_call_target="tpu_custom_call" | custom-call | tf_op jit(solution)/shard_map/cube_windows/pallas_call | solution.py:379
  10.3 1.8 %cube_windows.5.late_ref = f32[120,128]{1,0:T(8,128)S(1)} custom-call(s32[1]{0:T(128)} %bitcast.device_ref, s32[8,2048]{1,0:T(8,128)S(1)} %get-tuple-element.67.begin_ref, s32[8,2048]{1,0:T(8,128)S(1)} %get-tuple-element.68.span_ref, f32[240,2048]{1,0:T(8,128)S(1)} %get-tuple-element.69.cube_ref), custom_call_target="tpu_custom_call" | custom-call | tf_op jit(solution)/shard_map/cube_windows/pallas_call | solution.py:379
  12.2 0.5 %collective-permute-done.1.y_ref = f32[256,128]{1,0:T(8,128)S(1)} collective-permute-done((f32[256,128]{1,0:T(8,128)S(1)}, f32[256,128]{1,0:T(8,128)S(1)}, u32[]{:S(2)}, u32[]{:S(2)}) %collective-permute-start.1) | collective-permute-done | bytes 131104 | tf_op jit(solution)/shard_map/ppermute | solution.py:638
  12.7 1.9 %collective-permute-start.2 = (f32[448,128]{1,0:T(8,128)S(1)}, f32[448,128]{1,0:T(8,128)S(1)}, u32[]{:S(2)}, u32[]{:S(2)}) collective-permute-start(f32[448,128]{1,0:T(8,128)S(1)} %get-tuple-element.86), channel_id=1, source_target_pairs={{0,4},{1,5},{2,6},{3,7},{4,0},{5,1},{6,2},{7,3},{8,12},{9,13},{10,... | collective-permute-start | bytes 688136 | tf_op jit(solution)/shard_map/ppermute | solution.py:638
  14.6 4.4 %gram.1 = (f32[256,256]{1,0:T(8,128)S(1)}, f32[1,256]{1,0:T(1,128)S(1)}, bf16[256,3584]{1,0:T(8,128)(2,1)S(1)}, bf16[256,3584]{1,0:T(8,128)(2,1)}, bf16[256,3584]{1,0:T(8,128)(2,1)}) custom-call(f32[256,3584]{1,0:T(8,128)} %templates_ref.2), custom_call_target="tpu_custom_call" | custom-call | tf_op jit(solution)/shard_map/gram/pallas_call | solution.py:257
  19.0 0.9 %collective-permute-done.2.y_ref = f32[448,128]{1,0:T(8,128)S(1)} collective-permute-done((f32[448,128]{1,0:T(8,128)S(1)}, f32[448,128]{1,0:T(8,128)S(1)}, u32[]{:S(2)}, u32[]{:S(2)}) %collective-permute-start.2) | collective-permute-done | bytes 229408 | tf_op jit(solution)/shard_map/ppermute | solution.py:638
  19.9 2.6 %collective-permute-start.3 = (f32[352,128]{1,0:T(8,128)S(1)}, f32[352,128]{1,0:T(8,128)S(1)}, u32[]{:S(2)}, u32[]{:S(2)}) collective-permute-start(f32[352,128]{1,0:T(8,128)S(1)} %get-tuple-element.96), channel_id=1, source_target_pairs={{0,8},{1,9},{2,10},{3,11},{4,12},{5,13},{6,14},{7,15},{8,0},{9,1},... | collective-permute-start | bytes 540680 | tf_op jit(solution)/shard_map/ppermute | solution.py:638
  22.5 1.6 %cube_windows.7.sums_ref = f32[96,128]{1,0:T(8,128)S(1)} custom-call(s32[1]{0:T(128)} %bitcast.device_ref, s32[8,2048]{1,0:T(8,128)S(1)} %get-tuple-element.67.begin_ref, s32[8,2048]{1,0:T(8,128)S(1)} %get-tuple-element.68.span_ref, f32[240,2048]{1,0:T(8,128)S(1)} %get-tuple-element.69.cube_ref), custom_call_target="tpu_custom_call" | custom-call | tf_op jit(solution)/shard_map/cube_windows/pallas_call | solution.py:379
  24.2 6.0 %first.1 = (f32[128,128]{1,0:T(8,128)S(1)}, f32[128,128]{1,0:T(8,128)S(1)}, f32[128,128]{1,0:T(8,128)S(1)}) custom-call(f32[256,256]{1,0:T(8,128)S(1)} %get-tuple-element.98.gram_ref), custom_call_target="tpu_custom_call" | custom-call | tf_op jit(solution)/shard_map/first/pallas_call | solution.py:307
  30.1 0.0 collective-permute-done.3.y_ref
  30.2 1.6 %collective-permute-start.4 = (f32[304,128]{1,0:T(8,128)S(1)}, f32[304,128]{1,0:T(8,128)S(1)}, u32[]{:S(2)}, u32[]{:S(2)}) collective-permute-start(f32[304,128]{1,0:T(8,128)S(1)} %get-tuple-element.110), channel_id=1, source_target_pairs={{0,2},{1,3},{2,0},{3,1},{4,6},{5,7},{6,4},{7,5},{8,10},{9,11},{10,... | collective-permute-start | bytes 466952 | tf_op jit(solution)/shard_map/ppermute | solution.py:638
  31.7 0.0 collective-permute-start.5
  31.7 4.0 %finish.1.inverse_ref = f32[256,256]{1,0:T(8,128)S(1)} custom-call(f32[128,128]{1,0:T(8,128)S(1)} %get-tuple-element.111.first_ref, f32[128,128]{1,0:T(8,128)S(1)} %get-tuple-element.112.half_ref, f32[128,128]{1,0:T(8,128)S(1)} %get-tuple-element.113.second_ref, f32[1,256]{1,0:T(1,128)S(1)} %get-tuple-element.114.scale_ref), custom_call_target="tpu_custom_call" | custom-call | tf_op jit(solution)/shard_map/finish/pallas_call | solution.py:307
  35.8 0.0 collective-permute-done.4.by_x_ref
  35.8 0.0 collective-permute-done.5.by_core_ref
  35.8 0.6 %collective-permute-start.6 = (f32[304,128]{1,0:T(8,128)S(1)}, f32[304,128]{1,0:T(8,128)S(1)}, u32[]{:S(2)}, u32[]{:S(2)}) collective-permute-start(f32[304,128]{1,0:T(8,128)S(1)} %collective-permute-done.4.by_x_ref), channel_id=1, source_target_pairs={{0,1},{1,0},{2,3},{3,2},{4,5},{5,4},{6,7},{7,6},{8,9},{9,8},{10,11... | collective-permute-start | bytes 466952 | tf_op jit(solution)/shard_map/ppermute | solution.py:638
  36.3 0.5 %pick_early.1 = (f32[128,128]{1,0:T(8,128)S(1)}, f32[128,128]{1,0:T(8,128)S(1)}) custom-call(s32[1]{0:T(128)} %bitcast.device_ref, s32[1,2048]{1,0:T(1,128)S(1)} %get-tuple-element.64.bins_ref, f32[304,128]{1,0:T(8,128)S(1)} %get-tuple-element.109.kept_ref, f32[304,128]{1,0:T(8,128)S(1)} %collective-permute-done.4.by_x_ref, ...), custom_call_target="tpu_custom_call" | custom-call | tf_op jit(solution)/shard_map/pick_early/pallas_call | solution.py:465
  36.8 0.5 %collective-permute-done.6.by_both_ref = f32[304,128]{1,0:T(8,128)S(1)} collective-permute-done((f32[304,128]{1,0:T(8,128)S(1)}, f32[304,128]{1,0:T(8,128)S(1)}, u32[]{:S(2)}, u32[]{:S(2)}) %collective-permute-start.6) | collective-permute-done | bytes 155680 | tf_op jit(solution)/shard_map/ppermute | solution.py:638
  37.4 8.2 %owned.1 = (f32[32,256]{1,0:T(8,128)}, f32[24,128]{1,0:T(8,128)}) custom-call(s32[1]{0:T(128)} %bitcast.device_ref, s32[1,2048]{1,0:T(1,128)S(1)} %get-tuple-element.64.bins_ref, s32[1,512]{1,0:T(1,128)} %bitcast.6, s32[8,2048]{1,0:T(8,128)} %begin_ref.3, s32[8,2048]{1,0:T(8,128)} %span_ref.3, f32[304,128]{1,0:T(8,128)S(1)} %get-tuple-element.109.kept_ref, ...), custom_call_target="tpu_custom_call" | custom-call | tf_op jit(solution)/shard_map/owned/pallas_call | solution.py:597
  (4 shorter events, 0.1 us)
Async XLA Ops:
  4.2 1.7 %collective-permute-start = (f32[512,128]{1,0:T(8,128)S(1)}, f32[512,128]{1,0:T(8,128)S(1)}, u32[]{:S(2)}, u32[]{:S(2)}) collective-permute-start(f32[512,128]{1,0:T(8,128)S(1)} %get-tuple-element.66), channel_id=1, source_target_pairs={{0,1},{1,0},{2,3},{3,2},{4,5},{5,4},{6,7},{7,6},{8,9},{9,8},{10,11... | collective-permute-start | bytes 786440 | tf_op jit(solution)/shard_map/ppermute | solution.py:638
  5.9 6.7 %collective-permute-start.1 = (f32[256,128]{1,0:T(8,128)S(1)}, f32[256,128]{1,0:T(8,128)S(1)}, u32[]{:S(2)}, u32[]{:S(2)}) collective-permute-start(f32[256,128]{1,0:T(8,128)S(1)} %get-tuple-element.75), channel_id=1, source_target_pairs={{0,2},{1,3},{2,0},{3,1},{4,6},{5,7},{6,4},{7,5},{8,10},{9,11},{10,... | collective-permute-start | bytes 393224 | tf_op jit(solution)/shard_map/ppermute | solution.py:638
  12.7 7.2 %collective-permute-start.2 = (f32[448,128]{1,0:T(8,128)S(1)}, f32[448,128]{1,0:T(8,128)S(1)}, u32[]{:S(2)}, u32[]{:S(2)}) collective-permute-start(f32[448,128]{1,0:T(8,128)S(1)} %get-tuple-element.86), channel_id=1, source_target_pairs={{0,4},{1,5},{2,6},{3,7},{4,0},{5,1},{6,2},{7,3},{8,12},{9,13},{10,... | collective-permute-start | bytes 688136 | tf_op jit(solution)/shard_map/ppermute | solution.py:638
  19.9 10.2 %collective-permute-start.3 = (f32[352,128]{1,0:T(8,128)S(1)}, f32[352,128]{1,0:T(8,128)S(1)}, u32[]{:S(2)}, u32[]{:S(2)}) collective-permute-start(f32[352,128]{1,0:T(8,128)S(1)} %get-tuple-element.96), channel_id=1, source_target_pairs={{0,8},{1,9},{2,10},{3,11},{4,12},{5,13},{6,14},{7,15},{8,0},{9,1},... | collective-permute-start | bytes 540680 | tf_op jit(solution)/shard_map/ppermute | solution.py:638
  30.2 5.6 %collective-permute-start.4 = (f32[304,128]{1,0:T(8,128)S(1)}, f32[304,128]{1,0:T(8,128)S(1)}, u32[]{:S(2)}, u32[]{:S(2)}) collective-permute-start(f32[304,128]{1,0:T(8,128)S(1)} %get-tuple-element.110), channel_id=1, source_target_pairs={{0,2},{1,3},{2,0},{3,1},{4,6},{5,7},{6,4},{7,5},{8,10},{9,11},{10,... | collective-permute-start | bytes 466952 | tf_op jit(solution)/shard_map/ppermute | solution.py:638
  31.7 4.1 %collective-permute-start.5 = (f32[304,128]{1,0:T(8,128)S(1)}, f32[304,128]{1,0:T(8,128)S(1)}, u32[]{:S(2)}, u32[]{:S(2)}) collective-permute-start(f32[304,128]{1,0:T(8,128)S(1)} %get-tuple-element.109.kept_ref), channel_id=1, source_target_pairs={{0,1},{1,0},{2,3},{3,2},{4,5},{5,4},{6,7},{7,6},{8,9},{9,8},{10,11... | collective-permute-start | bytes 466952 | tf_op jit(solution)/shard_map/ppermute | solution.py:638
  35.8 1.6 %collective-permute-start.6 = (f32[304,128]{1,0:T(8,128)S(1)}, f32[304,128]{1,0:T(8,128)S(1)}, u32[]{:S(2)}, u32[]{:S(2)}) collective-permute-start(f32[304,128]{1,0:T(8,128)S(1)} %collective-permute-done.4.by_x_ref), channel_id=1, source_target_pairs={{0,1},{1,0},{2,3},{3,2},{4,5},{5,4},{6,7},{7,6},{8,9},{9,8},{10,11... | collective-permute-start | bytes 466952 | tf_op jit(solution)/shard_map/ppermute | solution.py:638

commit v13 on v12

--- a/solution.py
+++ b/solution.py
@@ -493,15 +493,11 @@
         pltpu.make_async_copy(span_ref.at[:, own_lanes], spans_ref, small_sem.at[3]),
         pltpu.make_async_copy(begin_ref.at[:, own_lanes], starts_ref, small_sem.at[4]),
     ]
-
-    def part_copies(i):
-        lanes = pl.ds(i * chunk, chunk)
-        return [
-            pltpu.make_async_copy(mid_ref.at[:, lanes], mid_held_ref.at[:, lanes], parts_sem.at[0, i]),
-            pltpu.make_async_copy(low_ref.at[:, lanes], low_held_ref.at[:, lanes], parts_sem.at[1, i]),
-        ]
-
-    for copy in small_copies + [copy for i in range(full_width // chunk) for copy in part_copies(i)]:
+    part_copies = [
+        pltpu.make_async_copy(mid_ref, mid_held_ref, parts_sem.at[0]),
+        pltpu.make_async_copy(low_ref, low_held_ref, parts_sem.at[1]),
+    ]
+    for copy in small_copies + part_copies:
         copy.start()
 
     core_low = device % 2 == 0
@@ -513,10 +509,20 @@
     def by_lanes(near, far):
         return jnp.concatenate(lane_halves(near, far), axis=1)
 
-    for copy in small_copies:
+    kept_first = jnp.where(low_kept, 0, half)
+    far = far_ref[...] + pick(bins_ref, device, (half - kept_first,), (by_both_ref,), own, half)
+    spaxel_weights = dot_f32(by_lanes(near_ref[...], far), inverse, NN)
+
+    hi, mid, low = split3(spaxel_weights)
+    tiles = chunk // LANES
+    for i in range(full_width // chunk):
+        first = hi_ref[:, i * chunk : (i + 1) * chunk]
+        value = dot(hi, first, NN) + (dot(mid, first, NN) + dot(low, first, NN))
+        for t in range(tiles):
+            continuum_ref[2 * (i * tiles + t)] = value[:, t * LANES : (t + 1) * LANES]
+    for copy in small_copies + part_copies:
         copy.wait()
 
-    kept_first = jnp.where(low_kept, 0, half)
     for i in range(own_slots):
         picked_bin = owner_held_ref[0, device * own_slots + i]
         in_kept = (picked_bin >= half) == (kept_first > 0)
@@ -529,21 +535,9 @@
         mine_ref[i : i + 1, LANES:] = high
     weights_ref[...] = dot_f32(mine_ref[...], inverse, NN)
 
-    far = far_ref[...] + pick(bins_ref, device, (half - kept_first,), (by_both_ref,), own, half)
-    spaxel_weights = dot_f32(by_lanes(near_ref[...], far), inverse, NN)
-
-    hi, mid, low = split3(spaxel_weights)
-    tiles = chunk // LANES
-    for i in range(full_width // chunk):
-        first = hi_ref[:, i * chunk : (i + 1) * chunk]
-        value = dot(hi, first, NN) + (dot(mid, first, NN) + dot(low, first, NN))
-        for t in range(tiles):
-            continuum_ref[2 * (i * tiles + t)] = value[:, t * LANES : (t + 1) * LANES]
     left_half = lax.broadcasted_iota(jnp.int32, (own, LANES), 1) < LANES // 2
     before = None
     for i in range(full_width // chunk):
-        for copy in part_copies(i):
-            copy.wait()
         lanes = slice(i * chunk, (i + 1) * chunk)
         second, third = mid_held_ref[:, lanes], low_held_ref[:, lanes]
         value = dot(hi, second, NN) + (dot(mid, second, NN) + dot(hi, third, NN))
@@ -610,7 +604,7 @@
             pltpu.VMEM((lines, own), jnp.int32),
             pltpu.VMEM((lines, own), jnp.int32),
             pltpu.SMEM((lines, own), jnp.int32),
-            pltpu.SemaphoreType.DMA((2, full_width // chunk)),
+            pltpu.SemaphoreType.DMA((2,)),
             pltpu.SemaphoreType.DMA((5,)),
         ],
         compiler_params=pltpu.CompilerParams(vmem_limit_bytes=VMEM_LIMIT),

time: 45.9 us -> 43.1 us (0.939)
  Pallas kernels: 32.7 us -> 29.9 us
    pallas_call x1, Pallas kernels: 8.17 us -> 5.33 us  [owned(): pl.pallas_call(functools.partial(owner_kernel, chunk=chunk), in_specs=[pl...]
  transfers between devices with their start and end apart: 7 -> 7, of which waited for: 4 -> 4; matrix products, arithmetic and copies ran while one was open for 0% -> 0% of each run, Pallas kernels for 46% -> 49%
where the time goes in v13:
time: 43.1 us; the launch traced here: 42.8 us
  Pallas kernels  29.9 us (69%)
  starting transfers between devices  10 us (23%)
  waiting for transfers between devices  2.01 us (5%)
  between operations  0.9 us (2%)
    pallas_call x5, Pallas kernels, in_vmem(): pl.pallas_call(kernel, out_shape=shapes, compiler_params=pltpu.CompilerPa...  10.1 us
    ppermute x7, starting transfers between devices, swap(): return lax.ppermute(x, 'spax', [(d, d ^ 1 << bit) for d in range(devices)])  10 us
    pallas_call x4, Pallas kernels, cube_windows(): pl.pallas_call(functools.partial(cube_kernel, devices=devices, start=star...  5.97 us
    pallas_call x1, Pallas kernels, owned(): pl.pallas_call(functools.partial(owner_kernel, chunk=chunk), in_specs=[pl...  5.33 us
    pallas_call x1, Pallas kernels, scaled_gram(): pl.pallas_call(functools.partial(gram_kernel, chunk=chunk), in_specs=[hbm...  4.43 us
    pallas_call x1, Pallas kernels, project(): pl.pallas_call(functools.partial(project_kernel, chunk=chunk), in_specs=[...  3.58 us
    ppermute x7, waiting for transfers between devices, swap(): return lax.ppermute(x, 'spax', [(d, d ^ 1 << bit) for d in range(devices)])  2.01 us
  transfers between devices with their start and end apart: 7, of which 4 were waited for; matrix products, arithmetic and copies ran while one was open for 0% of the time, Pallas kernels for 49%

profile of v13, /device:TPU:0, one launch (start us, length us, event | category | flops | bytes accessed | tf_op | source)
XLA Modules:
  0.0 42.8 jit_solution(17168798980671133923)
XLA Ops:
  0.6 3.6 %project.1 = (f32[512,128]{1,0:T(8,128)S(1)}, f32[512,128]{1,0:T(8,128)S(1)}, s32[8,2048]{1,0:T(8,128)S(1)}, s32[8,2048]{1,0:T(8,128)S(1)}, f32[240,2048]{1,0:T(8,128)S(1)}, /*index=5*/s32[1,2048]{1,0:T(1,128)S(1)}) custom-call(s32[1]{0:T(128)} %bitcast.device_ref, s32[1,2048]{1,0:T(1,128)} %bitcast.5, s32[8,2048]{1,0:T(8,128)} %begin_ref.3, ...), custom_call_target="tpu_custom_call" | custom-call | tf_op jit(solution)/shard_map/project/pallas_call | solution.py:120
  4.2 0.5 %collective-permute-start = (f32[512,128]{1,0:T(8,128)S(1)}, f32[512,128]{1,0:T(8,128)S(1)}, u32[]{:S(2)}, u32[]{:S(2)}) collective-permute-start(f32[512,128]{1,0:T(8,128)S(1)} %get-tuple-element.66), channel_id=1, source_target_pairs={{0,1},{1,0},{2,3},{3,2},{4,5},{5,4},{6,7},{7,6},{8,9},{9,8},{10,11... | collective-permute-start | bytes 786440 | tf_op jit(solution)/shard_map/ppermute | solution.py:632
  4.7 1.1 %cube_windows.4.early_ref = f32[72,128]{1,0:T(8,128)S(1)} custom-call(s32[1]{0:T(128)} %bitcast.device_ref, s32[8,2048]{1,0:T(8,128)S(1)} %get-tuple-element.67.begin_ref, s32[8,2048]{1,0:T(8,128)S(1)} %get-tuple-element.68.span_ref, f32[240,2048]{1,0:T(8,128)S(1)} %get-tuple-element.69.cube_ref), custom_call_target="tpu_custom_call" | custom-call | tf_op jit(solution)/shard_map/cube_windows/pallas_call | solution.py:379
  5.8 0.1 collective-permute-done.y_ref
  5.9 2.9 %collective-permute-start.1 = (f32[256,128]{1,0:T(8,128)S(1)}, f32[256,128]{1,0:T(8,128)S(1)}, u32[]{:S(2)}, u32[]{:S(2)}) collective-permute-start(f32[256,128]{1,0:T(8,128)S(1)} %get-tuple-element.75), channel_id=1, source_target_pairs={{0,2},{1,3},{2,0},{3,1},{4,6},{5,7},{6,4},{7,5},{8,10},{9,11},{10,... | collective-permute-start | bytes 393224 | tf_op jit(solution)/shard_map/ppermute | solution.py:632
  8.9 1.4 %cube_windows.6.sums_ref = f32[96,128]{1,0:T(8,128)S(1)} custom-call(s32[1]{0:T(128)} %bitcast.device_ref, s32[8,2048]{1,0:T(8,128)S(1)} %get-tuple-element.67.begin_ref, s32[8,2048]{1,0:T(8,128)S(1)} %get-tuple-element.68.span_ref, f32[240,2048]{1,0:T(8,128)S(1)} %get-tuple-element.69.cube_ref), custom_call_target="tpu_custom_call" | custom-call | tf_op jit(solution)/shard_map/cube_windows/pallas_call | solution.py:379
  10.3 1.8 %cube_windows.5.late_ref = f32[120,128]{1,0:T(8,128)S(1)} custom-call(s32[1]{0:T(128)} %bitcast.device_ref, s32[8,2048]{1,0:T(8,128)S(1)} %get-tuple-element.67.begin_ref, s32[8,2048]{1,0:T(8,128)S(1)} %get-tuple-element.68.span_ref, f32[240,2048]{1,0:T(8,128)S(1)} %get-tuple-element.69.cube_ref), custom_call_target="tpu_custom_call" | custom-call | tf_op jit(solution)/shard_map/cube_windows/pallas_call | solution.py:379
  12.1 0.5 %collective-permute-done.1.y_ref = f32[256,128]{1,0:T(8,128)S(1)} collective-permute-done((f32[256,128]{1,0:T(8,128)S(1)}, f32[256,128]{1,0:T(8,128)S(1)}, u32[]{:S(2)}, u32[]{:S(2)}) %collective-permute-start.1) | collective-permute-done | bytes 131104 | tf_op jit(solution)/shard_map/ppermute | solution.py:632
  12.7 1.9 %collective-permute-start.2 = (f32[448,128]{1,0:T(8,128)S(1)}, f32[448,128]{1,0:T(8,128)S(1)}, u32[]{:S(2)}, u32[]{:S(2)}) collective-permute-start(f32[448,128]{1,0:T(8,128)S(1)} %get-tuple-element.86), channel_id=1, source_target_pairs={{0,4},{1,5},{2,6},{3,7},{4,0},{5,1},{6,2},{7,3},{8,12},{9,13},{10,... | collective-permute-start | bytes 688136 | tf_op jit(solution)/shard_map/ppermute | solution.py:632
  14.6 4.4 %gram.1 = (f32[256,256]{1,0:T(8,128)S(1)}, f32[1,256]{1,0:T(1,128)S(1)}, bf16[256,3584]{1,0:T(8,128)(2,1)S(1)}, bf16[256,3584]{1,0:T(8,128)(2,1)}, bf16[256,3584]{1,0:T(8,128)(2,1)}) custom-call(f32[256,3584]{1,0:T(8,128)} %templates_ref.2), custom_call_target="tpu_custom_call" | custom-call | tf_op jit(solution)/shard_map/gram/pallas_call | solution.py:257
  19.0 0.9 %collective-permute-done.2.y_ref = f32[448,128]{1,0:T(8,128)S(1)} collective-permute-done((f32[448,128]{1,0:T(8,128)S(1)}, f32[448,128]{1,0:T(8,128)S(1)}, u32[]{:S(2)}, u32[]{:S(2)}) %collective-permute-start.2) | collective-permute-done | bytes 229408 | tf_op jit(solution)/shard_map/ppermute | solution.py:632
  19.9 2.6 %collective-permute-start.3 = (f32[352,128]{1,0:T(8,128)S(1)}, f32[352,128]{1,0:T(8,128)S(1)}, u32[]{:S(2)}, u32[]{:S(2)}) collective-permute-start(f32[352,128]{1,0:T(8,128)S(1)} %get-tuple-element.96), channel_id=1, source_target_pairs={{0,8},{1,9},{2,10},{3,11},{4,12},{5,13},{6,14},{7,15},{8,0},{9,1},... | collective-permute-start | bytes 540680 | tf_op jit(solution)/shard_map/ppermute | solution.py:632
  22.5 1.6 %cube_windows.7.sums_ref = f32[96,128]{1,0:T(8,128)S(1)} custom-call(s32[1]{0:T(128)} %bitcast.device_ref, s32[8,2048]{1,0:T(8,128)S(1)} %get-tuple-element.67.begin_ref, s32[8,2048]{1,0:T(8,128)S(1)} %get-tuple-element.68.span_ref, f32[240,2048]{1,0:T(8,128)S(1)} %get-tuple-element.69.cube_ref), custom_call_target="tpu_custom_call" | custom-call | tf_op jit(solution)/shard_map/cube_windows/pallas_call | solution.py:379
  24.1 6.0 %first.1 = (f32[128,128]{1,0:T(8,128)S(1)}, f32[128,128]{1,0:T(8,128)S(1)}, f32[128,128]{1,0:T(8,128)S(1)}) custom-call(f32[256,256]{1,0:T(8,128)S(1)} %get-tuple-element.98.gram_ref), custom_call_target="tpu_custom_call" | custom-call | tf_op jit(solution)/shard_map/first/pallas_call | solution.py:307
  30.1 0.0 collective-permute-done.3.y_ref
  30.1 1.6 %collective-permute-start.4 = (f32[304,128]{1,0:T(8,128)S(1)}, f32[304,128]{1,0:T(8,128)S(1)}, u32[]{:S(2)}, u32[]{:S(2)}) collective-permute-start(f32[304,128]{1,0:T(8,128)S(1)} %get-tuple-element.110), channel_id=1, source_target_pairs={{0,2},{1,3},{2,0},{3,1},{4,6},{5,7},{6,4},{7,5},{8,10},{9,11},{10,... | collective-permute-start | bytes 466952 | tf_op jit(solution)/shard_map/ppermute | solution.py:632
  31.7 0.0 collective-permute-start.5
  31.7 4.0 %finish.1.inverse_ref = f32[256,256]{1,0:T(8,128)S(1)} custom-call(f32[128,128]{1,0:T(8,128)S(1)} %get-tuple-element.111.first_ref, f32[128,128]{1,0:T(8,128)S(1)} %get-tuple-element.112.half_ref, f32[128,128]{1,0:T(8,128)S(1)} %get-tuple-element.113.second_ref, f32[1,256]{1,0:T(1,128)S(1)} %get-tuple-element.114.scale_ref), custom_call_target="tpu_custom_call" | custom-call | tf_op jit(solution)/shard_map/finish/pallas_call | solution.py:307
  35.7 0.0 collective-permute-done.4.by_x_ref
  35.8 0.0 collective-permute-done.5.by_core_ref
  35.8 0.6 %collective-permute-start.6 = (f32[304,128]{1,0:T(8,128)S(1)}, f32[304,128]{1,0:T(8,128)S(1)}, u32[]{:S(2)}, u32[]{:S(2)}) collective-permute-start(f32[304,128]{1,0:T(8,128)S(1)} %collective-permute-done.4.by_x_ref), channel_id=1, source_target_pairs={{0,1},{1,0},{2,3},{3,2},{4,5},{5,4},{6,7},{7,6},{8,9},{9,8},{10,11... | collective-permute-start | bytes 466952 | tf_op jit(solution)/shard_map/ppermute | solution.py:632
  36.3 0.5 %pick_early.1 = (f32[128,128]{1,0:T(8,128)S(1)}, f32[128,128]{1,0:T(8,128)S(1)}) custom-call(s32[1]{0:T(128)} %bitcast.device_ref, s32[1,2048]{1,0:T(1,128)S(1)} %get-tuple-element.64.bins_ref, f32[304,128]{1,0:T(8,128)S(1)} %get-tuple-element.109.kept_ref, f32[304,128]{1,0:T(8,128)S(1)} %collective-permute-done.4.by_x_ref, ...), custom_call_target="tpu_custom_call" | custom-call | tf_op jit(solution)/shard_map/pick_early/pallas_call | solution.py:465
  36.8 0.5 %collective-permute-done.6.by_both_ref = f32[304,128]{1,0:T(8,128)S(1)} collective-permute-done((f32[304,128]{1,0:T(8,128)S(1)}, f32[304,128]{1,0:T(8,128)S(1)}, u32[]{:S(2)}, u32[]{:S(2)}) %collective-permute-start.6) | collective-permute-done | bytes 155680 | tf_op jit(solution)/shard_map/ppermute | solution.py:632
  37.4 5.3 %owned.1 = (f32[32,256]{1,0:T(8,128)}, f32[24,128]{1,0:T(8,128)}) custom-call(s32[1]{0:T(128)} %bitcast.device_ref, s32[1,2048]{1,0:T(1,128)S(1)} %get-tuple-element.64.bins_ref, s32[1,512]{1,0:T(1,128)} %bitcast.6, s32[8,2048]{1,0:T(8,128)} %begin_ref.3, s32[8,2048]{1,0:T(8,128)} %span_ref.3, f32[304,128]{1,0:T(8,128)S(1)} %get-tuple-element.109.kept_ref, ...), custom_call_target="tpu_custom_call" | custom-call | tf_op jit(solution)/shard_map/owned/pallas_call | solution.py:591
  (4 shorter events, 0.1 us)
Async XLA Ops:
  4.2 1.7 %collective-permute-start = (f32[512,128]{1,0:T(8,128)S(1)}, f32[512,128]{1,0:T(8,128)S(1)}, u32[]{:S(2)}, u32[]{:S(2)}) collective-permute-start(f32[512,128]{1,0:T(8,128)S(1)} %get-tuple-element.66), channel_id=1, source_target_pairs={{0,1},{1,0},{2,3},{3,2},{4,5},{5,4},{6,7},{7,6},{8,9},{9,8},{10,11... | collective-permute-start | bytes 786440 | tf_op jit(solution)/shard_map/ppermute | solution.py:632
  5.9 6.7 %collective-permute-start.1 = (f32[256,128]{1,0:T(8,128)S(1)}, f32[256,128]{1,0:T(8,128)S(1)}, u32[]{:S(2)}, u32[]{:S(2)}) collective-permute-start(f32[256,128]{1,0:T(8,128)S(1)} %get-tuple-element.75), channel_id=1, source_target_pairs={{0,2},{1,3},{2,0},{3,1},{4,6},{5,7},{6,4},{7,5},{8,10},{9,11},{10,... | collective-permute-start | bytes 393224 | tf_op jit(solution)/shard_map/ppermute | solution.py:632
  12.7 7.2 %collective-permute-start.2 = (f32[448,128]{1,0:T(8,128)S(1)}, f32[448,128]{1,0:T(8,128)S(1)}, u32[]{:S(2)}, u32[]{:S(2)}) collective-permute-start(f32[448,128]{1,0:T(8,128)S(1)} %get-tuple-element.86), channel_id=1, source_target_pairs={{0,4},{1,5},{2,6},{3,7},{4,0},{5,1},{6,2},{7,3},{8,12},{9,13},{10,... | collective-permute-start | bytes 688136 | tf_op jit(solution)/shard_map/ppermute | solution.py:632
  19.9 10.2 %collective-permute-start.3 = (f32[352,128]{1,0:T(8,128)S(1)}, f32[352,128]{1,0:T(8,128)S(1)}, u32[]{:S(2)}, u32[]{:S(2)}) collective-permute-start(f32[352,128]{1,0:T(8,128)S(1)} %get-tuple-element.96), channel_id=1, source_target_pairs={{0,8},{1,9},{2,10},{3,11},{4,12},{5,13},{6,14},{7,15},{8,0},{9,1},... | collective-permute-start | bytes 540680 | tf_op jit(solution)/shard_map/ppermute | solution.py:632
  30.1 5.6 %collective-permute-start.4 = (f32[304,128]{1,0:T(8,128)S(1)}, f32[304,128]{1,0:T(8,128)S(1)}, u32[]{:S(2)}, u32[]{:S(2)}) collective-permute-start(f32[304,128]{1,0:T(8,128)S(1)} %get-tuple-element.110), channel_id=1, source_target_pairs={{0,2},{1,3},{2,0},{3,1},{4,6},{5,7},{6,4},{7,5},{8,10},{9,11},{10,... | collective-permute-start | bytes 466952 | tf_op jit(solution)/shard_map/ppermute | solution.py:632
  31.7 4.1 %collective-permute-start.5 = (f32[304,128]{1,0:T(8,128)S(1)}, f32[304,128]{1,0:T(8,128)S(1)}, u32[]{:S(2)}, u32[]{:S(2)}) collective-permute-start(f32[304,128]{1,0:T(8,128)S(1)} %get-tuple-element.109.kept_ref), channel_id=1, source_target_pairs={{0,1},{1,0},{2,3},{3,2},{4,5},{5,4},{6,7},{7,6},{8,9},{9,8},{10,11... | collective-permute-start | bytes 466952 | tf_op jit(solution)/shard_map/ppermute | solution.py:632
  35.8 1.6 %collective-permute-start.6 = (f32[304,128]{1,0:T(8,128)S(1)}, f32[304,128]{1,0:T(8,128)S(1)}, u32[]{:S(2)}, u32[]{:S(2)}) collective-permute-start(f32[304,128]{1,0:T(8,128)S(1)} %collective-permute-done.4.by_x_ref), channel_id=1, source_target_pairs={{0,1},{1,0},{2,3},{3,2},{4,5},{5,4},{6,7},{7,6},{8,9},{9,8},{10,11... | collective-permute-start | bytes 466952 | tf_op jit(solution)/shard_map/ppermute | solution.py:632

commit v14 on v13

--- a/solution.py
+++ b/solution.py
@@ -519,7 +519,7 @@
         first = hi_ref[:, i * chunk : (i + 1) * chunk]
         value = dot(hi, first, NN) + (dot(mid, first, NN) + dot(low, first, NN))
         for t in range(tiles):
-            continuum_ref[2 * (i * tiles + t)] = value[:, t * LANES : (t + 1) * LANES]
+            continuum_ref[i * tiles + t] = value[:, t * LANES : (t + 1) * LANES]
     for copy in small_copies + part_copies:
         copy.wait()
 
@@ -535,43 +535,44 @@
         mine_ref[i : i + 1, LANES:] = high
     weights_ref[...] = dot_f32(mine_ref[...], inverse, NN)
 
-    left_half = lax.broadcasted_iota(jnp.int32, (own, LANES), 1) < LANES // 2
-    before = None
     for i in range(full_width // chunk):
         lanes = slice(i * chunk, (i + 1) * chunk)
         second, third = mid_held_ref[:, lanes], low_held_ref[:, lanes]
         value = dot(hi, second, NN) + (dot(mid, second, NN) + dot(hi, third, NN))
         for t in range(tiles):
-            at = 2 * (i * tiles + t)
-            tile = continuum_ref[at] + value[:, t * LANES : (t + 1) * LANES]
-            continuum_ref[at] = tile
-            turned = pltpu.roll(tile, LANES // 2, 1)
-            if at:
-                continuum_ref[at - 1] = jnp.where(left_half, before, turned)
-            before = turned
-    continuum_ref[2 * (full_width // LANES) - 1] = jnp.where(left_half, before, 0.0)
+            continuum_ref[i * tiles + t] += value[:, t * LANES : (t + 1) * LANES]
+    continuum_ref[full_width // LANES] = jnp.zeros((own, LANES), F32)
 
     begin = begins_ref[...]
     span = spans_ref[...].astype(F32)
-    centre = 2.0 * (begin & (LANES // 2 - 1)).astype(F32) + span - 1.0
+    centre = 2.0 * (begin & (LANES - 1)).astype(F32) + span - 1.0
     rows_at = lax.broadcasted_iota(jnp.int32, (SUB, LANES), 0)
     at_row = [rows_at == r for r in range(SUB)]
     twice = 2.0 * lax.broadcasted_iota(jnp.int32, (LANES, own), 0).astype(F32)
     sums = [None] * (3 * lines)
     for j in range(lines):
-        picks = []
+        picks = ([], [])
         for g in range(own // SUB):
             rows = slice(g * SUB, (g + 1) * SUB)
-            block = None
+            left = right = None
             for r in range(SUB):
-                tile = continuum_ref[lax.shift_right_logical(starts_ref[j, g * SUB + r], 6), rows, :]
-                block = tile if block is None else jnp.where(at_row[r], tile, block)
-            picks.append(block)
-        m = twice - centre[j : j + 1]
-        masked = jnp.where(jnp.abs(m) < span[j : j + 1], jnp.concatenate(picks, axis=0).T, 0.0)
-        weighted = masked * m
-        for k, term in enumerate((masked, weighted, weighted * m)):
-            sums[k * lines + j] = jnp.sum(term, axis=0, keepdims=True)
+                tile = lax.shift_right_logical(starts_ref[j, g * SUB + r], 7)
+                a = continuum_ref[tile, rows, :]
+                b = continuum_ref[tile + 1, rows, :]
+                left = a if left is None else jnp.where(at_row[r], a, left)
+                right = b if right is None else jnp.where(at_row[r], b, right)
+            picks[0].append(left)
+            picks[1].append(right)
+        terms = None
+        for side in range(2):
+            block = jnp.concatenate(picks[side], axis=0).T
+            m = twice + (2.0 * LANES * side - centre[j : j + 1])
+            masked = jnp.where(jnp.abs(m) < span[j : j + 1], block, 0.0)
+            weighted = masked * m
+            new = [masked, weighted, weighted * m]
+            terms = new if terms is None else [x + y for x, y in zip(terms, new)]
+        for k in range(3):
+            sums[k * lines + j] = jnp.sum(terms[k], axis=0, keepdims=True)
     continuum_sums = jnp.concatenate(sums, axis=0)
 
     own_rows = slice(half, half + 3 * lines)
@@ -596,7 +597,7 @@
             jax.ShapeDtypeStruct((3 * lines, own), F32),
         ),
         scratch_shapes=[
-            pltpu.VMEM((2 * (full_width // LANES), own, LANES), F32),
+            pltpu.VMEM((full_width // LANES + 1, own, LANES), F32),
             pltpu.VMEM((own_slots, count), F32),
             pltpu.VMEM((count, full_width), BF16),
             pltpu.VMEM((count, full_width), BF16),

time: 43.1 us -> 43 us (level)
  no operation moved by 1% of the time
where the time goes in v14:
time: 43 us; the launch traced here: 42.8 us
  Pallas kernels  29.8 us (69%)
  starting transfers between devices  10 us (23%)
  waiting for transfers between devices  2.01 us (5%)
  between operations  0.9 us (2%)
    pallas_call x5, Pallas kernels, in_vmem(): pl.pallas_call(kernel, out_shape=shapes, compiler_params=pltpu.CompilerPa...  10.1 us
    ppermute x7, starting transfers between devices, swap(): return lax.ppermute(x, 'spax', [(d, d ^ 1 << bit) for d in range(devices)])  10 us
    pallas_call x4, Pallas kernels, cube_windows(): pl.pallas_call(functools.partial(cube_kernel, devices=devices, start=star...  5.97 us
    pallas_call x1, Pallas kernels, owned(): pl.pallas_call(functools.partial(owner_kernel, chunk=chunk), in_specs=[pl...  5.24 us
    pallas_call x1, Pallas kernels, scaled_gram(): pl.pallas_call(functools.partial(gram_kernel, chunk=chunk), in_specs=[hbm...  4.44 us
    pallas_call x1, Pallas kernels, project(): pl.pallas_call(functools.partial(project_kernel, chunk=chunk), in_specs=[...  3.61 us
    ppermute x7, waiting for transfers between devices, swap(): return lax.ppermute(x, 'spax', [(d, d ^ 1 << bit) for d in range(devices)])  2.01 us
  transfers between devices with their start and end apart: 7, of which 4 were waited for; matrix products, arithmetic and copies ran while one was open for 0% of the time, Pallas kernels for 49%

profile of v14, /device:TPU:0, one launch (start us, length us, event | category | flops | bytes accessed | tf_op | source)
XLA Modules:
  0.0 42.8 jit_solution(11769135103016101178)
XLA Ops:
  0.6 3.6 %project.1 = (f32[512,128]{1,0:T(8,128)S(1)}, f32[512,128]{1,0:T(8,128)S(1)}, s32[8,2048]{1,0:T(8,128)S(1)}, s32[8,2048]{1,0:T(8,128)S(1)}, f32[240,2048]{1,0:T(8,128)S(1)}, /*index=5*/s32[1,2048]{1,0:T(1,128)S(1)}) custom-call(s32[1]{0:T(128)} %bitcast.device_ref, s32[1,2048]{1,0:T(1,128)} %bitcast.5, s32[8,2048]{1,0:T(8,128)} %begin_ref.3, ...), custom_call_target="tpu_custom_call" | custom-call | tf_op jit(solution)/shard_map/project/pallas_call | solution.py:120
  4.2 0.5 %collective-permute-start = (f32[512,128]{1,0:T(8,128)S(1)}, f32[512,128]{1,0:T(8,128)S(1)}, u32[]{:S(2)}, u32[]{:S(2)}) collective-permute-start(f32[512,128]{1,0:T(8,128)S(1)} %get-tuple-element.66), channel_id=1, source_target_pairs={{0,1},{1,0},{2,3},{3,2},{4,5},{5,4},{6,7},{7,6},{8,9},{9,8},{10,11... | collective-permute-start | bytes 786440 | tf_op jit(solution)/shard_map/ppermute | solution.py:633
  4.8 1.1 %cube_windows.4.early_ref = f32[72,128]{1,0:T(8,128)S(1)} custom-call(s32[1]{0:T(128)} %bitcast.device_ref, s32[8,2048]{1,0:T(8,128)S(1)} %get-tuple-element.67.begin_ref, s32[8,2048]{1,0:T(8,128)S(1)} %get-tuple-element.68.span_ref, f32[240,2048]{1,0:T(8,128)S(1)} %get-tuple-element.69.cube_ref), custom_call_target="tpu_custom_call" | custom-call | tf_op jit(solution)/shard_map/cube_windows/pallas_call | solution.py:379
  5.9 0.1 collective-permute-done.y_ref
  6.0 2.9 %collective-permute-start.1 = (f32[256,128]{1,0:T(8,128)S(1)}, f32[256,128]{1,0:T(8,128)S(1)}, u32[]{:S(2)}, u32[]{:S(2)}) collective-permute-start(f32[256,128]{1,0:T(8,128)S(1)} %get-tuple-element.75), channel_id=1, source_target_pairs={{0,2},{1,3},{2,0},{3,1},{4,6},{5,7},{6,4},{7,5},{8,10},{9,11},{10,... | collective-permute-start | bytes 393224 | tf_op jit(solution)/shard_map/ppermute | solution.py:633
  8.9 1.4 %cube_windows.6.sums_ref = f32[96,128]{1,0:T(8,128)S(1)} custom-call(s32[1]{0:T(128)} %bitcast.device_ref, s32[8,2048]{1,0:T(8,128)S(1)} %get-tuple-element.67.begin_ref, s32[8,2048]{1,0:T(8,128)S(1)} %get-tuple-element.68.span_ref, f32[240,2048]{1,0:T(8,128)S(1)} %get-tuple-element.69.cube_ref), custom_call_target="tpu_custom_call" | custom-call | tf_op jit(solution)/shard_map/cube_windows/pallas_call | solution.py:379
  10.3 1.8 %cube_windows.5.late_ref = f32[120,128]{1,0:T(8,128)S(1)} custom-call(s32[1]{0:T(128)} %bitcast.device_ref, s32[8,2048]{1,0:T(8,128)S(1)} %get-tuple-element.67.begin_ref, s32[8,2048]{1,0:T(8,128)S(1)} %get-tuple-element.68.span_ref, f32[240,2048]{1,0:T(8,128)S(1)} %get-tuple-element.69.cube_ref), custom_call_target="tpu_custom_call" | custom-call | tf_op jit(solution)/shard_map/cube_windows/pallas_call | solution.py:379
  12.2 0.5 %collective-permute-done.1.y_ref = f32[256,128]{1,0:T(8,128)S(1)} collective-permute-done((f32[256,128]{1,0:T(8,128)S(1)}, f32[256,128]{1,0:T(8,128)S(1)}, u32[]{:S(2)}, u32[]{:S(2)}) %collective-permute-start.1) | collective-permute-done | bytes 131104 | tf_op jit(solution)/shard_map/ppermute | solution.py:633
  12.7 1.9 %collective-permute-start.2 = (f32[448,128]{1,0:T(8,128)S(1)}, f32[448,128]{1,0:T(8,128)S(1)}, u32[]{:S(2)}, u32[]{:S(2)}) collective-permute-start(f32[448,128]{1,0:T(8,128)S(1)} %get-tuple-element.86), channel_id=1, source_target_pairs={{0,4},{1,5},{2,6},{3,7},{4,0},{5,1},{6,2},{7,3},{8,12},{9,13},{10,... | collective-permute-start | bytes 688136 | tf_op jit(solution)/shard_map/ppermute | solution.py:633
  14.6 4.4 %gram.1 = (f32[256,256]{1,0:T(8,128)S(1)}, f32[1,256]{1,0:T(1,128)S(1)}, bf16[256,3584]{1,0:T(8,128)(2,1)S(1)}, bf16[256,3584]{1,0:T(8,128)(2,1)}, bf16[256,3584]{1,0:T(8,128)(2,1)}) custom-call(f32[256,3584]{1,0:T(8,128)} %templates_ref.2), custom_call_target="tpu_custom_call" | custom-call | tf_op jit(solution)/shard_map/gram/pallas_call | solution.py:257
  19.0 0.9 %collective-permute-done.2.y_ref = f32[448,128]{1,0:T(8,128)S(1)} collective-permute-done((f32[448,128]{1,0:T(8,128)S(1)}, f32[448,128]{1,0:T(8,128)S(1)}, u32[]{:S(2)}, u32[]{:S(2)}) %collective-permute-start.2) | collective-permute-done | bytes 229408 | tf_op jit(solution)/shard_map/ppermute | solution.py:633
  19.9 2.6 %collective-permute-start.3 = (f32[352,128]{1,0:T(8,128)S(1)}, f32[352,128]{1,0:T(8,128)S(1)}, u32[]{:S(2)}, u32[]{:S(2)}) collective-permute-start(f32[352,128]{1,0:T(8,128)S(1)} %get-tuple-element.96), channel_id=1, source_target_pairs={{0,8},{1,9},{2,10},{3,11},{4,12},{5,13},{6,14},{7,15},{8,0},{9,1},... | collective-permute-start | bytes 540680 | tf_op jit(solution)/shard_map/ppermute | solution.py:633
  22.5 1.6 %cube_windows.7.sums_ref = f32[96,128]{1,0:T(8,128)S(1)} custom-call(s32[1]{0:T(128)} %bitcast.device_ref, s32[8,2048]{1,0:T(8,128)S(1)} %get-tuple-element.67.begin_ref, s32[8,2048]{1,0:T(8,128)S(1)} %get-tuple-element.68.span_ref, f32[240,2048]{1,0:T(8,128)S(1)} %get-tuple-element.69.cube_ref), custom_call_target="tpu_custom_call" | custom-call | tf_op jit(solution)/shard_map/cube_windows/pallas_call | solution.py:379
  24.2 6.0 %first.1 = (f32[128,128]{1,0:T(8,128)S(1)}, f32[128,128]{1,0:T(8,128)S(1)}, f32[128,128]{1,0:T(8,128)S(1)}) custom-call(f32[256,256]{1,0:T(8,128)S(1)} %get-tuple-element.98.gram_ref), custom_call_target="tpu_custom_call" | custom-call | tf_op jit(solution)/shard_map/first/pallas_call | solution.py:307
  30.1 0.0 collective-permute-done.3.y_ref
  30.2 1.6 %collective-permute-start.4 = (f32[304,128]{1,0:T(8,128)S(1)}, f32[304,128]{1,0:T(8,128)S(1)}, u32[]{:S(2)}, u32[]{:S(2)}) collective-permute-start(f32[304,128]{1,0:T(8,128)S(1)} %get-tuple-element.110), channel_id=1, source_target_pairs={{0,2},{1,3},{2,0},{3,1},{4,6},{5,7},{6,4},{7,5},{8,10},{9,11},{10,... | collective-permute-start | bytes 466952 | tf_op jit(solution)/shard_map/ppermute | solution.py:633
  31.7 0.0 collective-permute-start.5
  31.7 4.0 %finish.1.inverse_ref = f32[256,256]{1,0:T(8,128)S(1)} custom-call(f32[128,128]{1,0:T(8,128)S(1)} %get-tuple-element.111.first_ref, f32[128,128]{1,0:T(8,128)S(1)} %get-tuple-element.112.half_ref, f32[128,128]{1,0:T(8,128)S(1)} %get-tuple-element.113.second_ref, f32[1,256]{1,0:T(1,128)S(1)} %get-tuple-element.114.scale_ref), custom_call_target="tpu_custom_call" | custom-call | tf_op jit(solution)/shard_map/finish/pallas_call | solution.py:307
  35.8 0.0 collective-permute-done.4.by_x_ref
  35.8 0.0 collective-permute-done.5.by_core_ref
  35.8 0.6 %collective-permute-start.6 = (f32[304,128]{1,0:T(8,128)S(1)}, f32[304,128]{1,0:T(8,128)S(1)}, u32[]{:S(2)}, u32[]{:S(2)}) collective-permute-start(f32[304,128]{1,0:T(8,128)S(1)} %collective-permute-done.4.by_x_ref), channel_id=1, source_target_pairs={{0,1},{1,0},{2,3},{3,2},{4,5},{5,4},{6,7},{7,6},{8,9},{9,8},{10,11... | collective-permute-start | bytes 466952 | tf_op jit(solution)/shard_map/ppermute | solution.py:633
  36.4 0.5 %pick_early.1 = (f32[128,128]{1,0:T(8,128)S(1)}, f32[128,128]{1,0:T(8,128)S(1)}) custom-call(s32[1]{0:T(128)} %bitcast.device_ref, s32[1,2048]{1,0:T(1,128)S(1)} %get-tuple-element.64.bins_ref, f32[304,128]{1,0:T(8,128)S(1)} %get-tuple-element.109.kept_ref, f32[304,128]{1,0:T(8,128)S(1)} %collective-permute-done.4.by_x_ref, ...), custom_call_target="tpu_custom_call" | custom-call | tf_op jit(solution)/shard_map/pick_early/pallas_call | solution.py:465
  36.8 0.5 %collective-permute-done.6.by_both_ref = f32[304,128]{1,0:T(8,128)S(1)} collective-permute-done((f32[304,128]{1,0:T(8,128)S(1)}, f32[304,128]{1,0:T(8,128)S(1)}, u32[]{:S(2)}, u32[]{:S(2)}) %collective-permute-start.6) | collective-permute-done | bytes 155680 | tf_op jit(solution)/shard_map/ppermute | solution.py:633
  37.4 5.2 %owned.1 = (f32[32,256]{1,0:T(8,128)}, f32[24,128]{1,0:T(8,128)}) custom-call(s32[1]{0:T(128)} %bitcast.device_ref, s32[1,2048]{1,0:T(1,128)S(1)} %get-tuple-element.64.bins_ref, s32[1,512]{1,0:T(1,128)} %bitcast.6, s32[8,2048]{1,0:T(8,128)} %begin_ref.3, s32[8,2048]{1,0:T(8,128)} %span_ref.3, f32[304,128]{1,0:T(8,128)S(1)} %get-tuple-element.109.kept_ref, ...), custom_call_target="tpu_custom_call" | custom-call | tf_op jit(solution)/shard_map/owned/pallas_call | solution.py:592
  (4 shorter events, 0.1 us)
Async XLA Ops:
  4.2 1.7 %collective-permute-start = (f32[512,128]{1,0:T(8,128)S(1)}, f32[512,128]{1,0:T(8,128)S(1)}, u32[]{:S(2)}, u32[]{:S(2)}) collective-permute-start(f32[512,128]{1,0:T(8,128)S(1)} %get-tuple-element.66), channel_id=1, source_target_pairs={{0,1},{1,0},{2,3},{3,2},{4,5},{5,4},{6,7},{7,6},{8,9},{9,8},{10,11... | collective-permute-start | bytes 786440 | tf_op jit(solution)/shard_map/ppermute | solution.py:633
  6.0 6.7 %collective-permute-start.1 = (f32[256,128]{1,0:T(8,128)S(1)}, f32[256,128]{1,0:T(8,128)S(1)}, u32[]{:S(2)}, u32[]{:S(2)}) collective-permute-start(f32[256,128]{1,0:T(8,128)S(1)} %get-tuple-element.75), channel_id=1, source_target_pairs={{0,2},{1,3},{2,0},{3,1},{4,6},{5,7},{6,4},{7,5},{8,10},{9,11},{10,... | collective-permute-start | bytes 393224 | tf_op jit(solution)/shard_map/ppermute | solution.py:633
  12.7 7.2 %collective-permute-start.2 = (f32[448,128]{1,0:T(8,128)S(1)}, f32[448,128]{1,0:T(8,128)S(1)}, u32[]{:S(2)}, u32[]{:S(2)}) collective-permute-start(f32[448,128]{1,0:T(8,128)S(1)} %get-tuple-element.86), channel_id=1, source_target_pairs={{0,4},{1,5},{2,6},{3,7},{4,0},{5,1},{6,2},{7,3},{8,12},{9,13},{10,... | collective-permute-start | bytes 688136 | tf_op jit(solution)/shard_map/ppermute | solution.py:633
  19.9 10.2 %collective-permute-start.3 = (f32[352,128]{1,0:T(8,128)S(1)}, f32[352,128]{1,0:T(8,128)S(1)}, u32[]{:S(2)}, u32[]{:S(2)}) collective-permute-start(f32[352,128]{1,0:T(8,128)S(1)} %get-tuple-element.96), channel_id=1, source_target_pairs={{0,8},{1,9},{2,10},{3,11},{4,12},{5,13},{6,14},{7,15},{8,0},{9,1},... | collective-permute-start | bytes 540680 | tf_op jit(solution)/shard_map/ppermute | solution.py:633
  30.2 5.6 %collective-permute-start.4 = (f32[304,128]{1,0:T(8,128)S(1)}, f32[304,128]{1,0:T(8,128)S(1)}, u32[]{:S(2)}, u32[]{:S(2)}) collective-permute-start(f32[304,128]{1,0:T(8,128)S(1)} %get-tuple-element.110), channel_id=1, source_target_pairs={{0,2},{1,3},{2,0},{3,1},{4,6},{5,7},{6,4},{7,5},{8,10},{9,11},{10,... | collective-permute-start | bytes 466952 | tf_op jit(solution)/shard_map/ppermute | solution.py:633
  31.7 4.1 %collective-permute-start.5 = (f32[304,128]{1,0:T(8,128)S(1)}, f32[304,128]{1,0:T(8,128)S(1)}, u32[]{:S(2)}, u32[]{:S(2)}) collective-permute-start(f32[304,128]{1,0:T(8,128)S(1)} %get-tuple-element.109.kept_ref), channel_id=1, source_target_pairs={{0,1},{1,0},{2,3},{3,2},{4,5},{5,4},{6,7},{7,6},{8,9},{9,8},{10,11... | collective-permute-start | bytes 466952 | tf_op jit(solution)/shard_map/ppermute | solution.py:633
  35.8 1.6 %collective-permute-start.6 = (f32[304,128]{1,0:T(8,128)S(1)}, f32[304,128]{1,0:T(8,128)S(1)}, u32[]{:S(2)}, u32[]{:S(2)}) collective-permute-start(f32[304,128]{1,0:T(8,128)S(1)} %collective-permute-done.4.by_x_ref), channel_id=1, source_target_pairs={{0,1},{1,0},{2,3},{3,2},{4,5},{5,4},{6,7},{7,6},{8,9},{9,8},{10,11... | collective-permute-start | bytes 466952 | tf_op jit(solution)/shard_map/ppermute | solution.py:633
